TPU v7x, 128 devices: a whole 4x4x4 slice. The times are simulated.
128 devices in a mesh: clu: 16 (over y, x_lo, core), sta: 8 (over z, x_hi).
Axes of the slice: x: 4 (x_hi: 2, x_lo: 2; x = x_hi * 2 + x_lo), y: 4, z: 4, core: 2. Of those that a mesh axis runs over, the one named last changes fastest.
Arguments:
- waves: bfloat16 [4096, 48, 256], P('clu', 'sta'), may hold values from -1000 to 1000, as said below
- owners: int32 [4], replicated, may hold values from 0 to 15
- neighbours: int32 [16, 4], P('clu'), may hold values 0 or 1
- pair_local: int32 [16, 4, 512], P('clu'), may hold values from 0 to 63
- pair_remote: int32 [16, 4, 512], P('clu'), may hold values from 0 to 255
Outputs:
- correlation: float32 [16, 4, 65, 512], P('clu', None, None, 'sta')
Inputs may be any that keep to these rules, and one draw needn't show every extreme that they name: `waves`: Real-valued waveforms.
All inputs are finite; a program needn't handle non-finite values. No bound on the sum of `neighbours` on one device may be relied on, other than what follows from the above.
Results may differ from a plain program's by a relative error of at most 0.0003.
Values may be sent and summed in bfloat16 or wider, within the bound.
No kernel may reach another device: no remote copies, remote signals or barrier semaphores. Data moves between devices by JAX's collectives and lax.ppermute only.
A program may use at most 192 MiB of HBM per device.

v0:
```python
import math

import jax
import jax.numpy as jnp
from jax import lax
from jax.sharding import PartitionSpec as P

CH = 48
SAMP = 256
HALF = 32


def broadcast(x, axis, root):
    mine = lax.axis_index(axis) == root
    return lax.psum(jnp.where(mine, x, jnp.zeros_like(x)), axis)


def spectra(block_waves, table):
    rows, channels, samples = block_waves.shape
    flat = block_waves.reshape(rows * channels, samples).astype(jnp.float32)
    result = jnp.dot(
        flat, table, precision=lax.Precision.HIGHEST, preferred_element_type=jnp.float32
    )
    return result.reshape(rows, channels, table.shape[1])


def local(waves, owners, neighbours, pair_local, pair_remote):
    ev_count, ch_count, samples = waves.shape
    steps = owners.shape[0]
    block = ev_count // steps
    pairs = pair_local.shape[2]
    lags = 2 * HALF + 1
    length = (samples + HALF + 127) // 128 * 128
    sample_index = jnp.arange(samples, dtype=jnp.int32)
    freq_index = jnp.arange(length, dtype=jnp.int32)
    forward_angle = (
        2.0
        * math.pi
        / length
        * (sample_index[:, None] * freq_index[None, :] % length).astype(jnp.float32)
    )
    forward_table = jnp.concatenate([jnp.cos(forward_angle), jnp.sin(forward_angle)], axis=1)
    lag_shift = (jnp.arange(lags, dtype=jnp.int32) - HALF) % length
    inverse_angle = (
        2.0
        * math.pi
        / length
        * (lag_shift[:, None] * freq_index[None, :] % length).astype(jnp.float32)
    )
    inverse_table = (
        jnp.concatenate([jnp.cos(inverse_angle), -jnp.sin(inverse_angle)], axis=1) / length
    )
    local_part = jnp.sum(jnp.square(waves.astype(jnp.float32)), axis=(1, 2))
    local_spec = spectra(waves, forward_table)
    remote_parts = []
    raw_steps = []
    for step in range(steps):
        remote = broadcast(waves, "clu", owners[step])
        remote_parts.append(jnp.sum(jnp.square(remote.astype(jnp.float32)), axis=(1, 2)))
        remote_spec = spectra(remote, forward_table)
        left = jnp.take(local_spec, step * block + pair_local[0, step], axis=0)
        right = jnp.take(remote_spec, pair_remote[0, step], axis=0)
        left_cos, left_sin = (left[..., :length], left[..., length:])
        right_cos, right_sin = (right[..., :length], right[..., length:])
        real_part = jnp.sum(left_cos * right_cos + left_sin * right_sin, axis=1)
        imag_part = jnp.sum(left_sin * right_cos - left_cos * right_sin, axis=1)
        joined = jnp.concatenate([real_part, imag_part], axis=1)
        raw_steps.append(
            jnp.einsum(
                "lf,pf->lp",
                inverse_table,
                joined,
                precision=lax.Precision.HIGHEST,
                preferred_element_type=jnp.float32,
            )
        )
    raw = jnp.stack(raw_steps, axis=0)
    local_total, remote_total = lax.psum((local_part, jnp.stack(remote_parts, axis=0)), "sta")
    local_scale = 1.0 / jnp.sqrt(local_total / (CH * SAMP) + 1e-06)
    remote_scale = 1.0 / jnp.sqrt(remote_total / (CH * SAMP) + 1e-06)
    share = pairs // lax.axis_size("sta")
    first = lax.axis_index("sta") * share
    summed = lax.psum(raw, "sta")
    total = lax.dynamic_slice_in_dim(summed, first, share, 2)
    local_share = lax.dynamic_slice_in_dim(pair_local[0], first, share, 1)
    remote_share = lax.dynamic_slice_in_dim(pair_remote[0], first, share, 1)
    local_index = jnp.arange(steps, dtype=jnp.int32)[:, None] * block + local_share
    factor = local_scale[local_index] * jnp.take_along_axis(remote_scale, remote_share, axis=1)
    factor = factor / (CH * SAMP) * neighbours[0].astype(jnp.float32)[:, None]
    return (total * factor[:, None, :])[None]


def solution(mesh):
    placed = (
        P("clu", "sta", None),
        P(),
        P("clu", None),
        P("clu", None, None),
        P("clu", None, None),
    )
    return jax.shard_map(
        local, mesh=mesh, in_specs=placed, out_specs=P("clu", None, None, "sta"), check_vma=False
    )
```

profile of v0, /device:TPU:0, one launch (start us, length us, event | category | flops | bytes accessed | tf_op | source)
XLA Modules:
  0.0 378.4 jit_solution(11850107144834018372)
XLA Ops:
  17.4 6.2 %convolution_bitcast_fusion = f32[1536,768]{0,1:T(8,128)} fusion(bf16[1536,256]{1,0:T(8,128)(2,1)S(1)} %reshape.166, f32[256,384]{1,0:T(8,128)S(1)} %get-tuple-element.42, f32[256,384]{1,0:T(8,128)S(1)} %get-tuple-element.43), kind=kOutput, calls=%fused_computation.26 | convolution fusion | flops 3624075264 | bytes 6291456 | tf_op jit(solution)/shard_map/dot_general | solution.py:21
  23.6 6.3 %copy.8 = f32[1536,768]{1,0:T(8,128)} copy(f32[1536,768]{0,1:T(8,128)} %convolution_bitcast_fusion) | data formatting | bytes 9437184 | tf_op jit(solution)/shard_map/dot_general | solution.py:21
  29.9 6.5 %reshape.167 = f32[256,6,768]{2,1,0:T(8,128)} reshape(f32[1536,768]{1,0:T(8,128)} %copy.8) | data formatting | bytes 9437184 | tf_op jit(solution)/shard_map/reshape | solution.py:24
  37.0 8.7 %gather_fusion.4 = f32[512,6,768]{2,1,0:T(8,128)} fusion(f32[256,6,768]{2,1,0:T(8,128)} %reshape.167, s32[1024]{0:T(1024)S(1)} %pad_clamp_fusion.6), kind=kCustom, calls=%fused_computation.2.clone | custom fusion | bytes 18876416 | tf_op jit(solution)/shard_map/jit(_take)/gather | solution.py:61
  45.6 8.8 %gather_fusion.2 = f32[512,6,768]{2,1,0:T(8,128)} fusion(f32[256,6,768]{2,1,0:T(8,128)} %reshape.167, s32[1024]{0:T(1024)S(1)} %pad_clamp_fusion.8), kind=kCustom, calls=%fused_computation.clone | custom fusion | bytes 18876416 | tf_op jit(solution)/shard_map/jit(_take)/gather | solution.py:61
  54.5 8.7 %gather_fusion.6 = f32[512,6,768]{2,1,0:T(8,128)} fusion(f32[256,6,768]{2,1,0:T(8,128)} %reshape.167, s32[1024]{0:T(1024)S(1)} %pad_clamp_fusion.4), kind=kCustom, calls=%fused_computation.4.clone | custom fusion | bytes 18876416 | tf_op jit(solution)/shard_map/jit(_take)/gather | solution.py:61
  63.2 8.8 %gather_fusion.8 = f32[512,6,768]{2,1,0:T(8,128)} fusion(f32[256,6,768]{2,1,0:T(8,128)} %reshape.167, s32[1024]{0:T(1024)S(1)} %pad_clamp_fusion.2), kind=kCustom, calls=%fused_computation.6.clone | custom fusion | bytes 18876416 | tf_op jit(solution)/shard_map/jit(_take)/gather | solution.py:61
  72.3 11.8 %broadcast_select_fusion.5 = f32[512,6,768]{2,1,0:T(8,128)} fusion(f32[512,6,768]{2,1,0:T(8,128)} %gather_fusion.4, pred[512]{0:T(512)(128)(4,1)S(1)} %compare_and_fusion.5), kind=kLoop, calls=%fused_computation.15 | loop fusion | flops 2359296 | bytes 18874880 | tf_op jit(solution)/shard_map/jit(_take)/select_n | solution.py:61
  84.1 11.9 %broadcast_select_fusion.7 = f32[512,6,768]{2,1,0:T(8,128)} fusion(f32[512,6,768]{2,1,0:T(8,128)} %gather_fusion.2, pred[512]{0:T(512)(128)(4,1)S(1)} %compare_and_fusion.7), kind=kLoop, calls=%fused_computation.17 | loop fusion | flops 2359296 | bytes 18874880 | tf_op jit(solution)/shard_map/jit(_take)/select_n | solution.py:61
  107.1 39.1 %all-reduce.7.cloned.1.call-done = (bf16[256,6,256]{2,0,1:T(8,128)(2,1)}, bf16[256,6,256]{2,0,1:T(8,128)(2,1)}, bf16[256,6,256]{2,0,1:T(8,128)(2,1)}, bf16[256,6,256]{2,0,1:T(8,128)(2,1)}) async-done(((bf16[256,6,256]{2,0,1:T(8,128)(2,1)}, bf16[256,6,256]{2,0,1:T(8,128)(2,1)}, bf16[256,6,256]{2,0,1:T(8,128)(2,1)}, bf16[256,6,256]{2,0,1:T(8,128)(2,1)}), (bf16[256,6,256]{2,0,1:T(8,128)(2,1)}, ...) | async-done | bytes 3145744 | tf_op jit(solution)/shard_map/psum | solution.py:15
  178.9 8.6 %gather_fusion.5 = f32[512,6,768]{2,1,0:T(8,128)} fusion(f32[256,6,768]{2,1,0:T(8,128)} %copy.10, s32[1024]{0:T(1024)S(1)} %pad_clamp_fusion.5), kind=kCustom, calls=%fused_computation.3.clone | custom fusion | bytes 18876416 | tf_op jit(solution)/shard_map/jit(_take)/gather | solution.py:62
  187.5 5.9 %broadcast_select_fusion.4 = f32[512,6,768]{2,1,0:T(8,128)S(1)} fusion(f32[512,6,768]{2,1,0:T(8,128)} %gather_fusion.5, pred[512]{0:T(512)(128)(4,1)S(1)} %compare_and_fusion.4), kind=kLoop, calls=%fused_computation.14 | loop fusion | flops 2359296 | bytes 18874880 | tf_op jit(solution)/shard_map/jit(_take)/select_n | solution.py:62
  193.4 9.5 %add_reduce_fusion.2 = (f32[512,384]{1,0:T(8,128)S(1)}, f32[512,384]{1,0:T(8,128)S(1)}) fusion(f32[512,6,768]{2,1,0:T(8,128)S(1)} %broadcast_select_fusion.4, f32[512,6,768]{2,1,0:T(8,128)} %broadcast_select_fusion.5), kind=kLoop, calls=%fused_computation.23 | loop fusion | flops 9043968 | bytes 20447232 | tf_op jit(solution)/shard_map/reduce_sum | solution.py:65
  203.0 8.6 %gather_fusion.3 = f32[512,6,768]{2,1,0:T(8,128)} fusion(f32[256,6,768]{2,1,0:T(8,128)} %copy.9, s32[1024]{0:T(1024)S(1)} %pad_clamp_fusion.7), kind=kCustom, calls=%fused_computation.1.clone | custom fusion | bytes 18876416 | tf_op jit(solution)/shard_map/jit(_take)/gather | solution.py:62
  211.6 5.9 %broadcast_select_fusion.6 = f32[512,6,768]{2,1,0:T(8,128)S(1)} fusion(f32[512,6,768]{2,1,0:T(8,128)} %gather_fusion.3, pred[512]{0:T(512)(128)(4,1)S(1)} %compare_and_fusion.6), kind=kLoop, calls=%fused_computation.16 | loop fusion | flops 2359296 | bytes 18874880 | tf_op jit(solution)/shard_map/jit(_take)/select_n | solution.py:62
  217.5 9.3 %add_reduce_fusion.3 = (f32[512,384]{1,0:T(8,128)S(1)}, f32[512,384]{1,0:T(8,128)S(1)}) fusion(f32[512,6,768]{2,1,0:T(8,128)S(1)} %broadcast_select_fusion.6, f32[512,6,768]{2,1,0:T(8,128)} %broadcast_select_fusion.7), kind=kLoop, calls=%fused_computation.25 | loop fusion | flops 9043968 | bytes 20447232 | tf_op jit(solution)/shard_map/reduce_sum | solution.py:65
  230.0 8.7 %gather_fusion.7 = f32[512,6,768]{2,1,0:T(8,128)} fusion(f32[256,6,768]{2,1,0:T(8,128)} %copy.11, s32[1024]{0:T(1024)S(1)} %pad_clamp_fusion.3), kind=kCustom, calls=%fused_computation.5.clone | custom fusion | bytes 18876416 | tf_op jit(solution)/shard_map/jit(_take)/gather | solution.py:62
  238.8 5.9 %broadcast_select_fusion.2 = f32[512,6,768]{2,1,0:T(8,128)S(1)} fusion(f32[512,6,768]{2,1,0:T(8,128)} %gather_fusion.7, pred[512]{0:T(512)(128)(4,1)S(1)} %compare_and_fusion.2), kind=kLoop, calls=%fused_computation.12 | loop fusion | flops 2359296 | bytes 18874880 | tf_op jit(solution)/shard_map/jit(_take)/select_n | solution.py:62
  244.7 9.6 %add_reduce_fusion.1 = (f32[512,384]{1,0:T(8,128)S(1)}, f32[512,384]{1,0:T(8,128)S(1)}) fusion(f32[512,6,768]{2,1,0:T(8,128)S(1)} %broadcast_select_fusion.2, f32[512,6,768]{2,1,0:T(8,128)} %broadcast_select_fusion.3), kind=kLoop, calls=%fused_computation.21 | loop fusion | flops 9043968 | bytes 20447232 | tf_op jit(solution)/shard_map/reduce_sum | solution.py:65
  255.9 8.6 %gather_fusion.9 = f32[512,6,768]{2,1,0:T(8,128)} fusion(f32[256,6,768]{2,1,0:T(8,128)} %copy.12, s32[1024]{0:T(1024)S(1)} %pad_clamp_fusion.1), kind=kCustom, calls=%fused_computation.7.clone | custom fusion | bytes 18876416 | tf_op jit(solution)/shard_map/jit(_take)/gather | solution.py:62
  264.5 5.9 %broadcast_select_fusion = f32[512,6,768]{2,1,0:T(8,128)S(1)} fusion(f32[512,6,768]{2,1,0:T(8,128)} %gather_fusion.9, pred[512]{0:T(512)(128)(4,1)S(1)} %copy-done.8), kind=kLoop, calls=%fused_computation.10 | loop fusion | flops 2359296 | bytes 18874880 | tf_op jit(solution)/shard_map/jit(_take)/select_n | solution.py:62
  270.4 9.3 %add_reduce_fusion = (f32[512,384]{1,0:T(8,128)S(1)}, f32[512,384]{1,0:T(8,128)S(1)}) fusion(f32[512,6,768]{2,1,0:T(8,128)S(1)} %broadcast_select_fusion, f32[512,6,768]{2,1,0:T(8,128)} %broadcast_select_fusion.1), kind=kLoop, calls=%fused_computation.19 | loop fusion | flops 9043968 | bytes 20447232 | tf_op jit(solution)/shard_map/reduce_sum | solution.py:65
  282.3 24.8 %all-reduce = (f32[256]{0:T(256)S(1)}, f32[4,256]{1,0:T(4,128)S(1)}) all-reduce(f32[256]{0:T(256)S(1)} %copy-done.7, f32[4,256]{1,0:T(4,128)S(1)} %pad_maximum_fusion.7), channel_id=1, replica_groups=mesh['clu'=16,'sta'=8] {'sta'}, use_global_device_ids=true, to_apply=%region_14.16 | all-reduce | flops 1280 | bytes 10240 | tf_op jit(solution)/shard_map/psum | solution.py:78
  311.8 57.6 %all-reduce.5.cloned.1.call-done = f32[4,65,512]{2,1,0:T(8,128)} async-done(((f32[4,65,512]{2,1,0:T(8,128)}), f32[4,65,512]{2,1,0:T(8,128)}) %all-reduce.5.cloned.1.call-update) | async-done | bytes 532496 | tf_op jit(solution)/shard_map/psum | solution.py:83
  (106 shorter events, 66.6 us)
Async XLA Ops:
  6.5 8.5 %copy-start = (bf16[256,6,256]{2,0,1:T(8,128)(2,1)S(1)}, bf16[256,6,256]{2,0,1:T(8,128)(2,1)}, u32[]{:S(2)}) copy-start(bf16[256,6,256]{2,0,1:T(8,128)(2,1)} %param.7) | copy-start | bytes 2359300
  6.5 8.5 %copy-start.5 = (s32[1,4,512]{2,1,0:T(4,128)S(1)}, s32[1,4,512]{2,1,0:T(4,128)}, u32[]{:S(2)}) copy-start(s32[1,4,512]{2,1,0:T(4,128)} %param.11) | copy-start | bytes 24580
  6.5 9.0 %copy-start.6 = (s32[1,4,512]{2,1,0:T(4,128)S(1)}, s32[1,4,512]{2,1,0:T(4,128)}, u32[]{:S(2)}) copy-start(s32[1,4,512]{2,1,0:T(4,128)} %param.10) | copy-start | bytes 24580
  6.5 139.7 %all-reduce.7.cloned.1.call-start = ((), (), s32[]{:S(2)}) async-start(), calls=%async_computation.1 | async-start | bytes 6291456 | tf_op jit(solution)/shard_map/psum | solution.py:15
  13.4 356.0 %all-reduce.5.cloned.1.call-start = ((), (), s32[]{:S(2)}) async-start(), calls=%async_computation | async-start | bytes 1179648 | tf_op jit(solution)/shard_map/psum | solution.py:83
  63.2 9.1 %copy-start.9 = (s32[1,4]{1,0:T(1,128)S(1)}, s32[1,4]{1,0:T(1,128)}, u32[]{:S(2)}) copy-start(s32[1,4]{1,0:T(1,128)} %param.9) | copy-start | bytes 52
  72.3 23.7 %slice-start = ((s8[12582912]{0:T(1024)(128)(4,1)}), s8[4194304]{0:T(1024)(128)(4,1)S(1)}, s32[]{:S(2)}) async-start(s8[12582912]{0:T(1024)(128)(4,1)} %bitcast.58), calls=%async_computation.2 | async-start | bytes 8388608
  72.3 23.7 %slice-start.1 = ((s8[12582912]{0:T(1024)(128)(4,1)}), s8[4194304]{0:T(1024)(128)(4,1)S(1)}, s32[]{:S(2)}) async-start(s8[12582912]{0:T(1024)(128)(4,1)} %bitcast.58), calls=%async_computation.3 | async-start | bytes 8388608
  84.1 11.9 %slice-start.2 = ((s8[12582912]{0:T(1024)(128)(4,1)}), s8[4194304]{0:T(1024)(128)(4,1)S(1)}, s32[]{:S(2)}) async-start(s8[12582912]{0:T(1024)(128)(4,1)} %bitcast.58), calls=%async_computation.4 | async-start | bytes 8388608
  84.1 17.3 %slice-start.3 = ((s8[12582912]{0:T(1024)(128)(4,1)}), s8[4194304]{0:T(1024)(128)(4,1)S(1)}, s32[]{:S(2)}) async-start(s8[12582912]{0:T(1024)(128)(4,1)} %bitcast.60), calls=%async_computation.5 | async-start | bytes 8388608
  84.1 17.3 %slice-start.4 = ((s8[12582912]{0:T(1024)(128)(4,1)}), s8[4194304]{0:T(1024)(128)(4,1)S(1)}, s32[]{:S(2)}) async-start(s8[12582912]{0:T(1024)(128)(4,1)} %bitcast.60), calls=%async_computation.6 | async-start | bytes 8388608
  96.0 5.4 %slice-start.5 = ((s8[12582912]{0:T(1024)(128)(4,1)}), s8[4194304]{0:T(1024)(128)(4,1)S(1)}, s32[]{:S(2)}) async-start(s8[12582912]{0:T(1024)(128)(4,1)} %bitcast.60), calls=%async_computation.7 | async-start | bytes 8388608
  146.2 3.4 copy-start.4
  146.2 5.6 %copy-start.3 = (bf16[256,6,256]{2,0,1:T(8,128)(2,1)S(1)}, bf16[256,6,256]{2,0,1:T(8,128)(2,1)}, u32[]{:S(2)}) copy-start(bf16[256,6,256]{2,0,1:T(8,128)(2,1)} %get-tuple-element.18) | copy-start | bytes 2359300
  146.2 6.0 %copy-start.2 = (bf16[256,6,256]{2,0,1:T(8,128)(2,1)S(1)}, bf16[256,6,256]{2,0,1:T(8,128)(2,1)}, u32[]{:S(2)}) copy-start(bf16[256,6,256]{2,0,1:T(8,128)(2,1)} %get-tuple-element.17) | copy-start | bytes 2359300
  149.6 4.7 %copy-start.1 = (bf16[256,6,256]{2,0,1:T(8,128)(2,1)S(1)}, bf16[256,6,256]{2,0,1:T(8,128)(2,1)}, u32[]{:S(2)}) copy-start(bf16[256,6,256]{2,0,1:T(8,128)(2,1)} %get-tuple-element.16) | copy-start | bytes 2359300
  255.9 8.6 %copy-start.8 = (pred[512]{0:T(512)(128)(4,1)S(1)}, pred[512]{0:T(512)(128)(4,1)}, u32[]{:S(2)}) copy-start(pred[512]{0:T(512)(128)(4,1)} %compare_and_fusion) | copy-start | bytes 1540
  270.4 11.9 %copy-start.7 = (f32[256]{0:T(256)S(1)}, f32[256]{0:T(256)}, u32[]{:S(2)}) copy-start(f32[256]{0:T(256)} %multiply_reduce_fusion.4) | copy-start | bytes 3076
Sparse Core Ops, SparseCore 0:
  13.5 132.6 all-reduce.6
  282.4 86.9 all-reduce.4
where the time goes:
time: 385 us; the launch traced here: 378 us
  local copies, waits for them, and re-layouts  112 us (29%)
  other arithmetic  105 us (27%)
  waiting for transfers between devices  96.7 us (25%)
  blocking collectives  24.8 us (6%)
  matrix products  22.5 us (6%)
  between operations  16.8 us (4%)
    psum x1, waiting for transfers between devices, local(): summed = lax.psum(raw, 'sta')  57.6 us
    psum x1, waiting for transfers between devices, broadcast(): return lax.psum(jnp.where(mine, x, jnp.zeros_like(x)), axis)  39.1 us
    reduce_sum x4, other arithmetic, local(): real_part = jnp.sum(left_cos * right_cos + left_sin * right_sin, axis=1)  37.7 us
    gather x4, local copies, waits for them, and re-layouts, local(): left = jnp.take(local_spec, step * block + pair_local[0, step], axis=0)  35 us
    select_n x8, other arithmetic, local(): left = jnp.take(local_spec, step * block + pair_local[0, step], axis=0)  34.8 us
    gather x4, local copies, waits for them, and re-layouts, local(): right = jnp.take(remote_spec, pair_remote[0, step], axis=0)  34.6 us
    dot_general x5, local copies, waits for them, and re-layouts, spectra(): jnp.dot(flat, table, precision=lax.Precision.HIGHEST, preferred_element_t...  28.4 us
    psum x1, blocking collectives, local(): lax.psum((local_part, jnp.stack(remote_parts, axis=0)), 'sta')  24.8 us
  transfers between devices with their start and end apart: 2, of which 2 were waited for; matrix products, arithmetic and copies ran while one was open for 26% of the time, Pallas kernels for 0%

commit v1 on v0

v1 whole, which is shorter than its diff:
```python
import math

import jax
import jax.numpy as jnp
import numpy as np
from jax import lax
from jax.experimental import pallas as pl
from jax.experimental.pallas import tpu as pltpu
from jax.sharding import PartitionSpec as P

CH, SAMP, HALF, LAGS = 48, 256, 32, 65
N = 288
LO, EXTRA = 128, 17
ROWS = 72
EI, EJ = 68, 69


def tables():
    u = np.arange(SAMP)[:, None]
    k = np.arange(N // 2 + 1)[None, :]
    angle = 2 * math.pi * ((u * k) % N) / N
    c, s = np.cos(angle), np.sin(angle)
    ch, sh = c[:, LO:], s[:, LO:]
    pad = np.zeros((SAMP, 128 - 4 * EXTRA))
    left = np.concatenate([c[:, :LO], s[:, :LO], ch, sh, sh, ch, pad], axis=1)
    right = np.concatenate([c[:, :LO], s[:, :LO], ch, sh, ch, sh, pad], axis=1)
    lag = np.arange(LAGS)[:, None] - HALF
    angle = 2 * math.pi * ((lag * k) % N) / N
    weight = np.where((k == 0) | (k == N // 2), 1.0, 2.0) / N
    c, s = np.cos(angle) * weight, np.sin(angle) * weight
    back = np.zeros((ROWS, 384))
    back[:LAGS, :LO] = c[:, :LO]
    back[:LAGS, LO:2 * LO] = -s[:, :LO]
    ch, sh = c[:, LO:], s[:, LO:]
    back[:LAGS, 256:256 + 4 * EXTRA] = np.concatenate([ch, ch, -sh, sh], axis=1)
    back[LAGS, 256 + EI] = 1.0
    back[LAGS + 1, 256 + EJ] = 1.0

    def split(t, axis):
        t = t.astype(np.float32)
        hi = t.astype(jnp.bfloat16)
        lo = (t - hi.astype(np.float32)).astype(jnp.bfloat16)
        return np.concatenate([hi, lo], axis=axis)

    return split(left, 1), split(right, 1), split(back, 0)


def spectrum(x, table, energy_lane, one_lane):
    d = jnp.dot(x, table, preferred_element_type=jnp.float32)
    d = d[:, :384] + d[:, 384:]
    xf = x.astype(jnp.float32)
    energy = jnp.sum(xf * xf, axis=1, keepdims=True)
    lane = lax.broadcasted_iota(jnp.int32, (1, 128), 1)
    third = jnp.where(lane == energy_lane, energy, d[:, 256:])
    third = jnp.where(lane == one_lane, 1.0, third)
    return d[:, :128], d[:, 128:256], third


def left_kernel(w_ref, table_ref, a_ref, b_ref, c_ref):
    events = a_ref.shape[0] // 8

    def body(c, carry):
        x = w_ref[pl.ds(pl.multiple_of(c * events, events), events), :]
        parts = spectrum(x, table_ref[...], EI, EJ)
        for ref, part in zip((a_ref, b_ref, c_ref), parts):
            ref[pl.ds(c, events, stride=8), :] = part
        return carry

    lax.fori_loop(0, w_ref.shape[0] // events, body, 0)


def pair_kernel(starts, counts, channels, *refs):
    pieces = len(starts)
    base_ref, local_ref, remote_ref, la, lb, lc, table_ref, back_ref = refs[:8]
    piece_refs = refs[8:8 + pieces]
    out_ref = refs[8 + pieces]
    ra, rb, rc, tmp, z = refs[9 + pieces:]
    steps, pairs = local_ref.shape
    shares = out_ref.shape[0]
    share = pairs // shares
    block = la.shape[0] // 8 // steps
    events = la.shape[0] // 8

    for n in range(pieces):
        for m in range(counts[n]):
            step = starts[n] + m
            x = piece_refs[n][m]
            parts = spectrum(x, table_ref[...], EJ, EI)
            for g in range(x.shape[0] // 32):
                row = base_ref[n] + 32 * g
                c = row // events
                to = (row - c * events) * 8 + c + step * events * 8
                for ref, part in zip((ra, rb, rc), parts):
                    ref[pl.ds(to, 32, stride=8), :] = part[32 * g:32 * g + 32]

    for step in range(steps):

        def body(it, carry):
            for half in range(2):
                g = it * 2 + half
                for p in range(8):
                    i = pl.multiple_of((local_ref[step, g * 8 + p] + step * block) * 8, 8)
                    j = pl.multiple_of((remote_ref[step, g * 8 + p] + step * events) * 8, 8)
                    xa, xb, xc = la[pl.ds(i, 8)], lb[pl.ds(i, 8)], lc[pl.ds(i, 8)]
                    ya, yb, yc = ra[pl.ds(j, 8)], rb[pl.ds(j, 8)], rc[pl.ds(j, 8)]
                    at = half * 192 + p * 8
                    tmp[at:at + 8] = xa * ya + xb * yb
                    tmp[at + 64:at + 72] = xb * ya - xa * yb
                    tmp[at + 128:at + 136] = xc * yc
                groups = share // 8
                k = g // groups
                to = k * (steps * share) + step * share + (g - k * groups) * 8
                to = pl.multiple_of(to, 8)
                for col in range(3):
                    at = half * 192 + col * 64
                    total = tmp[pl.ds(at, 8, stride=8), :]
                    for c in range(1, channels):
                        total = total + tmp[pl.ds(at + c, 8, stride=8), :]
                    z[pl.ds(to, 8), col * 128:col * 128 + 128] = total
            return carry

        lax.fori_loop(0, pairs // 16, body, 0)

    width = steps * share
    bh, bl = back_ref[:ROWS], back_ref[ROWS:]
    contract = (((1,), (1,)), ((), ()))
    for k in range(shares):
        zk = z[k * width:(k + 1) * width]
        zh = zk.astype(jnp.bfloat16)
        zl = (zk - zh.astype(jnp.float32)).astype(jnp.bfloat16)
        dot = lambda a, b: lax.dot_general(a, b, contract, preferred_element_type=jnp.float32)
        out_ref[k] = dot(bh, zh) + dot(bh, zl) + dot(bl, zh)


def final_kernel(near_ref, r_ref, out_ref):
    total = jnp.sum(r_ref[...], axis=0)
    count = CH * SAMP
    ni = 1.0 / jnp.sqrt(total[LAGS:LAGS + 1] / count + 1e-6)
    nj = 1.0 / jnp.sqrt(total[LAGS + 1:LAGS + 2] / count + 1e-6)
    total = total[:LAGS] * (ni * nj / count)
    steps, _, share = out_ref.shape[1:]
    for s in range(steps):
        out_ref[0, s] = total[:, s * share:(s + 1) * share] * near_ref[0, s].astype(jnp.float32)


SMEM = pl.BlockSpec(memory_space=pltpu.SMEM)
VMEM = pl.BlockSpec(memory_space=pltpu.VMEM)
PARAMS = pltpu.CompilerParams(vmem_limit_bytes=48 * 1024 * 1024)


def local(waves, owners, neighbours, pair_local, pair_remote):
    ev, ch, samp = waves.shape
    steps = owners.shape[0]
    pairs = pair_local.shape[2]
    n_clu, n_sta = lax.axis_size("clu"), lax.axis_size("sta")
    share = pairs // n_sta
    left_table, right_table, back_table = (jnp.asarray(t) for t in tables())
    rows = waves.transpose(1, 0, 2).reshape(ch * ev, samp)
    chunk = ch * ev // n_clu

    f32 = jnp.float32
    plane = jax.ShapeDtypeStruct((ev * 8, 128), f32)
    la, lb, lc = pl.pallas_call(
        left_kernel, out_shape=(plane,) * 3, in_specs=[VMEM] * 2, out_specs=(VMEM,) * 3,
        compiler_params=PARAMS, name="left",
        cost_estimate=pl.CostEstimate(flops=2 * ch * ev * samp * 768, bytes_accessed=4000000, transcendentals=0),
    )(rows, left_table)

    spread = lax.all_to_all(rows.reshape(n_clu, chunk, samp), "clu", 0, 0)
    mine = jnp.stack([lax.dynamic_index_in_dim(spread, owners[s], 0, False) for s in range(steps)])

    me = lax.axis_index("clu")
    y, x, core = me // 4, me // 2 % 2, me % 2
    index = lambda y, x, c: ((y % 4) * 2 + x) * 2 + c
    flip = lambda d: [(i, i ^ d) for i in range(n_clu)]
    turn = lambda d: [(i, (i + 4 * d) % n_clu) for i in range(n_clu)]
    send = lambda v, t: lax.ppermute(v, "clu", t)
    half = steps // 2
    got = []
    for b, bx in ((mine, x), (send(mine, flip(2)), 1 - x)):
        up, down = send(b, turn(1)), send(b, turn(-1))
        got += [(b, 0, y, bx), (up, 0, y + 3, bx), (down, 0, y + 1, bx)]
        got += [(send(up[:half], turn(1)), 0, y + 2, bx), (send(down[half:], turn(-1)), half, y + 2, bx)]
    pieces, starts, bases = [], [], []
    for v, first, by, bx in got:
        for c, piece in ((core, v), (1 - core, send(v, flip(1)))):
            pieces.append(piece)
            starts.append(first)
            bases.append(index(by, bx, c) * chunk)
    counts = [p.shape[0] for p in pieces]
    base = jnp.stack(bases).astype(jnp.int32)

    def kernel(*refs):
        pair_kernel(starts, counts, ch, *refs)

    raw = pl.pallas_call(
        kernel,
        out_shape=jax.ShapeDtypeStruct((n_sta, ROWS, steps * share), f32),
        in_specs=[SMEM] * 3 + [VMEM] * (5 + len(pieces)),
        out_specs=VMEM,
        scratch_shapes=[pltpu.VMEM((steps * ev * 8, 128), f32)] * 3
        + [pltpu.VMEM((384, 128), f32), pltpu.VMEM((steps * pairs, 384), f32)],
        compiler_params=PARAMS,
        name="pairs",
    )(base, pair_local[0], pair_remote[0], la, lb, lc, right_table, back_table, *pieces)

    parts = lax.all_to_all(raw, "sta", 0, 0)
    return pl.pallas_call(
        final_kernel,
        out_shape=jax.ShapeDtypeStruct((1, steps, LAGS, share), f32),
        in_specs=[SMEM, VMEM], out_specs=VMEM, compiler_params=PARAMS, name="finish",
    )(neighbours, parts)


def solution(mesh):
    placed = (
        P("clu", "sta", None),
        P(),
        P("clu", None),
        P("clu", None, None),
        P("clu", None, None),
    )
    return jax.shard_map(
        local, mesh=mesh, in_specs=placed, out_specs=P("clu", None, None, "sta"), check_vma=False
    )
```

time: 385 us -> 94.9 us (0.25); the launches traced: 378 us -> 94.5 us
  local copies, waits for them, and re-layouts: 112 us -> 5.14 us
  other arithmetic: 105 us -> 0.03 us
  waiting for transfers between devices: 96.7 us -> 22.6 us
  Pallas kernels: 0 us -> 23.2 us
  matrix products: 22.5 us -> 0 us
  starting transfers between devices: 0.04 us -> 15.7 us
  between operations: 16.8 us -> 7.52 us
  blocking collectives: 24.8 us -> 20.3 us
    psum x2 -> x0, waiting for transfers between devices: 96.6 us -> none  [the longest x1 57.6 us: local(): summed = lax.psum(raw, 'sta')]
    gather x13 -> x0, local copies, waits for them, and re-layouts: 74.3 us -> none  [the longest x4 35 us: local(): left = jnp.take(local_spec, step * block + pair_local[0, step], axis=0)]
    select_n x19 -> x0, other arithmetic: 61.2 us -> none  [the longest x8 34.8 us: local(): left = jnp.take(local_spec, step * block + pair_local[0, step], axis=0)]
    reduce_sum x7 -> x0, other arithmetic: 39.3 us -> none  [the longest x4 37.7 us: local(): real_part = jnp.sum(left_cos * right_cos + left_sin * right_sin, axis=1)]
    dot_general x5 -> x0, local copies, waits for them, and re-layouts: 28.4 us -> none  [spectra(): jnp.dot(flat, table, precision=lax.Precision.HIGHEST, preferred_element_t...]
    psum x1 -> x0, blocking collectives: 24.8 us -> none  [local(): lax.psum((local_part, jnp.stack(remote_parts, axis=0)), 'sta')]
    pallas_call x0 -> x3, Pallas kernels: none -> 23.2 us  [the longest x1 20.7 us: local(): pl.pallas_call(kernel, out_shape=jax.ShapeDtypeStruct((n_sta, ROWS, steps...]
    dot_general x9 -> x0, matrix products: 22.5 us -> none  [the longest x5 16 us: spectra(): jnp.dot(flat, table, precision=lax.Precision.HIGHEST, preferred_element_t...]
  transfers between devices with their start and end apart: 2 -> 20, of which waited for: 2 -> 8; matrix products, arithmetic and copies ran while one was open for 26% -> 1% of each run, Pallas kernels for 0% -> 2%
where the time goes in v1:
time: 94.9 us; the launch traced here: 94.5 us
  Pallas kernels  23.2 us (24%)
  waiting for transfers between devices  22.6 us (24%)
  blocking collectives  20.3 us (21%)
  starting transfers between devices  15.7 us (17%)
  between operations  7.52 us (8%)
  local copies, waits for them, and re-layouts  5.14 us (5%)
    pallas_call x1, Pallas kernels, local(): pl.pallas_call(kernel, out_shape=jax.ShapeDtypeStruct((n_sta, ROWS, steps...  20.7 us
    all_to_all x1, blocking collectives, local(): parts = lax.all_to_all(raw, 'sta', 0, 0)  20.3 us
    ppermute x19, waiting for transfers between devices, local(): send = lambda v, t: lax.ppermute(v, 'clu', t)  16.8 us
    ppermute x19, starting transfers between devices, local(): send = lambda v, t: lax.ppermute(v, 'clu', t)  9.94 us
    all_to_all x1, waiting for transfers between devices, local(): spread = lax.all_to_all(rows.reshape(n_clu, chunk, samp), 'clu', 0, 0)  5.75 us
    all_to_all x1, starting transfers between devices, local(): spread = lax.all_to_all(rows.reshape(n_clu, chunk, samp), 'clu', 0, 0)  5.72 us
    unnamed x20, local copies, waits for them, and re-layouts  3.58 us
  transfers between devices with their start and end apart: 20, of which 8 were waited for; matrix products, arithmetic and copies ran while one was open for 1% of the time, Pallas kernels for 2%

profile of v1, /device:TPU:0, one launch (start us, length us, event | category | flops | bytes accessed | tf_op | source)
XLA Modules:
  0.0 94.5 jit_solution(14800045753734195116)
XLA Ops:
  0.0 5.7 %all-to-all-start = ((bf16[16,96,256]{2,1,0:T(8,128)(2,1)}), bf16[16,96,256]{2,1,0:T(8,128)(2,1)S(1)}, u32[]{:S(2)}, u32[]{:S(2)}) async-start(bf16[16,96,256]{2,1,0:T(8,128)(2,1)} %bitcast.27), calls=%async_computation | async-start | bytes 1572864 | tf_op jit(solution)/shard_map/all_to_all | solution.py:169
  5.7 0.7 fusion
  13.7 5.7 %all-to-all-done = bf16[16,96,256]{2,1,0:T(8,128)(2,1)S(1)} async-done(((bf16[16,96,256]{2,1,0:T(8,128)(2,1)}), bf16[16,96,256]{2,1,0:T(8,128)(2,1)S(1)}, u32[]{:S(2)}, u32[]{:S(2)}) %all-to-all-start) | async-done | bytes 786464 | tf_op jit(solution)/shard_map/all_to_all | solution.py:169
  19.6 0.8 collective-permute-start.9
  20.7 1.7 %collective-permute-start.1 = (bf16[4,96,256]{2,1,0:T(8,128)(2,1)S(1)}, bf16[4,96,256]{2,1,0:T(8,128)(2,1)S(1)}, u32[]{:S(2)}, u32[]{:S(2)}) collective-permute-start(bf16[4,96,256]{2,1,0:T(8,128)(2,1)S(1)} %pad_maximum_fusion.refs_8_), channel_id=1, source_target_pairs={{0,32},{8,40},{16,48},{24,56},{32,64},{40,72},{48,80},{56,88},{64,... | collective-permute-start | bytes 589832 | tf_op jit(solution)/shard_map/ppermute | solution.py:177
  22.4 3.7 %collective-permute-done.9.refs_18_ = bf16[4,96,256]{2,1,0:T(8,128)(2,1)S(1)} collective-permute-done((bf16[4,96,256]{2,1,0:T(8,128)(2,1)S(1)}, bf16[4,96,256]{2,1,0:T(8,128)(2,1)S(1)}, u32[]{:S(2)}, u32[]{:S(2)}) %collective-permute-start.9) | collective-permute-done | bytes 196640 | tf_op jit(solution)/shard_map/ppermute | solution.py:177
  26.1 0.8 collective-permute-start.13
  26.9 1.2 %collective-permute-start.11 = (bf16[4,96,256]{2,1,0:T(8,128)(2,1)S(1)}, bf16[4,96,256]{2,1,0:T(8,128)(2,1)S(1)}, u32[]{:S(2)}, u32[]{:S(2)}) collective-permute-start(bf16[4,96,256]{2,1,0:T(8,128)(2,1)S(1)} %collective-permute-done.9.refs_18_), channel_id=1, source_target_pairs={{0,32},{8,40},{16,48},{24,56},{32,64},{40,72},{48,80},{56,88},{64,... | collective-permute-start | bytes 589832 | tf_op jit(solution)/shard_map/ppermute | solution.py:177
  28.7 3.0 %collective-permute-done.13.refs_22_ = bf16[4,96,256]{2,1,0:T(8,128)(2,1)S(1)} collective-permute-done((bf16[4,96,256]{2,1,0:T(8,128)(2,1)S(1)}, bf16[4,96,256]{2,1,0:T(8,128)(2,1)S(1)}, u32[]{:S(2)}, u32[]{:S(2)}) %collective-permute-start.13) | collective-permute-done | bytes 196640 | tf_op jit(solution)/shard_map/ppermute | solution.py:177
  31.7 2.0 %collective-permute-start.7 = (bf16[2,96,256]{2,1,0:T(8,128)(2,1)S(1)}, bf16[2,96,256]{2,1,0:T(8,128)(2,1)S(1)}, u32[]{:S(2)}, u32[]{:S(2)}) collective-permute-start(bf16[2,96,256]{2,1,0:T(8,128)(2,1)S(1)} %slice.33), channel_id=1, source_target_pairs={{0,96},{8,104},{16,112},{24,120},{32,0},{40,8},{48,16},{56,24},{64... | collective-permute-start | bytes 294920 | tf_op jit(solution)/shard_map/ppermute | solution.py:177
  33.8 2.6 %collective-permute-done.7.refs_16_ = bf16[2,96,256]{2,1,0:T(8,128)(2,1)S(1)} collective-permute-done((bf16[2,96,256]{2,1,0:T(8,128)(2,1)S(1)}, bf16[2,96,256]{2,1,0:T(8,128)(2,1)S(1)}, u32[]{:S(2)}, u32[]{:S(2)}) %collective-permute-start.7) | collective-permute-done | bytes 98336 | tf_op jit(solution)/shard_map/ppermute | solution.py:177
  36.4 3.2 %collective-permute-done.5.refs_14_ = bf16[2,96,256]{2,1,0:T(8,128)(2,1)S(1)} collective-permute-done((bf16[2,96,256]{2,1,0:T(8,128)(2,1)S(1)}, bf16[2,96,256]{2,1,0:T(8,128)(2,1)S(1)}, u32[]{:S(2)}, u32[]{:S(2)}) %collective-permute-start.5) | collective-permute-done | bytes 98336 | tf_op jit(solution)/shard_map/ppermute | solution.py:177
  40.1 2.0 %collective-permute-start.15 = (bf16[2,96,256]{2,1,0:T(8,128)(2,1)S(1)}, bf16[2,96,256]{2,1,0:T(8,128)(2,1)}, u32[]{:S(2)}, u32[]{:S(2)}) collective-permute-start(bf16[2,96,256]{2,1,0:T(8,128)(2,1)S(1)} %slice.34), channel_id=1, source_target_pairs={{0,32},{8,40},{16,48},{24,56},{32,64},{40,72},{48,80},{56,88},{64,... | collective-permute-start | bytes 294920 | tf_op jit(solution)/shard_map/ppermute | solution.py:177
  42.2 2.1 %collective-permute-done.17.refs_26_ = bf16[2,96,256]{2,1,0:T(8,128)(2,1)S(1)} collective-permute-done((bf16[2,96,256]{2,1,0:T(8,128)(2,1)S(1)}, bf16[2,96,256]{2,1,0:T(8,128)(2,1)S(1)}, u32[]{:S(2)}, u32[]{:S(2)}) %collective-permute-start.17) | collective-permute-done | bytes 98336 | tf_op jit(solution)/shard_map/ppermute | solution.py:177
  44.2 2.1 %collective-permute-done.15.refs_24_ = bf16[2,96,256]{2,1,0:T(8,128)(2,1)} collective-permute-done((bf16[2,96,256]{2,1,0:T(8,128)(2,1)S(1)}, bf16[2,96,256]{2,1,0:T(8,128)(2,1)}, u32[]{:S(2)}, u32[]{:S(2)}) %collective-permute-start.15) | collective-permute-done | bytes 98336 | tf_op jit(solution)/shard_map/ppermute | solution.py:177
  46.5 1.0 %copy-done.8 = bf16[256,768]{1,0:T(8,128)(2,1)S(1)} copy-done((bf16[256,768]{1,0:T(8,128)(2,1)S(1)}, bf16[256,768]{1,0:T(8,128)(2,1)}, u32[]{:S(2)}) %copy-start.8) | copy-done | bytes 393240
  47.5 1.9 %left.1 = (f32[2048,128]{1,0:T(8,128)S(1)}, f32[2048,128]{1,0:T(8,128)S(1)}, f32[2048,128]{1,0:T(8,128)S(1)}) custom-call(bf16[1536,256]{1,0:T(8,128)(2,1)S(1)} %bitcast.28, bf16[256,768]{1,0:T(8,128)(2,1)S(1)} %copy-done.8), custom_call_target="tpu_custom_call" | custom-call | flops 603979776 | bytes 4000000 | tf_op jit(solution)/shard_map/left/pallas_call | solution.py:163
  49.4 1.0 %copy-done = f32[2048,128]{1,0:T(8,128)} copy-done((f32[2048,128]{1,0:T(8,128)}, f32[2048,128]{1,0:T(8,128)S(1)}, u32[]{:S(2)}) %copy-start) | copy-done | bytes 1048600
  50.4 1.0 %copy-done.1 = f32[2048,128]{1,0:T(8,128)} copy-done((f32[2048,128]{1,0:T(8,128)}, f32[2048,128]{1,0:T(8,128)S(1)}, u32[]{:S(2)}) %copy-start.1) | copy-done | bytes 1048600
  51.4 0.6 copy-done.5
  52.0 20.7 %pairs.1 = f32[8,72,256]{2,1,0:T(8,128)S(1)} custom-call(s32[20]{0:T(128)S(1)} %stack.78.refs_0_, s32[4,512]{1,0:T(4,128)S(1)} %bitcast.29, s32[4,512]{1,0:T(4,128)S(1)} %bitcast.30, f32[2048,128]{1,0:T(8,128)S(1)} %get-tuple-element.8.refs_3_, f32[2048,128]{1,0:T(8,128)} %copy-done, f32[2048,128]{1,0:T(8,128)} %copy-done.1, bf16[256,768]{1,0:T(8,128)(2,1)S(1)} %copy-done.3, ...), custom_call_target="tpu_custom_call" | custom-call | tf_op jit(solution)/shard_map/pairs/pallas_call | solution.py:196
  72.7 20.3 %all_to_all.10.r_ref = f32[8,72,256]{2,1,0:T(8,128)S(1)} all-to-all(f32[8,72,256]{2,1,0:T(8,128)S(1)} %pairs.1), channel_id=1, replica_groups=mesh['clu'=16,'sta'=8] {'sta'}, dimensions={0} | all-to-all | bytes 1179648 | tf_op jit(solution)/shard_map/all_to_all | solution.py:207
  93.1 0.7 finish.1
  93.7 0.8 copy.9
  (49 shorter events, 1.7 us)
Async XLA Ops:
  0.0 5.7 %copy-start.9 = (s32[4]{0:T(128)S(1)}, s32[4]{0:T(128)}, u32[]{:S(2)}) copy-start(s32[4]{0:T(128)} %param.9) | copy-start | bytes 52
  0.0 19.5 %all-to-all-start = ((bf16[16,96,256]{2,1,0:T(8,128)(2,1)}), bf16[16,96,256]{2,1,0:T(8,128)(2,1)S(1)}, u32[]{:S(2)}, u32[]{:S(2)}) async-start(bf16[16,96,256]{2,1,0:T(8,128)(2,1)} %bitcast.27), calls=%async_computation | async-start | bytes 1572864 | tf_op jit(solution)/shard_map/all_to_all | solution.py:169
  19.5 27.0 %copy-start.2 = (bf16[256,6,256]{2,0,1:T(8,128)(2,1)S(1)}, bf16[256,6,256]{2,0,1:T(8,128)(2,1)}, u32[]{:S(2)}) copy-start(bf16[256,6,256]{2,0,1:T(8,128)(2,1)} %param.8) | copy-start | bytes 2359300
  19.6 6.5 %collective-permute-start.9 = (bf16[4,96,256]{2,1,0:T(8,128)(2,1)S(1)}, bf16[4,96,256]{2,1,0:T(8,128)(2,1)S(1)}, u32[]{:S(2)}, u32[]{:S(2)}) collective-permute-start(bf16[4,96,256]{2,1,0:T(8,128)(2,1)S(1)} %pad_maximum_fusion.refs_8_), channel_id=1, source_target_pairs={{0,16},{8,24},{16,0},{24,8},{32,48},{40,56},{48,32},{56,40},{64,80... | collective-permute-start | bytes 589832 | tf_op jit(solution)/shard_map/ppermute | solution.py:177
  20.3 7.8 %collective-permute-start.3 = (bf16[4,96,256]{2,1,0:T(8,128)(2,1)S(1)}, bf16[4,96,256]{2,1,0:T(8,128)(2,1)S(1)}, u32[]{:S(2)}, u32[]{:S(2)}) collective-permute-start(bf16[4,96,256]{2,1,0:T(8,128)(2,1)S(1)} %pad_maximum_fusion.refs_8_), channel_id=1, source_target_pairs={{0,96},{8,104},{16,112},{24,120},{32,0},{40,8},{48,16},{56,24},{64... | collective-permute-start | bytes 589832 | tf_op jit(solution)/shard_map/ppermute | solution.py:177
  20.7 7.5 %collective-permute-start.1 = (bf16[4,96,256]{2,1,0:T(8,128)(2,1)S(1)}, bf16[4,96,256]{2,1,0:T(8,128)(2,1)S(1)}, u32[]{:S(2)}, u32[]{:S(2)}) collective-permute-start(bf16[4,96,256]{2,1,0:T(8,128)(2,1)S(1)} %pad_maximum_fusion.refs_8_), channel_id=1, source_target_pairs={{0,32},{8,40},{16,48},{24,56},{32,64},{40,72},{48,80},{56,88},{64,... | collective-permute-start | bytes 589832 | tf_op jit(solution)/shard_map/ppermute | solution.py:177
  22.4 6.2 %collective-permute-start = (bf16[4,96,256]{2,1,0:T(8,128)(2,1)S(1)}, bf16[4,96,256]{2,1,0:T(8,128)(2,1)S(1)}, u32[]{:S(2)}, u32[]{:S(2)}) collective-permute-start(bf16[4,96,256]{2,1,0:T(8,128)(2,1)S(1)} %pad_maximum_fusion.refs_8_), channel_id=1, source_target_pairs={{0,8},{8,0},{16,24},{24,16},{32,40},{40,32},{48,56},{56,48},{64,72... | collective-permute-start | bytes 589832 | tf_op jit(solution)/shard_map/ppermute | solution.py:177
  26.1 5.7 %collective-permute-start.13 = (bf16[4,96,256]{2,1,0:T(8,128)(2,1)S(1)}, bf16[4,96,256]{2,1,0:T(8,128)(2,1)S(1)}, u32[]{:S(2)}, u32[]{:S(2)}) collective-permute-start(bf16[4,96,256]{2,1,0:T(8,128)(2,1)S(1)} %collective-permute-done.9.refs_18_), channel_id=1, source_target_pairs={{0,96},{8,104},{16,112},{24,120},{32,0},{40,8},{48,16},{56,24},{64... | collective-permute-start | bytes 589832 | tf_op jit(solution)/shard_map/ppermute | solution.py:177
  26.9 6.9 %collective-permute-start.11 = (bf16[4,96,256]{2,1,0:T(8,128)(2,1)S(1)}, bf16[4,96,256]{2,1,0:T(8,128)(2,1)S(1)}, u32[]{:S(2)}, u32[]{:S(2)}) collective-permute-start(bf16[4,96,256]{2,1,0:T(8,128)(2,1)S(1)} %collective-permute-done.9.refs_18_), channel_id=1, source_target_pairs={{0,32},{8,40},{16,48},{24,56},{32,64},{40,72},{48,80},{56,88},{64,... | collective-permute-start | bytes 589832 | tf_op jit(solution)/shard_map/ppermute | solution.py:177
  28.1 11.5 %collective-permute-start.10 = (bf16[4,96,256]{2,1,0:T(8,128)(2,1)S(1)}, bf16[4,96,256]{2,1,0:T(8,128)(2,1)S(1)}, u32[]{:S(2)}, u32[]{:S(2)}) collective-permute-start(bf16[4,96,256]{2,1,0:T(8,128)(2,1)S(1)} %collective-permute-done.9.refs_18_), channel_id=1, source_target_pairs={{0,8},{8,0},{16,24},{24,16},{32,40},{40,32},{48,56},{56,48},{64,72... | collective-permute-start | bytes 589832 | tf_op jit(solution)/shard_map/ppermute | solution.py:177
  28.2 11.6 %collective-permute-start.4 = (bf16[4,96,256]{2,1,0:T(8,128)(2,1)S(1)}, bf16[4,96,256]{2,1,0:T(8,128)(2,1)S(1)}, u32[]{:S(2)}, u32[]{:S(2)}) collective-permute-start(bf16[4,96,256]{2,1,0:T(8,128)(2,1)S(1)} %collective-permute-done.3.refs_12_), channel_id=1, source_target_pairs={{0,8},{8,0},{16,24},{24,16},{32,40},{40,32},{48,56},{56,48},{64,72... | collective-permute-start | bytes 589832 | tf_op jit(solution)/shard_map/ppermute | solution.py:177
  28.6 11.5 %collective-permute-start.2 = (bf16[4,96,256]{2,1,0:T(8,128)(2,1)S(1)}, bf16[4,96,256]{2,1,0:T(8,128)(2,1)S(1)}, u32[]{:S(2)}, u32[]{:S(2)}) collective-permute-start(bf16[4,96,256]{2,1,0:T(8,128)(2,1)S(1)} %collective-permute-done.1.refs_10_), channel_id=1, source_target_pairs={{0,8},{8,0},{16,24},{24,16},{32,40},{40,32},{48,56},{56,48},{64,72... | collective-permute-start | bytes 589832 | tf_op jit(solution)/shard_map/ppermute | solution.py:177
  31.7 4.6 %collective-permute-start.7 = (bf16[2,96,256]{2,1,0:T(8,128)(2,1)S(1)}, bf16[2,96,256]{2,1,0:T(8,128)(2,1)S(1)}, u32[]{:S(2)}, u32[]{:S(2)}) collective-permute-start(bf16[2,96,256]{2,1,0:T(8,128)(2,1)S(1)} %slice.33), channel_id=1, source_target_pairs={{0,96},{8,104},{16,112},{24,120},{32,0},{40,8},{48,16},{56,24},{64... | collective-permute-start | bytes 294920 | tf_op jit(solution)/shard_map/ppermute | solution.py:177
  33.8 5.8 %collective-permute-start.5 = (bf16[2,96,256]{2,1,0:T(8,128)(2,1)S(1)}, bf16[2,96,256]{2,1,0:T(8,128)(2,1)S(1)}, u32[]{:S(2)}, u32[]{:S(2)}) collective-permute-start(bf16[2,96,256]{2,1,0:T(8,128)(2,1)S(1)} %slice.32), channel_id=1, source_target_pairs={{0,32},{8,40},{16,48},{24,56},{32,64},{40,72},{48,80},{56,88},{64,... | collective-permute-start | bytes 294920 | tf_op jit(solution)/shard_map/ppermute | solution.py:177
  36.4 5.8 %collective-permute-start.8 = (bf16[2,96,256]{2,1,0:T(8,128)(2,1)S(1)}, bf16[2,96,256]{2,1,0:T(8,128)(2,1)S(1)}, u32[]{:S(2)}, u32[]{:S(2)}) collective-permute-start(bf16[2,96,256]{2,1,0:T(8,128)(2,1)S(1)} %collective-permute-done.7.refs_16_), channel_id=1, source_target_pairs={{0,8},{8,0},{16,24},{24,16},{32,40},{40,32},{48,56},{56,48},{64,72... | collective-permute-start | bytes 294920 | tf_op jit(solution)/shard_map/ppermute | solution.py:177
  39.6 4.6 %collective-permute-start.17 = (bf16[2,96,256]{2,1,0:T(8,128)(2,1)S(1)}, bf16[2,96,256]{2,1,0:T(8,128)(2,1)S(1)}, u32[]{:S(2)}, u32[]{:S(2)}) collective-permute-start(bf16[2,96,256]{2,1,0:T(8,128)(2,1)S(1)} %slice.35), channel_id=1, source_target_pairs={{0,96},{8,104},{16,112},{24,120},{32,0},{40,8},{48,16},{56,24},{64... | collective-permute-start | bytes 294920 | tf_op jit(solution)/shard_map/ppermute | solution.py:177
  39.6 11.7 %collective-permute-start.14 = (bf16[4,96,256]{2,1,0:T(8,128)(2,1)S(1)}, bf16[4,96,256]{2,1,0:T(8,128)(2,1)S(1)}, u32[]{:S(2)}, u32[]{:S(2)}) collective-permute-start(bf16[4,96,256]{2,1,0:T(8,128)(2,1)S(1)} %collective-permute-done.13.refs_22_), channel_id=1, source_target_pairs={{0,8},{8,0},{16,24},{24,16},{32,40},{40,32},{48,56},{56,48},{64,72... | collective-permute-start | bytes 589832 | tf_op jit(solution)/shard_map/ppermute | solution.py:177
  39.8 11.5 %collective-permute-start.12 = (bf16[4,96,256]{2,1,0:T(8,128)(2,1)S(1)}, bf16[4,96,256]{2,1,0:T(8,128)(2,1)S(1)}, u32[]{:S(2)}, u32[]{:S(2)}) collective-permute-start(bf16[4,96,256]{2,1,0:T(8,128)(2,1)S(1)} %collective-permute-done.11.refs_20_), channel_id=1, source_target_pairs={{0,8},{8,0},{16,24},{24,16},{32,40},{40,32},{48,56},{56,48},{64,72... | collective-permute-start | bytes 589832 | tf_op jit(solution)/shard_map/ppermute | solution.py:177
  40.1 6.2 %collective-permute-start.15 = (bf16[2,96,256]{2,1,0:T(8,128)(2,1)S(1)}, bf16[2,96,256]{2,1,0:T(8,128)(2,1)}, u32[]{:S(2)}, u32[]{:S(2)}) collective-permute-start(bf16[2,96,256]{2,1,0:T(8,128)(2,1)S(1)} %slice.34), channel_id=1, source_target_pairs={{0,32},{8,40},{16,48},{24,56},{32,64},{40,72},{48,80},{56,88},{64,... | collective-permute-start | bytes 294920 | tf_op jit(solution)/shard_map/ppermute | solution.py:177
  42.2 9.2 %collective-permute-start.6 = (bf16[2,96,256]{2,1,0:T(8,128)(2,1)S(1)}, bf16[2,96,256]{2,1,0:T(8,128)(2,1)}, u32[]{:S(2)}, u32[]{:S(2)}) collective-permute-start(bf16[2,96,256]{2,1,0:T(8,128)(2,1)S(1)} %collective-permute-done.5.refs_14_), channel_id=1, source_target_pairs={{0,8},{8,0},{16,24},{24,16},{32,40},{40,32},{48,56},{56,48},{64,72... | collective-permute-start | bytes 294920 | tf_op jit(solution)/shard_map/ppermute | solution.py:177
  44.2 7.1 %collective-permute-start.18 = (bf16[2,96,256]{2,1,0:T(8,128)(2,1)S(1)}, bf16[2,96,256]{2,1,0:T(8,128)(2,1)}, u32[]{:S(2)}, u32[]{:S(2)}) collective-permute-start(bf16[2,96,256]{2,1,0:T(8,128)(2,1)S(1)} %collective-permute-done.17.refs_26_), channel_id=1, source_target_pairs={{0,8},{8,0},{16,24},{24,16},{32,40},{40,32},{48,56},{56,48},{64,72... | collective-permute-start | bytes 294920 | tf_op jit(solution)/shard_map/ppermute | solution.py:177
  46.4 5.0 %collective-permute-start.16 = (bf16[2,96,256]{2,1,0:T(8,128)(2,1)}, bf16[2,96,256]{2,1,0:T(8,128)(2,1)}, u32[]{:S(2)}, u32[]{:S(2)}) collective-permute-start(bf16[2,96,256]{2,1,0:T(8,128)(2,1)} %collective-permute-done.15.refs_24_), channel_id=1, source_target_pairs={{0,8},{8,0},{16,24},{24,16},{32,40},{40,32},{48,56},{56,48},{64,72... | collective-permute-start | bytes 294920 | tf_op jit(solution)/shard_map/ppermute | solution.py:177
  47.5 3.9 %copy-start.6 = (s32[1,4,512]{2,1,0:T(4,128)S(1)}, s32[1,4,512]{2,1,0:T(4,128)}, u32[]{:S(2)}) copy-start(s32[1,4,512]{2,1,0:T(4,128)} %param.12) | copy-start | bytes 24580
  72.7 20.4 %copy-start.7 = (s32[1,4]{1,0:T(1,128)S(1)}, s32[1,4]{1,0:T(1,128)}, u32[]{:S(2)}) copy-start(s32[1,4]{1,0:T(1,128)} %near_ref.1) | copy-start | bytes 52
  (6 other events, 11.5 us)

commit v2 on v1

v2 whole, which is shorter than its diff:
```python
import math

import jax
import jax.numpy as jnp
import numpy as np
from jax import lax
from jax.experimental import pallas as pl
from jax.experimental.pallas import tpu as pltpu
from jax.sharding import PartitionSpec as P

CH, SAMP, HALF, LAGS = 48, 256, 32, 65
N = 288
LO, EXTRA = 128, 17
ROWS = 72
EI, EJ = 68, 69


def tables():
    u = np.arange(SAMP)[:, None]
    k = np.arange(N // 2 + 1)[None, :]
    angle = 2 * math.pi * ((u * k) % N) / N
    c, s = np.cos(angle), np.sin(angle)
    ch, sh = c[:, LO:], s[:, LO:]
    pad = np.zeros((SAMP, 128 - 4 * EXTRA))
    left = np.concatenate([c[:, :LO], s[:, :LO], ch, sh, sh, ch, pad], axis=1)
    right = np.concatenate([c[:, :LO], s[:, :LO], ch, sh, ch, sh, pad], axis=1)
    lag = np.arange(LAGS)[:, None] - HALF
    angle = 2 * math.pi * ((lag * k) % N) / N
    weight = np.where((k == 0) | (k == N // 2), 1.0, 2.0) / N
    c, s = np.cos(angle) * weight, np.sin(angle) * weight
    back = np.zeros((ROWS, 384))
    back[:LAGS, :LO] = c[:, :LO]
    back[:LAGS, LO:2 * LO] = -s[:, :LO]
    ch, sh = c[:, LO:], s[:, LO:]
    back[:LAGS, 256:256 + 4 * EXTRA] = np.concatenate([ch, ch, -sh, sh], axis=1)
    back[LAGS, 256 + EI] = 1.0
    back[LAGS + 1, 256 + EJ] = 1.0

    def split(t, axis):
        t = t.astype(np.float32)
        hi = t.astype(jnp.bfloat16)
        lo = (t - hi.astype(np.float32)).astype(jnp.bfloat16)
        return np.concatenate([hi, lo], axis=axis)

    return split(left, 1), split(right, 1), split(back, 0)


def spectrum(x, table, energy_lane, one_lane):
    d = jnp.dot(x, table, preferred_element_type=jnp.float32)
    d = d[:, :384] + d[:, 384:]
    xf = x.astype(jnp.float32)
    energy = jnp.sum(xf * xf, axis=1, keepdims=True)
    lane = lax.broadcasted_iota(jnp.int32, (1, 128), 1)
    third = jnp.where(lane == energy_lane, energy, d[:, 256:])
    third = jnp.where(lane == one_lane, 1.0, third)
    return d[:, :128], d[:, 128:256], third


def left_kernel(table_ref, b0, b1, b2, b3, a_ref, b_ref, c_ref):
    events = a_ref.shape[0] // 8 // 4
    channels = b0.shape[0] // events
    for q, w_ref in enumerate((b0, b1, b2, b3)):
        parts = spectrum(w_ref[:channels * events], table_ref[...], EI, EJ)
        for c in range(channels):
            for ref, part in zip((a_ref, b_ref, c_ref), parts):
                ref[pl.ds(q * events * 8 + c, events, stride=8), :] = part[c * events:(c + 1) * events]


def pair_kernel(channels, base_ref, index_ref, la, lb, lc, table_ref, back_ref, p0, p1, p2, p3, out_ref, ra, rb, rc, tmp, z):
    groups4 = index_ref.shape[0]
    shares = out_ref.shape[0]
    width = out_ref.shape[2]
    share = width // groups4
    pairs = share * shares
    block = la.shape[0] // 8 // groups4
    events = ra.shape[0] // 8

    for n, p_ref in enumerate((p0, p1, p2, p3)):
        for m in range(p_ref.shape[0]):
            x = p_ref[m]
            parts = spectrum(x, table_ref[...], EJ, EI)
            for g in range(x.shape[0] // 32):
                row = base_ref[4 * n + m] + 32 * g
                c = row // events
                to = (row - c * events) * 8 + c
                for ref, part in zip((ra, rb, rc), parts):
                    ref[pl.ds(to, 32, stride=8), :] = part[32 * g:32 * g + 32]

    for q in range(groups4):

        def body(it, carry):
            for half in range(2):
                g = it * 2 + half
                for p in range(8):
                    at = g * 8 + p
                    hi, lo = at // 256, at % 256
                    i = pl.multiple_of((index_ref[q, hi, lo] + q * block) * 8, 8)
                    j = pl.multiple_of(index_ref[q, hi + pairs // 256, lo] * 8, 8)
                    xa, xb, xc = la[pl.ds(i, 8)], lb[pl.ds(i, 8)], lc[pl.ds(i, 8)]
                    ya, yb, yc = ra[pl.ds(j, 8)], rb[pl.ds(j, 8)], rc[pl.ds(j, 8)]
                    at = half * 192 + p * 8
                    tmp[at:at + 8] = xa * ya + xb * yb
                    tmp[at + 64:at + 72] = xb * ya - xa * yb
                    tmp[at + 128:at + 136] = xc * yc
                groups = share // 8
                k = g // groups
                to = k * width + q * share + (g - k * groups) * 8
                to = pl.multiple_of(to, 8)
                for col in range(3):
                    at = half * 192 + col * 64
                    total = tmp[pl.ds(at, 8, stride=8), :]
                    for c in range(1, channels):
                        total = total + tmp[pl.ds(at + c, 8, stride=8), :]
                    z[pl.ds(to, 8), col * 128:col * 128 + 128] = total
            return carry

        lax.fori_loop(0, pairs // 16, body, 0)

    bh, bl = back_ref[:ROWS], back_ref[ROWS:]
    contract = (((1,), (1,)), ((), ()))
    for k in range(shares):
        zk = z[k * width:(k + 1) * width]
        zh = zk.astype(jnp.bfloat16)
        zl = (zk - zh.astype(jnp.float32)).astype(jnp.bfloat16)
        dot = lambda a, b: lax.dot_general(a, b, contract, preferred_element_type=jnp.float32)
        out_ref[k] = dot(bh, zh) + dot(bh, zl) + dot(bl, zh)


def sum_kernel(r_ref, *out_refs):
    total = jnp.sum(r_ref[...], axis=0)
    count = CH * SAMP
    ni = 1.0 / jnp.sqrt(total[LAGS:LAGS + 1] / count + 1e-6)
    nj = 1.0 / jnp.sqrt(total[LAGS + 1:LAGS + 2] / count + 1e-6)
    total = total * (ni * nj / count)
    share = out_refs[0].shape[1]
    for q, ref in enumerate(out_refs):
        ref[...] = total[:, q * share:(q + 1) * share]


def final_kernel(step_ref, near_ref, *refs):
    out_ref = refs[-1]
    for r, ref in enumerate(refs[:-1]):
        s = step_ref[r]
        out_ref[0, s] = ref[:LAGS] * near_ref[0, s].astype(jnp.float32)


SMEM = pl.BlockSpec(memory_space=pltpu.SMEM)
VMEM = pl.BlockSpec(memory_space=pltpu.VMEM)
PARAMS = pltpu.CompilerParams(vmem_limit_bytes=48 * 1024 * 1024)


def local(waves, owners, neighbours, pair_local, pair_remote):
    ev, ch, samp = waves.shape
    steps = owners.shape[0]
    pairs = pair_local.shape[2]
    n_clu, n_sta = lax.axis_size("clu"), lax.axis_size("sta")
    share = pairs // n_sta
    block = ev // steps
    left_table, right_table, back_table = (jnp.asarray(t) for t in tables())
    cube = waves.transpose(1, 0, 2)
    rows = cube.reshape(ch * ev, samp)
    chunk = ch * ev // n_clu
    f32, bf16 = jnp.float32, jnp.bfloat16
    shaped = jax.ShapeDtypeStruct

    me = lax.axis_index("clu")
    row, step = me // 4, me % 4
    near = lambda v, d: v if d == 0 else lax.ppermute(v, "clu", [(i, i ^ d) for i in range(n_clu)])
    turn = lambda v, d: lax.ppermute(v, "clu", [(i, (i + 4 * d) % n_clu) for i in range(n_clu)])

    spread = lax.all_to_all(rows.reshape(n_clu, chunk, samp), "clu", 0, 0)
    pick = lambda d: lax.dynamic_index_in_dim(spread, owners[step ^ d], 0, False)
    mine = jnp.stack([near(pick(d), d) for d in range(4)])
    pieces = [mine, turn(mine, 1), turn(mine, -1), turn(mine, 2)]
    base = jnp.stack([((row + r) % 4 * 4 + (step ^ d)) * chunk for r in (0, 3, 1, 2) for d in range(4)])

    lists = jnp.concatenate([pair_local[0], pair_remote[0]], axis=1).astype(bf16)
    lists = lists.reshape(steps, 2 * pairs // samp, samp)
    blocks = []
    for d in range(4):
        events = lax.dynamic_slice_in_dim(cube, (step ^ d) * block, block, 1).reshape(ch * block, samp)
        listed = lax.dynamic_index_in_dim(lists, step ^ d, 0, False)
        listed = jnp.pad(listed, ((0, 16 - listed.shape[0]), (0, 0)))
        blocks.append(near(jnp.concatenate([events, listed]), d))
    index = jnp.stack([b[ch * block:ch * block + 2 * pairs // samp] for b in blocks]).astype(jnp.int32)

    plane = shaped((ev * 8, 128), f32)
    la, lb, lc = pl.pallas_call(
        left_kernel, out_shape=(plane,) * 3, in_specs=[VMEM] * 5, out_specs=(VMEM,) * 3,
        compiler_params=PARAMS, name="left",
        cost_estimate=pl.CostEstimate(flops=2 * ch * ev * samp * 768, bytes_accessed=4000000, transcendentals=0),
    )(left_table, *blocks)

    raw = pl.pallas_call(
        lambda *refs: pair_kernel(ch, *refs),
        out_shape=shaped((n_sta, ROWS, 4 * share), f32),
        in_specs=[SMEM] * 2 + [VMEM] * 9,
        out_specs=VMEM,
        scratch_shapes=[pltpu.VMEM((ev * 8, 128), f32)] * 3
        + [pltpu.VMEM((384, 128), f32), pltpu.VMEM((4 * pairs, 384), f32)],
        compiler_params=PARAMS,
        name="pairs",
    )(base, index, la, lb, lc, right_table, back_table, *pieces)

    parts = lax.all_to_all(raw, "sta", 0, 0)
    done = pl.pallas_call(
        sum_kernel, out_shape=(shaped((ROWS, share), f32),) * 4,
        in_specs=[VMEM], out_specs=(VMEM,) * 4, compiler_params=PARAMS, name="total",
    )(parts)
    done = [near(v, d) for d, v in enumerate(done)]
    order = jnp.stack([step ^ d for d in range(4)])
    return pl.pallas_call(
        final_kernel, out_shape=shaped((1, steps, LAGS, share), f32),
        in_specs=[SMEM] * 2 + [VMEM] * 4, out_specs=VMEM, compiler_params=PARAMS, name="finish",
    )(order, neighbours, *done)


def solution(mesh):
    placed = (
        P("clu", "sta", None),
        P(),
        P("clu", None),
        P("clu", None, None),
        P("clu", None, None),
    )
    return jax.shard_map(
        local, mesh=mesh, in_specs=placed, out_specs=P("clu", None, None, "sta"), check_vma=False
    )
```

time: 94.9 us -> 102 us (1.075); the launches traced: 94.5 us -> 100 us
  Pallas kernels: 23.2 us -> 36.5 us
  waiting for transfers between devices: 22.6 us -> 16.5 us
  starting transfers between devices: 15.7 us -> 17.5 us
  blocking collectives: 20.3 us -> 18.6 us
  local copies, waits for them, and re-layouts: 5.14 us -> 3.67 us
    pallas_call x3 -> x4, Pallas kernels: 23.2 us -> 36.5 us  [the longest x1 34.8 us: local(): pl.pallas_call(lambda *refs: pair_kernel(ch, *refs), out_shape=shaped((n_...]
    all_to_all x1, waiting for transfers between devices: 5.75 us -> 0.01 us  [local(): spread = lax.all_to_all(rows.reshape(n_clu, chunk, samp), 'clu', 0, 0)]
    ppermute x19 -> x12, starting transfers between devices: 9.94 us -> 11.8 us  [the longest x9 6.69 us: local(): lax.ppermute(v, 'clu', [(i, i ^ d) for i in range(n_clu)])]
    all_to_all x1, blocking collectives: 20.3 us -> 18.6 us  [local(): parts = lax.all_to_all(raw, 'sta', 0, 0)]
    unnamed x20 -> x16, local copies, waits for them, and re-layouts: 3.58 us -> 2.03 us
    ppermute x19 -> x12, waiting for transfers between devices: 16.8 us -> 16.5 us  [the longest x9 9.74 us: local(): lax.ppermute(v, 'clu', [(i, i ^ d) for i in range(n_clu)])]
  transfers between devices with their start and end apart: 20 -> 13, of which waited for: 8 -> 8; matrix products, arithmetic and copies ran while one was open for 1% -> 1% of each run, Pallas kernels for 2% -> 1%
where the time goes in v2:
time: 102 us; the launch traced here: 100 us
  Pallas kernels  36.5 us (36%)
  blocking collectives  18.6 us (18%)
  starting transfers between devices  17.5 us (17%)
  waiting for transfers between devices  16.5 us (16%)
  between operations  7.46 us (7%)
  local copies, waits for them, and re-layouts  3.67 us (4%)
    pallas_call x1, Pallas kernels, local(): pl.pallas_call(lambda *refs: pair_kernel(ch, *refs), out_shape=shaped((n_...  34.8 us
    all_to_all x1, blocking collectives, local(): parts = lax.all_to_all(raw, 'sta', 0, 0)  18.6 us
    ppermute x9, waiting for transfers between devices, local(): lax.ppermute(v, 'clu', [(i, i ^ d) for i in range(n_clu)])  9.74 us
    ppermute x3, waiting for transfers between devices, local(): lax.ppermute(v, 'clu', [(i, (i + 4 * d) % n_clu) for i in range(n_clu)])  6.75 us
    ppermute x9, starting transfers between devices, local(): lax.ppermute(v, 'clu', [(i, i ^ d) for i in range(n_clu)])  6.69 us
    all_to_all x1, starting transfers between devices, local(): spread = lax.all_to_all(rows.reshape(n_clu, chunk, samp), 'clu', 0, 0)  5.72 us
    ppermute x3, starting transfers between devices, local(): lax.ppermute(v, 'clu', [(i, (i + 4 * d) % n_clu) for i in range(n_clu)])  5.07 us
  transfers between devices with their start and end apart: 13, of which 8 were waited for; matrix products, arithmetic and copies ran while one was open for 1% of the time, Pallas kernels for 1%

profile of v2, /device:TPU:0, one launch (start us, length us, event | category | flops | bytes accessed | tf_op | source)
XLA Modules:
  0.0 100.4 jit_solution(651917320219945377)
XLA Ops:
  0.0 5.7 %all-to-all-start = ((bf16[16,96,256]{2,1,0:T(8,128)(2,1)}), bf16[16,96,256]{2,1,0:T(8,128)(2,1)S(1)}, u32[]{:S(2)}, u32[]{:S(2)}) async-start(bf16[16,96,256]{2,1,0:T(8,128)(2,1)} %bitcast.61), calls=%async_computation | async-start | bytes 1572864 | tf_op jit(solution)/shard_map/all_to_all | solution.py:171
  5.8 0.7 copy-done.6
  6.5 0.7 copy-done.7
  7.4 1.7 %collective-permute-start.2 = (bf16[400,256]{1,0:T(8,128)(2,1)S(1)}, bf16[400,256]{1,0:T(8,128)(2,1)S(1)}, u32[]{:S(2)}, u32[]{:S(2)}) collective-permute-start(bf16[400,256]{1,0:T(8,128)(2,1)S(1)} %fusion.6), channel_id=1, source_target_pairs={{0,24},{8,16},{16,8},{24,0},{32,56},{40,48},{48,40},{56,32},{64,88... | collective-permute-start | bytes 614408 | tf_op jit(solution)/shard_map/ppermute | solution.py:168
  9.7 0.6 copy-done.5
  10.4 0.6 fusion.15
  18.3 2.9 %collective-permute-done.2.b3 = bf16[400,256]{1,0:T(8,128)(2,1)S(1)} collective-permute-done((bf16[400,256]{1,0:T(8,128)(2,1)S(1)}, bf16[400,256]{1,0:T(8,128)(2,1)S(1)}, u32[]{:S(2)}, u32[]{:S(2)}) %collective-permute-start.2) | collective-permute-done | bytes 204832 | tf_op jit(solution)/shard_map/ppermute | solution.py:168
  21.3 0.6 collective-permute-start.5
  21.8 1.9 %collective-permute-start.4 = (bf16[96,256]{1,0:T(8,128)(2,1)S(1)}, bf16[96,256]{1,0:T(8,128)(2,1)S(1)}, u32[]{:S(2)}, u32[]{:S(2)}) collective-permute-start(bf16[96,256]{1,0:T(8,128)(2,1)S(1)} %get-tuple-element.21), channel_id=1, source_target_pairs={{0,16},{8,24},{16,0},{24,8},{32,48},{40,56},{48,32},{56,40},{64,80... | collective-permute-start | bytes 147464 | tf_op jit(solution)/shard_map/ppermute | solution.py:168
  23.8 2.8 %collective-permute-done.1.b2 = bf16[400,256]{1,0:T(8,128)(2,1)S(1)} collective-permute-done((bf16[400,256]{1,0:T(8,128)(2,1)S(1)}, bf16[400,256]{1,0:T(8,128)(2,1)S(1)}, u32[]{:S(2)}, u32[]{:S(2)}) %collective-permute-start.1) | collective-permute-done | bytes 204832 | tf_op jit(solution)/shard_map/ppermute | solution.py:168
  26.7 1.5 %collective-permute-done.4 = bf16[96,256]{1,0:T(8,128)(2,1)S(1)} collective-permute-done((bf16[96,256]{1,0:T(8,128)(2,1)S(1)}, bf16[96,256]{1,0:T(8,128)(2,1)S(1)}, u32[]{:S(2)}, u32[]{:S(2)}) %collective-permute-start.4) | collective-permute-done | bytes 49184 | tf_op jit(solution)/shard_map/ppermute | solution.py:168
  28.2 1.6 %collective-permute-start.6 = (bf16[4,96,256]{2,1,0:T(8,128)(2,1)S(1)}, bf16[4,96,256]{2,1,0:T(8,128)(2,1)S(1)}, u32[]{:S(2)}, u32[]{:S(2)}) collective-permute-start(bf16[4,96,256]{2,1,0:T(8,128)(2,1)S(1)} %pad_maximum_fusion.refs_7_), channel_id=1, source_target_pairs={{0,32},{8,40},{16,48},{24,56},{32,64},{40,72},{48,80},{56,88},{64,... | collective-permute-start | bytes 589832 | tf_op jit(solution)/shard_map/ppermute | solution.py:169
  29.8 1.7 %collective-permute-start.7 = (bf16[4,96,256]{2,1,0:T(8,128)(2,1)S(1)}, bf16[4,96,256]{2,1,0:T(8,128)(2,1)S(1)}, u32[]{:S(2)}, u32[]{:S(2)}) collective-permute-start(bf16[4,96,256]{2,1,0:T(8,128)(2,1)S(1)} %pad_maximum_fusion.refs_7_), channel_id=1, source_target_pairs={{0,96},{8,104},{16,112},{24,120},{32,0},{40,8},{48,16},{56,24},{64... | collective-permute-start | bytes 589832 | tf_op jit(solution)/shard_map/ppermute | solution.py:169
  31.6 1.8 %collective-permute-start.8 = (bf16[4,96,256]{2,1,0:T(8,128)(2,1)S(1)}, bf16[4,96,256]{2,1,0:T(8,128)(2,1)S(1)}, u32[]{:S(2)}, u32[]{:S(2)}) collective-permute-start(bf16[4,96,256]{2,1,0:T(8,128)(2,1)S(1)} %pad_maximum_fusion.refs_7_), channel_id=1, source_target_pairs={{0,64},{8,72},{16,80},{24,88},{32,96},{40,104},{48,112},{56,120},{... | collective-permute-start | bytes 589832 | tf_op jit(solution)/shard_map/ppermute | solution.py:169
  33.4 1.0 left.1
  34.4 2.0 %collective-permute-done.6.refs_8_ = bf16[4,96,256]{2,1,0:T(8,128)(2,1)S(1)} collective-permute-done((bf16[4,96,256]{2,1,0:T(8,128)(2,1)S(1)}, bf16[4,96,256]{2,1,0:T(8,128)(2,1)S(1)}, u32[]{:S(2)}, u32[]{:S(2)}) %collective-permute-start.6) | collective-permute-done | bytes 196640 | tf_op jit(solution)/shard_map/ppermute | solution.py:169
  36.4 1.3 %collective-permute-done.7.refs_9_ = bf16[4,96,256]{2,1,0:T(8,128)(2,1)S(1)} collective-permute-done((bf16[4,96,256]{2,1,0:T(8,128)(2,1)S(1)}, bf16[4,96,256]{2,1,0:T(8,128)(2,1)S(1)}, u32[]{:S(2)}, u32[]{:S(2)}) %collective-permute-start.7) | collective-permute-done | bytes 196640 | tf_op jit(solution)/shard_map/ppermute | solution.py:169
  37.7 3.5 %collective-permute-done.8.refs_10_ = bf16[4,96,256]{2,1,0:T(8,128)(2,1)S(1)} collective-permute-done((bf16[4,96,256]{2,1,0:T(8,128)(2,1)S(1)}, bf16[4,96,256]{2,1,0:T(8,128)(2,1)S(1)}, u32[]{:S(2)}, u32[]{:S(2)}) %collective-permute-start.8) | collective-permute-done | bytes 196640 | tf_op jit(solution)/shard_map/ppermute | solution.py:169
  41.1 34.8 %pairs.1 = f32[8,72,256]{2,1,0:T(8,128)S(1)} custom-call(s32[16]{0:T(128)S(1)} %stack.113.refs_0_, s32[4,4,256]{2,1,0:T(4,128)S(1)} %maximum_convert_fusion.refs_1_, f32[2048,128]{1,0:T(8,128)S(1)} %get-tuple-element.12.refs_2_, f32[2048,128]{1,0:T(8,128)S(1)} %get-tuple-element.13.refs_3_, f32[2048,128]{1,0:T(8,128)S(1)} %get-tuple-element.14.refs_4_, ...), custom_call_target="tpu_custom_call" | custom-call | tf_op jit(solution)/shard_map/pairs/pallas_call | solution.py:194
  75.9 18.6 %all_to_all.10.r_ref = f32[8,72,256]{2,1,0:T(8,128)S(1)} all-to-all(f32[8,72,256]{2,1,0:T(8,128)S(1)} %pairs.1), channel_id=1, replica_groups=mesh['clu'=16,'sta'=8] {'sta'}, dimensions={0} | all-to-all | bytes 1179648 | tf_op jit(solution)/shard_map/all_to_all | solution.py:205
  94.8 1.8 %collective-permute-start.11 = (f32[72,64]{1,0:T(8,128)S(1)}, f32[72,64]{1,0:T(8,128)S(1)}, u32[]{:S(2)}, u32[]{:S(2)}) collective-permute-start(f32[72,64]{1,0:T(8,128)S(1)} %get-tuple-element.18), channel_id=1, source_target_pairs={{0,24},{8,16},{16,8},{24,0},{32,56},{40,48},{48,40},{56,32},{64,88... | collective-permute-start | bytes 55304 | tf_op jit(solution)/shard_map/ppermute | solution.py:168
  96.7 2.3 %collective-permute-done.10.refs_2_ = f32[72,64]{1,0:T(8,128)S(1)} collective-permute-done((f32[72,64]{1,0:T(8,128)S(1)}, f32[72,64]{1,0:T(8,128)S(1)}, u32[]{:S(2)}, u32[]{:S(2)}) %collective-permute-start.10) | collective-permute-done | bytes 18464 | tf_op jit(solution)/shard_map/ppermute | solution.py:168
  99.0 0.6 finish.1
  99.6 0.8 copy.9
  (43 shorter events, 1.4 us)
Async XLA Ops:
  0.0 7.2 %copy-start.4 = (bf16[256,6,256]{2,0,1:T(8,128)(2,1)S(1)}, bf16[256,6,256]{2,0,1:T(8,128)(2,1)}, u32[]{:S(2)}) copy-start(bf16[256,6,256]{2,0,1:T(8,128)(2,1)} %param.8) | copy-start | bytes 2359300
  0.0 21.2 %all-to-all-start = ((bf16[16,96,256]{2,1,0:T(8,128)(2,1)}), bf16[16,96,256]{2,1,0:T(8,128)(2,1)S(1)}, u32[]{:S(2)}, u32[]{:S(2)}) async-start(bf16[16,96,256]{2,1,0:T(8,128)(2,1)} %bitcast.61), calls=%async_computation | async-start | bytes 1572864 | tf_op jit(solution)/shard_map/all_to_all | solution.py:171
  5.8 0.7 copy-start.6
  6.5 0.7 copy-start.7
  7.4 13.9 %collective-permute-start.2 = (bf16[400,256]{1,0:T(8,128)(2,1)S(1)}, bf16[400,256]{1,0:T(8,128)(2,1)S(1)}, u32[]{:S(2)}, u32[]{:S(2)}) collective-permute-start(bf16[400,256]{1,0:T(8,128)(2,1)S(1)} %fusion.6), channel_id=1, source_target_pairs={{0,24},{8,16},{16,8},{24,0},{32,56},{40,48},{48,40},{56,32},{64,88... | collective-permute-start | bytes 614408 | tf_op jit(solution)/shard_map/ppermute | solution.py:168
  9.1 17.5 %collective-permute-start.1 = (bf16[400,256]{1,0:T(8,128)(2,1)S(1)}, bf16[400,256]{1,0:T(8,128)(2,1)S(1)}, u32[]{:S(2)}, u32[]{:S(2)}) collective-permute-start(bf16[400,256]{1,0:T(8,128)(2,1)S(1)} %fusion.5), channel_id=1, source_target_pairs={{0,16},{8,24},{16,0},{24,8},{32,48},{40,56},{48,32},{56,40},{64,80... | collective-permute-start | bytes 614408 | tf_op jit(solution)/shard_map/ppermute | solution.py:168
  9.6 23.8 %collective-permute-start = (bf16[400,256]{1,0:T(8,128)(2,1)S(1)}, bf16[400,256]{1,0:T(8,128)(2,1)S(1)}, u32[]{:S(2)}, u32[]{:S(2)}) collective-permute-start(bf16[400,256]{1,0:T(8,128)(2,1)S(1)} %fusion.4), channel_id=1, source_target_pairs={{0,8},{8,0},{16,24},{24,16},{32,40},{40,32},{48,56},{56,48},{64,72... | collective-permute-start | bytes 614408 | tf_op jit(solution)/shard_map/ppermute | solution.py:168
  9.7 0.7 copy-start.5
  21.2 12.1 %copy-start.3 = (bf16[256,768]{1,0:T(8,128)(2,1)S(1)}, bf16[256,768]{1,0:T(8,128)(2,1)}, u32[]{:S(2)}) copy-start(bf16[256,768]{1,0:T(8,128)(2,1)} %constant.111.clone.table_ref) | copy-start | bytes 1179652
  21.3 5.4 %collective-permute-start.5 = (bf16[96,256]{1,0:T(8,128)(2,1)S(1)}, bf16[96,256]{1,0:T(8,128)(2,1)S(1)}, u32[]{:S(2)}, u32[]{:S(2)}) collective-permute-start(bf16[96,256]{1,0:T(8,128)(2,1)S(1)} %get-tuple-element.20), channel_id=1, source_target_pairs={{0,24},{8,16},{16,8},{24,0},{32,56},{40,48},{48,40},{56,32},{64,88... | collective-permute-start | bytes 147464 | tf_op jit(solution)/shard_map/ppermute | solution.py:168
  21.8 6.4 %collective-permute-start.4 = (bf16[96,256]{1,0:T(8,128)(2,1)S(1)}, bf16[96,256]{1,0:T(8,128)(2,1)S(1)}, u32[]{:S(2)}, u32[]{:S(2)}) collective-permute-start(bf16[96,256]{1,0:T(8,128)(2,1)S(1)} %get-tuple-element.21), channel_id=1, source_target_pairs={{0,16},{8,24},{16,0},{24,8},{32,48},{40,56},{48,32},{56,40},{64,80... | collective-permute-start | bytes 147464 | tf_op jit(solution)/shard_map/ppermute | solution.py:168
  23.8 4.4 %collective-permute-start.3 = (bf16[96,256]{1,0:T(8,128)(2,1)S(1)}, bf16[96,256]{1,0:T(8,128)(2,1)S(1)}, u32[]{:S(2)}, u32[]{:S(2)}) collective-permute-start(bf16[96,256]{1,0:T(8,128)(2,1)S(1)} %get-tuple-element.22), channel_id=1, source_target_pairs={{0,8},{8,0},{16,24},{24,16},{32,40},{40,32},{48,56},{56,48},{64,72... | collective-permute-start | bytes 147464 | tf_op jit(solution)/shard_map/ppermute | solution.py:168
  28.2 8.1 %collective-permute-start.6 = (bf16[4,96,256]{2,1,0:T(8,128)(2,1)S(1)}, bf16[4,96,256]{2,1,0:T(8,128)(2,1)S(1)}, u32[]{:S(2)}, u32[]{:S(2)}) collective-permute-start(bf16[4,96,256]{2,1,0:T(8,128)(2,1)S(1)} %pad_maximum_fusion.refs_7_), channel_id=1, source_target_pairs={{0,32},{8,40},{16,48},{24,56},{32,64},{40,72},{48,80},{56,88},{64,... | collective-permute-start | bytes 589832 | tf_op jit(solution)/shard_map/ppermute | solution.py:169
  29.8 7.8 %collective-permute-start.7 = (bf16[4,96,256]{2,1,0:T(8,128)(2,1)S(1)}, bf16[4,96,256]{2,1,0:T(8,128)(2,1)S(1)}, u32[]{:S(2)}, u32[]{:S(2)}) collective-permute-start(bf16[4,96,256]{2,1,0:T(8,128)(2,1)S(1)} %pad_maximum_fusion.refs_7_), channel_id=1, source_target_pairs={{0,96},{8,104},{16,112},{24,120},{32,0},{40,8},{48,16},{56,24},{64... | collective-permute-start | bytes 589832 | tf_op jit(solution)/shard_map/ppermute | solution.py:169
  31.6 9.6 %collective-permute-start.8 = (bf16[4,96,256]{2,1,0:T(8,128)(2,1)S(1)}, bf16[4,96,256]{2,1,0:T(8,128)(2,1)S(1)}, u32[]{:S(2)}, u32[]{:S(2)}) collective-permute-start(bf16[4,96,256]{2,1,0:T(8,128)(2,1)S(1)} %pad_maximum_fusion.refs_7_), channel_id=1, source_target_pairs={{0,64},{8,72},{16,80},{24,88},{32,96},{40,104},{48,112},{56,120},{... | collective-permute-start | bytes 589832 | tf_op jit(solution)/shard_map/ppermute | solution.py:169
  33.3 7.8 %copy-start = (bf16[256,768]{1,0:T(8,128)(2,1)S(1)}, bf16[256,768]{1,0:T(8,128)(2,1)}, u32[]{:S(2)}) copy-start(bf16[256,768]{1,0:T(8,128)(2,1)} %constant.112.clone.refs_5_) | copy-start | bytes 1179652
  33.3 7.8 %copy-start.1 = (bf16[144,384]{1,0:T(8,128)(2,1)S(1)}, bf16[144,384]{1,0:T(8,128)(2,1)}, u32[]{:S(2)}) copy-start(bf16[144,384]{1,0:T(8,128)(2,1)} %constant.113.clone.refs_6_) | copy-start | bytes 331780
  94.6 2.0 %collective-permute-start.9 = (f32[72,64]{1,0:T(8,128)S(1)}, f32[72,64]{1,0:T(8,128)S(1)}, u32[]{:S(2)}, u32[]{:S(2)}) collective-permute-start(f32[72,64]{1,0:T(8,128)S(1)} %get-tuple-element.16), channel_id=1, source_target_pairs={{0,8},{8,0},{16,24},{24,16},{32,40},{40,32},{48,56},{56,48},{64,72... | collective-permute-start | bytes 55304 | tf_op jit(solution)/shard_map/ppermute | solution.py:168
  94.7 4.3 %collective-permute-start.10 = (f32[72,64]{1,0:T(8,128)S(1)}, f32[72,64]{1,0:T(8,128)S(1)}, u32[]{:S(2)}, u32[]{:S(2)}) collective-permute-start(f32[72,64]{1,0:T(8,128)S(1)} %get-tuple-element.17), channel_id=1, source_target_pairs={{0,16},{8,24},{16,0},{24,8},{32,48},{40,56},{48,32},{56,40},{64,80... | collective-permute-start | bytes 55304 | tf_op jit(solution)/shard_map/ppermute | solution.py:168
  94.8 4.2 %collective-permute-start.11 = (f32[72,64]{1,0:T(8,128)S(1)}, f32[72,64]{1,0:T(8,128)S(1)}, u32[]{:S(2)}, u32[]{:S(2)}) collective-permute-start(f32[72,64]{1,0:T(8,128)S(1)} %get-tuple-element.18), channel_id=1, source_target_pairs={{0,24},{8,16},{16,8},{24,0},{32,56},{40,48},{48,40},{56,32},{64,88... | collective-permute-start | bytes 55304 | tf_op jit(solution)/shard_map/ppermute | solution.py:168
  96.7 2.4 %copy-start.2 = (s32[1,4]{1,0:T(1,128)S(1)}, s32[1,4]{1,0:T(1,128)}, u32[]{:S(2)}) copy-start(s32[1,4]{1,0:T(1,128)} %near_ref.1) | copy-start | bytes 52

commit v3 on v2

v3 whole, which is shorter than its diff:
```python
import math

import jax
import jax.numpy as jnp
import numpy as np
from jax import lax
from jax.experimental import pallas as pl
from jax.experimental.pallas import tpu as pltpu
from jax.sharding import PartitionSpec as P

CH, SAMP, HALF, LAGS = 48, 256, 32, 65
N = 288
LO, EXTRA = 128, 17
ROWS = 72
EI, EJ = 68, 69


def tables():
    u = np.arange(SAMP)[:, None]
    k = np.arange(N // 2 + 1)[None, :]
    angle = 2 * math.pi * ((u * k) % N) / N
    c, s = np.cos(angle), np.sin(angle)
    ch, sh = c[:, LO:], s[:, LO:]
    pad = np.zeros((SAMP, 128 - 4 * EXTRA))
    left = np.concatenate([c[:, :LO], s[:, :LO], ch, sh, sh, ch, pad], axis=1)
    right = np.concatenate([c[:, :LO], s[:, :LO], ch, sh, ch, sh, pad], axis=1)
    lag = np.arange(LAGS)[:, None] - HALF
    angle = 2 * math.pi * ((lag * k) % N) / N
    weight = np.where((k == 0) | (k == N // 2), 1.0, 2.0) / N
    c, s = np.cos(angle) * weight, np.sin(angle) * weight
    back = np.zeros((ROWS, 384))
    back[:LAGS, :LO] = c[:, :LO]
    back[:LAGS, LO:2 * LO] = -s[:, :LO]
    ch, sh = c[:, LO:], s[:, LO:]
    back[:LAGS, 256:256 + 4 * EXTRA] = np.concatenate([ch, ch, -sh, sh], axis=1)
    back[LAGS, 256 + EI] = 1.0
    back[LAGS + 1, 256 + EJ] = 1.0

    def split(t, axis):
        t = t.astype(np.float32)
        hi = t.astype(jnp.bfloat16)
        lo = (t - hi.astype(np.float32)).astype(jnp.bfloat16)
        return np.concatenate([hi, lo], axis=axis)

    return split(left, 1), split(right, 1), split(back, 0)


def spectrum(x, table, energy_lane, one_lane):
    d = jnp.dot(x, table, preferred_element_type=jnp.float32)
    d = d[:, :384] + d[:, 384:]
    xf = x.astype(jnp.float32)
    energy = jnp.sum(xf * xf, axis=1, keepdims=True)
    lane = lax.broadcasted_iota(jnp.int32, (1, 128), 1)
    third = jnp.where(lane == energy_lane, energy, d[:, 256:])
    third = jnp.where(lane == one_lane, 1.0, third)
    return d[:, :128], d[:, 128:256], third


def clear_rest(out_ref, channels):
    events = out_ref.shape[0] // 24
    for k in range(3):
        for c in range(channels, 8):
            out_ref[pl.ds(k * 8 + c, events, stride=24), :] = jnp.zeros((events, 128), jnp.float32)


def left_kernel(table_ref, b0, b1, b2, b3, out_ref):
    events = out_ref.shape[0] // 24 // 4
    channels = b0.shape[0] // events
    clear_rest(out_ref, channels)
    for q, w_ref in enumerate((b0, b1, b2, b3)):
        parts = spectrum(w_ref[:channels * events], table_ref[...], EI, EJ)
        for c in range(channels):
            for n, part in enumerate(parts):
                to = pl.ds(q * events * 24 + n * 8 + c, events, stride=24)
                out_ref[to, :] = part[c * events:(c + 1) * events]


def right_kernel(base_ref, table_ref, p0, p1, p2, p3, out_ref):
    events = out_ref.shape[0] // 24
    clear_rest(out_ref, 4 * p0.shape[0] * p0.shape[1] // events)
    for n, p_ref in enumerate((p0, p1, p2, p3)):
        for m in range(p_ref.shape[0]):
            x = p_ref[m]
            parts = spectrum(x, table_ref[...], EJ, EI)
            for g in range(x.shape[0] // 32):
                row = base_ref[4 * n + m] + 32 * g
                c = row // events
                to = (row - c * events) * 24 + c
                for k, part in enumerate(parts):
                    out_ref[pl.ds(to + 8 * k, 32, stride=24), :] = part[32 * g:32 * g + 32]


def channel_sum(vs, sub):
    for shift in (4, 2, 1):
        keep = (sub & shift) == 0
        half = len(vs) // 2
        vs = [
            jnp.where(keep, a + pltpu.roll(a, 8 - shift, 0), b + pltpu.roll(b, shift, 0))
            for a, b in zip(vs[:half], vs[half:])
        ]
    return vs[0]


def pair_kernel(order_ref, local_ref, remote_ref, left, right, back_ref, *refs):
    out_refs, z = refs[:-1], refs[-1]
    width = out_refs[0].shape[1]
    share = width // 4
    pairs = local_ref.shape[0] // 4
    bh, bl = back_ref[:ROWS], back_ref[ROWS:]
    contract = (((1,), (1,)), ((), ()))
    dot = lambda a, b: lax.dot_general(a, b, contract, preferred_element_type=jnp.float32)
    sub = lax.broadcasted_iota(jnp.int32, (8, 128), 0)
    for t, out_ref in enumerate(out_refs):
        first = order_ref[t] * share

        def body(it, carry):
            for part in range(4):
                g = it * 4 + part
                q = g >> 3
                at = q * pairs + first + (g & 7) * 8
                products = [[], [], []]
                for p in range(8):
                    i = pl.multiple_of(local_ref[at + p], 8)
                    j = pl.multiple_of(remote_ref[at + p], 8)
                    xa, xb, xc = left[pl.ds(i, 8)], left[pl.ds(i + 8, 8)], left[pl.ds(i + 16, 8)]
                    ya, yb, yc = right[pl.ds(j, 8)], right[pl.ds(j + 8, 8)], right[pl.ds(j + 16, 8)]
                    for col, v in enumerate((xa * ya + xb * yb, xb * ya - xa * yb, xc * yc)):
                        products[col].append(v)
                to = pl.multiple_of(g * 8, 8)
                for col in range(3):
                    z[pl.ds(to, 8), col * 128:col * 128 + 128] = channel_sum(products[col], sub)
            return carry

        lax.fori_loop(0, width // 32, body, 0)
        zk = z[...]
        zh = zk.astype(jnp.bfloat16)
        zl = (zk - zh.astype(jnp.float32)).astype(jnp.bfloat16)
        out_ref[...] = dot(bh, zh) + dot(bh, zl) + dot(bl, zh)


def sum_kernel(*refs):
    parts, out_refs = refs[:-4], refs[-4:]
    total = parts[0][...]
    for ref in parts[1:]:
        total = total + ref[...]
    count = CH * SAMP
    ni = 1.0 / jnp.sqrt(total[LAGS:LAGS + 1] / count + 1e-6)
    nj = 1.0 / jnp.sqrt(total[LAGS + 1:LAGS + 2] / count + 1e-6)
    total = total * (ni * nj / count)
    share = out_refs[0].shape[1]
    for q, ref in enumerate(out_refs):
        ref[...] = total[:, q * share:(q + 1) * share]


def final_kernel(step_ref, near_ref, *refs):
    out_ref = refs[-1]
    for r, ref in enumerate(refs[:-1]):
        s = step_ref[r]
        out_ref[0, s] = (ref[...] * near_ref[0, s].astype(jnp.float32)).T[:, :LAGS]


SMEM = pl.BlockSpec(memory_space=pltpu.SMEM)
VMEM = pl.BlockSpec(memory_space=pltpu.VMEM)
PARAMS = pltpu.CompilerParams(vmem_limit_bytes=48 * 1024 * 1024)


def local(waves, owners, neighbours, pair_local, pair_remote):
    ev, ch, samp = waves.shape
    steps = owners.shape[0]
    pairs = pair_local.shape[2]
    n_clu, n_sta = lax.axis_size("clu"), lax.axis_size("sta")
    share = pairs // n_sta
    block = ev // steps
    left_table, right_table, back_table = (jnp.asarray(t) for t in tables())
    cube = waves.transpose(1, 0, 2)
    rows = cube.reshape(ch * ev, samp)
    chunk = ch * ev // n_clu
    f32, bf16 = jnp.float32, jnp.bfloat16
    shaped = jax.ShapeDtypeStruct

    me = lax.axis_index("clu")
    row, step = me // 4, me % 4
    near = lambda v, d: v if d == 0 else lax.ppermute(v, "clu", [(i, i ^ d) for i in range(n_clu)])
    turn = lambda v, d: lax.ppermute(v, "clu", [(i, (i + 4 * d) % n_clu) for i in range(n_clu)])

    spread = lax.all_to_all(rows.reshape(n_clu, chunk, samp), "clu", 0, 0)
    pick = lambda d: lax.dynamic_index_in_dim(spread, owners[step ^ d], 0, False)
    mine = jnp.stack([near(pick(d), d) for d in range(4)])
    pieces = [mine, turn(mine, 1), turn(mine, -1), turn(mine, 2)]
    base = jnp.stack([((row + r) % 4 * 4 + (step ^ d)) * chunk for r in (0, 3, 1, 2) for d in range(4)])

    lists = jnp.concatenate([pair_local[0], pair_remote[0]], axis=1).astype(bf16)
    lists = lists.reshape(steps, 2 * pairs // samp, samp)
    blocks = []
    for d in range(4):
        events = lax.dynamic_slice_in_dim(cube, (step ^ d) * block, block, 1).reshape(ch * block, samp)
        listed = lax.dynamic_index_in_dim(lists, step ^ d, 0, False)
        listed = jnp.pad(listed, ((0, 16 - listed.shape[0]), (0, 0)))
        blocks.append(near(jnp.concatenate([events, listed]), d))
    listed = jnp.stack([b[ch * block:ch * block + 2 * pairs // samp] for b in blocks]).astype(jnp.int32)
    listed = listed.reshape(4, 2, pairs) * 24
    first = listed[:, 0] + jnp.arange(4, dtype=jnp.int32)[:, None] * (block * 24)
    first, second = first.reshape(4 * pairs), listed[:, 1].reshape(4 * pairs)

    spectra = shaped((ev * 24, 128), f32)
    cost = pl.CostEstimate(flops=2 * ch * ev * samp * 768, bytes_accessed=4000000, transcendentals=0)
    left = pl.pallas_call(
        left_kernel, out_shape=spectra, in_specs=[VMEM] * 5, out_specs=VMEM,
        compiler_params=PARAMS, name="left", cost_estimate=cost,
    )(left_table, *blocks)
    right = pl.pallas_call(
        right_kernel, out_shape=spectra, in_specs=[SMEM] + [VMEM] * 5, out_specs=VMEM,
        compiler_params=PARAMS, name="right", cost_estimate=cost,
    )(base, right_table, *pieces)

    sta = lax.axis_index("sta")
    moves = [(2, 1), (1, 1), (3, 1), (0, 1), (2, 0), (1, 0), (3, 0), (0, 0)]
    target = lambda k, dz, dh: ((k // 2 + dz) % (n_sta // 2)) * 2 + (k % 2 + dh) % 2
    received = []
    for some in (moves[:4], moves[4:]):
        order = jnp.stack([target(sta, *m) for m in some]).astype(jnp.int32)
        raw = pl.pallas_call(
            pair_kernel, out_shape=(shaped((ROWS, 4 * share), f32),) * len(some),
            in_specs=[SMEM] * 3 + [VMEM] * 3, out_specs=(VMEM,) * len(some),
            scratch_shapes=[pltpu.VMEM((4 * share, 384), f32)],
            compiler_params=PARAMS, name="pairs", cost_estimate=cost,
        )(order, first, second, left, right, back_table)
        for m, v in zip(some, raw):
            if m != (0, 0):
                v = lax.ppermute(v, "sta", [(k, target(k, *m)) for k in range(n_sta)])
            received.append(v)

    done = pl.pallas_call(
        sum_kernel, out_shape=(shaped((ROWS, share), f32),) * 4,
        in_specs=[VMEM] * len(received), out_specs=(VMEM,) * 4, compiler_params=PARAMS, name="total",
    )(*received)
    done = [near(v, d) for d, v in enumerate(done)]
    order = jnp.stack([step ^ d for d in range(4)])
    out = pl.pallas_call(
        final_kernel, out_shape=shaped((1, steps, share, LAGS), f32),
        in_specs=[SMEM] * 2 + [VMEM] * 4, out_specs=VMEM, compiler_params=PARAMS, name="finish",
    )(order, neighbours, *done)
    return out.transpose(0, 1, 3, 2)


def solution(mesh):
    placed = (
        P("clu", "sta", None),
        P(),
        P("clu", None),
        P("clu", None, None),
        P("clu", None, None),
    )
    return jax.shard_map(
        local, mesh=mesh, in_specs=placed, out_specs=P("clu", None, None, "sta"), check_vma=False
    )
```

time: 102 us -> 89.3 us (0.88)
  blocking collectives: 18.6 us -> 0 us
  Pallas kernels: 36.5 us -> 18.6 us
  starting transfers between devices: 17.5 us -> 32.7 us
  waiting for transfers between devices: 16.5 us -> 22.8 us
  other arithmetic: 0.21 us -> 1.7 us
    all_to_all x1 -> x0, blocking collectives: 18.6 us -> none  [local(): parts = lax.all_to_all(raw, 'sta', 0, 0)]
    pallas_call x3 -> x5, Pallas kernels: 36.4 us -> 18.5 us  [the longest x2 14 us: local(): pl.pallas_call(pair_kernel, out_shape=(shaped((ROWS, 4 * share), f32),) *...]
    ppermute x0 -> x7, starting transfers between devices: none -> 15.7 us  [local(): v = lax.ppermute(v, 'sta', [(k, target(k, *m)) for k in range(n_sta)])]
    ppermute x0 -> x7, waiting for transfers between devices: none -> 5.07 us  [local(): v = lax.ppermute(v, 'sta', [(k, target(k, *m)) for k in range(n_sta)])]
    ppermute x9, waiting for transfers between devices: 9.74 us -> 11.5 us  [local(): lax.ppermute(v, 'clu', [(i, i ^ d) for i in range(n_clu)])]
    another operation x2 -> x3, other arithmetic: 0.01 us -> 1.48 us
    another operation x1, local copies, waits for them, and re-layouts: 0.07 us -> 1.28 us
  transfers between devices with their start and end apart: 13 -> 20, of which waited for: 8 -> 12; matrix products, arithmetic and copies ran while one was open for 1% -> 4% of each run, Pallas kernels for 1% -> 9%
where the time goes in v3:
time: 89.3 us; the launch traced here: 87.7 us
  starting transfers between devices  32.7 us (37%)
  waiting for transfers between devices  22.8 us (26%)
  Pallas kernels  18.6 us (21%)
  between operations  7.95 us (9%)
  local copies, waits for them, and re-layouts  3.91 us (4%)
  other arithmetic  1.7 us (2%)
    ppermute x7, starting transfers between devices, local(): v = lax.ppermute(v, 'sta', [(k, target(k, *m)) for k in range(n_sta)])  15.7 us
    pallas_call x2, Pallas kernels, local(): pl.pallas_call(pair_kernel, out_shape=(shaped((ROWS, 4 * share), f32),) *...  14 us
    ppermute x9, waiting for transfers between devices, local(): lax.ppermute(v, 'clu', [(i, i ^ d) for i in range(n_clu)])  11.5 us
    ppermute x9, starting transfers between devices, local(): lax.ppermute(v, 'clu', [(i, i ^ d) for i in range(n_clu)])  6.23 us
    ppermute x3, waiting for transfers between devices, local(): lax.ppermute(v, 'clu', [(i, (i + 4 * d) % n_clu) for i in range(n_clu)])  6.23 us
    all_to_all x1, starting transfers between devices, local(): spread = lax.all_to_all(rows.reshape(n_clu, chunk, samp), 'clu', 0, 0)  5.72 us
    ppermute x3, starting transfers between devices, local(): lax.ppermute(v, 'clu', [(i, (i + 4 * d) % n_clu) for i in range(n_clu)])  5.08 us
    ppermute x7, waiting for transfers between devices, local(): v = lax.ppermute(v, 'sta', [(k, target(k, *m)) for k in range(n_sta)])  5.07 us
  transfers between devices with their start and end apart: 20, of which 12 were waited for; matrix products, arithmetic and copies ran while one was open for 4% of the time, Pallas kernels for 9%

profile of v3, /device:TPU:0, one launch (start us, length us, event | category | flops | bytes accessed | tf_op | source)
XLA Modules:
  0.0 87.7 jit_solution(13736054301849976429)
XLA Ops:
  0.0 5.7 %all-to-all-start = ((bf16[16,96,256]{2,1,0:T(8,128)(2,1)}), bf16[16,96,256]{2,1,0:T(8,128)(2,1)S(1)}, u32[]{:S(2)}, u32[]{:S(2)}) async-start(bf16[16,96,256]{2,1,0:T(8,128)(2,1)} %bitcast.71), calls=%async_computation | async-start | bytes 1572864 | tf_op jit(solution)/shard_map/all_to_all | solution.py:186
  7.2 1.3 %constant_dynamic-slice_fusion.1 = (bf16[64,6,256]{2,0,1:T(8,128)(2,1)S(1)}, bf16[64,6,256]{2,0,1:T(8,128)(2,1)S(1)}, bf16[64,6,256]{2,0,1:T(8,128)(2,1)S(1)}, bf16[64,6,256]{2,0,1:T(8,128)(2,1)S(1)}) fusion(bf16[256,6,256]{2,0,1:T(8,128)(2,1)} %param.8, s32[]{:T(128)S(6)} %select_n.180, s32[]{:T(128)S(6)} %select_n.178, s32[]{:T(128)S(6)} %select_n.176, ...), kind=kLoop, calls=%fused_computation.24 | loop fusion | bytes 1572880 | tf_op jit(solution)/shard_map/dynamic-slice.3
  9.0 1.8 %collective-permute-start.1 = (bf16[400,256]{1,0:T(8,128)(2,1)S(1)}, bf16[400,256]{1,0:T(8,128)(2,1)S(1)}, u32[]{:S(2)}, u32[]{:S(2)}) collective-permute-start(bf16[400,256]{1,0:T(8,128)(2,1)S(1)} %fusion.5), channel_id=1, source_target_pairs={{0,16},{8,24},{16,0},{24,8},{32,48},{40,56},{48,32},{56,40},{64,80... | collective-permute-start | bytes 614408 | tf_op jit(solution)/shard_map/ppermute | solution.py:183
  19.6 2.6 %collective-permute-done.1.b2 = bf16[400,256]{1,0:T(8,128)(2,1)S(1)} collective-permute-done((bf16[400,256]{1,0:T(8,128)(2,1)S(1)}, bf16[400,256]{1,0:T(8,128)(2,1)S(1)}, u32[]{:S(2)}, u32[]{:S(2)}) %collective-permute-start.1) | collective-permute-done | bytes 204832 | tf_op jit(solution)/shard_map/ppermute | solution.py:183
  22.2 3.4 %collective-permute-done.2.b3 = bf16[400,256]{1,0:T(8,128)(2,1)S(1)} collective-permute-done((bf16[400,256]{1,0:T(8,128)(2,1)S(1)}, bf16[400,256]{1,0:T(8,128)(2,1)S(1)}, u32[]{:S(2)}, u32[]{:S(2)}) %collective-permute-start.2) | collective-permute-done | bytes 204832 | tf_op jit(solution)/shard_map/ppermute | solution.py:183
  26.2 1.5 %collective-permute-start.4 = (bf16[96,256]{1,0:T(8,128)(2,1)S(1)}, bf16[96,256]{1,0:T(8,128)(2,1)S(1)}, u32[]{:S(2)}, u32[]{:S(2)}) collective-permute-start(bf16[96,256]{1,0:T(8,128)(2,1)S(1)} %get-tuple-element.31), channel_id=1, source_target_pairs={{0,16},{8,24},{16,0},{24,8},{32,48},{40,56},{48,32},{56,40},{64,80... | collective-permute-start | bytes 147464 | tf_op jit(solution)/shard_map/ppermute | solution.py:183
  27.7 1.7 %collective-permute-done.5 = bf16[96,256]{1,0:T(8,128)(2,1)S(1)} collective-permute-done((bf16[96,256]{1,0:T(8,128)(2,1)S(1)}, bf16[96,256]{1,0:T(8,128)(2,1)S(1)}, u32[]{:S(2)}, u32[]{:S(2)}) %collective-permute-start.5) | collective-permute-done | bytes 49184 | tf_op jit(solution)/shard_map/ppermute | solution.py:183
  29.4 1.5 %collective-permute-done.4 = bf16[96,256]{1,0:T(8,128)(2,1)S(1)} collective-permute-done((bf16[96,256]{1,0:T(8,128)(2,1)S(1)}, bf16[96,256]{1,0:T(8,128)(2,1)S(1)}, u32[]{:S(2)}, u32[]{:S(2)}) %collective-permute-start.4) | collective-permute-done | bytes 49184 | tf_op jit(solution)/shard_map/ppermute | solution.py:183
  30.9 3.1 %collective-permute-start.8 = (bf16[4,96,256]{2,1,0:T(8,128)(2,1)S(1)}, bf16[4,96,256]{2,1,0:T(8,128)(2,1)S(1)}, u32[]{:S(2)}, u32[]{:S(2)}) collective-permute-start(bf16[4,96,256]{2,1,0:T(8,128)(2,1)S(1)} %pad_maximum_fusion.p0), channel_id=1, source_target_pairs={{0,64},{8,72},{16,80},{24,88},{32,96},{40,104},{48,112},{56,120},{... | collective-permute-start | bytes 589832 | tf_op jit(solution)/shard_map/ppermute | solution.py:184
  37.2 3.1 %collective-permute-done.8.p3 = bf16[4,96,256]{2,1,0:T(8,128)(2,1)S(1)} collective-permute-done((bf16[4,96,256]{2,1,0:T(8,128)(2,1)S(1)}, bf16[4,96,256]{2,1,0:T(8,128)(2,1)S(1)}, u32[]{:S(2)}, u32[]{:S(2)}) %collective-permute-start.8) | collective-permute-done | bytes 196640 | tf_op jit(solution)/shard_map/ppermute | solution.py:184
  40.3 3.0 %collective-permute-done.7.p2 = bf16[4,96,256]{2,1,0:T(8,128)(2,1)S(1)} collective-permute-done((bf16[4,96,256]{2,1,0:T(8,128)(2,1)S(1)}, bf16[4,96,256]{2,1,0:T(8,128)(2,1)S(1)}, u32[]{:S(2)}, u32[]{:S(2)}) %collective-permute-start.7) | collective-permute-done | bytes 196640 | tf_op jit(solution)/shard_map/ppermute | solution.py:184
  43.4 2.1 %right.1 = f32[6144,128]{1,0:T(8,128)S(1)} custom-call(s32[16]{0:T(128)S(1)} %stack.155.base_ref, bf16[256,768]{1,0:T(8,128)(2,1)S(1)} %copy-done.2, bf16[4,96,256]{2,1,0:T(8,128)(2,1)S(1)} %pad_maximum_fusion.p0, bf16[4,96,256]{2,1,0:T(8,128)(2,1)S(1)} %collective-permute-done.6.p1, bf16[4,96,256]{2,1,0:T(8,128)(2,1)S(1)} %collective-permute-done.7.p2, ...), custom_call_target="tpu_custom_call" | custom-call | flops 603979776 | bytes 4000000 | tf_op jit(solution)/shard_map/right/pallas_call | solution.py:211
  45.5 1.6 %copy-done = f32[6144,128]{1,0:T(8,128)} copy-done((f32[6144,128]{1,0:T(8,128)}, f32[6144,128]{1,0:T(8,128)S(1)}, u32[]{:S(2)}) %copy-start) | copy-done | bytes 3145752
  47.1 7.0 %pairs.3 = (f32[72,256]{1,0:T(8,128)S(1)}, f32[72,256]{1,0:T(8,128)S(1)}, f32[72,256]{1,0:T(8,128)S(1)}, f32[72,256]{1,0:T(8,128)S(1)}) custom-call(s32[4]{0:T(128)S(1)} %get-tuple-element.48.order_ref, s32[2048]{0:T(1024)S(1)} %add.261.local_ref, s32[2048]{0:T(1024)S(1)} %bitcast.69, f32[6144,128]{1,0:T(8,128)S(1)} %left.1, f32[6144,128]{1,0:T(8,128)} %copy-done, ...), custom_call_target="tpu_custom_call" | custom-call | flops 603979776 | bytes 4000000 | tf_op jit(solution)/shard_map/pairs/pallas_call | solution.py:222
  54.1 3.9 %collective-permute-start.13 = (f32[72,256]{1,0:T(8,128)S(1)}, f32[72,256]{1,0:T(8,128)S(1)}, u32[]{:S(2)}, u32[]{:S(2)}) collective-permute-start(f32[72,256]{1,0:T(8,128)S(1)} %get-tuple-element.21), channel_id=1, source_target_pairs={{0,4},{1,5},{2,6},{3,7},{4,0},{5,1},{6,2},{7,3},{8,12},{9,13},{10,... | collective-permute-start | bytes 221192 | tf_op jit(solution)/shard_map/ppermute | solution.py:230
  59.1 2.2 %collective-permute-start.15 = (f32[72,256]{1,0:T(8,128)S(1)}, f32[72,256]{1,0:T(8,128)S(1)}, u32[]{:S(2)}, u32[]{:S(2)}) collective-permute-start(f32[72,256]{1,0:T(8,128)S(1)} %get-tuple-element.23), channel_id=1, source_target_pairs={{0,6},{1,7},{2,0},{3,1},{4,2},{5,3},{6,4},{7,5},{8,14},{9,15},{10,... | collective-permute-start | bytes 221192 | tf_op jit(solution)/shard_map/ppermute | solution.py:230
  61.3 7.0 %pairs.2 = (f32[72,256]{1,0:T(8,128)S(1)}, f32[72,256]{1,0:T(8,128)S(1)}, f32[72,256]{1,0:T(8,128)S(1)}, f32[72,256]{1,0:T(8,128)S(1)}) custom-call(s32[4]{0:T(128)S(1)} %get-tuple-element.47.order_ref, s32[2048]{0:T(1024)S(1)} %add.261.local_ref, s32[2048]{0:T(1024)S(1)} %bitcast.70, f32[6144,128]{1,0:T(8,128)S(1)} %left.1, f32[6144,128]{1,0:T(8,128)} %copy-done, ...), custom_call_target="tpu_custom_call" | custom-call | flops 603979776 | bytes 4000000 | tf_op jit(solution)/shard_map/pairs/pallas_call | solution.py:222
  68.3 2.1 %collective-permute-start.9 = (f32[72,256]{1,0:T(8,128)S(1)}, f32[72,256]{1,0:T(8,128)S(1)}, u32[]{:S(2)}, u32[]{:S(2)}) collective-permute-start(f32[72,256]{1,0:T(8,128)S(1)} %get-tuple-element.17), channel_id=1, source_target_pairs={{0,5},{1,4},{2,7},{3,6},{4,1},{5,0},{6,3},{7,2},{8,13},{9,12},{10,... | collective-permute-start | bytes 221192 | tf_op jit(solution)/shard_map/ppermute | solution.py:230
  71.6 4.4 %collective-permute-start.11 = (f32[72,256]{1,0:T(8,128)S(1)}, f32[72,256]{1,0:T(8,128)S(1)}, u32[]{:S(2)}, u32[]{:S(2)}) collective-permute-start(f32[72,256]{1,0:T(8,128)S(1)} %get-tuple-element.19), channel_id=1, source_target_pairs={{0,7},{1,6},{2,1},{3,0},{4,3},{5,2},{6,5},{7,4},{8,15},{9,14},{10,... | collective-permute-start | bytes 221192 | tf_op jit(solution)/shard_map/ppermute | solution.py:230
  77.0 1.3 %collective-permute-done.10.refs_1_ = f32[72,256]{1,0:T(8,128)S(1)} collective-permute-done((f32[72,256]{1,0:T(8,128)S(1)}, f32[72,256]{1,0:T(8,128)S(1)}, u32[]{:S(2)}, u32[]{:S(2)}) %collective-permute-start.10) | collective-permute-done | bytes 73760 | tf_op jit(solution)/shard_map/ppermute | solution.py:230
  79.5 2.3 %collective-permute-done.12.refs_3_ = f32[72,256]{1,0:T(8,128)S(1)} collective-permute-done((f32[72,256]{1,0:T(8,128)S(1)}, f32[72,256]{1,0:T(8,128)S(1)}, u32[]{:S(2)}, u32[]{:S(2)}) %collective-permute-start.12) | collective-permute-done | bytes 73760 | tf_op jit(solution)/shard_map/ppermute | solution.py:230
  82.2 1.8 %collective-permute-start.18 = (f32[72,64]{1,0:T(8,128)S(1)}, f32[72,64]{1,0:T(8,128)S(1)}, u32[]{:S(2)}, u32[]{:S(2)}) collective-permute-start(f32[72,64]{1,0:T(8,128)S(1)} %get-tuple-element.28), channel_id=1, source_target_pairs={{0,24},{8,16},{16,8},{24,0},{32,56},{40,48},{48,40},{56,32},{64,88... | collective-permute-start | bytes 55304 | tf_op jit(solution)/shard_map/ppermute | solution.py:183
  84.0 2.3 %collective-permute-done.17.refs_2_ = f32[72,64]{1,0:T(8,128)S(1)} collective-permute-done((f32[72,64]{1,0:T(8,128)S(1)}, f32[72,64]{1,0:T(8,128)S(1)}, u32[]{:S(2)}, u32[]{:S(2)}) %collective-permute-start.17) | collective-permute-done | bytes 18464 | tf_op jit(solution)/shard_map/ppermute | solution.py:183
  86.4 1.3 %finish.1 = f32[1,4,64,65]{3,2,1,0:T(8,128)} custom-call(s32[4]{0:T(128)S(1)} %pad_add_fusion.step_ref, s32[1,4]{1,0:T(1,128)S(1)} %copy-done.4, f32[72,64]{1,0:T(8,128)S(1)} %get-tuple-element.25.refs_0_, f32[72,64]{1,0:T(8,128)S(1)} %collective-permute-done.16.refs_1_, f32[72,64]{1,0:T(8,128)S(1)} %collective-permute-done.17.refs_2_, ...), custom_call_target="tpu_custom_call" | custom-call | tf_op jit(solution)/shard_map/finish/pallas_call | solution.py:239
  (63 shorter events, 11.7 us)
Async XLA Ops:
  0.0 11.1 %copy-start.5 = (s32[4]{0:T(128)S(1)}, s32[4]{0:T(128)}, u32[]{:S(2)}) copy-start(s32[4]{0:T(128)} %param.9) | copy-start | bytes 52
  0.0 36.0 %copy-start.3 = (bf16[256,768]{1,0:T(8,128)(2,1)S(1)}, bf16[256,768]{1,0:T(8,128)(2,1)}, u32[]{:S(2)}) copy-start(bf16[256,768]{1,0:T(8,128)(2,1)} %constant.205.clone.table_ref) | copy-start | bytes 1179652
  0.0 25.6 %all-to-all-start = ((bf16[16,96,256]{2,1,0:T(8,128)(2,1)}), bf16[16,96,256]{2,1,0:T(8,128)(2,1)S(1)}, u32[]{:S(2)}, u32[]{:S(2)}) async-start(bf16[16,96,256]{2,1,0:T(8,128)(2,1)} %bitcast.71), calls=%async_computation | async-start | bytes 1572864 | tf_op jit(solution)/shard_map/all_to_all | solution.py:186
  8.5 11.0 %collective-permute-start = (bf16[400,256]{1,0:T(8,128)(2,1)S(1)}, bf16[400,256]{1,0:T(8,128)(2,1)S(1)}, u32[]{:S(2)}, u32[]{:S(2)}) collective-permute-start(bf16[400,256]{1,0:T(8,128)(2,1)S(1)} %fusion.4), channel_id=1, source_target_pairs={{0,8},{8,0},{16,24},{24,16},{32,40},{40,32},{48,56},{56,48},{64,72... | collective-permute-start | bytes 614408 | tf_op jit(solution)/shard_map/ppermute | solution.py:183
  9.0 13.2 %collective-permute-start.1 = (bf16[400,256]{1,0:T(8,128)(2,1)S(1)}, bf16[400,256]{1,0:T(8,128)(2,1)S(1)}, u32[]{:S(2)}, u32[]{:S(2)}) collective-permute-start(bf16[400,256]{1,0:T(8,128)(2,1)S(1)} %fusion.5), channel_id=1, source_target_pairs={{0,16},{8,24},{16,0},{24,8},{32,48},{40,56},{48,32},{56,40},{64,80... | collective-permute-start | bytes 614408 | tf_op jit(solution)/shard_map/ppermute | solution.py:183
  10.8 32.6 %copy-start.2 = (bf16[256,768]{1,0:T(8,128)(2,1)S(1)}, bf16[256,768]{1,0:T(8,128)(2,1)}, u32[]{:S(2)}) copy-start(bf16[256,768]{1,0:T(8,128)(2,1)} %constant.206.clone.table_ref) | copy-start | bytes 1179652
  10.8 14.8 %collective-permute-start.2 = (bf16[400,256]{1,0:T(8,128)(2,1)S(1)}, bf16[400,256]{1,0:T(8,128)(2,1)S(1)}, u32[]{:S(2)}, u32[]{:S(2)}) collective-permute-start(bf16[400,256]{1,0:T(8,128)(2,1)S(1)} %fusion.6), channel_id=1, source_target_pairs={{0,24},{8,16},{16,8},{24,0},{32,56},{40,48},{48,40},{56,32},{64,88... | collective-permute-start | bytes 614408 | tf_op jit(solution)/shard_map/ppermute | solution.py:183
  25.7 3.7 %collective-permute-start.5 = (bf16[96,256]{1,0:T(8,128)(2,1)S(1)}, bf16[96,256]{1,0:T(8,128)(2,1)S(1)}, u32[]{:S(2)}, u32[]{:S(2)}) collective-permute-start(bf16[96,256]{1,0:T(8,128)(2,1)S(1)} %get-tuple-element.30), channel_id=1, source_target_pairs={{0,24},{8,16},{16,8},{24,0},{32,56},{40,48},{48,40},{56,32},{64,88... | collective-permute-start | bytes 147464 | tf_op jit(solution)/shard_map/ppermute | solution.py:183
  26.2 4.7 %collective-permute-start.4 = (bf16[96,256]{1,0:T(8,128)(2,1)S(1)}, bf16[96,256]{1,0:T(8,128)(2,1)S(1)}, u32[]{:S(2)}, u32[]{:S(2)}) collective-permute-start(bf16[96,256]{1,0:T(8,128)(2,1)S(1)} %get-tuple-element.31), channel_id=1, source_target_pairs={{0,16},{8,24},{16,0},{24,8},{32,48},{40,56},{48,32},{56,40},{64,80... | collective-permute-start | bytes 147464 | tf_op jit(solution)/shard_map/ppermute | solution.py:183
  27.7 3.2 %collective-permute-start.3 = (bf16[96,256]{1,0:T(8,128)(2,1)S(1)}, bf16[96,256]{1,0:T(8,128)(2,1)S(1)}, u32[]{:S(2)}, u32[]{:S(2)}) collective-permute-start(bf16[96,256]{1,0:T(8,128)(2,1)S(1)} %get-tuple-element.32), channel_id=1, source_target_pairs={{0,8},{8,0},{16,24},{24,16},{32,40},{40,32},{48,56},{56,48},{64,72... | collective-permute-start | bytes 147464 | tf_op jit(solution)/shard_map/ppermute | solution.py:183
  30.9 9.4 %collective-permute-start.8 = (bf16[4,96,256]{2,1,0:T(8,128)(2,1)S(1)}, bf16[4,96,256]{2,1,0:T(8,128)(2,1)S(1)}, u32[]{:S(2)}, u32[]{:S(2)}) collective-permute-start(bf16[4,96,256]{2,1,0:T(8,128)(2,1)S(1)} %pad_maximum_fusion.p0), channel_id=1, source_target_pairs={{0,64},{8,72},{16,80},{24,88},{32,96},{40,104},{48,112},{56,120},{... | collective-permute-start | bytes 589832 | tf_op jit(solution)/shard_map/ppermute | solution.py:184
  33.9 9.4 %collective-permute-start.7 = (bf16[4,96,256]{2,1,0:T(8,128)(2,1)S(1)}, bf16[4,96,256]{2,1,0:T(8,128)(2,1)S(1)}, u32[]{:S(2)}, u32[]{:S(2)}) collective-permute-start(bf16[4,96,256]{2,1,0:T(8,128)(2,1)S(1)} %pad_maximum_fusion.p0), channel_id=1, source_target_pairs={{0,96},{8,104},{16,112},{24,120},{32,0},{40,8},{48,16},{56,24},{64... | collective-permute-start | bytes 589832 | tf_op jit(solution)/shard_map/ppermute | solution.py:184
  35.2 8.3 %collective-permute-start.6 = (bf16[4,96,256]{2,1,0:T(8,128)(2,1)S(1)}, bf16[4,96,256]{2,1,0:T(8,128)(2,1)S(1)}, u32[]{:S(2)}, u32[]{:S(2)}) collective-permute-start(bf16[4,96,256]{2,1,0:T(8,128)(2,1)S(1)} %pad_maximum_fusion.p0), channel_id=1, source_target_pairs={{0,32},{8,40},{16,48},{24,56},{32,64},{40,72},{48,80},{56,88},{64,... | collective-permute-start | bytes 589832 | tf_op jit(solution)/shard_map/ppermute | solution.py:184
  54.1 17.5 %collective-permute-start.13 = (f32[72,256]{1,0:T(8,128)S(1)}, f32[72,256]{1,0:T(8,128)S(1)}, u32[]{:S(2)}, u32[]{:S(2)}) collective-permute-start(f32[72,256]{1,0:T(8,128)S(1)} %get-tuple-element.21), channel_id=1, source_target_pairs={{0,4},{1,5},{2,6},{3,7},{4,0},{5,1},{6,2},{7,3},{8,12},{9,13},{10,... | collective-permute-start | bytes 221192 | tf_op jit(solution)/shard_map/ppermute | solution.py:230
  58.1 18.0 %collective-permute-start.14 = (f32[72,256]{1,0:T(8,128)S(1)}, f32[72,256]{1,0:T(8,128)S(1)}, u32[]{:S(2)}, u32[]{:S(2)}) collective-permute-start(f32[72,256]{1,0:T(8,128)S(1)} %get-tuple-element.22), channel_id=1, source_target_pairs={{0,2},{1,3},{2,4},{3,5},{4,6},{5,7},{6,0},{7,1},{8,10},{9,11},{10,... | collective-permute-start | bytes 221192 | tf_op jit(solution)/shard_map/ppermute | solution.py:230
  59.1 17.8 %collective-permute-start.15 = (f32[72,256]{1,0:T(8,128)S(1)}, f32[72,256]{1,0:T(8,128)S(1)}, u32[]{:S(2)}, u32[]{:S(2)}) collective-permute-start(f32[72,256]{1,0:T(8,128)S(1)} %get-tuple-element.23), channel_id=1, source_target_pairs={{0,6},{1,7},{2,0},{3,1},{4,2},{5,3},{6,4},{7,5},{8,14},{9,15},{10,... | collective-permute-start | bytes 221192 | tf_op jit(solution)/shard_map/ppermute | solution.py:230
  61.3 25.1 %copy-start.4 = (s32[1,4]{1,0:T(1,128)S(1)}, s32[1,4]{1,0:T(1,128)}, u32[]{:S(2)}) copy-start(s32[1,4]{1,0:T(1,128)} %near_ref.1) | copy-start | bytes 52
  68.3 8.7 %collective-permute-start.9 = (f32[72,256]{1,0:T(8,128)S(1)}, f32[72,256]{1,0:T(8,128)S(1)}, u32[]{:S(2)}, u32[]{:S(2)}) collective-permute-start(f32[72,256]{1,0:T(8,128)S(1)} %get-tuple-element.17), channel_id=1, source_target_pairs={{0,5},{1,4},{2,7},{3,6},{4,1},{5,0},{6,3},{7,2},{8,13},{9,12},{10,... | collective-permute-start | bytes 221192 | tf_op jit(solution)/shard_map/ppermute | solution.py:230
  70.4 8.0 %collective-permute-start.10 = (f32[72,256]{1,0:T(8,128)S(1)}, f32[72,256]{1,0:T(8,128)S(1)}, u32[]{:S(2)}, u32[]{:S(2)}) collective-permute-start(f32[72,256]{1,0:T(8,128)S(1)} %get-tuple-element.18), channel_id=1, source_target_pairs={{0,3},{1,2},{2,5},{3,4},{4,7},{5,6},{6,1},{7,0},{8,11},{9,10},{10,... | collective-permute-start | bytes 221192 | tf_op jit(solution)/shard_map/ppermute | solution.py:230
  71.6 7.9 %collective-permute-start.11 = (f32[72,256]{1,0:T(8,128)S(1)}, f32[72,256]{1,0:T(8,128)S(1)}, u32[]{:S(2)}, u32[]{:S(2)}) collective-permute-start(f32[72,256]{1,0:T(8,128)S(1)} %get-tuple-element.19), channel_id=1, source_target_pairs={{0,7},{1,6},{2,1},{3,0},{4,3},{5,2},{6,5},{7,4},{8,15},{9,14},{10,... | collective-permute-start | bytes 221192 | tf_op jit(solution)/shard_map/ppermute | solution.py:230
  76.0 5.9 %collective-permute-start.12 = (f32[72,256]{1,0:T(8,128)S(1)}, f32[72,256]{1,0:T(8,128)S(1)}, u32[]{:S(2)}, u32[]{:S(2)}) collective-permute-start(f32[72,256]{1,0:T(8,128)S(1)} %get-tuple-element.20), channel_id=1, source_target_pairs={{0,1},{1,0},{2,3},{3,2},{4,5},{5,4},{6,7},{7,6},{8,9},{9,8},{10,11... | collective-permute-start | bytes 221192 | tf_op jit(solution)/shard_map/ppermute | solution.py:230
  82.0 2.0 %collective-permute-start.16 = (f32[72,64]{1,0:T(8,128)S(1)}, f32[72,64]{1,0:T(8,128)S(1)}, u32[]{:S(2)}, u32[]{:S(2)}) collective-permute-start(f32[72,64]{1,0:T(8,128)S(1)} %get-tuple-element.26), channel_id=1, source_target_pairs={{0,8},{8,0},{16,24},{24,16},{32,40},{40,32},{48,56},{56,48},{64,72... | collective-permute-start | bytes 55304 | tf_op jit(solution)/shard_map/ppermute | solution.py:183
  82.1 4.3 %collective-permute-start.17 = (f32[72,64]{1,0:T(8,128)S(1)}, f32[72,64]{1,0:T(8,128)S(1)}, u32[]{:S(2)}, u32[]{:S(2)}) collective-permute-start(f32[72,64]{1,0:T(8,128)S(1)} %get-tuple-element.27), channel_id=1, source_target_pairs={{0,16},{8,24},{16,0},{24,8},{32,48},{40,56},{48,32},{56,40},{64,80... | collective-permute-start | bytes 55304 | tf_op jit(solution)/shard_map/ppermute | solution.py:183
  82.2 4.2 %collective-permute-start.18 = (f32[72,64]{1,0:T(8,128)S(1)}, f32[72,64]{1,0:T(8,128)S(1)}, u32[]{:S(2)}, u32[]{:S(2)}) collective-permute-start(f32[72,64]{1,0:T(8,128)S(1)} %get-tuple-element.28), channel_id=1, source_target_pairs={{0,24},{8,16},{16,8},{24,0},{32,56},{40,48},{48,40},{56,32},{64,88... | collective-permute-start | bytes 55304 | tf_op jit(solution)/shard_map/ppermute | solution.py:183
  (2 other events, 11.6 us)

commit v4 on v3

--- a/solution.py
+++ b/solution.py
@@ -56,6 +56,16 @@
     return d[:, :128], d[:, 128:256], third
 
 
+def pick_kernel(from_ref, g0, g1, g2, g3, keep_ref, give_ref):
+    for d in range(4):
+        to = (keep_ref, give_ref)[d % 2]
+        for n, ref in enumerate((g0, g1, g2, g3)):
+
+            @pl.when(from_ref[d] == n)
+            def _():
+                to[d // 2] = ref[...]
+
+
 def clear_rest(out_ref, channels):
     events = out_ref.shape[0] // 24
     for k in range(3):
@@ -77,17 +87,16 @@
 
 def right_kernel(base_ref, table_ref, p0, p1, p2, p3, out_ref):
     events = out_ref.shape[0] // 24
-    clear_rest(out_ref, 4 * p0.shape[0] * p0.shape[1] // events)
+    clear_rest(out_ref, 4 * p0.shape[0] // events)
     for n, p_ref in enumerate((p0, p1, p2, p3)):
-        for m in range(p_ref.shape[0]):
-            x = p_ref[m]
-            parts = spectrum(x, table_ref[...], EJ, EI)
-            for g in range(x.shape[0] // 32):
-                row = base_ref[4 * n + m] + 32 * g
-                c = row // events
-                to = (row - c * events) * 24 + c
-                for k, part in enumerate(parts):
-                    out_ref[pl.ds(to + 8 * k, 32, stride=24), :] = part[32 * g:32 * g + 32]
+        x = p_ref[...]
+        parts = spectrum(x, table_ref[...], EJ, EI)
+        for g in range(x.shape[0] // 32):
+            row = base_ref[n] + 32 * g
+            c = row // events
+            to = (row - c * events) * 24 + c
+            for k, part in enumerate(parts):
+                out_ref[pl.ds(to + 8 * k, 32, stride=24), :] = part[32 * g:32 * g + 32]
 
 
 def channel_sum(vs, sub):
@@ -101,16 +110,18 @@
     return vs[0]
 
 
-def pair_kernel(order_ref, local_ref, remote_ref, left, right, back_ref, *refs):
-    out_refs, z = refs[:-1], refs[-1]
-    width = out_refs[0].shape[1]
+def pair_kernel(order_ref, local_ref, remote_ref, left, right, back_ref, out_ref, next_ref, z):
+    width = out_ref.shape[2]
+    half = out_ref.shape[0]
+    for t in range(2 * half):
+        next_ref[t] = order_ref[(t + half) % (2 * half)]
     share = width // 4
     pairs = local_ref.shape[0] // 4
     bh, bl = back_ref[:ROWS], back_ref[ROWS:]
     contract = (((1,), (1,)), ((), ()))
     dot = lambda a, b: lax.dot_general(a, b, contract, preferred_element_type=jnp.float32)
     sub = lax.broadcasted_iota(jnp.int32, (8, 128), 0)
-    for t, out_ref in enumerate(out_refs):
+    for t in range(half):
         first = order_ref[t] * share
 
         def body(it, carry):
@@ -135,7 +146,12 @@
         zk = z[...]
         zh = zk.astype(jnp.bfloat16)
         zl = (zk - zh.astype(jnp.float32)).astype(jnp.bfloat16)
-        out_ref[...] = dot(bh, zh) + dot(bh, zl) + dot(bl, zh)
+        out_ref[t] = dot(bh, zh) + dot(bh, zl) + dot(bl, zh)
+
+
+def add_kernel(a_ref, b_ref, *out_refs):
+    for t, ref in enumerate(out_refs):
+        ref[...] = a_ref[t] + b_ref[t]
 
 
 def sum_kernel(*refs):
@@ -161,7 +177,8 @@
 
 SMEM = pl.BlockSpec(memory_space=pltpu.SMEM)
 VMEM = pl.BlockSpec(memory_space=pltpu.VMEM)
-PARAMS = pltpu.CompilerParams(vmem_limit_bytes=48 * 1024 * 1024)
+PARAMS = pltpu.CompilerParams(vmem_limit_bytes=20 * 1024 * 1024)
+SMALL = pltpu.CompilerParams(vmem_limit_bytes=8 * 1024 * 1024)
 
 
 def local(waves, owners, neighbours, pair_local, pair_remote):
@@ -174,7 +191,6 @@
     left_table, right_table, back_table = (jnp.asarray(t) for t in tables())
     cube = waves.transpose(1, 0, 2)
     rows = cube.reshape(ch * ev, samp)
-    chunk = ch * ev // n_clu
     f32, bf16 = jnp.float32, jnp.bfloat16
     shaped = jax.ShapeDtypeStruct
 
@@ -183,11 +199,22 @@
     near = lambda v, d: v if d == 0 else lax.ppermute(v, "clu", [(i, i ^ d) for i in range(n_clu)])
     turn = lambda v, d: lax.ppermute(v, "clu", [(i, (i + 4 * d) % n_clu) for i in range(n_clu)])
 
-    spread = lax.all_to_all(rows.reshape(n_clu, chunk, samp), "clu", 0, 0)
-    pick = lambda d: lax.dynamic_index_in_dim(spread, owners[step ^ d], 0, False)
-    mine = jnp.stack([near(pick(d), d) for d in range(4)])
-    pieces = [mine, turn(mine, 1), turn(mine, -1), turn(mine, 2)]
-    base = jnp.stack([((row + r) % 4 * 4 + (step ^ d)) * chunk for r in (0, 3, 1, 2) for d in range(4)])
+    quarter = ch * ev // 4
+    got = []
+    for d in range(4):
+        part = lax.dynamic_slice_in_dim(rows, (row + d) % 4 * quarter, quarter, 0)
+        got.append(part if d == 0 else turn(part, d))
+    source = [owners[step ^ d] for d in range(4)]
+    keep, give = pl.pallas_call(
+        pick_kernel, out_shape=(shaped((2, quarter, samp), bf16),) * 2,
+        in_specs=[SMEM] + [VMEM] * 4, out_specs=(VMEM,) * 2, compiler_params=SMALL, name="pick",
+    )(jnp.stack([(row + 4 - o // 4) % 4 for o in source]), *got)
+    other = near(give, 1)
+    mine = jnp.where(source[0] % 2 == me % 2, keep[0], other[0])
+    theirs = jnp.where(source[2] % 2 == me % 2, keep[1], other[1])
+    mine = jnp.where(source[0] // 2 % 2 == me // 2 % 2, mine, near(theirs, 2))
+    pieces = [mine] + [turn(mine, d) for d in (1, -1, 2)]
+    base = jnp.stack([(row + r) % 4 * quarter for r in (0, 3, 1, 2)])
 
     lists = jnp.concatenate([pair_local[0], pair_remote[0]], axis=1).astype(bf16)
     lists = lists.reshape(steps, 2 * pairs // samp, samp)
@@ -214,25 +241,32 @@
     )(base, right_table, *pieces)
 
     sta = lax.axis_index("sta")
-    moves = [(2, 1), (1, 1), (3, 1), (0, 1), (2, 0), (1, 0), (3, 0), (0, 0)]
+    moves = (2, 1, 3, 0)
     target = lambda k, dz, dh: ((k // 2 + dz) % (n_sta // 2)) * 2 + (k % 2 + dh) % 2
-    received = []
-    for some in (moves[:4], moves[4:]):
-        order = jnp.stack([target(sta, *m) for m in some]).astype(jnp.int32)
-        raw = pl.pallas_call(
-            pair_kernel, out_shape=(shaped((ROWS, 4 * share), f32),) * len(some),
-            in_specs=[SMEM] * 3 + [VMEM] * 3, out_specs=(VMEM,) * len(some),
+    order = jnp.stack([target(sta, dz, dh) for dh in (1, 0) for dz in moves]).astype(jnp.int32)
+    halves = []
+    for _ in range(2):
+        raw, order = pl.pallas_call(
+            pair_kernel,
+            out_shape=(shaped((n_sta // 2, ROWS, 4 * share), f32), shaped((n_sta,), jnp.int32)),
+            in_specs=[SMEM] * 3 + [VMEM] * 3, out_specs=(VMEM, SMEM),
             scratch_shapes=[pltpu.VMEM((4 * share, 384), f32)],
             compiler_params=PARAMS, name="pairs", cost_estimate=cost,
         )(order, first, second, left, right, back_table)
-        for m, v in zip(some, raw):
-            if m != (0, 0):
-                v = lax.ppermute(v, "sta", [(k, target(k, *m)) for k in range(n_sta)])
-            received.append(v)
+        halves.append(raw)
+    across = lax.ppermute(halves[0], "sta", [(k, target(k, 0, 1)) for k in range(n_sta)])
+    sums = pl.pallas_call(
+        add_kernel, out_shape=(shaped((ROWS, 4 * share), f32),) * 4,
+        in_specs=[VMEM] * 2, out_specs=(VMEM,) * 4, compiler_params=SMALL, name="add",
+    )(across, halves[1])
+    received = [
+        v if dz == 0 else lax.ppermute(v, "sta", [(k, target(k, dz, 0)) for k in range(n_sta)])
+        for dz, v in zip(moves, sums)
+    ]
 
     done = pl.pallas_call(
         sum_kernel, out_shape=(shaped((ROWS, share), f32),) * 4,
-        in_specs=[VMEM] * len(received), out_specs=(VMEM,) * 4, compiler_params=PARAMS, name="total",
+        in_specs=[VMEM] * len(received), out_specs=(VMEM,) * 4, compiler_params=SMALL, name="total",
     )(*received)
     done = [near(v, d) for d, v in enumerate(done)]
     order = jnp.stack([step ^ d for d in range(4)])

time: 89.3 us -> 81.4 us (0.912)
  starting transfers between devices: 32.7 us -> 25.2 us
  between operations: 7.95 us -> 9.92 us
  waiting for transfers between devices: 22.8 us -> 21 us
  Pallas kernels: 18.6 us -> 17.1 us
  other arithmetic: 1.7 us -> 3.16 us
    all_to_all x1 -> x0, starting transfers between devices: 5.72 us -> none  [local(): spread = lax.all_to_all(rows.reshape(n_clu, chunk, samp), 'clu', 0, 0)]
    ppermute x7 -> x4, starting transfers between devices: 15.7 us -> 10 us  [the longest x3 7.2 us: local(): lax.ppermute(v, 'sta', [(k, target(k, dz, 0)) for k in range(n_sta)])]
    ppermute x3 -> x6, starting transfers between devices: 5.08 us -> 9.41 us  [local(): lax.ppermute(v, 'clu', [(i, (i + 4 * d) % n_clu) for i in range(n_clu)])]
    ppermute x7 -> x4, waiting for transfers between devices: 5.07 us -> 3.25 us  [the longest x3 2.33 us: local(): lax.ppermute(v, 'sta', [(k, target(k, dz, 0)) for k in range(n_sta)])]
    unnamed x14 -> x12, local copies, waits for them, and re-layouts: 1.72 us -> 0.1 us
    concatenate x4, other arithmetic: 0.06 us -> 1.42 us  [local(): blocks.append(near(jnp.concatenate([events, listed]), d))]
    pallas_call x2 -> x4, Pallas kernels: 14 us -> 12.7 us  [the longest x2 11.9 us: local(): pl.pallas_call(pair_kernel, out_shape=(shaped((n_sta // 2, ROWS, 4 * shar...]
    dynamic_slice x2, local copies, waits for them, and re-layouts: 0.71 us -> 1.94 us  [the longest x1 1.28 us: local(): part = lax.dynamic_slice_in_dim(rows, (row + d) % 4 * quarter, quarter, 0)]
  transfers between devices with their start and end apart: 20 -> 18, of which waited for: 12 -> 9; matrix products, arithmetic and copies ran while one was open for 4% -> 7% of each run, Pallas kernels for 9% -> 10%
where the time goes in v4:
time: 81.4 us; the launch traced here: 79.9 us
  starting transfers between devices  25.2 us (31%)
  waiting for transfers between devices  21 us (26%)
  Pallas kernels  17.1 us (21%)
  between operations  9.92 us (12%)
  local copies, waits for them, and re-layouts  3.5 us (4%)
  other arithmetic  3.16 us (4%)
    pallas_call x2, Pallas kernels, local(): pl.pallas_call(pair_kernel, out_shape=(shaped((n_sta // 2, ROWS, 4 * shar...  11.9 us
    ppermute x8, waiting for transfers between devices, local(): lax.ppermute(v, 'clu', [(i, i ^ d) for i in range(n_clu)])  10.8 us
    ppermute x6, starting transfers between devices, local(): lax.ppermute(v, 'clu', [(i, (i + 4 * d) % n_clu) for i in range(n_clu)])  9.41 us
    ppermute x3, starting transfers between devices, local(): lax.ppermute(v, 'sta', [(k, target(k, dz, 0)) for k in range(n_sta)])  7.2 us
    ppermute x6, waiting for transfers between devices, local(): lax.ppermute(v, 'clu', [(i, (i + 4 * d) % n_clu) for i in range(n_clu)])  6.9 us
    ppermute x8, starting transfers between devices, local(): lax.ppermute(v, 'clu', [(i, i ^ d) for i in range(n_clu)])  5.82 us
    ppermute x1, starting transfers between devices, local(): lax.ppermute(halves[0], 'sta', [(k, target(k, 0, 1)) for k in range(n_sta)])  2.81 us
    ppermute x3, waiting for transfers between devices, local(): lax.ppermute(v, 'sta', [(k, target(k, dz, 0)) for k in range(n_sta)])  2.33 us
  transfers between devices with their start and end apart: 18, of which 9 were waited for; matrix products, arithmetic and copies ran while one was open for 7% of the time, Pallas kernels for 10%

profile of v4, /device:TPU:0, one launch (start us, length us, event | category | flops | bytes accessed | tf_op | source)
XLA Modules:
  0.0 79.9 jit_solution(541201487242740681)
XLA Ops:
  0.0 1.3 %constant_dynamic-slice_fusion = (bf16[384,256]{1,0:T(8,128)(2,1)S(1)}, bf16[384,256]{1,0:T(8,128)(2,1)S(1)}, bf16[384,256]{1,0:T(8,128)(2,1)S(1)}, bf16[384,256]{1,0:T(8,128)(2,1)S(1)}) fusion(bf16[1536,256]{1,0:T(8,128)(2,1)} %bitcast.60, s32[]{:T(128)S(6)} %select_n.271, s32[]{:T(128)S(6)} %select_n.270, s32[]{:T(128)S(6)} %select_n.269, s32[]{:T(128)S(6)} %select_n.268), kind=kLoop, calls=%fused_computation.24 | loop fusion | bytes 1572880 | tf_op jit(solution)/shard_map/dynamic_slice | solution.py:205
  1.3 3.2 %collective-permute-start.5 = (bf16[384,256]{1,0:T(8,128)(2,1)S(1)}, bf16[384,256]{1,0:T(8,128)(2,1)S(1)}, u32[]{:S(2)}, u32[]{:S(2)}) collective-permute-start(bf16[384,256]{1,0:T(8,128)(2,1)S(1)} %get-tuple-element.31), channel_id=1, source_target_pairs={{0,96},{8,104},{16,112},{24,120},{32,0},{40,8},{48,16},{56,24},{64... | collective-permute-start | bytes 589832 | tf_op jit(solution)/shard_map/ppermute | solution.py:200
  7.5 1.3 %constant_dynamic-slice_fusion.4 = (bf16[64,6,256]{2,0,1:T(8,128)(2,1)S(1)}, bf16[64,6,256]{2,0,1:T(8,128)(2,1)S(1)}, bf16[64,6,256]{2,0,1:T(8,128)(2,1)S(1)}, bf16[64,6,256]{2,0,1:T(8,128)(2,1)S(1)}) fusion(bf16[256,6,256]{2,0,1:T(8,128)(2,1)} %param.8, s32[]{:T(128)S(6)} %select_n.246, s32[]{:T(128)S(6)} %select_n.244, s32[]{:T(128)S(6)} %select_n.242, ...), kind=kLoop, calls=%fused_computation.28 | loop fusion | bytes 1572880 | tf_op jit(solution)/shard_map/dynamic-slice.3
  9.6 1.5 %collective-permute-start.1 = (bf16[400,256]{1,0:T(8,128)(2,1)}, bf16[400,256]{1,0:T(8,128)(2,1)S(1)}, u32[]{:S(2)}, u32[]{:S(2)}) collective-permute-start(bf16[400,256]{1,0:T(8,128)(2,1)} %fusion.5), channel_id=1, source_target_pairs={{0,16},{8,24},{16,0},{24,8},{32,48},{40,56},{48,32},{56,40},{64,80... | collective-permute-start | bytes 614408 | tf_op jit(solution)/shard_map/ppermute | solution.py:199
  23.9 1.2 %collective-permute-done.6 = bf16[2,384,256]{2,1,0:T(8,128)(2,1)S(1)} collective-permute-done((bf16[2,384,256]{2,1,0:T(8,128)(2,1)S(1)}, bf16[2,384,256]{2,1,0:T(8,128)(2,1)S(1)}, u32[]{:S(2)}, u32[]{:S(2)}) %collective-permute-start.6) | collective-permute-done | bytes 393248 | tf_op jit(solution)/shard_map/ppermute | solution.py:199
  25.2 1.6 %collective-permute-start.7 = (bf16[384,256]{1,0:T(8,128)(2,1)S(1)}, bf16[384,256]{1,0:T(8,128)(2,1)S(1)}, u32[]{:S(2)}, u32[]{:S(2)}) collective-permute-start(bf16[384,256]{1,0:T(8,128)(2,1)S(1)} %fusion.8), channel_id=1, source_target_pairs={{0,16},{8,24},{16,0},{24,8},{32,48},{40,56},{48,32},{56,40},{64,80... | collective-permute-start | bytes 589832 | tf_op jit(solution)/shard_map/ppermute | solution.py:199
  26.9 2.7 %collective-permute-done.2.b3 = bf16[400,256]{1,0:T(8,128)(2,1)S(1)} collective-permute-done((bf16[400,256]{1,0:T(8,128)(2,1)}, bf16[400,256]{1,0:T(8,128)(2,1)S(1)}, u32[]{:S(2)}, u32[]{:S(2)}) %collective-permute-start.2) | collective-permute-done | bytes 204832 | tf_op jit(solution)/shard_map/ppermute | solution.py:199
  29.6 4.5 %collective-permute-done.7 = bf16[384,256]{1,0:T(8,128)(2,1)S(1)} collective-permute-done((bf16[384,256]{1,0:T(8,128)(2,1)S(1)}, bf16[384,256]{1,0:T(8,128)(2,1)S(1)}, u32[]{:S(2)}, u32[]{:S(2)}) %collective-permute-start.7) | collective-permute-done | bytes 196640 | tf_op jit(solution)/shard_map/ppermute | solution.py:199
  34.1 2.0 %collective-permute-start.10 = (bf16[384,256]{1,0:T(8,128)(2,1)S(1)}, bf16[384,256]{1,0:T(8,128)(2,1)S(1)}, u32[]{:S(2)}, u32[]{:S(2)}) collective-permute-start(bf16[384,256]{1,0:T(8,128)(2,1)S(1)} %fusion.10.p0), channel_id=1, source_target_pairs={{0,64},{8,72},{16,80},{24,88},{32,96},{40,104},{48,112},{56,120},{... | collective-permute-start | bytes 589832 | tf_op jit(solution)/shard_map/ppermute | solution.py:200
  36.1 2.6 %collective-permute-start.9 = (bf16[384,256]{1,0:T(8,128)(2,1)S(1)}, bf16[384,256]{1,0:T(8,128)(2,1)S(1)}, u32[]{:S(2)}, u32[]{:S(2)}) collective-permute-start(bf16[384,256]{1,0:T(8,128)(2,1)S(1)} %fusion.10.p0), channel_id=1, source_target_pairs={{0,96},{8,104},{16,112},{24,120},{32,0},{40,8},{48,16},{56,24},{64... | collective-permute-start | bytes 589832 | tf_op jit(solution)/shard_map/ppermute | solution.py:200
  38.8 1.2 %left.1 = f32[6144,128]{1,0:T(8,128)S(1)} custom-call(bf16[256,768]{1,0:T(8,128)(2,1)S(1)} %copy-done.2, bf16[400,256]{1,0:T(8,128)(2,1)S(1)} %fusion.7.b0, bf16[400,256]{1,0:T(8,128)(2,1)S(1)} %collective-permute-done.b1, bf16[400,256]{1,0:T(8,128)(2,1)S(1)} %collective-permute-done.1.b2, bf16[400,256]{1,0:T(8,128)(2,1)S(1)} %collective-permute-done.2.b3), custom_call_target="tpu_custom_call" | custom-call | flops 603979776 | bytes 4000000 | tf_op jit(solution)/shard_map/left/pallas_call | solution.py:234
  40.0 3.5 %collective-permute-done.10.p3 = bf16[384,256]{1,0:T(8,128)(2,1)S(1)} collective-permute-done((bf16[384,256]{1,0:T(8,128)(2,1)S(1)}, bf16[384,256]{1,0:T(8,128)(2,1)S(1)}, u32[]{:S(2)}, u32[]{:S(2)}) %collective-permute-start.10) | collective-permute-done | bytes 196640 | tf_op jit(solution)/shard_map/ppermute | solution.py:200
  43.5 2.6 %collective-permute-done.9.p2 = bf16[384,256]{1,0:T(8,128)(2,1)S(1)} collective-permute-done((bf16[384,256]{1,0:T(8,128)(2,1)S(1)}, bf16[384,256]{1,0:T(8,128)(2,1)S(1)}, u32[]{:S(2)}, u32[]{:S(2)}) %collective-permute-start.9) | collective-permute-done | bytes 196640 | tf_op jit(solution)/shard_map/ppermute | solution.py:200
  46.9 1.8 %right.1 = f32[6144,128]{1,0:T(8,128)S(1)} custom-call(s32[4]{0:T(128)S(1)} %pad_add_fusion.1.base_ref, bf16[256,768]{1,0:T(8,128)(2,1)S(1)} %copy-done.1, bf16[384,256]{1,0:T(8,128)(2,1)S(1)} %fusion.10.p0, bf16[384,256]{1,0:T(8,128)(2,1)S(1)} %collective-permute-done.8.p1, bf16[384,256]{1,0:T(8,128)(2,1)S(1)} %collective-permute-done.9.p2, ...), custom_call_target="tpu_custom_call" | custom-call | flops 603979776 | bytes 4000000 | tf_op jit(solution)/shard_map/right/pallas_call | solution.py:238
  48.7 6.0 %pairs.2 = (f32[4,72,256]{2,1,0:T(8,128)S(1)}, s32[8]{0:T(128)S(1)}) custom-call(s32[8]{0:T(128)S(1)} %stack.100.order_ref, s32[2048]{0:T(1024)S(1)} %add.244.local_ref, s32[2048]{0:T(1024)S(1)} %bitcast.58, f32[6144,128]{1,0:T(8,128)S(1)} %left.1, f32[6144,128]{1,0:T(8,128)S(1)} %right.1, bf16[144,384]{1,0:T(8,128)(2,1)S(1)} %copy-done), custom_call_target="tpu_custom_call" | custom-call | flops 603979776 | bytes 4000000 | tf_op jit(solution)/shard_map/pairs/pallas_call | solution.py:249
  54.7 2.8 %collective-permute-start.11 = (f32[4,72,256]{2,1,0:T(8,128)S(1)}, f32[4,72,256]{2,1,0:T(8,128)S(1)}, u32[]{:S(2)}, u32[]{:S(2)}) collective-permute-start(f32[4,72,256]{2,1,0:T(8,128)S(1)} %get-tuple-element.20), channel_id=1, source_target_pairs={{0,1},{1,0},{2,3},{3,2},{4,5},{5,4},{6,7},{7,6},{8,9},{9,8},{10,11... | collective-permute-start | bytes 884744 | tf_op jit(solution)/shard_map/ppermute | solution.py:257
  57.5 5.9 %pairs.3 = (f32[4,72,256]{2,1,0:T(8,128)S(1)}, s32[8]{0:T(128)}) custom-call(s32[8]{0:T(128)S(1)} %get-tuple-element.21.order_ref, s32[2048]{0:T(1024)S(1)} %add.244.local_ref, s32[2048]{0:T(1024)S(1)} %bitcast.59, f32[6144,128]{1,0:T(8,128)S(1)} %left.1, f32[6144,128]{1,0:T(8,128)S(1)} %right.1, bf16[144,384]{1,0:T(8,128)(2,1)S(1)} %copy-done), custom_call_target="tpu_custom_call" | custom-call | flops 603979776 | bytes 4000000 | tf_op jit(solution)/shard_map/pairs/pallas_call | solution.py:249
  64.4 4.0 %collective-permute-start.12 = (f32[72,256]{1,0:T(8,128)S(1)}, f32[72,256]{1,0:T(8,128)S(1)}, u32[]{:S(2)}, u32[]{:S(2)}) collective-permute-start(f32[72,256]{1,0:T(8,128)S(1)} %get-tuple-element.23), channel_id=1, source_target_pairs={{0,4},{1,5},{2,6},{3,7},{4,0},{5,1},{6,2},{7,3},{8,12},{9,13},{10,... | collective-permute-start | bytes 221192 | tf_op jit(solution)/shard_map/ppermute | solution.py:263
  68.4 1.0 %collective-permute-start.13 = (f32[72,256]{1,0:T(8,128)S(1)}, f32[72,256]{1,0:T(8,128)S(1)}, u32[]{:S(2)}, u32[]{:S(2)}) collective-permute-start(f32[72,256]{1,0:T(8,128)S(1)} %get-tuple-element.24), channel_id=1, source_target_pairs={{0,2},{1,3},{2,4},{3,5},{4,6},{5,7},{6,0},{7,1},{8,10},{9,11},{10,... | collective-permute-start | bytes 221192 | tf_op jit(solution)/shard_map/ppermute | solution.py:263
  69.4 2.2 %collective-permute-start.14 = (f32[72,256]{1,0:T(8,128)S(1)}, f32[72,256]{1,0:T(8,128)S(1)}, u32[]{:S(2)}, u32[]{:S(2)}) collective-permute-start(f32[72,256]{1,0:T(8,128)S(1)} %get-tuple-element.25), channel_id=1, source_target_pairs={{0,6},{1,7},{2,0},{3,1},{4,2},{5,3},{6,4},{7,5},{8,14},{9,15},{10,... | collective-permute-start | bytes 221192 | tf_op jit(solution)/shard_map/ppermute | solution.py:263
  71.6 2.3 %collective-permute-done.13.refs_1_ = f32[72,256]{1,0:T(8,128)S(1)} collective-permute-done((f32[72,256]{1,0:T(8,128)S(1)}, f32[72,256]{1,0:T(8,128)S(1)}, u32[]{:S(2)}, u32[]{:S(2)}) %collective-permute-start.13) | collective-permute-done | bytes 73760 | tf_op jit(solution)/shard_map/ppermute | solution.py:263
  74.8 1.2 %collective-permute-start.17 = (f32[72,64]{1,0:T(8,128)S(1)}, f32[72,64]{1,0:T(8,128)S(1)}, u32[]{:S(2)}, u32[]{:S(2)}) collective-permute-start(f32[72,64]{1,0:T(8,128)S(1)} %get-tuple-element.30), channel_id=1, source_target_pairs={{0,24},{8,16},{16,8},{24,0},{32,56},{40,48},{48,40},{56,32},{64,88... | collective-permute-start | bytes 55304 | tf_op jit(solution)/shard_map/ppermute | solution.py:199
  76.1 2.5 %collective-permute-done.16.refs_2_ = f32[72,64]{1,0:T(8,128)S(1)} collective-permute-done((f32[72,64]{1,0:T(8,128)S(1)}, f32[72,64]{1,0:T(8,128)S(1)}, u32[]{:S(2)}, u32[]{:S(2)}) %collective-permute-start.16) | collective-permute-done | bytes 18464 | tf_op jit(solution)/shard_map/ppermute | solution.py:199
  78.6 1.3 %finish.1 = f32[1,4,64,65]{3,2,1,0:T(8,128)} custom-call(s32[4]{0:T(128)S(1)} %pad_add_fusion.step_ref, s32[1,4]{1,0:T(1,128)S(1)} %copy-done.3, f32[72,64]{1,0:T(8,128)S(1)} %get-tuple-element.27.refs_0_, f32[72,64]{1,0:T(8,128)S(1)} %collective-permute-done.15.refs_1_, f32[72,64]{1,0:T(8,128)S(1)} %collective-permute-done.16.refs_2_, ...), custom_call_target="tpu_custom_call" | custom-call | tf_op jit(solution)/shard_map/finish/pallas_call | solution.py:273
  (61 shorter events, 9.8 us)
Async XLA Ops:
  0.0 11.1 %copy-start.4 = (s32[4]{0:T(128)S(1)}, s32[4]{0:T(128)}, u32[]{:S(2)}) copy-start(s32[4]{0:T(128)} %param.9) | copy-start | bytes 52
  1.3 37.5 %copy-start.2 = (bf16[256,768]{1,0:T(8,128)(2,1)S(1)}, bf16[256,768]{1,0:T(8,128)(2,1)}, u32[]{:S(2)}) copy-start(bf16[256,768]{1,0:T(8,128)(2,1)} %constant.259.clone.table_ref) | copy-start | bytes 1179652
  1.3 21.0 %collective-permute-start.5 = (bf16[384,256]{1,0:T(8,128)(2,1)S(1)}, bf16[384,256]{1,0:T(8,128)(2,1)S(1)}, u32[]{:S(2)}, u32[]{:S(2)}) collective-permute-start(bf16[384,256]{1,0:T(8,128)(2,1)S(1)} %get-tuple-element.31), channel_id=1, source_target_pairs={{0,96},{8,104},{16,112},{24,120},{32,0},{40,8},{48,16},{56,24},{64... | collective-permute-start | bytes 589832 | tf_op jit(solution)/shard_map/ppermute | solution.py:200
  4.5 18.2 %collective-permute-start.4 = (bf16[384,256]{1,0:T(8,128)(2,1)S(1)}, bf16[384,256]{1,0:T(8,128)(2,1)S(1)}, u32[]{:S(2)}, u32[]{:S(2)}) collective-permute-start(bf16[384,256]{1,0:T(8,128)(2,1)S(1)} %get-tuple-element.32), channel_id=1, source_target_pairs={{0,64},{8,72},{16,80},{24,88},{32,96},{40,104},{48,112},{56,120},{... | collective-permute-start | bytes 589832 | tf_op jit(solution)/shard_map/ppermute | solution.py:200
  5.1 17.5 %collective-permute-start.3 = (bf16[384,256]{1,0:T(8,128)(2,1)S(1)}, bf16[384,256]{1,0:T(8,128)(2,1)S(1)}, u32[]{:S(2)}, u32[]{:S(2)}) collective-permute-start(bf16[384,256]{1,0:T(8,128)(2,1)S(1)} %get-tuple-element.33), channel_id=1, source_target_pairs={{0,32},{8,40},{16,48},{24,56},{32,64},{40,72},{48,80},{56,88},{64,... | collective-permute-start | bytes 589832 | tf_op jit(solution)/shard_map/ppermute | solution.py:200
  8.8 18.0 %collective-permute-start = (bf16[400,256]{1,0:T(8,128)(2,1)S(1)}, bf16[400,256]{1,0:T(8,128)(2,1)S(1)}, u32[]{:S(2)}, u32[]{:S(2)}) collective-permute-start(bf16[400,256]{1,0:T(8,128)(2,1)S(1)} %fusion.4), channel_id=1, source_target_pairs={{0,8},{8,0},{16,24},{24,16},{32,40},{40,32},{48,56},{56,48},{64,72... | collective-permute-start | bytes 614408 | tf_op jit(solution)/shard_map/ppermute | solution.py:199
  9.6 17.2 %collective-permute-start.1 = (bf16[400,256]{1,0:T(8,128)(2,1)}, bf16[400,256]{1,0:T(8,128)(2,1)S(1)}, u32[]{:S(2)}, u32[]{:S(2)}) collective-permute-start(bf16[400,256]{1,0:T(8,128)(2,1)} %fusion.5), channel_id=1, source_target_pairs={{0,16},{8,24},{16,0},{24,8},{32,48},{40,56},{48,32},{56,40},{64,80... | collective-permute-start | bytes 614408 | tf_op jit(solution)/shard_map/ppermute | solution.py:199
  22.3 7.3 %collective-permute-start.2 = (bf16[400,256]{1,0:T(8,128)(2,1)}, bf16[400,256]{1,0:T(8,128)(2,1)S(1)}, u32[]{:S(2)}, u32[]{:S(2)}) collective-permute-start(bf16[400,256]{1,0:T(8,128)(2,1)} %fusion.6), channel_id=1, source_target_pairs={{0,24},{8,16},{16,8},{24,0},{32,56},{40,48},{48,40},{56,32},{64,88... | collective-permute-start | bytes 614408 | tf_op jit(solution)/shard_map/ppermute | solution.py:199
  23.4 1.8 %collective-permute-start.6 = (bf16[2,384,256]{2,1,0:T(8,128)(2,1)S(1)}, bf16[2,384,256]{2,1,0:T(8,128)(2,1)S(1)}, u32[]{:S(2)}, u32[]{:S(2)}) collective-permute-start(bf16[2,384,256]{2,1,0:T(8,128)(2,1)S(1)} %get-tuple-element.19), channel_id=1, source_target_pairs={{0,8},{8,0},{16,24},{24,16},{32,40},{40,32},{48,56},{56,48},{64,72... | collective-permute-start | bytes 1179656 | tf_op jit(solution)/shard_map/ppermute | solution.py:199
  23.8 23.1 %copy-start.1 = (bf16[256,768]{1,0:T(8,128)(2,1)S(1)}, bf16[256,768]{1,0:T(8,128)(2,1)}, u32[]{:S(2)}) copy-start(bf16[256,768]{1,0:T(8,128)(2,1)} %constant.260.clone.table_ref) | copy-start | bytes 1179652
  25.2 8.9 %collective-permute-start.7 = (bf16[384,256]{1,0:T(8,128)(2,1)S(1)}, bf16[384,256]{1,0:T(8,128)(2,1)S(1)}, u32[]{:S(2)}, u32[]{:S(2)}) collective-permute-start(bf16[384,256]{1,0:T(8,128)(2,1)S(1)} %fusion.8), channel_id=1, source_target_pairs={{0,16},{8,24},{16,0},{24,8},{32,48},{40,56},{48,32},{56,40},{64,80... | collective-permute-start | bytes 589832 | tf_op jit(solution)/shard_map/ppermute | solution.py:199
  34.1 9.4 %collective-permute-start.10 = (bf16[384,256]{1,0:T(8,128)(2,1)S(1)}, bf16[384,256]{1,0:T(8,128)(2,1)S(1)}, u32[]{:S(2)}, u32[]{:S(2)}) collective-permute-start(bf16[384,256]{1,0:T(8,128)(2,1)S(1)} %fusion.10.p0), channel_id=1, source_target_pairs={{0,64},{8,72},{16,80},{24,88},{32,96},{40,104},{48,112},{56,120},{... | collective-permute-start | bytes 589832 | tf_op jit(solution)/shard_map/ppermute | solution.py:200
  36.1 10.0 %collective-permute-start.9 = (bf16[384,256]{1,0:T(8,128)(2,1)S(1)}, bf16[384,256]{1,0:T(8,128)(2,1)S(1)}, u32[]{:S(2)}, u32[]{:S(2)}) collective-permute-start(bf16[384,256]{1,0:T(8,128)(2,1)S(1)} %fusion.10.p0), channel_id=1, source_target_pairs={{0,96},{8,104},{16,112},{24,120},{32,0},{40,8},{48,16},{56,24},{64... | collective-permute-start | bytes 589832 | tf_op jit(solution)/shard_map/ppermute | solution.py:200
  38.8 8.1 %collective-permute-start.8 = (bf16[384,256]{1,0:T(8,128)(2,1)S(1)}, bf16[384,256]{1,0:T(8,128)(2,1)S(1)}, u32[]{:S(2)}, u32[]{:S(2)}) collective-permute-start(bf16[384,256]{1,0:T(8,128)(2,1)S(1)} %fusion.10.p0), channel_id=1, source_target_pairs={{0,32},{8,40},{16,48},{24,56},{32,64},{40,72},{48,80},{56,88},{64,... | collective-permute-start | bytes 589832 | tf_op jit(solution)/shard_map/ppermute | solution.py:200
  40.0 8.7 %copy-start = (bf16[144,384]{1,0:T(8,128)(2,1)S(1)}, bf16[144,384]{1,0:T(8,128)(2,1)}, u32[]{:S(2)}) copy-start(bf16[144,384]{1,0:T(8,128)(2,1)} %constant.261.clone.back_ref) | copy-start | bytes 331780
  54.7 9.7 %collective-permute-start.11 = (f32[4,72,256]{2,1,0:T(8,128)S(1)}, f32[4,72,256]{2,1,0:T(8,128)S(1)}, u32[]{:S(2)}, u32[]{:S(2)}) collective-permute-start(f32[4,72,256]{2,1,0:T(8,128)S(1)} %get-tuple-element.20), channel_id=1, source_target_pairs={{0,1},{1,0},{2,3},{3,2},{4,5},{5,4},{6,7},{7,6},{8,9},{9,8},{10,11... | collective-permute-start | bytes 884744 | tf_op jit(solution)/shard_map/ppermute | solution.py:257
  57.5 21.0 %copy-start.3 = (s32[1,4]{1,0:T(1,128)S(1)}, s32[1,4]{1,0:T(1,128)}, u32[]{:S(2)}) copy-start(s32[1,4]{1,0:T(1,128)} %near_ref.1) | copy-start | bytes 52
  64.4 7.2 %collective-permute-start.12 = (f32[72,256]{1,0:T(8,128)S(1)}, f32[72,256]{1,0:T(8,128)S(1)}, u32[]{:S(2)}, u32[]{:S(2)}) collective-permute-start(f32[72,256]{1,0:T(8,128)S(1)} %get-tuple-element.23), channel_id=1, source_target_pairs={{0,4},{1,5},{2,6},{3,7},{4,0},{5,1},{6,2},{7,3},{8,12},{9,13},{10,... | collective-permute-start | bytes 221192 | tf_op jit(solution)/shard_map/ppermute | solution.py:263
  68.4 5.6 %collective-permute-start.13 = (f32[72,256]{1,0:T(8,128)S(1)}, f32[72,256]{1,0:T(8,128)S(1)}, u32[]{:S(2)}, u32[]{:S(2)}) collective-permute-start(f32[72,256]{1,0:T(8,128)S(1)} %get-tuple-element.24), channel_id=1, source_target_pairs={{0,2},{1,3},{2,4},{3,5},{4,6},{5,7},{6,0},{7,1},{8,10},{9,11},{10,... | collective-permute-start | bytes 221192 | tf_op jit(solution)/shard_map/ppermute | solution.py:263
  69.4 4.5 %collective-permute-start.14 = (f32[72,256]{1,0:T(8,128)S(1)}, f32[72,256]{1,0:T(8,128)S(1)}, u32[]{:S(2)}, u32[]{:S(2)}) collective-permute-start(f32[72,256]{1,0:T(8,128)S(1)} %get-tuple-element.25), channel_id=1, source_target_pairs={{0,6},{1,7},{2,0},{3,1},{4,2},{5,3},{6,4},{7,5},{8,14},{9,15},{10,... | collective-permute-start | bytes 221192 | tf_op jit(solution)/shard_map/ppermute | solution.py:263
  74.1 2.0 %collective-permute-start.15 = (f32[72,64]{1,0:T(8,128)S(1)}, f32[72,64]{1,0:T(8,128)S(1)}, u32[]{:S(2)}, u32[]{:S(2)}) collective-permute-start(f32[72,64]{1,0:T(8,128)S(1)} %get-tuple-element.28), channel_id=1, source_target_pairs={{0,8},{8,0},{16,24},{24,16},{32,40},{40,32},{48,56},{56,48},{64,72... | collective-permute-start | bytes 55304 | tf_op jit(solution)/shard_map/ppermute | solution.py:199
  74.2 4.4 %collective-permute-start.16 = (f32[72,64]{1,0:T(8,128)S(1)}, f32[72,64]{1,0:T(8,128)S(1)}, u32[]{:S(2)}, u32[]{:S(2)}) collective-permute-start(f32[72,64]{1,0:T(8,128)S(1)} %get-tuple-element.29), channel_id=1, source_target_pairs={{0,16},{8,24},{16,0},{24,8},{32,48},{40,56},{48,32},{56,40},{64,80... | collective-permute-start | bytes 55304 | tf_op jit(solution)/shard_map/ppermute | solution.py:199
  74.8 3.8 %collective-permute-start.17 = (f32[72,64]{1,0:T(8,128)S(1)}, f32[72,64]{1,0:T(8,128)S(1)}, u32[]{:S(2)}, u32[]{:S(2)}) collective-permute-start(f32[72,64]{1,0:T(8,128)S(1)} %get-tuple-element.30), channel_id=1, source_target_pairs={{0,24},{8,16},{16,8},{24,0},{32,56},{40,48},{48,40},{56,32},{64,88... | collective-permute-start | bytes 55304 | tf_op jit(solution)/shard_map/ppermute | solution.py:199

commit v5 on v4

--- a/solution.py
+++ b/solution.py
@@ -1,3 +1,4 @@
+import functools
 import math
 
 import jax
@@ -56,14 +57,48 @@
     return d[:, :128], d[:, 128:256], third
 
 
-def pick_kernel(from_ref, g0, g1, g2, g3, keep_ref, give_ref):
+def place():
+    me = lax.axis_index("clu")
+    return me >> 2, me & 3, (me >> 1) & 1, me & 1
+
+
+def pick_kernel(owners_ref, g0, g1, g2, g3, keep_ref, give_ref):
+    row, step, _, _ = place()
     for d in range(4):
         to = (keep_ref, give_ref)[d % 2]
+        behind = (row + 4 - (owners_ref[step ^ d] >> 2)) & 3
         for n, ref in enumerate((g0, g1, g2, g3)):
 
-            @pl.when(from_ref[d] == n)
+            @pl.when(behind == n)
             def _():
                 to[d // 2] = ref[...]
+
+
+def core_kernel(owners_ref, kept_ref, got_ref, mine_ref, theirs_ref):
+    _, step, _, core = place()
+    for d, to in ((0, mine_ref), (2, theirs_ref)):
+        here = (owners_ref[step ^ d] & 1) == core
+
+        @pl.when(here)
+        def _():
+            to[...] = kept_ref[d // 2]
+
+        @pl.when(jnp.logical_not(here))
+        def _():
+            to[...] = got_ref[d // 2]
+
+
+def chip_kernel(owners_ref, mine_ref, got_ref, out_ref):
+    _, step, x, _ = place()
+    here = ((owners_ref[step] >> 1) & 1) == x
+
+    @pl.when(here)
+    def _():
+        out_ref[...] = mine_ref[...]
+
+    @pl.when(jnp.logical_not(here))
+    def _():
+        out_ref[...] = got_ref[...]
 
 
 def clear_rest(out_ref, channels):
@@ -85,16 +120,18 @@
                 out_ref[to, :] = part[c * events:(c + 1) * events]
 
 
-def right_kernel(base_ref, table_ref, p0, p1, p2, p3, out_ref):
+def right_kernel(table_ref, p0, p1, p2, p3, out_ref):
     events = out_ref.shape[0] // 24
     clear_rest(out_ref, 4 * p0.shape[0] // events)
-    for n, p_ref in enumerate((p0, p1, p2, p3)):
+    row = place()[0]
+    for behind, p_ref in ((0, p0), (1, p1), (3, p2), (2, p3)):
+        base = ((row + 4 - behind) & 3) * p_ref.shape[0]
         x = p_ref[...]
         parts = spectrum(x, table_ref[...], EJ, EI)
         for g in range(x.shape[0] // 32):
-            row = base_ref[n] + 32 * g
-            c = row // events
-            to = (row - c * events) * 24 + c
+            at = base + 32 * g
+            c = at // events
+            to = (at - c * events) * 24 + c
             for k, part in enumerate(parts):
                 out_ref[pl.ds(to + 8 * k, 32, stride=24), :] = part[32 * g:32 * g + 32]
 
@@ -110,11 +147,18 @@
     return vs[0]
 
 
-def pair_kernel(order_ref, local_ref, remote_ref, left, right, back_ref, out_ref, next_ref, z):
+MOVES = (2, 1, 3, 0)
+
+
+def target(k, dz, dh, count):
+    return ((k // 2 + dz) % (count // 2)) * 2 + (k % 2 + dh) % 2
+
+
+def pair_kernel(across, token_ref, local_ref, remote_ref, left, right, back_ref, out_ref, next_ref, z):
     width = out_ref.shape[2]
     half = out_ref.shape[0]
-    for t in range(2 * half):
-        next_ref[t] = order_ref[(t + half) % (2 * half)]
+    next_ref[0] = token_ref[0]
+    sta = lax.axis_index("sta")
     share = width // 4
     pairs = local_ref.shape[0] // 4
     bh, bl = back_ref[:ROWS], back_ref[ROWS:]
@@ -122,7 +166,7 @@
     dot = lambda a, b: lax.dot_general(a, b, contract, preferred_element_type=jnp.float32)
     sub = lax.broadcasted_iota(jnp.int32, (8, 128), 0)
     for t in range(half):
-        first = order_ref[t] * share
+        first = target(sta, MOVES[t], across, 2 * half) * share
 
         def body(it, carry):
             for part in range(4):
@@ -168,10 +212,11 @@
         ref[...] = total[:, q * share:(q + 1) * share]
 
 
-def final_kernel(step_ref, near_ref, *refs):
+def final_kernel(near_ref, *refs):
     out_ref = refs[-1]
+    step = place()[1]
     for r, ref in enumerate(refs[:-1]):
-        s = step_ref[r]
+        s = step ^ r
         out_ref[0, s] = (ref[...] * near_ref[0, s].astype(jnp.float32)).T[:, :LAGS]
 
 
@@ -204,17 +249,21 @@
     for d in range(4):
         part = lax.dynamic_slice_in_dim(rows, (row + d) % 4 * quarter, quarter, 0)
         got.append(part if d == 0 else turn(part, d))
-    source = [owners[step ^ d] for d in range(4)]
+    piece = shaped((quarter, samp), bf16)
+    two = shaped((2, quarter, samp), bf16)
     keep, give = pl.pallas_call(
-        pick_kernel, out_shape=(shaped((2, quarter, samp), bf16),) * 2,
-        in_specs=[SMEM] + [VMEM] * 4, out_specs=(VMEM,) * 2, compiler_params=SMALL, name="pick",
-    )(jnp.stack([(row + 4 - o // 4) % 4 for o in source]), *got)
-    other = near(give, 1)
-    mine = jnp.where(source[0] % 2 == me % 2, keep[0], other[0])
-    theirs = jnp.where(source[2] % 2 == me % 2, keep[1], other[1])
-    mine = jnp.where(source[0] // 2 % 2 == me // 2 % 2, mine, near(theirs, 2))
+        pick_kernel, out_shape=(two, two), in_specs=[SMEM] + [VMEM] * 4, out_specs=(VMEM,) * 2,
+        compiler_params=SMALL, name="pick",
+    )(owners, *got)
+    mine, theirs = pl.pallas_call(
+        core_kernel, out_shape=(piece, piece), in_specs=[SMEM] + [VMEM] * 2, out_specs=(VMEM,) * 2,
+        compiler_params=SMALL, name="over_core",
+    )(owners, keep, near(give, 1))
+    mine = pl.pallas_call(
+        chip_kernel, out_shape=piece, in_specs=[SMEM] + [VMEM] * 2, out_specs=VMEM,
+        compiler_params=SMALL, name="over_x",
+    )(owners, mine, near(theirs, 2))
     pieces = [mine] + [turn(mine, d) for d in (1, -1, 2)]
-    base = jnp.stack([(row + r) % 4 * quarter for r in (0, 3, 1, 2)])
 
     lists = jnp.concatenate([pair_local[0], pair_remote[0]], axis=1).astype(bf16)
     lists = lists.reshape(steps, 2 * pairs // samp, samp)
@@ -236,44 +285,37 @@
         compiler_params=PARAMS, name="left", cost_estimate=cost,
     )(left_table, *blocks)
     right = pl.pallas_call(
-        right_kernel, out_shape=spectra, in_specs=[SMEM] + [VMEM] * 5, out_specs=VMEM,
+        right_kernel, out_shape=spectra, in_specs=[VMEM] * 5, out_specs=VMEM,
         compiler_params=PARAMS, name="right", cost_estimate=cost,
-    )(base, right_table, *pieces)
-
-    sta = lax.axis_index("sta")
-    moves = (2, 1, 3, 0)
-    target = lambda k, dz, dh: ((k // 2 + dz) % (n_sta // 2)) * 2 + (k % 2 + dh) % 2
-    order = jnp.stack([target(sta, dz, dh) for dh in (1, 0) for dz in moves]).astype(jnp.int32)
+    )(right_table, *pieces)
+
     halves = []
-    for _ in range(2):
-        raw, order = pl.pallas_call(
-            pair_kernel,
-            out_shape=(shaped((n_sta // 2, ROWS, 4 * share), f32), shaped((n_sta,), jnp.int32)),
+    token = owners
+    for across in (1, 0):
+        raw, token = pl.pallas_call(
+            functools.partial(pair_kernel, across),
+            out_shape=(shaped((n_sta // 2, ROWS, 4 * share), f32), shaped((steps,), jnp.int32)),
             in_specs=[SMEM] * 3 + [VMEM] * 3, out_specs=(VMEM, SMEM),
             scratch_shapes=[pltpu.VMEM((4 * share, 384), f32)],
             compiler_params=PARAMS, name="pairs", cost_estimate=cost,
-        )(order, first, second, left, right, back_table)
+        )(token, first, second, left, right, back_table)
         halves.append(raw)
-    across = lax.ppermute(halves[0], "sta", [(k, target(k, 0, 1)) for k in range(n_sta)])
+    hop = lambda v, dz, dh: lax.ppermute(v, "sta", [(k, target(k, dz, dh, n_sta)) for k in range(n_sta)])
     sums = pl.pallas_call(
         add_kernel, out_shape=(shaped((ROWS, 4 * share), f32),) * 4,
         in_specs=[VMEM] * 2, out_specs=(VMEM,) * 4, compiler_params=SMALL, name="add",
-    )(across, halves[1])
-    received = [
-        v if dz == 0 else lax.ppermute(v, "sta", [(k, target(k, dz, 0)) for k in range(n_sta)])
-        for dz, v in zip(moves, sums)
-    ]
+    )(hop(halves[0], 0, 1), halves[1])
+    received = [v if dz == 0 else hop(v, dz, 0) for dz, v in zip(MOVES, sums)]
 
     done = pl.pallas_call(
         sum_kernel, out_shape=(shaped((ROWS, share), f32),) * 4,
         in_specs=[VMEM] * len(received), out_specs=(VMEM,) * 4, compiler_params=SMALL, name="total",
     )(*received)
     done = [near(v, d) for d, v in enumerate(done)]
-    order = jnp.stack([step ^ d for d in range(4)])
     out = pl.pallas_call(
         final_kernel, out_shape=shaped((1, steps, share, LAGS), f32),
-        in_specs=[SMEM] * 2 + [VMEM] * 4, out_specs=VMEM, compiler_params=PARAMS, name="finish",
-    )(order, neighbours, *done)
+        in_specs=[SMEM] + [VMEM] * 4, out_specs=VMEM, compiler_params=SMALL, name="finish",
+    )(neighbours, *done)
     return out.transpose(0, 1, 3, 2)
 
 

time: 81.4 us -> 77.6 us (0.953)
  between operations: 9.92 us -> 0.21 us
  waiting for transfers between devices: 21 us -> 28.9 us
  starting transfers between devices: 25.2 us -> 23.9 us
    ppermute x6, waiting for transfers between devices: 6.9 us -> 13.6 us  [local(): lax.ppermute(v, 'clu', [(i, (i + 4 * d) % n_clu) for i in range(n_clu)])]
    ppermute x6, starting transfers between devices: 9.41 us -> 7.5 us  [local(): lax.ppermute(v, 'clu', [(i, (i + 4 * d) % n_clu) for i in range(n_clu)])]
    pallas_call x4 -> x6, Pallas kernels: 14.5 us -> 15.1 us  [the longest x2 11.9 us: local(): pl.pallas_call(functools.partial(pair_kernel, across), out_shape=(shaped(...]
    another operation x5 -> x2, other arithmetic: 1.63 us -> 1.4 us
  transfers between devices with their start and end apart: 18 -> 18, of which waited for: 9 -> 12; matrix products, arithmetic and copies ran while one was open for 7% -> 6% of each run, Pallas kernels for 10% -> 11%
where the time goes in v5:
time: 77.6 us; the launch traced here: 76.3 us
  waiting for transfers between devices  28.9 us (37%)
  starting transfers between devices  23.9 us (31%)
  Pallas kernels  17.7 us (23%)
  other arithmetic  2.87 us (4%)
  local copies, waits for them, and re-layouts  2.75 us (4%)
    ppermute x6, waiting for transfers between devices, local(): lax.ppermute(v, 'clu', [(i, (i + 4 * d) % n_clu) for i in range(n_clu)])  13.6 us
    pallas_call x2, Pallas kernels, local(): pl.pallas_call(functools.partial(pair_kernel, across), out_shape=(shaped(...  11.9 us
    ppermute x8, waiting for transfers between devices, local(): lax.ppermute(v, 'clu', [(i, i ^ d) for i in range(n_clu)])  11.6 us
    ppermute x4, starting transfers between devices, local(): lax.ppermute(v, 'sta', [(k, target(k, dz, dh, n_sta)) for k in range(n_st...  10.3 us
    ppermute x6, starting transfers between devices, local(): lax.ppermute(v, 'clu', [(i, (i + 4 * d) % n_clu) for i in range(n_clu)])  7.5 us
    ppermute x8, starting transfers between devices, local(): lax.ppermute(v, 'clu', [(i, i ^ d) for i in range(n_clu)])  6.1 us
    ppermute x4, waiting for transfers between devices, local(): lax.ppermute(v, 'sta', [(k, target(k, dz, dh, n_sta)) for k in range(n_st...  3.71 us
  transfers between devices with their start and end apart: 18, of which 12 were waited for; matrix products, arithmetic and copies ran while one was open for 6% of the time, Pallas kernels for 11%

profile of v5, /device:TPU:0, one launch (start us, length us, event | category | flops | bytes accessed | tf_op | source)
XLA Modules:
  0.0 76.3 jit_solution(12065217847443981490)
XLA Ops:
  0.0 1.3 %constant_dynamic-slice_fusion = (bf16[384,256]{1,0:T(8,128)(2,1)S(1)}, bf16[384,256]{1,0:T(8,128)(2,1)S(1)}, bf16[384,256]{1,0:T(8,128)(2,1)S(1)}, bf16[384,256]{1,0:T(8,128)(2,1)S(1)}) fusion(bf16[1536,256]{1,0:T(8,128)(2,1)} %bitcast.30, s32[]{:T(128)S(6)} %select_n.81, s32[]{:T(128)S(6)} %select_n.79, s32[]{:T(128)S(6)} %select_n.77, s32[]{:T(128)S(6)} %select_n.75), kind=kLoop, calls=%fused_computation.19 | loop fusion | bytes 1572880 | tf_op jit(solution)/shard_map/dynamic_slice | solution.py:250
  1.3 3.2 %collective-permute-start.5 = (bf16[384,256]{1,0:T(8,128)(2,1)S(1)}, bf16[384,256]{1,0:T(8,128)(2,1)S(1)}, u32[]{:S(2)}, u32[]{:S(2)}) collective-permute-start(bf16[384,256]{1,0:T(8,128)(2,1)S(1)} %get-tuple-element.35), channel_id=1, source_target_pairs={{0,96},{8,104},{16,112},{24,120},{32,0},{40,8},{48,16},{56,24},{64... | collective-permute-start | bytes 589832 | tf_op jit(solution)/shard_map/ppermute | solution.py:245
  7.5 1.3 %constant_dynamic-slice_fusion.4 = (bf16[64,6,256]{2,0,1:T(8,128)(2,1)S(1)}, bf16[64,6,256]{2,0,1:T(8,128)(2,1)S(1)}, bf16[64,6,256]{2,0,1:T(8,128)(2,1)S(1)}, bf16[64,6,256]{2,0,1:T(8,128)(2,1)S(1)}) fusion(bf16[256,6,256]{2,0,1:T(8,128)(2,1)} %param.8, s32[]{:T(128)S(6)} %select_n.72, s32[]{:T(128)S(6)} %select_n.70, s32[]{:T(128)S(6)} %select_n.68, ...), kind=kLoop, calls=%fused_computation.23 | loop fusion | bytes 1572880 | tf_op jit(solution)/shard_map/dynamic-slice.3
  9.6 1.5 %collective-permute-start.1 = (bf16[400,256]{1,0:T(8,128)(2,1)}, bf16[400,256]{1,0:T(8,128)(2,1)S(1)}, u32[]{:S(2)}, u32[]{:S(2)}) collective-permute-start(bf16[400,256]{1,0:T(8,128)(2,1)} %fusion.5), channel_id=1, source_target_pairs={{0,16},{8,24},{16,0},{24,8},{32,48},{40,56},{48,32},{56,40},{64,80... | collective-permute-start | bytes 614408 | tf_op jit(solution)/shard_map/ppermute | solution.py:244
  11.1 1.7 %collective-permute-done.5.g3 = bf16[384,256]{1,0:T(8,128)(2,1)S(1)} collective-permute-done((bf16[384,256]{1,0:T(8,128)(2,1)S(1)}, bf16[384,256]{1,0:T(8,128)(2,1)S(1)}, u32[]{:S(2)}, u32[]{:S(2)}) %collective-permute-start.5) | collective-permute-done | bytes 196640 | tf_op jit(solution)/shard_map/ppermute | solution.py:245
  13.8 2.7 %collective-permute-done.3.g1 = bf16[384,256]{1,0:T(8,128)(2,1)S(1)} collective-permute-done((bf16[384,256]{1,0:T(8,128)(2,1)S(1)}, bf16[384,256]{1,0:T(8,128)(2,1)S(1)}, u32[]{:S(2)}, u32[]{:S(2)}) %collective-permute-start.3) | collective-permute-done | bytes 196640 | tf_op jit(solution)/shard_map/ppermute | solution.py:245
  18.0 1.6 %collective-permute-start.2 = (bf16[400,256]{1,0:T(8,128)(2,1)}, bf16[400,256]{1,0:T(8,128)(2,1)S(1)}, u32[]{:S(2)}, u32[]{:S(2)}) collective-permute-start(bf16[400,256]{1,0:T(8,128)(2,1)} %fusion.6), channel_id=1, source_target_pairs={{0,24},{8,16},{16,8},{24,0},{32,56},{40,48},{48,40},{56,32},{64,88... | collective-permute-start | bytes 614408 | tf_op jit(solution)/shard_map/ppermute | solution.py:244
  21.3 4.0 %collective-permute-done.2.b3 = bf16[400,256]{1,0:T(8,128)(2,1)S(1)} collective-permute-done((bf16[400,256]{1,0:T(8,128)(2,1)}, bf16[400,256]{1,0:T(8,128)(2,1)S(1)}, u32[]{:S(2)}, u32[]{:S(2)}) %collective-permute-start.2) | collective-permute-done | bytes 204832 | tf_op jit(solution)/shard_map/ppermute | solution.py:244
  25.4 4.4 %collective-permute-done.7.got_ref = bf16[384,256]{1,0:T(8,128)(2,1)S(1)} collective-permute-done((bf16[384,256]{1,0:T(8,128)(2,1)S(1)}, bf16[384,256]{1,0:T(8,128)(2,1)S(1)}, u32[]{:S(2)}, u32[]{:S(2)}) %collective-permute-start.7) | collective-permute-done | bytes 196640 | tf_op jit(solution)/shard_map/ppermute | solution.py:244
  31.1 1.2 %collective-permute-start.9 = (bf16[384,256]{1,0:T(8,128)(2,1)S(1)}, bf16[384,256]{1,0:T(8,128)(2,1)S(1)}, u32[]{:S(2)}, u32[]{:S(2)}) collective-permute-start(bf16[384,256]{1,0:T(8,128)(2,1)S(1)} %over_x.1.p0), channel_id=1, source_target_pairs={{0,96},{8,104},{16,112},{24,120},{32,0},{40,8},{48,16},{56,24},{64... | collective-permute-start | bytes 589832 | tf_op jit(solution)/shard_map/ppermute | solution.py:245
  33.2 1.2 %left.1 = f32[6144,128]{1,0:T(8,128)S(1)} custom-call(bf16[256,768]{1,0:T(8,128)(2,1)S(1)} %copy-done.2, bf16[400,256]{1,0:T(8,128)(2,1)S(1)} %fusion.7.b0, bf16[400,256]{1,0:T(8,128)(2,1)S(1)} %collective-permute-done.b1, bf16[400,256]{1,0:T(8,128)(2,1)S(1)} %collective-permute-done.1.b2, bf16[400,256]{1,0:T(8,128)(2,1)S(1)} %collective-permute-done.2.b3), custom_call_target="tpu_custom_call" | custom-call | flops 603979776 | bytes 4000000 | tf_op jit(solution)/shard_map/left/pallas_call | solution.py:283
  34.4 5.5 %collective-permute-done.10.p3 = bf16[384,256]{1,0:T(8,128)(2,1)S(1)} collective-permute-done((bf16[384,256]{1,0:T(8,128)(2,1)S(1)}, bf16[384,256]{1,0:T(8,128)(2,1)S(1)}, u32[]{:S(2)}, u32[]{:S(2)}) %collective-permute-start.10) | collective-permute-done | bytes 196640 | tf_op jit(solution)/shard_map/ppermute | solution.py:245
  40.5 2.0 %collective-permute-done.8.p1 = bf16[384,256]{1,0:T(8,128)(2,1)S(1)} collective-permute-done((bf16[384,256]{1,0:T(8,128)(2,1)S(1)}, bf16[384,256]{1,0:T(8,128)(2,1)S(1)}, u32[]{:S(2)}, u32[]{:S(2)}) %collective-permute-start.8) | collective-permute-done | bytes 196640 | tf_op jit(solution)/shard_map/ppermute | solution.py:245
  42.5 1.3 %right.1 = f32[6144,128]{1,0:T(8,128)S(1)} custom-call(bf16[256,768]{1,0:T(8,128)(2,1)S(1)} %copy-done.1, bf16[384,256]{1,0:T(8,128)(2,1)S(1)} %over_x.1.p0, bf16[384,256]{1,0:T(8,128)(2,1)S(1)} %collective-permute-done.8.p1, bf16[384,256]{1,0:T(8,128)(2,1)S(1)} %collective-permute-done.9.p2, bf16[384,256]{1,0:T(8,128)(2,1)S(1)} %collective-permute-done.10.p3), custom_call_target="tpu_custom_call" | custom-call | flops 603979776 | bytes 4000000 | tf_op jit(solution)/shard_map/right/pallas_call | solution.py:287
  43.8 6.0 %pairs.2 = (f32[4,72,256]{2,1,0:T(8,128)S(1)}, s32[4]{0:T(128)S(1)}) custom-call(s32[4]{0:T(128)S(1)} %copy-done.3, s32[2048]{0:T(1024)S(1)} %add.93.local_ref, s32[2048]{0:T(1024)S(1)} %bitcast.28, f32[6144,128]{1,0:T(8,128)S(1)} %left.1, f32[6144,128]{1,0:T(8,128)S(1)} %right.1, bf16[144,384]{1,0:T(8,128)(2,1)S(1)} %copy-done), custom_call_target="tpu_custom_call" | custom-call | flops 603979776 | bytes 4000000 | tf_op jit(solution)/shard_map/pairs/pallas_call | solution.py:295
  49.8 3.1 %collective-permute-start.11 = (f32[4,72,256]{2,1,0:T(8,128)S(1)}, f32[4,72,256]{2,1,0:T(8,128)S(1)}, u32[]{:S(2)}, u32[]{:S(2)}) collective-permute-start(f32[4,72,256]{2,1,0:T(8,128)S(1)} %get-tuple-element.24), channel_id=1, source_target_pairs={{0,1},{1,0},{2,3},{3,2},{4,5},{5,4},{6,7},{7,6},{8,9},{9,8},{10,11... | collective-permute-start | bytes 884744 | tf_op jit(solution)/shard_map/ppermute | solution.py:303
  52.9 5.9 %pairs.3 = (f32[4,72,256]{2,1,0:T(8,128)S(1)}, s32[4]{0:T(128)}) custom-call(s32[4]{0:T(128)S(1)} %get-tuple-element.25.token_ref, s32[2048]{0:T(1024)S(1)} %add.93.local_ref, s32[2048]{0:T(1024)S(1)} %bitcast.29, f32[6144,128]{1,0:T(8,128)S(1)} %left.1, f32[6144,128]{1,0:T(8,128)S(1)} %right.1, bf16[144,384]{1,0:T(8,128)(2,1)S(1)} %copy-done), custom_call_target="tpu_custom_call" | custom-call | flops 603979776 | bytes 4000000 | tf_op jit(solution)/shard_map/pairs/pallas_call | solution.py:295
  58.9 1.4 %collective-permute-done.11.a_ref = f32[4,72,256]{2,1,0:T(8,128)S(1)} collective-permute-done((f32[4,72,256]{2,1,0:T(8,128)S(1)}, f32[4,72,256]{2,1,0:T(8,128)S(1)}, u32[]{:S(2)}, u32[]{:S(2)}) %collective-permute-start.11) | collective-permute-done | bytes 294944 | tf_op jit(solution)/shard_map/ppermute | solution.py:303
  60.3 4.0 %collective-permute-start.12 = (f32[72,256]{1,0:T(8,128)S(1)}, f32[72,256]{1,0:T(8,128)S(1)}, u32[]{:S(2)}, u32[]{:S(2)}) collective-permute-start(f32[72,256]{1,0:T(8,128)S(1)} %get-tuple-element.27), channel_id=1, source_target_pairs={{0,4},{1,5},{2,6},{3,7},{4,0},{5,1},{6,2},{7,3},{8,12},{9,13},{10,... | collective-permute-start | bytes 221192 | tf_op jit(solution)/shard_map/ppermute | solution.py:303
  65.3 2.2 %collective-permute-start.14 = (f32[72,256]{1,0:T(8,128)S(1)}, f32[72,256]{1,0:T(8,128)S(1)}, u32[]{:S(2)}, u32[]{:S(2)}) collective-permute-start(f32[72,256]{1,0:T(8,128)S(1)} %get-tuple-element.29), channel_id=1, source_target_pairs={{0,6},{1,7},{2,0},{3,1},{4,2},{5,3},{6,4},{7,5},{8,14},{9,15},{10,... | collective-permute-start | bytes 221192 | tf_op jit(solution)/shard_map/ppermute | solution.py:303
  67.5 2.3 %collective-permute-done.13.refs_1_ = f32[72,256]{1,0:T(8,128)S(1)} collective-permute-done((f32[72,256]{1,0:T(8,128)S(1)}, f32[72,256]{1,0:T(8,128)S(1)}, u32[]{:S(2)}, u32[]{:S(2)}) %collective-permute-start.13) | collective-permute-done | bytes 73760 | tf_op jit(solution)/shard_map/ppermute | solution.py:303
  70.0 1.6 %collective-permute-start.16 = (f32[72,64]{1,0:T(8,128)S(1)}, f32[72,64]{1,0:T(8,128)S(1)}, u32[]{:S(2)}, u32[]{:S(2)}) collective-permute-start(f32[72,64]{1,0:T(8,128)S(1)} %get-tuple-element.33), channel_id=1, source_target_pairs={{0,16},{8,24},{16,0},{24,8},{32,48},{40,56},{48,32},{56,40},{64,80... | collective-permute-start | bytes 55304 | tf_op jit(solution)/shard_map/ppermute | solution.py:244
  71.9 2.2 %collective-permute-done.16.refs_2_ = f32[72,64]{1,0:T(8,128)S(1)} collective-permute-done((f32[72,64]{1,0:T(8,128)S(1)}, f32[72,64]{1,0:T(8,128)S(1)}, u32[]{:S(2)}, u32[]{:S(2)}) %collective-permute-start.16) | collective-permute-done | bytes 18464 | tf_op jit(solution)/shard_map/ppermute | solution.py:244
  75.0 1.3 %finish.1 = f32[1,4,64,65]{3,2,1,0:T(8,128)} custom-call(s32[1,4]{1,0:T(1,128)S(1)} %copy-done.4, f32[72,64]{1,0:T(8,128)S(1)} %get-tuple-element.31.refs_0_, f32[72,64]{1,0:T(8,128)S(1)} %collective-permute-done.15.refs_1_, f32[72,64]{1,0:T(8,128)S(1)} %collective-permute-done.16.refs_2_, f32[72,64]{1,0:T(8,128)S(1)} %collective-permute-done.17.refs_3_), custom_call_target="tpu_custom_call" | custom-call | tf_op jit(solution)/shard_map/finish/pallas_call | solution.py:315
  (56 shorter events, 13.3 us)
Async XLA Ops:
  0.0 16.5 %copy-start.3 = (s32[4]{0:T(128)S(1)}, s32[4]{0:T(128)}, u32[]{:S(2)}) copy-start(s32[4]{0:T(128)} %token_ref.1) | copy-start | bytes 52
  1.3 31.9 %copy-start.2 = (bf16[256,768]{1,0:T(8,128)(2,1)S(1)}, bf16[256,768]{1,0:T(8,128)(2,1)}, u32[]{:S(2)}) copy-start(bf16[256,768]{1,0:T(8,128)(2,1)} %constant.81.clone.table_ref) | copy-start | bytes 1179652
  1.3 11.5 %collective-permute-start.5 = (bf16[384,256]{1,0:T(8,128)(2,1)S(1)}, bf16[384,256]{1,0:T(8,128)(2,1)S(1)}, u32[]{:S(2)}, u32[]{:S(2)}) collective-permute-start(bf16[384,256]{1,0:T(8,128)(2,1)S(1)} %get-tuple-element.35), channel_id=1, source_target_pairs={{0,96},{8,104},{16,112},{24,120},{32,0},{40,8},{48,16},{56,24},{64... | collective-permute-start | bytes 589832 | tf_op jit(solution)/shard_map/ppermute | solution.py:245
  4.5 9.4 %collective-permute-start.4 = (bf16[384,256]{1,0:T(8,128)(2,1)S(1)}, bf16[384,256]{1,0:T(8,128)(2,1)S(1)}, u32[]{:S(2)}, u32[]{:S(2)}) collective-permute-start(bf16[384,256]{1,0:T(8,128)(2,1)S(1)} %get-tuple-element.36), channel_id=1, source_target_pairs={{0,64},{8,72},{16,80},{24,88},{32,96},{40,104},{48,112},{56,120},{... | collective-permute-start | bytes 589832 | tf_op jit(solution)/shard_map/ppermute | solution.py:245
  5.1 11.4 %collective-permute-start.3 = (bf16[384,256]{1,0:T(8,128)(2,1)S(1)}, bf16[384,256]{1,0:T(8,128)(2,1)S(1)}, u32[]{:S(2)}, u32[]{:S(2)}) collective-permute-start(bf16[384,256]{1,0:T(8,128)(2,1)S(1)} %get-tuple-element.37), channel_id=1, source_target_pairs={{0,32},{8,40},{16,48},{24,56},{32,64},{40,72},{48,80},{56,88},{64,... | collective-permute-start | bytes 589832 | tf_op jit(solution)/shard_map/ppermute | solution.py:245
  8.8 12.4 %collective-permute-start = (bf16[400,256]{1,0:T(8,128)(2,1)S(1)}, bf16[400,256]{1,0:T(8,128)(2,1)S(1)}, u32[]{:S(2)}, u32[]{:S(2)}) collective-permute-start(bf16[400,256]{1,0:T(8,128)(2,1)S(1)} %fusion.4), channel_id=1, source_target_pairs={{0,8},{8,0},{16,24},{24,16},{32,40},{40,32},{48,56},{56,48},{64,72... | collective-permute-start | bytes 614408 | tf_op jit(solution)/shard_map/ppermute | solution.py:244
  9.6 11.7 %collective-permute-start.1 = (bf16[400,256]{1,0:T(8,128)(2,1)}, bf16[400,256]{1,0:T(8,128)(2,1)S(1)}, u32[]{:S(2)}, u32[]{:S(2)}) collective-permute-start(bf16[400,256]{1,0:T(8,128)(2,1)} %fusion.5), channel_id=1, source_target_pairs={{0,16},{8,24},{16,0},{24,8},{32,48},{40,56},{48,32},{56,40},{64,80... | collective-permute-start | bytes 614408 | tf_op jit(solution)/shard_map/ppermute | solution.py:244
  17.2 2.5 %collective-permute-start.6 = (bf16[2,384,256]{2,1,0:T(8,128)(2,1)S(1)}, bf16[2,384,256]{2,1,0:T(8,128)(2,1)S(1)}, u32[]{:S(2)}, u32[]{:S(2)}) collective-permute-start(bf16[2,384,256]{2,1,0:T(8,128)(2,1)S(1)} %get-tuple-element.21), channel_id=1, source_target_pairs={{0,8},{8,0},{16,24},{24,16},{32,40},{40,32},{48,56},{56,48},{64,72... | collective-permute-start | bytes 1179656 | tf_op jit(solution)/shard_map/ppermute | solution.py:244
  18.0 7.3 %collective-permute-start.2 = (bf16[400,256]{1,0:T(8,128)(2,1)}, bf16[400,256]{1,0:T(8,128)(2,1)S(1)}, u32[]{:S(2)}, u32[]{:S(2)}) collective-permute-start(bf16[400,256]{1,0:T(8,128)(2,1)} %fusion.6), channel_id=1, source_target_pairs={{0,24},{8,16},{16,8},{24,0},{32,56},{40,48},{48,40},{56,32},{64,88... | collective-permute-start | bytes 614408 | tf_op jit(solution)/shard_map/ppermute | solution.py:244
  19.6 22.9 %copy-start.1 = (bf16[256,768]{1,0:T(8,128)(2,1)S(1)}, bf16[256,768]{1,0:T(8,128)(2,1)}, u32[]{:S(2)}) copy-start(bf16[256,768]{1,0:T(8,128)(2,1)} %constant.82.clone.table_ref) | copy-start | bytes 1179652
  20.3 9.5 %collective-permute-start.7 = (bf16[384,256]{1,0:T(8,128)(2,1)S(1)}, bf16[384,256]{1,0:T(8,128)(2,1)S(1)}, u32[]{:S(2)}, u32[]{:S(2)}) collective-permute-start(bf16[384,256]{1,0:T(8,128)(2,1)S(1)} %get-tuple-element.23), channel_id=1, source_target_pairs={{0,16},{8,24},{16,0},{24,8},{32,48},{40,56},{48,32},{56,40},{64,80... | collective-permute-start | bytes 589832 | tf_op jit(solution)/shard_map/ppermute | solution.py:244
  30.4 9.4 %collective-permute-start.10 = (bf16[384,256]{1,0:T(8,128)(2,1)S(1)}, bf16[384,256]{1,0:T(8,128)(2,1)S(1)}, u32[]{:S(2)}, u32[]{:S(2)}) collective-permute-start(bf16[384,256]{1,0:T(8,128)(2,1)S(1)} %over_x.1.p0), channel_id=1, source_target_pairs={{0,64},{8,72},{16,80},{24,88},{32,96},{40,104},{48,112},{56,120},{... | collective-permute-start | bytes 589832 | tf_op jit(solution)/shard_map/ppermute | solution.py:245
  31.1 9.4 %collective-permute-start.9 = (bf16[384,256]{1,0:T(8,128)(2,1)S(1)}, bf16[384,256]{1,0:T(8,128)(2,1)S(1)}, u32[]{:S(2)}, u32[]{:S(2)}) collective-permute-start(bf16[384,256]{1,0:T(8,128)(2,1)S(1)} %over_x.1.p0), channel_id=1, source_target_pairs={{0,96},{8,104},{16,112},{24,120},{32,0},{40,8},{48,16},{56,24},{64... | collective-permute-start | bytes 589832 | tf_op jit(solution)/shard_map/ppermute | solution.py:245
  32.3 10.2 %collective-permute-start.8 = (bf16[384,256]{1,0:T(8,128)(2,1)S(1)}, bf16[384,256]{1,0:T(8,128)(2,1)S(1)}, u32[]{:S(2)}, u32[]{:S(2)}) collective-permute-start(bf16[384,256]{1,0:T(8,128)(2,1)S(1)} %over_x.1.p0), channel_id=1, source_target_pairs={{0,32},{8,40},{16,48},{24,56},{32,64},{40,72},{48,80},{56,88},{64,... | collective-permute-start | bytes 589832 | tf_op jit(solution)/shard_map/ppermute | solution.py:245
  34.4 9.4 %copy-start = (bf16[144,384]{1,0:T(8,128)(2,1)S(1)}, bf16[144,384]{1,0:T(8,128)(2,1)}, u32[]{:S(2)}) copy-start(bf16[144,384]{1,0:T(8,128)(2,1)} %constant.83.clone.back_ref) | copy-start | bytes 331780
  49.8 10.4 %collective-permute-start.11 = (f32[4,72,256]{2,1,0:T(8,128)S(1)}, f32[4,72,256]{2,1,0:T(8,128)S(1)}, u32[]{:S(2)}, u32[]{:S(2)}) collective-permute-start(f32[4,72,256]{2,1,0:T(8,128)S(1)} %get-tuple-element.24), channel_id=1, source_target_pairs={{0,1},{1,0},{2,3},{3,2},{4,5},{5,4},{6,7},{7,6},{8,9},{9,8},{10,11... | collective-permute-start | bytes 884744 | tf_op jit(solution)/shard_map/ppermute | solution.py:303
  52.9 22.1 %copy-start.4 = (s32[1,4]{1,0:T(1,128)S(1)}, s32[1,4]{1,0:T(1,128)}, u32[]{:S(2)}) copy-start(s32[1,4]{1,0:T(1,128)} %near_ref.1) | copy-start | bytes 52
  60.3 7.2 %collective-permute-start.12 = (f32[72,256]{1,0:T(8,128)S(1)}, f32[72,256]{1,0:T(8,128)S(1)}, u32[]{:S(2)}, u32[]{:S(2)}) collective-permute-start(f32[72,256]{1,0:T(8,128)S(1)} %get-tuple-element.27), channel_id=1, source_target_pairs={{0,4},{1,5},{2,6},{3,7},{4,0},{5,1},{6,2},{7,3},{8,12},{9,13},{10,... | collective-permute-start | bytes 221192 | tf_op jit(solution)/shard_map/ppermute | solution.py:303
  64.2 5.6 %collective-permute-start.13 = (f32[72,256]{1,0:T(8,128)S(1)}, f32[72,256]{1,0:T(8,128)S(1)}, u32[]{:S(2)}, u32[]{:S(2)}) collective-permute-start(f32[72,256]{1,0:T(8,128)S(1)} %get-tuple-element.28), channel_id=1, source_target_pairs={{0,2},{1,3},{2,4},{3,5},{4,6},{5,7},{6,0},{7,1},{8,10},{9,11},{10,... | collective-permute-start | bytes 221192 | tf_op jit(solution)/shard_map/ppermute | solution.py:303
  65.3 4.5 %collective-permute-start.14 = (f32[72,256]{1,0:T(8,128)S(1)}, f32[72,256]{1,0:T(8,128)S(1)}, u32[]{:S(2)}, u32[]{:S(2)}) collective-permute-start(f32[72,256]{1,0:T(8,128)S(1)} %get-tuple-element.29), channel_id=1, source_target_pairs={{0,6},{1,7},{2,0},{3,1},{4,2},{5,3},{6,4},{7,5},{8,14},{9,15},{10,... | collective-permute-start | bytes 221192 | tf_op jit(solution)/shard_map/ppermute | solution.py:303
  69.9 2.0 %collective-permute-start.15 = (f32[72,64]{1,0:T(8,128)S(1)}, f32[72,64]{1,0:T(8,128)S(1)}, u32[]{:S(2)}, u32[]{:S(2)}) collective-permute-start(f32[72,64]{1,0:T(8,128)S(1)} %get-tuple-element.32), channel_id=1, source_target_pairs={{0,8},{8,0},{16,24},{24,16},{32,40},{40,32},{48,56},{56,48},{64,72... | collective-permute-start | bytes 55304 | tf_op jit(solution)/shard_map/ppermute | solution.py:244
  70.0 4.0 %collective-permute-start.16 = (f32[72,64]{1,0:T(8,128)S(1)}, f32[72,64]{1,0:T(8,128)S(1)}, u32[]{:S(2)}, u32[]{:S(2)}) collective-permute-start(f32[72,64]{1,0:T(8,128)S(1)} %get-tuple-element.33), channel_id=1, source_target_pairs={{0,16},{8,24},{16,0},{24,8},{32,48},{40,56},{48,32},{56,40},{64,80... | collective-permute-start | bytes 55304 | tf_op jit(solution)/shard_map/ppermute | solution.py:244
  71.6 3.4 %collective-permute-start.17 = (f32[72,64]{1,0:T(8,128)S(1)}, f32[72,64]{1,0:T(8,128)S(1)}, u32[]{:S(2)}, u32[]{:S(2)}) collective-permute-start(f32[72,64]{1,0:T(8,128)S(1)} %get-tuple-element.34), channel_id=1, source_target_pairs={{0,24},{8,16},{16,8},{24,0},{32,56},{40,48},{48,40},{56,32},{64,88... | collective-permute-start | bytes 55304 | tf_op jit(solution)/shard_map/ppermute | solution.py:244

commit v6 on v5

--- a/solution.py
+++ b/solution.py
@@ -62,28 +62,62 @@
     return me >> 2, me & 3, (me >> 1) & 1, me & 1
 
 
-def pick_kernel(owners_ref, g0, g1, g2, g3, keep_ref, give_ref):
+def pack_kernel(cube_ref, rows_ref, local_ref, remote_ref, *refs):
+    parts, own_ref, core_ref, chip_ref, sems = refs[:4], *refs[4:]
     row, step, _, _ = place()
-    for d in range(4):
-        to = (keep_ref, give_ref)[d % 2]
+    quarter = parts[0].shape[0]
+    copies = [
+        pltpu.make_async_copy(rows_ref.at[pl.ds(pl.multiple_of(((row + d) & 3) * quarter, quarter), quarter)], out, sems.at[d])
+        for d, out in enumerate(parts)
+    ]
+    channels, _, width = cube_ref.shape
+    size = cube_ref.shape[1] // 4
+    outs = (own_ref, core_ref, chip_ref.at[0], chip_ref.at[1])
+    for d, out in enumerate(outs):
+        at = pl.multiple_of((step ^ d) * size, size)
+        for c in range(channels):
+            copies.append(pltpu.make_async_copy(
+                cube_ref.at[c, pl.ds(at, size)], out.at[pl.ds(c * size, size)], sems.at[4 + d * channels + c]
+            ))
+    for copy in copies:
+        copy.start()
+    line = lax.broadcasted_iota(jnp.int32, (16, width), 0)
+    for d, out in enumerate(outs):
+        lists = jnp.zeros((16, width), jnp.float32)
+        for n, ref in enumerate((local_ref, remote_ref)):
+            listed = ref[pl.ds(step ^ d, 1), :].astype(jnp.float32)
+            per = listed.shape[1] // width
+            for k in range(per):
+                lists = jnp.where(line == n * per + k, listed[:, k * width:(k + 1) * width], lists)
+        out[pl.ds(channels * size, 16), :] = lists.astype(jnp.bfloat16)
+    for copy in copies:
+        copy.wait()
+
+
+def pick_kernel(owners_ref, g0, g1, g2, g3, give_ref):
+    row, step, _, _ = place()
+    for d in (1, 3):
         behind = (row + 4 - (owners_ref[step ^ d] >> 2)) & 3
         for n, ref in enumerate((g0, g1, g2, g3)):
 
             @pl.when(behind == n)
             def _():
-                to[d // 2] = ref[...]
-
-
-def core_kernel(owners_ref, kept_ref, got_ref, mine_ref, theirs_ref):
-    _, step, _, core = place()
+                give_ref[d // 2] = ref[...]
+
+
+def core_kernel(owners_ref, g0, g1, g2, g3, got_ref, _, mine_ref, theirs_ref):
+    row, step, _, core = place()
     for d, to in ((0, mine_ref), (2, theirs_ref)):
-        here = (owners_ref[step ^ d] & 1) == core
-
-        @pl.when(here)
-        def _():
-            to[...] = kept_ref[d // 2]
-
-        @pl.when(jnp.logical_not(here))
+        owner = owners_ref[step ^ d]
+        here = (owner & 1) == core
+        behind = jnp.where(here, (row + 4 - (owner >> 2)) & 3, 4)
+        for n, ref in enumerate((g0, g1, g2, g3)):
+
+            @pl.when(behind == n)
+            def _():
+                to[...] = ref[...]
+
+        @pl.when(behind == 4)
         def _():
             to[...] = got_ref[d // 2]
 
@@ -245,34 +279,32 @@
     turn = lambda v, d: lax.ppermute(v, "clu", [(i, (i + 4 * d) % n_clu) for i in range(n_clu)])
 
     quarter = ch * ev // 4
-    got = []
-    for d in range(4):
-        part = lax.dynamic_slice_in_dim(rows, (row + d) % 4 * quarter, quarter, 0)
-        got.append(part if d == 0 else turn(part, d))
     piece = shaped((quarter, samp), bf16)
-    two = shaped((2, quarter, samp), bf16)
-    keep, give = pl.pallas_call(
-        pick_kernel, out_shape=(two, two), in_specs=[SMEM] + [VMEM] * 4, out_specs=(VMEM,) * 2,
+    height = ch * block + 16
+    payload = shaped((height, samp), bf16)
+    *parts, own, core, chip = pl.pallas_call(
+        pack_kernel, out_shape=(piece,) * 4 + (payload, payload, shaped((2, height, samp), bf16)),
+        in_specs=[pl.BlockSpec(memory_space=pl.ANY)] * 2 + [VMEM] * 2, out_specs=(VMEM,) * 7,
+        scratch_shapes=[pltpu.SemaphoreType.DMA((4 + 4 * ch,))], compiler_params=SMALL, name="pack",
+    )(cube, rows, pair_local[0], pair_remote[0])
+    chip = near(chip, 2)
+    blocks = [own, near(core, 1), chip[0], near(chip[1], 1)]
+    got = [part if d == 0 else turn(part, d) for d, part in enumerate(parts)]
+    give = pl.pallas_call(
+        pick_kernel, out_shape=shaped((2, quarter, samp), bf16), in_specs=[SMEM] + [VMEM] * 4, out_specs=VMEM,
         compiler_params=SMALL, name="pick",
     )(owners, *got)
     mine, theirs = pl.pallas_call(
-        core_kernel, out_shape=(piece, piece), in_specs=[SMEM] + [VMEM] * 2, out_specs=(VMEM,) * 2,
+        core_kernel, out_shape=(piece, piece),
+        in_specs=[SMEM] + [VMEM] * 5 + [pl.BlockSpec(memory_space=pl.ANY)], out_specs=(VMEM,) * 2,
         compiler_params=SMALL, name="over_core",
-    )(owners, keep, near(give, 1))
+    )(owners, *got, near(give, 1), chip)
     mine = pl.pallas_call(
         chip_kernel, out_shape=piece, in_specs=[SMEM] + [VMEM] * 2, out_specs=VMEM,
         compiler_params=SMALL, name="over_x",
     )(owners, mine, near(theirs, 2))
     pieces = [mine] + [turn(mine, d) for d in (1, -1, 2)]
 
-    lists = jnp.concatenate([pair_local[0], pair_remote[0]], axis=1).astype(bf16)
-    lists = lists.reshape(steps, 2 * pairs // samp, samp)
-    blocks = []
-    for d in range(4):
-        events = lax.dynamic_slice_in_dim(cube, (step ^ d) * block, block, 1).reshape(ch * block, samp)
-        listed = lax.dynamic_index_in_dim(lists, step ^ d, 0, False)
-        listed = jnp.pad(listed, ((0, 16 - listed.shape[0]), (0, 0)))
-        blocks.append(near(jnp.concatenate([events, listed]), d))
     listed = jnp.stack([b[ch * block:ch * block + 2 * pairs // samp] for b in blocks]).astype(jnp.int32)
     listed = listed.reshape(4, 2, pairs) * 24
     first = listed[:, 0] + jnp.arange(4, dtype=jnp.int32)[:, None] * (block * 24)

time: 77.6 us -> 76.6 us (0.987)
  other arithmetic: 2.87 us -> 0.03 us
  waiting for transfers between devices: 28.9 us -> 26.2 us
  Pallas kernels: 17.7 us -> 20 us
  starting transfers between devices: 23.9 us -> 25.5 us
    unnamed x12 -> x20, local copies, waits for them, and re-layouts: 0.1 us -> 3.3 us
    ppermute x6, starting transfers between devices: 7.5 us -> 10.5 us  [local(): lax.ppermute(v, 'clu', [(i, (i + 4 * d) % n_clu) for i in range(n_clu)])]
    pallas_call x1 -> x2, Pallas kernels: 0.68 us -> 2.94 us  [the longest x1 2.33 us: local(): pl.pallas_call(pack_kernel, out_shape=(piece,) * 4 + (payload, payload, s...]
    ppermute x8, waiting for transfers between devices: 11.6 us -> 9.72 us  [local(): lax.ppermute(v, 'clu', [(i, i ^ d) for i in range(n_clu)])]
    concatenate x5 -> x0, other arithmetic: 1.44 us -> none  [the longest x4 1.41 us: local(): blocks.append(near(jnp.concatenate([events, listed]), d))]
    another operation x2 -> x0, other arithmetic: 1.4 us -> none
    dynamic_slice x1 -> x0, local copies, waits for them, and re-layouts: 1.28 us -> none  [local(): part = lax.dynamic_slice_in_dim(rows, (row + d) % 4 * quarter, quarter, 0)]
    another operation x1 -> x0, local copies, waits for them, and re-layouts: 1.28 us -> none
  transfers between devices with their start and end apart: 18 -> 18, of which waited for: 12 -> 10; matrix products, arithmetic and copies ran while one was open for 6% -> 0% of each run, Pallas kernels for 11% -> 11%
where the time goes in v6:
time: 76.6 us; the launch traced here: 75.3 us
  waiting for transfers between devices  26.2 us (34%)
  starting transfers between devices  25.5 us (33%)
  Pallas kernels  20 us (26%)
  local copies, waits for them, and re-layouts  3.4 us (4%)
    ppermute x6, waiting for transfers between devices, local(): lax.ppermute(v, 'clu', [(i, (i + 4 * d) % n_clu) for i in range(n_clu)])  13.5 us
    pallas_call x2, Pallas kernels, local(): pl.pallas_call(functools.partial(pair_kernel, across), out_shape=(shaped(...  12 us
    ppermute x6, starting transfers between devices, local(): lax.ppermute(v, 'clu', [(i, (i + 4 * d) % n_clu) for i in range(n_clu)])  10.5 us
    ppermute x4, starting transfers between devices, local(): lax.ppermute(v, 'sta', [(k, target(k, dz, dh, n_sta)) for k in range(n_st...  9.99 us
    ppermute x8, waiting for transfers between devices, local(): lax.ppermute(v, 'clu', [(i, i ^ d) for i in range(n_clu)])  9.72 us
    ppermute x8, starting transfers between devices, local(): lax.ppermute(v, 'clu', [(i, i ^ d) for i in range(n_clu)])  4.97 us
    unnamed x20, local copies, waits for them, and re-layouts  3.3 us
    ppermute x4, waiting for transfers between devices, local(): lax.ppermute(v, 'sta', [(k, target(k, dz, dh, n_sta)) for k in range(n_st...  3.02 us
  transfers between devices with their start and end apart: 18, of which 10 were waited for; matrix products, arithmetic and copies ran while one was open for 0% of the time, Pallas kernels for 11%

profile of v6, /device:TPU:0, one launch (start us, length us, event | category | flops | bytes accessed | tf_op | source)
XLA Modules:
  0.0 75.3 jit_solution(882688322655665662)
XLA Ops:
  0.0 1.1 %copy-done = bf16[256,6,256]{2,0,1:T(8,128)(2,1)S(1)} copy-done((bf16[256,6,256]{2,0,1:T(8,128)(2,1)S(1)}, bf16[256,6,256]{2,0,1:T(8,128)(2,1)}, u32[]{:S(2)}) %copy-start) | copy-done | bytes 786456
  2.5 2.3 %pack.1 = (bf16[384,256]{1,0:T(8,128)(2,1)S(1)}, bf16[384,256]{1,0:T(8,128)(2,1)S(1)}, bf16[384,256]{1,0:T(8,128)(2,1)S(1)}, bf16[384,256]{1,0:T(8,128)(2,1)S(1)...) custom-call(bf16[6,256,256]{2,1,0:T(8,128)(2,1)S(1)} %bitcast.15, ...), custom_call_target="tpu_custom_call" | custom-call | tf_op jit(solution)/shard_map/pack/pallas_call | solution.py:285
  4.9 1.7 %collective-permute-start.1 = (bf16[2,400,256]{2,1,0:T(8,128)(2,1)S(1)}, bf16[2,400,256]{2,1,0:T(8,128)(2,1)S(1)}, u32[]{:S(2)}, u32[]{:S(2)}) collective-permute-start(bf16[2,400,256]{2,1,0:T(8,128)(2,1)S(1)} %get-tuple-element.27), channel_id=1, source_target_pairs={{0,16},{8,24},{16,0},{24,8},{32,48},{40,56},{48,32},{56,40},{64,80... | collective-permute-start | bytes 1228808 | tf_op jit(solution)/shard_map/ppermute | solution.py:278
  6.5 1.6 %collective-permute-start.3 = (bf16[384,256]{1,0:T(8,128)(2,1)S(1)}, bf16[384,256]{1,0:T(8,128)(2,1)S(1)}, u32[]{:S(2)}, u32[]{:S(2)}) collective-permute-start(bf16[384,256]{1,0:T(8,128)(2,1)S(1)} %get-tuple-element.29), channel_id=1, source_target_pairs={{0,32},{8,40},{16,48},{24,56},{32,64},{40,72},{48,80},{56,88},{64,... | collective-permute-start | bytes 589832 | tf_op jit(solution)/shard_map/ppermute | solution.py:279
  8.1 2.9 %collective-permute-start.4 = (bf16[384,256]{1,0:T(8,128)(2,1)S(1)}, bf16[384,256]{1,0:T(8,128)(2,1)S(1)}, u32[]{:S(2)}, u32[]{:S(2)}) collective-permute-start(bf16[384,256]{1,0:T(8,128)(2,1)S(1)} %get-tuple-element.30), channel_id=1, source_target_pairs={{0,64},{8,72},{16,80},{24,88},{32,96},{40,104},{48,112},{56,120},{... | collective-permute-start | bytes 589832 | tf_op jit(solution)/shard_map/ppermute | solution.py:279
  11.0 1.3 %collective-permute-start.5 = (bf16[384,256]{1,0:T(8,128)(2,1)S(1)}, bf16[384,256]{1,0:T(8,128)(2,1)S(1)}, u32[]{:S(2)}, u32[]{:S(2)}) collective-permute-start(bf16[384,256]{1,0:T(8,128)(2,1)S(1)} %get-tuple-element.31), channel_id=1, source_target_pairs={{0,96},{8,104},{16,112},{24,120},{32,0},{40,8},{48,16},{56,24},{64... | collective-permute-start | bytes 589832 | tf_op jit(solution)/shard_map/ppermute | solution.py:279
  12.4 2.1 %collective-permute-done.3.g1 = bf16[384,256]{1,0:T(8,128)(2,1)S(1)} collective-permute-done((bf16[384,256]{1,0:T(8,128)(2,1)S(1)}, bf16[384,256]{1,0:T(8,128)(2,1)S(1)}, u32[]{:S(2)}, u32[]{:S(2)}) %collective-permute-start.3) | collective-permute-done | bytes 196640 | tf_op jit(solution)/shard_map/ppermute | solution.py:279
  14.4 5.1 %collective-permute-done.4.g2 = bf16[384,256]{1,0:T(8,128)(2,1)S(1)} collective-permute-done((bf16[384,256]{1,0:T(8,128)(2,1)S(1)}, bf16[384,256]{1,0:T(8,128)(2,1)S(1)}, u32[]{:S(2)}, u32[]{:S(2)}) %collective-permute-start.4) | collective-permute-done | bytes 196640 | tf_op jit(solution)/shard_map/ppermute | solution.py:279
  24.1 6.2 %collective-permute-done.7.got_ref = bf16[384,256]{1,0:T(8,128)(2,1)S(1)} collective-permute-done((bf16[384,256]{1,0:T(8,128)(2,1)S(1)}, bf16[384,256]{1,0:T(8,128)(2,1)S(1)}, u32[]{:S(2)}, u32[]{:S(2)}) %collective-permute-start.7) | collective-permute-done | bytes 196640 | tf_op jit(solution)/shard_map/ppermute | solution.py:278
  30.9 2.7 %collective-permute-start.10 = (bf16[384,256]{1,0:T(8,128)(2,1)S(1)}, bf16[384,256]{1,0:T(8,128)(2,1)S(1)}, u32[]{:S(2)}, u32[]{:S(2)}) collective-permute-start(bf16[384,256]{1,0:T(8,128)(2,1)S(1)} %over_x.1.p0), channel_id=1, source_target_pairs={{0,64},{8,72},{16,80},{24,88},{32,96},{40,104},{48,112},{56,120},{... | collective-permute-start | bytes 589832 | tf_op jit(solution)/shard_map/ppermute | solution.py:279
  33.5 1.2 %collective-permute-start.9 = (bf16[384,256]{1,0:T(8,128)(2,1)S(1)}, bf16[384,256]{1,0:T(8,128)(2,1)S(1)}, u32[]{:S(2)}, u32[]{:S(2)}) collective-permute-start(bf16[384,256]{1,0:T(8,128)(2,1)S(1)} %over_x.1.p0), channel_id=1, source_target_pairs={{0,96},{8,104},{16,112},{24,120},{32,0},{40,8},{48,16},{56,24},{64... | collective-permute-start | bytes 589832 | tf_op jit(solution)/shard_map/ppermute | solution.py:279
  35.6 1.1 %left.1 = f32[6144,128]{1,0:T(8,128)S(1)} custom-call(bf16[256,768]{1,0:T(8,128)(2,1)S(1)} %copy-done.3, bf16[400,256]{1,0:T(8,128)(2,1)S(1)} %get-tuple-element.25.b0, bf16[400,256]{1,0:T(8,128)(2,1)S(1)} %collective-permute-done.b1, bf16[400,256]{1,0:T(8,128)(2,1)S(1)} %get-tuple-element.45.b2, bf16[400,256]{1,0:T(8,128)(2,1)S(1)} %collective-permute-done.2.b3), custom_call_target="tpu_custom_call" | custom-call | flops 603979776 | bytes 4000000 | tf_op jit(solution)/shard_map/left/pallas_call | solution.py:315
  36.8 3.5 %collective-permute-done.10.p3 = bf16[384,256]{1,0:T(8,128)(2,1)S(1)} collective-permute-done((bf16[384,256]{1,0:T(8,128)(2,1)S(1)}, bf16[384,256]{1,0:T(8,128)(2,1)S(1)}, u32[]{:S(2)}, u32[]{:S(2)}) %collective-permute-start.10) | collective-permute-done | bytes 196640 | tf_op jit(solution)/shard_map/ppermute | solution.py:279
  40.3 1.9 %collective-permute-done.9.p2 = bf16[384,256]{1,0:T(8,128)(2,1)S(1)} collective-permute-done((bf16[384,256]{1,0:T(8,128)(2,1)S(1)}, bf16[384,256]{1,0:T(8,128)(2,1)S(1)}, u32[]{:S(2)}, u32[]{:S(2)}) %collective-permute-start.9) | collective-permute-done | bytes 196640 | tf_op jit(solution)/shard_map/ppermute | solution.py:279
  43.0 1.3 %right.1 = f32[6144,128]{1,0:T(8,128)S(1)} custom-call(bf16[256,768]{1,0:T(8,128)(2,1)S(1)} %copy-done.2, bf16[384,256]{1,0:T(8,128)(2,1)S(1)} %over_x.1.p0, bf16[384,256]{1,0:T(8,128)(2,1)S(1)} %collective-permute-done.8.p1, bf16[384,256]{1,0:T(8,128)(2,1)S(1)} %collective-permute-done.9.p2, bf16[384,256]{1,0:T(8,128)(2,1)S(1)} %collective-permute-done.10.p3), custom_call_target="tpu_custom_call" | custom-call | flops 603979776 | bytes 4000000 | tf_op jit(solution)/shard_map/right/pallas_call | solution.py:319
  44.3 6.0 %pairs.2 = (f32[4,72,256]{2,1,0:T(8,128)S(1)}, s32[4]{0:T(128)S(1)}) custom-call(s32[4]{0:T(128)S(1)} %copy-done.7, s32[2048]{0:T(1024)S(1)} %add.14.local_ref, s32[2048]{0:T(1024)S(1)} %bitcast.17, f32[6144,128]{1,0:T(8,128)S(1)} %left.1, f32[6144,128]{1,0:T(8,128)S(1)} %right.1, bf16[144,384]{1,0:T(8,128)(2,1)S(1)} %copy-done.1), custom_call_target="tpu_custom_call" | custom-call | flops 603979776 | bytes 4000000 | tf_op jit(solution)/shard_map/pairs/pallas_call | solution.py:327
  50.4 2.8 %collective-permute-start.11 = (f32[4,72,256]{2,1,0:T(8,128)S(1)}, f32[4,72,256]{2,1,0:T(8,128)S(1)}, u32[]{:S(2)}, u32[]{:S(2)}) collective-permute-start(f32[4,72,256]{2,1,0:T(8,128)S(1)} %get-tuple-element.34), channel_id=1, source_target_pairs={{0,1},{1,0},{2,3},{3,2},{4,5},{5,4},{6,7},{7,6},{8,9},{9,8},{10,11... | collective-permute-start | bytes 884744 | tf_op jit(solution)/shard_map/ppermute | solution.py:335
  53.2 5.9 %pairs.3 = (f32[4,72,256]{2,1,0:T(8,128)S(1)}, s32[4]{0:T(128)}) custom-call(s32[4]{0:T(128)S(1)} %get-tuple-element.35.token_ref, s32[2048]{0:T(1024)S(1)} %add.14.local_ref, s32[2048]{0:T(1024)S(1)} %bitcast.18, f32[6144,128]{1,0:T(8,128)S(1)} %left.1, f32[6144,128]{1,0:T(8,128)S(1)} %right.1, bf16[144,384]{1,0:T(8,128)(2,1)S(1)} %copy-done.1), custom_call_target="tpu_custom_call" | custom-call | flops 603979776 | bytes 4000000 | tf_op jit(solution)/shard_map/pairs/pallas_call | solution.py:327
  59.8 4.0 %collective-permute-start.12 = (f32[72,256]{1,0:T(8,128)S(1)}, f32[72,256]{1,0:T(8,128)S(1)}, u32[]{:S(2)}, u32[]{:S(2)}) collective-permute-start(f32[72,256]{1,0:T(8,128)S(1)} %get-tuple-element.37), channel_id=1, source_target_pairs={{0,4},{1,5},{2,6},{3,7},{4,0},{5,1},{6,2},{7,3},{8,12},{9,13},{10,... | collective-permute-start | bytes 221192 | tf_op jit(solution)/shard_map/ppermute | solution.py:335
  64.8 2.2 %collective-permute-start.14 = (f32[72,256]{1,0:T(8,128)S(1)}, f32[72,256]{1,0:T(8,128)S(1)}, u32[]{:S(2)}, u32[]{:S(2)}) collective-permute-start(f32[72,256]{1,0:T(8,128)S(1)} %get-tuple-element.39), channel_id=1, source_target_pairs={{0,6},{1,7},{2,0},{3,1},{4,2},{5,3},{6,4},{7,5},{8,14},{9,15},{10,... | collective-permute-start | bytes 221192 | tf_op jit(solution)/shard_map/ppermute | solution.py:335
  67.0 2.3 %collective-permute-done.13.refs_1_ = f32[72,256]{1,0:T(8,128)S(1)} collective-permute-done((f32[72,256]{1,0:T(8,128)S(1)}, f32[72,256]{1,0:T(8,128)S(1)}, u32[]{:S(2)}, u32[]{:S(2)}) %collective-permute-start.13) | collective-permute-done | bytes 73760 | tf_op jit(solution)/shard_map/ppermute | solution.py:335
  70.2 1.3 %collective-permute-start.17 = (f32[72,64]{1,0:T(8,128)S(1)}, f32[72,64]{1,0:T(8,128)S(1)}, u32[]{:S(2)}, u32[]{:S(2)}) collective-permute-start(f32[72,64]{1,0:T(8,128)S(1)} %get-tuple-element.44), channel_id=1, source_target_pairs={{0,24},{8,16},{16,8},{24,0},{32,56},{40,48},{48,40},{56,32},{64,88... | collective-permute-start | bytes 55304 | tf_op jit(solution)/shard_map/ppermute | solution.py:278
  71.4 2.5 %collective-permute-done.16.refs_2_ = f32[72,64]{1,0:T(8,128)S(1)} collective-permute-done((f32[72,64]{1,0:T(8,128)S(1)}, f32[72,64]{1,0:T(8,128)S(1)}, u32[]{:S(2)}, u32[]{:S(2)}) %collective-permute-start.16) | collective-permute-done | bytes 18464 | tf_op jit(solution)/shard_map/ppermute | solution.py:278
  73.9 1.3 %finish.1 = f32[1,4,64,65]{3,2,1,0:T(8,128)} custom-call(s32[1,4]{1,0:T(1,128)S(1)} %copy-done.8, f32[72,64]{1,0:T(8,128)S(1)} %get-tuple-element.41.refs_0_, f32[72,64]{1,0:T(8,128)S(1)} %collective-permute-done.15.refs_1_, f32[72,64]{1,0:T(8,128)S(1)} %collective-permute-done.16.refs_2_, f32[72,64]{1,0:T(8,128)S(1)} %collective-permute-done.17.refs_3_), custom_call_target="tpu_custom_call" | custom-call | tf_op jit(solution)/shard_map/finish/pallas_call | solution.py:347
  (56 shorter events, 10.7 us)
Async XLA Ops:
  0.0 22.7 %copy-start.7 = (s32[4]{0:T(128)S(1)}, s32[4]{0:T(128)}, u32[]{:S(2)}) copy-start(s32[4]{0:T(128)} %token_ref.1) | copy-start | bytes 52
  0.0 1.1 %copy-start = (bf16[256,6,256]{2,0,1:T(8,128)(2,1)S(1)}, bf16[256,6,256]{2,0,1:T(8,128)(2,1)}, u32[]{:S(2)}) copy-start(bf16[256,6,256]{2,0,1:T(8,128)(2,1)} %param.8) | copy-start | bytes 2359300
  2.5 33.1 %copy-start.3 = (bf16[256,768]{1,0:T(8,128)(2,1)S(1)}, bf16[256,768]{1,0:T(8,128)(2,1)}, u32[]{:S(2)}) copy-start(bf16[256,768]{1,0:T(8,128)(2,1)} %constant.10.clone.table_ref) | copy-start | bytes 1179652
  4.9 16.6 %collective-permute-start.1 = (bf16[2,400,256]{2,1,0:T(8,128)(2,1)S(1)}, bf16[2,400,256]{2,1,0:T(8,128)(2,1)S(1)}, u32[]{:S(2)}, u32[]{:S(2)}) collective-permute-start(bf16[2,400,256]{2,1,0:T(8,128)(2,1)S(1)} %get-tuple-element.27), channel_id=1, source_target_pairs={{0,16},{8,24},{16,0},{24,8},{32,48},{40,56},{48,32},{56,40},{64,80... | collective-permute-start | bytes 1228808 | tf_op jit(solution)/shard_map/ppermute | solution.py:278
  6.5 7.9 %collective-permute-start.3 = (bf16[384,256]{1,0:T(8,128)(2,1)S(1)}, bf16[384,256]{1,0:T(8,128)(2,1)S(1)}, u32[]{:S(2)}, u32[]{:S(2)}) collective-permute-start(bf16[384,256]{1,0:T(8,128)(2,1)S(1)} %get-tuple-element.29), channel_id=1, source_target_pairs={{0,32},{8,40},{16,48},{24,56},{32,64},{40,72},{48,80},{56,88},{64,... | collective-permute-start | bytes 589832 | tf_op jit(solution)/shard_map/ppermute | solution.py:279
  8.1 11.4 %collective-permute-start.4 = (bf16[384,256]{1,0:T(8,128)(2,1)S(1)}, bf16[384,256]{1,0:T(8,128)(2,1)S(1)}, u32[]{:S(2)}, u32[]{:S(2)}) collective-permute-start(bf16[384,256]{1,0:T(8,128)(2,1)S(1)} %get-tuple-element.30), channel_id=1, source_target_pairs={{0,64},{8,72},{16,80},{24,88},{32,96},{40,104},{48,112},{56,120},{... | collective-permute-start | bytes 589832 | tf_op jit(solution)/shard_map/ppermute | solution.py:279
  11.0 8.6 %collective-permute-start.5 = (bf16[384,256]{1,0:T(8,128)(2,1)S(1)}, bf16[384,256]{1,0:T(8,128)(2,1)S(1)}, u32[]{:S(2)}, u32[]{:S(2)}) collective-permute-start(bf16[384,256]{1,0:T(8,128)(2,1)S(1)} %get-tuple-element.31), channel_id=1, source_target_pairs={{0,96},{8,104},{16,112},{24,120},{32,0},{40,8},{48,16},{56,24},{64... | collective-permute-start | bytes 589832 | tf_op jit(solution)/shard_map/ppermute | solution.py:279
  20.8 1.8 %collective-permute-start.6 = (bf16[2,384,256]{2,1,0:T(8,128)(2,1)S(1)}, bf16[2,384,256]{2,1,0:T(8,128)(2,1)S(1)}, u32[]{:S(2)}, u32[]{:S(2)}) collective-permute-start(bf16[2,384,256]{2,1,0:T(8,128)(2,1)S(1)} %pick.1), channel_id=1, source_target_pairs={{0,8},{8,0},{16,24},{24,16},{32,40},{40,32},{48,56},{56,48},{64,72... | collective-permute-start | bytes 1179656 | tf_op jit(solution)/shard_map/ppermute | solution.py:278
  20.9 3.1 %collective-permute-start = (bf16[400,256]{1,0:T(8,128)(2,1)S(1)}, bf16[400,256]{1,0:T(8,128)(2,1)S(1)}, u32[]{:S(2)}, u32[]{:S(2)}) collective-permute-start(bf16[400,256]{1,0:T(8,128)(2,1)S(1)} %get-tuple-element.26), channel_id=1, source_target_pairs={{0,8},{8,0},{16,24},{24,16},{32,40},{40,32},{48,56},{56,48},{64,72... | collective-permute-start | bytes 614408 | tf_op jit(solution)/shard_map/ppermute | solution.py:278
  21.5 21.6 %copy-start.2 = (bf16[256,768]{1,0:T(8,128)(2,1)S(1)}, bf16[256,768]{1,0:T(8,128)(2,1)}, u32[]{:S(2)}) copy-start(bf16[256,768]{1,0:T(8,128)(2,1)} %constant.11.clone.table_ref) | copy-start | bytes 1179652
  21.5 2.6 %collective-permute-start.2 = (bf16[400,256]{1,0:T(8,128)(2,1)S(1)}, bf16[400,256]{1,0:T(8,128)(2,1)S(1)}, u32[]{:S(2)}, u32[]{:S(2)}) collective-permute-start(bf16[400,256]{1,0:T(8,128)(2,1)S(1)} %get-tuple-element.46), channel_id=1, source_target_pairs={{0,8},{8,0},{16,24},{24,16},{32,40},{40,32},{48,56},{56,48},{64,72... | collective-permute-start | bytes 614408 | tf_op jit(solution)/shard_map/ppermute | solution.py:278
  23.3 7.0 %collective-permute-start.7 = (bf16[384,256]{1,0:T(8,128)(2,1)S(1)}, bf16[384,256]{1,0:T(8,128)(2,1)S(1)}, u32[]{:S(2)}, u32[]{:S(2)}) collective-permute-start(bf16[384,256]{1,0:T(8,128)(2,1)S(1)} %get-tuple-element.33), channel_id=1, source_target_pairs={{0,16},{8,24},{16,0},{24,8},{32,48},{40,56},{48,32},{56,40},{64,80... | collective-permute-start | bytes 589832 | tf_op jit(solution)/shard_map/ppermute | solution.py:278
  30.9 9.4 %collective-permute-start.10 = (bf16[384,256]{1,0:T(8,128)(2,1)S(1)}, bf16[384,256]{1,0:T(8,128)(2,1)S(1)}, u32[]{:S(2)}, u32[]{:S(2)}) collective-permute-start(bf16[384,256]{1,0:T(8,128)(2,1)S(1)} %over_x.1.p0), channel_id=1, source_target_pairs={{0,64},{8,72},{16,80},{24,88},{32,96},{40,104},{48,112},{56,120},{... | collective-permute-start | bytes 589832 | tf_op jit(solution)/shard_map/ppermute | solution.py:279
  33.5 8.7 %collective-permute-start.9 = (bf16[384,256]{1,0:T(8,128)(2,1)S(1)}, bf16[384,256]{1,0:T(8,128)(2,1)S(1)}, u32[]{:S(2)}, u32[]{:S(2)}) collective-permute-start(bf16[384,256]{1,0:T(8,128)(2,1)S(1)} %over_x.1.p0), channel_id=1, source_target_pairs={{0,96},{8,104},{16,112},{24,120},{32,0},{40,8},{48,16},{56,24},{64... | collective-permute-start | bytes 589832 | tf_op jit(solution)/shard_map/ppermute | solution.py:279
  34.8 8.3 %collective-permute-start.8 = (bf16[384,256]{1,0:T(8,128)(2,1)S(1)}, bf16[384,256]{1,0:T(8,128)(2,1)S(1)}, u32[]{:S(2)}, u32[]{:S(2)}) collective-permute-start(bf16[384,256]{1,0:T(8,128)(2,1)S(1)} %over_x.1.p0), channel_id=1, source_target_pairs={{0,32},{8,40},{16,48},{24,56},{32,64},{40,72},{48,80},{56,88},{64,... | collective-permute-start | bytes 589832 | tf_op jit(solution)/shard_map/ppermute | solution.py:279
  36.8 7.6 %copy-start.1 = (bf16[144,384]{1,0:T(8,128)(2,1)S(1)}, bf16[144,384]{1,0:T(8,128)(2,1)}, u32[]{:S(2)}) copy-start(bf16[144,384]{1,0:T(8,128)(2,1)} %constant.12.clone.back_ref) | copy-start | bytes 331780
  50.4 9.4 %collective-permute-start.11 = (f32[4,72,256]{2,1,0:T(8,128)S(1)}, f32[4,72,256]{2,1,0:T(8,128)S(1)}, u32[]{:S(2)}, u32[]{:S(2)}) collective-permute-start(f32[4,72,256]{2,1,0:T(8,128)S(1)} %get-tuple-element.34), channel_id=1, source_target_pairs={{0,1},{1,0},{2,3},{3,2},{4,5},{5,4},{6,7},{7,6},{8,9},{9,8},{10,11... | collective-permute-start | bytes 884744 | tf_op jit(solution)/shard_map/ppermute | solution.py:335
  53.1 20.8 %copy-start.8 = (s32[1,4]{1,0:T(1,128)S(1)}, s32[1,4]{1,0:T(1,128)}, u32[]{:S(2)}) copy-start(s32[1,4]{1,0:T(1,128)} %near_ref.1) | copy-start | bytes 52
  59.8 7.2 %collective-permute-start.12 = (f32[72,256]{1,0:T(8,128)S(1)}, f32[72,256]{1,0:T(8,128)S(1)}, u32[]{:S(2)}, u32[]{:S(2)}) collective-permute-start(f32[72,256]{1,0:T(8,128)S(1)} %get-tuple-element.37), channel_id=1, source_target_pairs={{0,4},{1,5},{2,6},{3,7},{4,0},{5,1},{6,2},{7,3},{8,12},{9,13},{10,... | collective-permute-start | bytes 221192 | tf_op jit(solution)/shard_map/ppermute | solution.py:335
  63.8 5.6 %collective-permute-start.13 = (f32[72,256]{1,0:T(8,128)S(1)}, f32[72,256]{1,0:T(8,128)S(1)}, u32[]{:S(2)}, u32[]{:S(2)}) collective-permute-start(f32[72,256]{1,0:T(8,128)S(1)} %get-tuple-element.38), channel_id=1, source_target_pairs={{0,2},{1,3},{2,4},{3,5},{4,6},{5,7},{6,0},{7,1},{8,10},{9,11},{10,... | collective-permute-start | bytes 221192 | tf_op jit(solution)/shard_map/ppermute | solution.py:335
  64.8 4.6 %collective-permute-start.14 = (f32[72,256]{1,0:T(8,128)S(1)}, f32[72,256]{1,0:T(8,128)S(1)}, u32[]{:S(2)}, u32[]{:S(2)}) collective-permute-start(f32[72,256]{1,0:T(8,128)S(1)} %get-tuple-element.39), channel_id=1, source_target_pairs={{0,6},{1,7},{2,0},{3,1},{4,2},{5,3},{6,4},{7,5},{8,14},{9,15},{10,... | collective-permute-start | bytes 221192 | tf_op jit(solution)/shard_map/ppermute | solution.py:335
  69.5 2.0 %collective-permute-start.15 = (f32[72,64]{1,0:T(8,128)S(1)}, f32[72,64]{1,0:T(8,128)S(1)}, u32[]{:S(2)}, u32[]{:S(2)}) collective-permute-start(f32[72,64]{1,0:T(8,128)S(1)} %get-tuple-element.42), channel_id=1, source_target_pairs={{0,8},{8,0},{16,24},{24,16},{32,40},{40,32},{48,56},{56,48},{64,72... | collective-permute-start | bytes 55304 | tf_op jit(solution)/shard_map/ppermute | solution.py:278
  69.6 4.4 %collective-permute-start.16 = (f32[72,64]{1,0:T(8,128)S(1)}, f32[72,64]{1,0:T(8,128)S(1)}, u32[]{:S(2)}, u32[]{:S(2)}) collective-permute-start(f32[72,64]{1,0:T(8,128)S(1)} %get-tuple-element.43), channel_id=1, source_target_pairs={{0,16},{8,24},{16,0},{24,8},{32,48},{40,56},{48,32},{56,40},{64,80... | collective-permute-start | bytes 55304 | tf_op jit(solution)/shard_map/ppermute | solution.py:278
  70.2 3.8 %collective-permute-start.17 = (f32[72,64]{1,0:T(8,128)S(1)}, f32[72,64]{1,0:T(8,128)S(1)}, u32[]{:S(2)}, u32[]{:S(2)}) collective-permute-start(f32[72,64]{1,0:T(8,128)S(1)} %get-tuple-element.44), channel_id=1, source_target_pairs={{0,24},{8,16},{16,8},{24,0},{32,56},{40,48},{48,40},{56,32},{64,88... | collective-permute-start | bytes 55304 | tf_op jit(solution)/shard_map/ppermute | solution.py:278
  (3 other events, 2.1 us)

commit v7 on v6

--- a/solution.py
+++ b/solution.py
@@ -10,9 +10,11 @@
 from jax.sharding import PartitionSpec as P
 
 CH, SAMP, HALF, LAGS = 48, 256, 32, 65
+CLU, STA = ("y", "xl", "core"), ("z", "xh")
 N = 288
 LO, EXTRA = 128, 17
 ROWS = 72
+TALL = 40
 EI, EJ = 68, 69
 
 
@@ -58,34 +60,46 @@
 
 
 def place():
-    me = lax.axis_index("clu")
-    return me >> 2, me & 3, (me >> 1) & 1, me & 1
-
-
-def pack_kernel(cube_ref, rows_ref, local_ref, remote_ref, *refs):
-    parts, own_ref, core_ref, chip_ref, sems = refs[:4], *refs[4:]
-    row, step, _, _ = place()
-    quarter = parts[0].shape[0]
+    x, core = lax.axis_index("xl"), lax.axis_index("core")
+    return lax.axis_index("y"), x * 2 + core, x, core
+
+
+def cut_kernel(rows_ref, *refs):
+    outs, sems = refs[:-1], refs[-1]
+    row = place()[0]
+    size = outs[0].shape[0]
     copies = [
-        pltpu.make_async_copy(rows_ref.at[pl.ds(pl.multiple_of(((row + d) & 3) * quarter, quarter), quarter)], out, sems.at[d])
-        for d, out in enumerate(parts)
+        pltpu.make_async_copy(rows_ref.at[pl.ds(pl.multiple_of(((row + d) & 3) * size, size), size)], out, sems.at[d])
+        for d, out in enumerate(outs)
     ]
+    for copy in copies:
+        copy.start()
+    for copy in copies:
+        copy.wait()
+
+
+def pack_kernel(_, cube_ref, local_ref, remote_ref, own_ref, core_ref, chip_ref, lists_ref, sems):
+    step = place()[1]
     channels, _, width = cube_ref.shape
     size = cube_ref.shape[1] // 4
     outs = (own_ref, core_ref, chip_ref.at[0], chip_ref.at[1])
+    first = [pltpu.make_async_copy(ref.at[0], lists_ref.at[n], sems.at[n]) for n, ref in enumerate((local_ref, remote_ref))]
+    copies = []
     for d, out in enumerate(outs):
         at = pl.multiple_of((step ^ d) * size, size)
         for c in range(channels):
             copies.append(pltpu.make_async_copy(
-                cube_ref.at[c, pl.ds(at, size)], out.at[pl.ds(c * size, size)], sems.at[4 + d * channels + c]
+                cube_ref.at[c, pl.ds(at, size)], out.at[pl.ds(c * size, size)], sems.at[2 + d * channels + c]
             ))
-    for copy in copies:
+    for copy in first + copies:
         copy.start()
+    for copy in first:
+        copy.wait()
     line = lax.broadcasted_iota(jnp.int32, (16, width), 0)
     for d, out in enumerate(outs):
         lists = jnp.zeros((16, width), jnp.float32)
-        for n, ref in enumerate((local_ref, remote_ref)):
-            listed = ref[pl.ds(step ^ d, 1), :].astype(jnp.float32)
+        for n in range(2):
+            listed = lists_ref[n, pl.ds(step ^ d, 1), :].astype(jnp.float32)
             per = listed.shape[1] // width
             for k in range(per):
                 lists = jnp.where(line == n * per + k, listed[:, k * width:(k + 1) * width], lists)
@@ -94,7 +108,7 @@
         copy.wait()
 
 
-def pick_kernel(owners_ref, g0, g1, g2, g3, give_ref):
+def pick_kernel(owners_ref, g0, g1, g2, g3, _, give_ref):
     row, step, _, _ = place()
     for d in (1, 3):
         behind = (row + 4 - (owners_ref[step ^ d] >> 2)) & 3
@@ -192,7 +206,7 @@
     width = out_ref.shape[2]
     half = out_ref.shape[0]
     next_ref[0] = token_ref[0]
-    sta = lax.axis_index("sta")
+    sta = lax.axis_index(STA)
     share = width // 4
     pairs = local_ref.shape[0] // 4
     bh, bl = back_ref[:ROWS], back_ref[ROWS:]
@@ -227,44 +241,46 @@
         out_ref[t] = dot(bh, zh) + dot(bh, zl) + dot(bl, zh)
 
 
-def add_kernel(a_ref, b_ref, *out_refs):
-    for t, ref in enumerate(out_refs):
-        ref[...] = a_ref[t] + b_ref[t]
-
-
-def sum_kernel(*refs):
-    parts, out_refs = refs[:-4], refs[-4:]
-    total = parts[0][...]
-    for ref in parts[1:]:
-        total = total + ref[...]
+def add_kernel(a_ref, b_ref, out_ref):
+    z, step = lax.axis_index("z"), place()[1]
+    share = a_ref.shape[2] // 4
+    for t, dz in enumerate(MOVES):
+        total = a_ref[t] + b_ref[t]
+        for q in range(4):
+            part = total[:, q * share:(q + 1) * share]
+            slot = ((z + dz) & 3) * 4 + (step ^ q)
+            out_ref[slot, :, :share] = part[:TALL]
+            out_ref[slot, :ROWS - TALL, share:] = part[TALL:]
+
+
+def final_kernel(near_ref, got_ref, out_ref):
+    share = out_ref.shape[2]
     count = CH * SAMP
-    ni = 1.0 / jnp.sqrt(total[LAGS:LAGS + 1] / count + 1e-6)
-    nj = 1.0 / jnp.sqrt(total[LAGS + 1:LAGS + 2] / count + 1e-6)
-    total = total * (ni * nj / count)
-    share = out_refs[0].shape[1]
-    for q, ref in enumerate(out_refs):
-        ref[...] = total[:, q * share:(q + 1) * share]
-
-
-def final_kernel(near_ref, *refs):
-    out_ref = refs[-1]
-    step = place()[1]
-    for r, ref in enumerate(refs[:-1]):
-        s = step ^ r
-        out_ref[0, s] = (ref[...] * near_ref[0, s].astype(jnp.float32)).T[:, :LAGS]
-
-
+    for s in range(4):
+        total = (got_ref[s] + got_ref[4 + s]) + (got_ref[8 + s] + got_ref[12 + s])
+        total = jnp.concatenate([total[:, :share], total[:ROWS - TALL, share:]], axis=0)
+        ni = 1.0 / jnp.sqrt(total[LAGS:LAGS + 1] / count + 1e-6)
+        nj = 1.0 / jnp.sqrt(total[LAGS + 1:LAGS + 2] / count + 1e-6)
+        out_ref[0, s] = (total * (ni * nj / count * near_ref[0, s].astype(jnp.float32))).T[:, :LAGS]
+
+
+HBM = pl.BlockSpec(memory_space=pltpu.HBM)
+ANY = pl.BlockSpec(memory_space=pl.ANY)
 SMEM = pl.BlockSpec(memory_space=pltpu.SMEM)
 VMEM = pl.BlockSpec(memory_space=pltpu.VMEM)
 PARAMS = pltpu.CompilerParams(vmem_limit_bytes=20 * 1024 * 1024)
 SMALL = pltpu.CompilerParams(vmem_limit_bytes=8 * 1024 * 1024)
 
 
+def in_hbm(v):
+    return pltpu.with_memory_space_constraint(v, pltpu.HBM)
+
+
 def local(waves, owners, neighbours, pair_local, pair_remote):
     ev, ch, samp = waves.shape
     steps = owners.shape[0]
     pairs = pair_local.shape[2]
-    n_clu, n_sta = lax.axis_size("clu"), lax.axis_size("sta")
+    n_clu, n_sta = lax.axis_size(CLU), lax.axis_size(STA)
     share = pairs // n_sta
     block = ev // steps
     left_table, right_table, back_table = (jnp.asarray(t) for t in tables())
@@ -273,36 +289,41 @@
     f32, bf16 = jnp.float32, jnp.bfloat16
     shaped = jax.ShapeDtypeStruct
 
-    me = lax.axis_index("clu")
+    me = lax.axis_index(CLU)
     row, step = me // 4, me % 4
-    near = lambda v, d: v if d == 0 else lax.ppermute(v, "clu", [(i, i ^ d) for i in range(n_clu)])
-    turn = lambda v, d: lax.ppermute(v, "clu", [(i, (i + 4 * d) % n_clu) for i in range(n_clu)])
+    near = lambda v, d: v if d == 0 else lax.ppermute(v, CLU, [(i, i ^ d) for i in range(n_clu)])
+    turn = lambda v, d: lax.ppermute(v, CLU, [(i, (i + 4 * d) % n_clu) for i in range(n_clu)])
 
     quarter = ch * ev // 4
     piece = shaped((quarter, samp), bf16)
     height = ch * block + 16
     payload = shaped((height, samp), bf16)
-    *parts, own, core, chip = pl.pallas_call(
-        pack_kernel, out_shape=(piece,) * 4 + (payload, payload, shaped((2, height, samp), bf16)),
-        in_specs=[pl.BlockSpec(memory_space=pl.ANY)] * 2 + [VMEM] * 2, out_specs=(VMEM,) * 7,
-        scratch_shapes=[pltpu.SemaphoreType.DMA((4 + 4 * ch,))], compiler_params=SMALL, name="pack",
-    )(cube, rows, pair_local[0], pair_remote[0])
+    parts = pl.pallas_call(
+        cut_kernel, out_shape=(piece,) * 4, in_specs=[HBM], out_specs=(VMEM,) * 4,
+        scratch_shapes=[pltpu.SemaphoreType.DMA((4,))], compiler_params=SMALL, name="cut",
+    )(in_hbm(rows))
+    own, core, chip = pl.pallas_call(
+        pack_kernel, out_shape=(payload, payload, shaped((2, height, samp), bf16)),
+        in_specs=[ANY] + [HBM] * 3, out_specs=(VMEM,) * 3,
+        scratch_shapes=[pltpu.VMEM((2, steps, pairs), jnp.int32), pltpu.SemaphoreType.DMA((2 + 4 * ch,))],
+        compiler_params=SMALL, name="pack",
+    )(parts[0], in_hbm(cube), in_hbm(pair_local), in_hbm(pair_remote))
     chip = near(chip, 2)
     blocks = [own, near(core, 1), chip[0], near(chip[1], 1)]
     got = [part if d == 0 else turn(part, d) for d, part in enumerate(parts)]
     give = pl.pallas_call(
-        pick_kernel, out_shape=shaped((2, quarter, samp), bf16), in_specs=[SMEM] + [VMEM] * 4, out_specs=VMEM,
+        pick_kernel, out_shape=shaped((2, quarter, samp), bf16), in_specs=[SMEM] + [VMEM] * 4 + [ANY], out_specs=VMEM,
         compiler_params=SMALL, name="pick",
-    )(owners, *got)
+    )(in_hbm(owners), *got, own)
     mine, theirs = pl.pallas_call(
         core_kernel, out_shape=(piece, piece),
-        in_specs=[SMEM] + [VMEM] * 5 + [pl.BlockSpec(memory_space=pl.ANY)], out_specs=(VMEM,) * 2,
+        in_specs=[SMEM] + [VMEM] * 5 + [ANY], out_specs=(VMEM,) * 2,
         compiler_params=SMALL, name="over_core",
-    )(owners, *got, near(give, 1), chip)
+    )(in_hbm(owners), *got, near(give, 1), chip)
     mine = pl.pallas_call(
         chip_kernel, out_shape=piece, in_specs=[SMEM] + [VMEM] * 2, out_specs=VMEM,
         compiler_params=SMALL, name="over_x",
-    )(owners, mine, near(theirs, 2))
+    )(in_hbm(owners), mine, near(theirs, 2))
     pieces = [mine] + [turn(mine, d) for d in (1, -1, 2)]
 
     listed = jnp.stack([b[ch * block:ch * block + 2 * pairs // samp] for b in blocks]).astype(jnp.int32)
@@ -332,33 +353,28 @@
             compiler_params=PARAMS, name="pairs", cost_estimate=cost,
         )(token, first, second, left, right, back_table)
         halves.append(raw)
-    hop = lambda v, dz, dh: lax.ppermute(v, "sta", [(k, target(k, dz, dh, n_sta)) for k in range(n_sta)])
-    sums = pl.pallas_call(
-        add_kernel, out_shape=(shaped((ROWS, 4 * share), f32),) * 4,
-        in_specs=[VMEM] * 2, out_specs=(VMEM,) * 4, compiler_params=SMALL, name="add",
+    hop = lambda v, dz, dh: lax.ppermute(v, STA, [(k, target(k, dz, dh, n_sta)) for k in range(n_sta)])
+    slots = pl.pallas_call(
+        add_kernel, out_shape=shaped((2 * n_sta, TALL, 2 * share), f32), in_specs=[VMEM] * 2, out_specs=VMEM,
+        compiler_params=SMALL, name="add",
     )(hop(halves[0], 0, 1), halves[1])
-    received = [v if dz == 0 else hop(v, dz, 0) for dz, v in zip(MOVES, sums)]
-
-    done = pl.pallas_call(
-        sum_kernel, out_shape=(shaped((ROWS, share), f32),) * 4,
-        in_specs=[VMEM] * len(received), out_specs=(VMEM,) * 4, compiler_params=SMALL, name="total",
-    )(*received)
-    done = [near(v, d) for d, v in enumerate(done)]
+    slots = lax.all_to_all(slots, ("z", "xl", "core"), 0, 0)
     out = pl.pallas_call(
         final_kernel, out_shape=shaped((1, steps, share, LAGS), f32),
-        in_specs=[SMEM] + [VMEM] * 4, out_specs=VMEM, compiler_params=SMALL, name="finish",
-    )(neighbours, *done)
+        in_specs=[SMEM, VMEM], out_specs=VMEM, compiler_params=SMALL, name="finish",
+    )(in_hbm(neighbours), slots)
     return out.transpose(0, 1, 3, 2)
 
 
 def solution(mesh):
+    fine = jax.sharding.Mesh(mesh.devices.reshape(4, 2, 2, 4, 2), CLU + STA)
     placed = (
-        P("clu", "sta", None),
+        P(CLU, STA, None),
         P(),
-        P("clu", None),
-        P("clu", None, None),
-        P("clu", None, None),
+        P(CLU, None),
+        P(CLU, None, None),
+        P(CLU, None, None),
     )
     return jax.shard_map(
-        local, mesh=mesh, in_specs=placed, out_specs=P("clu", None, None, "sta"), check_vma=False
+        local, mesh=fine, in_specs=placed, out_specs=P(CLU, None, None, STA), check_vma=False
     )

time: 76.6 us -> 73.5 us (0.960)
  blocking collectives: 0 us -> 14 us
  starting transfers between devices: 25.5 us -> 16.3 us
  waiting for transfers between devices: 26.2 us -> 21.3 us
  local copies, waits for them, and re-layouts: 3.4 us -> 0.2 us
  Pallas kernels: 20 us -> 20.8 us
    all_to_all x0 -> x1, blocking collectives: none -> 14 us  [local(): slots = lax.all_to_all(slots, ('z', 'xl', 'core'), 0, 0)]
    ppermute x18 -> x12, starting transfers between devices: 25.5 us -> 16.3 us  [the longest x6 10.5 us: local(): lax.ppermute(v, CLU, [(i, (i + 4 * d) % n_clu) for i in range(n_clu)])]
    ppermute x18 -> x12, waiting for transfers between devices: 26.2 us -> 21.3 us  [the longest x6 13.5 us: local(): lax.ppermute(v, CLU, [(i, (i + 4 * d) % n_clu) for i in range(n_clu)])]
    unnamed x20 -> x10, local copies, waits for them, and re-layouts: 3.3 us -> 0.1 us
  transfers between devices with their start and end apart: 18 -> 12, of which waited for: 10 -> 8; matrix products, arithmetic and copies ran while one was open for 0% -> 0% of each run, Pallas kernels for 11% -> 12%
where the time goes in v7:
time: 73.5 us; the launch traced here: 72.9 us
  waiting for transfers between devices  21.3 us (29%)
  Pallas kernels  20.8 us (28%)
  starting transfers between devices  16.3 us (22%)
  blocking collectives  14 us (19%)
    all_to_all x1, blocking collectives, local(): slots = lax.all_to_all(slots, ('z', 'xl', 'core'), 0, 0)  14 us
    ppermute x6, waiting for transfers between devices, local(): lax.ppermute(v, CLU, [(i, (i + 4 * d) % n_clu) for i in range(n_clu)])  13.5 us
    pallas_call x2, Pallas kernels, local(): pl.pallas_call(functools.partial(pair_kernel, across), out_shape=(shaped(...  12 us
    ppermute x6, starting transfers between devices, local(): lax.ppermute(v, CLU, [(i, (i + 4 * d) % n_clu) for i in range(n_clu)])  10.5 us
    ppermute x5, waiting for transfers between devices, local(): lax.ppermute(v, CLU, [(i, i ^ d) for i in range(n_clu)])  7.19 us
    ppermute x5, starting transfers between devices, local(): lax.ppermute(v, CLU, [(i, i ^ d) for i in range(n_clu)])  3.02 us
    ppermute x1, starting transfers between devices, local(): lax.ppermute(v, STA, [(k, target(k, dz, dh, n_sta)) for k in range(n_sta)])  2.82 us
    pallas_call x1, Pallas kernels, local(): pl.pallas_call(final_kernel, out_shape=shaped((1, steps, share, LAGS), f3...  1.52 us
  transfers between devices with their start and end apart: 12, of which 8 were waited for; matrix products, arithmetic and copies ran while one was open for 0% of the time, Pallas kernels for 12%

profile of v7, /device:TPU:0, one launch (start us, length us, event | category | flops | bytes accessed | tf_op | source)
XLA Modules:
  0.0 72.9 jit_solution(7615417163976095520)
XLA Ops:
  0.0 1.3 %cut.1 = (bf16[384,256]{1,0:T(8,128)(2,1)S(1)}, bf16[384,256]{1,0:T(8,128)(2,1)S(1)}, bf16[384,256]{1,0:T(8,128)(2,1)S(1)}, bf16[384,256]{1,0:T(8,128)(2,1)S(1)}) custom-call(bf16[1536,256]{1,0:T(8,128)(2,1)} %bitcast.15), custom_call_target="tpu_custom_call" | custom-call | tf_op jit(solution)/shard_map/cut/pallas_call | solution.py:301
  1.3 1.3 %pack.1 = (bf16[400,256]{1,0:T(8,128)(2,1)S(1)}, bf16[400,256]{1,0:T(8,128)(2,1)S(1)}, bf16[2,400,256]{2,1,0:T(8,128)(2,1)S(1)}) custom-call(bf16[384,256]{1,0:T(8,128)(2,1)S(1)} %get-tuple-element.17._.g0, bf16[6,256,256]{2,1,0:T(8,128)(2,1)} %bitcast.16, s32[1,4,512]{2,1,0:T(4,128)} %local_ref.1, s32[1,4,512]{2,1,0:T(4,128)} %remote_ref.1), custom_call_target="tpu_custom_call" | custom-call | tf_op jit(solution)/shard_map/pack/pallas_call | solution.py:305
  2.7 1.7 %collective-permute-start.1 = (bf16[2,400,256]{2,1,0:T(8,128)(2,1)S(1)}, bf16[2,400,256]{2,1,0:T(8,128)(2,1)S(1)}, u32[]{:S(2)}, u32[]{:S(2)}) collective-permute-start(bf16[2,400,256]{2,1,0:T(8,128)(2,1)S(1)} %get-tuple-element.20), channel_id=1, source_target_pairs={{0,16},{8,24},{16,0},{24,8},{32,48},{40,56},{48,32},{56,40},{64,80... | collective-permute-start | bytes 1228808 | tf_op jit(solution)/shard_map/ppermute | solution.py:294
  4.3 1.6 %collective-permute-start.3 = (bf16[384,256]{1,0:T(8,128)(2,1)S(1)}, bf16[384,256]{1,0:T(8,128)(2,1)S(1)}, u32[]{:S(2)}, u32[]{:S(2)}) collective-permute-start(bf16[384,256]{1,0:T(8,128)(2,1)S(1)} %get-tuple-element.21), channel_id=1, source_target_pairs={{0,32},{8,40},{16,48},{24,56},{32,64},{40,72},{48,80},{56,88},{64,... | collective-permute-start | bytes 589832 | tf_op jit(solution)/shard_map/ppermute | solution.py:295
  5.9 2.9 %collective-permute-start.4 = (bf16[384,256]{1,0:T(8,128)(2,1)S(1)}, bf16[384,256]{1,0:T(8,128)(2,1)S(1)}, u32[]{:S(2)}, u32[]{:S(2)}) collective-permute-start(bf16[384,256]{1,0:T(8,128)(2,1)S(1)} %get-tuple-element.22), channel_id=1, source_target_pairs={{0,64},{8,72},{16,80},{24,88},{32,96},{40,104},{48,112},{56,120},{... | collective-permute-start | bytes 589832 | tf_op jit(solution)/shard_map/ppermute | solution.py:295
  8.8 1.3 %collective-permute-start.5 = (bf16[384,256]{1,0:T(8,128)(2,1)S(1)}, bf16[384,256]{1,0:T(8,128)(2,1)S(1)}, u32[]{:S(2)}, u32[]{:S(2)}) collective-permute-start(bf16[384,256]{1,0:T(8,128)(2,1)S(1)} %get-tuple-element.23), channel_id=1, source_target_pairs={{0,96},{8,104},{16,112},{24,120},{32,0},{40,8},{48,16},{56,24},{64... | collective-permute-start | bytes 589832 | tf_op jit(solution)/shard_map/ppermute | solution.py:295
  10.1 2.1 %collective-permute-done.3.g1 = bf16[384,256]{1,0:T(8,128)(2,1)S(1)} collective-permute-done((bf16[384,256]{1,0:T(8,128)(2,1)S(1)}, bf16[384,256]{1,0:T(8,128)(2,1)S(1)}, u32[]{:S(2)}, u32[]{:S(2)}) %collective-permute-start.3) | collective-permute-done | bytes 196640 | tf_op jit(solution)/shard_map/ppermute | solution.py:295
  12.2 5.1 %collective-permute-done.4.g2 = bf16[384,256]{1,0:T(8,128)(2,1)S(1)} collective-permute-done((bf16[384,256]{1,0:T(8,128)(2,1)S(1)}, bf16[384,256]{1,0:T(8,128)(2,1)S(1)}, u32[]{:S(2)}, u32[]{:S(2)}) %collective-permute-start.4) | collective-permute-done | bytes 196640 | tf_op jit(solution)/shard_map/ppermute | solution.py:295
  18.9 1.0 %collective-permute-done.6.got_ref = bf16[2,384,256]{2,1,0:T(8,128)(2,1)S(1)} collective-permute-done((bf16[2,384,256]{2,1,0:T(8,128)(2,1)S(1)}, bf16[2,384,256]{2,1,0:T(8,128)(2,1)S(1)}, u32[]{:S(2)}, u32[]{:S(2)}) %collective-permute-start.6) | collective-permute-done | bytes 393248 | tf_op jit(solution)/shard_map/ppermute | solution.py:294
  19.9 0.8 %over_core.1 = (bf16[384,256]{1,0:T(8,128)(2,1)S(1)}, bf16[384,256]{1,0:T(8,128)(2,1)S(1)}) custom-call(s32[4]{0:T(128)} %token_ref.1, bf16[384,256]{1,0:T(8,128)(2,1)S(1)} %get-tuple-element.17._.g0, bf16[384,256]{1,0:T(8,128)(2,1)S(1)} %collective-permute-done.3.g1, bf16[384,256]{1,0:T(8,128)(2,1)S(1)} %collective-permute-done.4.g2, ...), custom_call_target="tpu_custom_call" | custom-call | tf_op jit(solution)/shard_map/over_core/pallas_call | solution.py:318
  21.5 6.2 %collective-permute-done.7.got_ref = bf16[384,256]{1,0:T(8,128)(2,1)S(1)} collective-permute-done((bf16[384,256]{1,0:T(8,128)(2,1)S(1)}, bf16[384,256]{1,0:T(8,128)(2,1)S(1)}, u32[]{:S(2)}, u32[]{:S(2)}) %collective-permute-start.7) | collective-permute-done | bytes 196640 | tf_op jit(solution)/shard_map/ppermute | solution.py:294
  28.4 2.7 %collective-permute-start.10 = (bf16[384,256]{1,0:T(8,128)(2,1)S(1)}, bf16[384,256]{1,0:T(8,128)(2,1)S(1)}, u32[]{:S(2)}, u32[]{:S(2)}) collective-permute-start(bf16[384,256]{1,0:T(8,128)(2,1)S(1)} %over_x.1.p0), channel_id=1, source_target_pairs={{0,64},{8,72},{16,80},{24,88},{32,96},{40,104},{48,112},{56,120},{... | collective-permute-start | bytes 589832 | tf_op jit(solution)/shard_map/ppermute | solution.py:295
  31.0 1.2 %collective-permute-start.9 = (bf16[384,256]{1,0:T(8,128)(2,1)S(1)}, bf16[384,256]{1,0:T(8,128)(2,1)S(1)}, u32[]{:S(2)}, u32[]{:S(2)}) collective-permute-start(bf16[384,256]{1,0:T(8,128)(2,1)S(1)} %over_x.1.p0), channel_id=1, source_target_pairs={{0,96},{8,104},{16,112},{24,120},{32,0},{40,8},{48,16},{56,24},{64... | collective-permute-start | bytes 589832 | tf_op jit(solution)/shard_map/ppermute | solution.py:295
  32.3 0.8 %collective-permute-start.8 = (bf16[384,256]{1,0:T(8,128)(2,1)S(1)}, bf16[384,256]{1,0:T(8,128)(2,1)S(1)}, u32[]{:S(2)}, u32[]{:S(2)}) collective-permute-start(bf16[384,256]{1,0:T(8,128)(2,1)S(1)} %over_x.1.p0), channel_id=1, source_target_pairs={{0,32},{8,40},{16,48},{24,56},{32,64},{40,72},{48,80},{56,88},{64,... | collective-permute-start | bytes 589832 | tf_op jit(solution)/shard_map/ppermute | solution.py:295
  33.1 1.1 %left.1 = f32[6144,128]{1,0:T(8,128)S(1)} custom-call(bf16[256,768]{1,0:T(8,128)(2,1)S(1)} %copy-done.2, bf16[400,256]{1,0:T(8,128)(2,1)S(1)} %get-tuple-element.18.b0._, bf16[400,256]{1,0:T(8,128)(2,1)S(1)} %collective-permute-done.b1, bf16[400,256]{1,0:T(8,128)(2,1)S(1)} %get-tuple-element.29.b2, bf16[400,256]{1,0:T(8,128)(2,1)S(1)} %collective-permute-done.2.b3), custom_call_target="tpu_custom_call" | custom-call | flops 603979776 | bytes 4000000 | tf_op jit(solution)/shard_map/left/pallas_call | solution.py:336
  34.3 3.5 %collective-permute-done.10.p3 = bf16[384,256]{1,0:T(8,128)(2,1)S(1)} collective-permute-done((bf16[384,256]{1,0:T(8,128)(2,1)S(1)}, bf16[384,256]{1,0:T(8,128)(2,1)S(1)}, u32[]{:S(2)}, u32[]{:S(2)}) %collective-permute-start.10) | collective-permute-done | bytes 196640 | tf_op jit(solution)/shard_map/ppermute | solution.py:295
  37.8 1.9 %collective-permute-done.9.p2 = bf16[384,256]{1,0:T(8,128)(2,1)S(1)} collective-permute-done((bf16[384,256]{1,0:T(8,128)(2,1)S(1)}, bf16[384,256]{1,0:T(8,128)(2,1)S(1)}, u32[]{:S(2)}, u32[]{:S(2)}) %collective-permute-start.9) | collective-permute-done | bytes 196640 | tf_op jit(solution)/shard_map/ppermute | solution.py:295
  39.7 0.8 %collective-permute-done.8.p1 = bf16[384,256]{1,0:T(8,128)(2,1)S(1)} collective-permute-done((bf16[384,256]{1,0:T(8,128)(2,1)S(1)}, bf16[384,256]{1,0:T(8,128)(2,1)S(1)}, u32[]{:S(2)}, u32[]{:S(2)}) %collective-permute-start.8) | collective-permute-done | bytes 196640 | tf_op jit(solution)/shard_map/ppermute | solution.py:295
  40.5 1.2 %right.1 = f32[6144,128]{1,0:T(8,128)S(1)} custom-call(bf16[256,768]{1,0:T(8,128)(2,1)S(1)} %copy-done.1, bf16[384,256]{1,0:T(8,128)(2,1)S(1)} %over_x.1.p0, bf16[384,256]{1,0:T(8,128)(2,1)S(1)} %collective-permute-done.8.p1, bf16[384,256]{1,0:T(8,128)(2,1)S(1)} %collective-permute-done.9.p2, bf16[384,256]{1,0:T(8,128)(2,1)S(1)} %collective-permute-done.10.p3), custom_call_target="tpu_custom_call" | custom-call | flops 603979776 | bytes 4000000 | tf_op jit(solution)/shard_map/right/pallas_call | solution.py:340
  41.8 6.0 %pairs.2 = (f32[4,72,256]{2,1,0:T(8,128)S(1)}, s32[4]{0:T(128)S(1)}) custom-call(s32[4]{0:T(128)S(1)} %copy-done.3, s32[2048]{0:T(1024)S(1)} %add.14.local_ref, s32[2048]{0:T(1024)S(1)} %bitcast.13, f32[6144,128]{1,0:T(8,128)S(1)} %left.1, f32[6144,128]{1,0:T(8,128)S(1)} %right.1, bf16[144,384]{1,0:T(8,128)(2,1)S(1)} %copy-done), custom_call_target="tpu_custom_call" | custom-call | flops 603979776 | bytes 4000000 | tf_op jit(solution)/shard_map/pairs/pallas_call | solution.py:348
  47.8 2.8 %collective-permute-start.11 = (f32[4,72,256]{2,1,0:T(8,128)S(1)}, f32[4,72,256]{2,1,0:T(8,128)S(1)}, u32[]{:S(2)}, u32[]{:S(2)}) collective-permute-start(f32[4,72,256]{2,1,0:T(8,128)S(1)} %get-tuple-element.26), channel_id=1, source_target_pairs={{0,1},{1,0},{2,3},{3,2},{4,5},{5,4},{6,7},{7,6},{8,9},{9,8},{10,11... | collective-permute-start | bytes 884744 | tf_op jit(solution)/shard_map/ppermute | solution.py:356
  50.6 5.9 %pairs.3 = (f32[4,72,256]{2,1,0:T(8,128)S(1)}, s32[4]{0:T(128)}) custom-call(s32[4]{0:T(128)S(1)} %get-tuple-element.27.token_ref, s32[2048]{0:T(1024)S(1)} %add.14.local_ref, s32[2048]{0:T(1024)S(1)} %bitcast.14, f32[6144,128]{1,0:T(8,128)S(1)} %left.1, f32[6144,128]{1,0:T(8,128)S(1)} %right.1, bf16[144,384]{1,0:T(8,128)(2,1)S(1)} %copy-done), custom_call_target="tpu_custom_call" | custom-call | flops 603979776 | bytes 4000000 | tf_op jit(solution)/shard_map/pairs/pallas_call | solution.py:348
  57.4 14.0 %all_to_all.5.got_ref = f32[16,40,128]{2,1,0:T(8,128)S(1)} all-to-all(f32[16,40,128]{2,1,0:T(8,128)S(1)} %add.16), channel_id=1, replica_groups=mesh['y'=4,'xl'=2,'core'=2,'z'=4,'xh'=2] {'z','xl','core'}, dimensions={0} | all-to-all | bytes 655360 | tf_op jit(solution)/shard_map/all_to_all | solution.py:361
  71.4 1.5 %finish.1 = f32[1,4,64,65]{3,2,1,0:T(8,128)} custom-call(s32[1,4]{1,0:T(1,128)} %near_ref.1, f32[16,40,128]{2,1,0:T(8,128)S(1)} %all_to_all.5.got_ref), custom_call_target="tpu_custom_call" | custom-call | tf_op jit(solution)/shard_map/finish/pallas_call | solution.py:362
  (35 shorter events, 3.9 us)
Async XLA Ops:
  0.0 33.1 %copy-start.2 = (bf16[256,768]{1,0:T(8,128)(2,1)S(1)}, bf16[256,768]{1,0:T(8,128)(2,1)}, u32[]{:S(2)}) copy-start(bf16[256,768]{1,0:T(8,128)(2,1)} %constant.10.clone.table_ref) | copy-start | bytes 1179652
  2.7 16.0 %collective-permute-start.1 = (bf16[2,400,256]{2,1,0:T(8,128)(2,1)S(1)}, bf16[2,400,256]{2,1,0:T(8,128)(2,1)S(1)}, u32[]{:S(2)}, u32[]{:S(2)}) collective-permute-start(bf16[2,400,256]{2,1,0:T(8,128)(2,1)S(1)} %get-tuple-element.20), channel_id=1, source_target_pairs={{0,16},{8,24},{16,0},{24,8},{32,48},{40,56},{48,32},{56,40},{64,80... | collective-permute-start | bytes 1228808 | tf_op jit(solution)/shard_map/ppermute | solution.py:294
  4.3 7.9 %collective-permute-start.3 = (bf16[384,256]{1,0:T(8,128)(2,1)S(1)}, bf16[384,256]{1,0:T(8,128)(2,1)S(1)}, u32[]{:S(2)}, u32[]{:S(2)}) collective-permute-start(bf16[384,256]{1,0:T(8,128)(2,1)S(1)} %get-tuple-element.21), channel_id=1, source_target_pairs={{0,32},{8,40},{16,48},{24,56},{32,64},{40,72},{48,80},{56,88},{64,... | collective-permute-start | bytes 589832 | tf_op jit(solution)/shard_map/ppermute | solution.py:295
  5.9 11.4 %collective-permute-start.4 = (bf16[384,256]{1,0:T(8,128)(2,1)S(1)}, bf16[384,256]{1,0:T(8,128)(2,1)S(1)}, u32[]{:S(2)}, u32[]{:S(2)}) collective-permute-start(bf16[384,256]{1,0:T(8,128)(2,1)S(1)} %get-tuple-element.22), channel_id=1, source_target_pairs={{0,64},{8,72},{16,80},{24,88},{32,96},{40,104},{48,112},{56,120},{... | collective-permute-start | bytes 589832 | tf_op jit(solution)/shard_map/ppermute | solution.py:295
  8.8 8.6 %collective-permute-start.5 = (bf16[384,256]{1,0:T(8,128)(2,1)S(1)}, bf16[384,256]{1,0:T(8,128)(2,1)S(1)}, u32[]{:S(2)}, u32[]{:S(2)}) collective-permute-start(bf16[384,256]{1,0:T(8,128)(2,1)S(1)} %get-tuple-element.23), channel_id=1, source_target_pairs={{0,96},{8,104},{16,112},{24,120},{32,0},{40,8},{48,16},{56,24},{64... | collective-permute-start | bytes 589832 | tf_op jit(solution)/shard_map/ppermute | solution.py:295
  18.1 1.8 %collective-permute-start.6 = (bf16[2,384,256]{2,1,0:T(8,128)(2,1)S(1)}, bf16[2,384,256]{2,1,0:T(8,128)(2,1)S(1)}, u32[]{:S(2)}, u32[]{:S(2)}) collective-permute-start(bf16[2,384,256]{2,1,0:T(8,128)(2,1)S(1)} %pick.1), channel_id=1, source_target_pairs={{0,8},{8,0},{16,24},{24,16},{32,40},{40,32},{48,56},{56,48},{64,72... | collective-permute-start | bytes 1179656 | tf_op jit(solution)/shard_map/ppermute | solution.py:294
  18.2 3.2 %collective-permute-start = (bf16[400,256]{1,0:T(8,128)(2,1)S(1)}, bf16[400,256]{1,0:T(8,128)(2,1)S(1)}, u32[]{:S(2)}, u32[]{:S(2)}) collective-permute-start(bf16[400,256]{1,0:T(8,128)(2,1)S(1)} %get-tuple-element.19), channel_id=1, source_target_pairs={{0,8},{8,0},{16,24},{24,16},{32,40},{40,32},{48,56},{56,48},{64,72... | collective-permute-start | bytes 614408 | tf_op jit(solution)/shard_map/ppermute | solution.py:294
  18.7 21.8 %copy-start.1 = (bf16[256,768]{1,0:T(8,128)(2,1)S(1)}, bf16[256,768]{1,0:T(8,128)(2,1)}, u32[]{:S(2)}) copy-start(bf16[256,768]{1,0:T(8,128)(2,1)} %constant.11.clone.table_ref) | copy-start | bytes 1179652
  18.7 2.7 %collective-permute-start.2 = (bf16[400,256]{1,0:T(8,128)(2,1)S(1)}, bf16[400,256]{1,0:T(8,128)(2,1)S(1)}, u32[]{:S(2)}, u32[]{:S(2)}) collective-permute-start(bf16[400,256]{1,0:T(8,128)(2,1)S(1)} %get-tuple-element.30), channel_id=1, source_target_pairs={{0,8},{8,0},{16,24},{24,16},{32,40},{40,32},{48,56},{56,48},{64,72... | collective-permute-start | bytes 614408 | tf_op jit(solution)/shard_map/ppermute | solution.py:294
  20.7 7.0 %collective-permute-start.7 = (bf16[384,256]{1,0:T(8,128)(2,1)S(1)}, bf16[384,256]{1,0:T(8,128)(2,1)S(1)}, u32[]{:S(2)}, u32[]{:S(2)}) collective-permute-start(bf16[384,256]{1,0:T(8,128)(2,1)S(1)} %get-tuple-element.25), channel_id=1, source_target_pairs={{0,16},{8,24},{16,0},{24,8},{32,48},{40,56},{48,32},{56,40},{64,80... | collective-permute-start | bytes 589832 | tf_op jit(solution)/shard_map/ppermute | solution.py:294
  28.4 9.4 %collective-permute-start.10 = (bf16[384,256]{1,0:T(8,128)(2,1)S(1)}, bf16[384,256]{1,0:T(8,128)(2,1)S(1)}, u32[]{:S(2)}, u32[]{:S(2)}) collective-permute-start(bf16[384,256]{1,0:T(8,128)(2,1)S(1)} %over_x.1.p0), channel_id=1, source_target_pairs={{0,64},{8,72},{16,80},{24,88},{32,96},{40,104},{48,112},{56,120},{... | collective-permute-start | bytes 589832 | tf_op jit(solution)/shard_map/ppermute | solution.py:295
  31.0 8.7 %collective-permute-start.9 = (bf16[384,256]{1,0:T(8,128)(2,1)S(1)}, bf16[384,256]{1,0:T(8,128)(2,1)S(1)}, u32[]{:S(2)}, u32[]{:S(2)}) collective-permute-start(bf16[384,256]{1,0:T(8,128)(2,1)S(1)} %over_x.1.p0), channel_id=1, source_target_pairs={{0,96},{8,104},{16,112},{24,120},{32,0},{40,8},{48,16},{56,24},{64... | collective-permute-start | bytes 589832 | tf_op jit(solution)/shard_map/ppermute | solution.py:295
  32.3 8.3 %collective-permute-start.8 = (bf16[384,256]{1,0:T(8,128)(2,1)S(1)}, bf16[384,256]{1,0:T(8,128)(2,1)S(1)}, u32[]{:S(2)}, u32[]{:S(2)}) collective-permute-start(bf16[384,256]{1,0:T(8,128)(2,1)S(1)} %over_x.1.p0), channel_id=1, source_target_pairs={{0,32},{8,40},{16,48},{24,56},{32,64},{40,72},{48,80},{56,88},{64,... | collective-permute-start | bytes 589832 | tf_op jit(solution)/shard_map/ppermute | solution.py:295
  34.2 7.5 %copy-start = (bf16[144,384]{1,0:T(8,128)(2,1)S(1)}, bf16[144,384]{1,0:T(8,128)(2,1)}, u32[]{:S(2)}) copy-start(bf16[144,384]{1,0:T(8,128)(2,1)} %constant.12.clone.back_ref) | copy-start | bytes 331780
  34.3 7.5 %copy-start.3 = (s32[4]{0:T(128)S(1)}, s32[4]{0:T(128)}, u32[]{:S(2)}) copy-start(s32[4]{0:T(128)} %token_ref.1) | copy-start | bytes 52
  47.8 9.4 %collective-permute-start.11 = (f32[4,72,256]{2,1,0:T(8,128)S(1)}, f32[4,72,256]{2,1,0:T(8,128)S(1)}, u32[]{:S(2)}, u32[]{:S(2)}) collective-permute-start(f32[4,72,256]{2,1,0:T(8,128)S(1)} %get-tuple-element.26), channel_id=1, source_target_pairs={{0,1},{1,0},{2,3},{3,2},{4,5},{5,4},{6,7},{7,6},{8,9},{9,8},{10,11... | collective-permute-start | bytes 884744 | tf_op jit(solution)/shard_map/ppermute | solution.py:356

commit v8 on v7

--- a/solution.py
+++ b/solution.py
@@ -64,34 +64,26 @@
     return lax.axis_index("y"), x * 2 + core, x, core
 
 
-def cut_kernel(rows_ref, *refs):
-    outs, sems = refs[:-1], refs[-1]
-    row = place()[0]
-    size = outs[0].shape[0]
-    copies = [
-        pltpu.make_async_copy(rows_ref.at[pl.ds(pl.multiple_of(((row + d) & 3) * size, size), size)], out, sems.at[d])
-        for d, out in enumerate(outs)
+def pack_kernel(rows_ref, cube_ref, local_ref, remote_ref, *refs):
+    parts, (own_ref, core_ref, chip_ref, lists_ref, sems) = refs[:4], refs[4:]
+    row, step, _, _ = place()
+    quarter = parts[0].shape[0]
+    cuts = [
+        pltpu.make_async_copy(rows_ref.at[pl.ds(pl.multiple_of(((row + d) & 3) * quarter, quarter), quarter)], out, sems.at[d])
+        for d, out in enumerate(parts)
     ]
-    for copy in copies:
-        copy.start()
-    for copy in copies:
-        copy.wait()
-
-
-def pack_kernel(_, cube_ref, local_ref, remote_ref, own_ref, core_ref, chip_ref, lists_ref, sems):
-    step = place()[1]
     channels, _, width = cube_ref.shape
     size = cube_ref.shape[1] // 4
     outs = (own_ref, core_ref, chip_ref.at[0], chip_ref.at[1])
-    first = [pltpu.make_async_copy(ref.at[0], lists_ref.at[n], sems.at[n]) for n, ref in enumerate((local_ref, remote_ref))]
+    first = [pltpu.make_async_copy(ref.at[0], lists_ref.at[n], sems.at[4 + n]) for n, ref in enumerate((local_ref, remote_ref))]
     copies = []
     for d, out in enumerate(outs):
         at = pl.multiple_of((step ^ d) * size, size)
         for c in range(channels):
             copies.append(pltpu.make_async_copy(
-                cube_ref.at[c, pl.ds(at, size)], out.at[pl.ds(c * size, size)], sems.at[2 + d * channels + c]
+                cube_ref.at[c, pl.ds(at, size)], out.at[pl.ds(c * size, size)], sems.at[6 + d * channels + c]
             ))
-    for copy in first + copies:
+    for copy in first + cuts + copies:
         copy.start()
     for copy in first:
         copy.wait()
@@ -104,11 +96,11 @@
             for k in range(per):
                 lists = jnp.where(line == n * per + k, listed[:, k * width:(k + 1) * width], lists)
         out[pl.ds(channels * size, 16), :] = lists.astype(jnp.bfloat16)
-    for copy in copies:
+    for copy in cuts + copies:
         copy.wait()
 
 
-def pick_kernel(owners_ref, g0, g1, g2, g3, _, give_ref):
+def pick_kernel(owners_ref, g0, g1, g2, g3, give_ref):
     row, step, _, _ = place()
     for d in (1, 3):
         behind = (row + 4 - (owners_ref[step ^ d] >> 2)) & 3
@@ -188,10 +180,11 @@
     for shift in (4, 2, 1):
         keep = (sub & shift) == 0
         half = len(vs) // 2
-        vs = [
-            jnp.where(keep, a + pltpu.roll(a, 8 - shift, 0), b + pltpu.roll(b, shift, 0))
-            for a, b in zip(vs[:half], vs[half:])
-        ]
+        couples = list(zip(vs[:half], vs[half:]))
+        if shift == 4:
+            vs = [jnp.where(keep, a, b) + pltpu.roll(jnp.where(keep, b, a), 4, 0) for a, b in couples]
+        else:
+            vs = [jnp.where(keep, a + pltpu.roll(a, 8 - shift, 0), b + pltpu.roll(b, shift, 0)) for a, b in couples]
     return vs[0]
 
 
@@ -209,7 +202,7 @@
     sta = lax.axis_index(STA)
     share = width // 4
     pairs = local_ref.shape[0] // 4
-    bh, bl = back_ref[:ROWS], back_ref[ROWS:]
+    back = back_ref[...]
     contract = (((1,), (1,)), ((), ()))
     dot = lambda a, b: lax.dot_general(a, b, contract, preferred_element_type=jnp.float32)
     sub = lax.broadcasted_iota(jnp.int32, (8, 128), 0)
@@ -217,8 +210,9 @@
         first = target(sta, MOVES[t], across, 2 * half) * share
 
         def body(it, carry):
-            for part in range(4):
-                g = it * 4 + part
+            sums = []
+            for part in range(8):
+                g = it * 8 + part
                 q = g >> 3
                 at = q * pairs + first + (g & 7) * 8
                 products = [[], [], []]
@@ -229,16 +223,17 @@
                     ya, yb, yc = right[pl.ds(j, 8)], right[pl.ds(j + 8, 8)], right[pl.ds(j + 16, 8)]
                     for col, v in enumerate((xa * ya + xb * yb, xb * ya - xa * yb, xc * yc)):
                         products[col].append(v)
-                to = pl.multiple_of(g * 8, 8)
-                for col in range(3):
-                    z[pl.ds(to, 8), col * 128:col * 128 + 128] = channel_sum(products[col], sub)
+                sums += [(g, col, channel_sum(products[col], sub)) for col in range(3)]
+            for g, col, v in sums:
+                z[pl.ds(pl.multiple_of(g * 8, 8), 8), col * 128:col * 128 + 128] = v
             return carry
 
-        lax.fori_loop(0, width // 32, body, 0)
+        lax.fori_loop(0, width // 64, body, 0)
         zk = z[...]
         zh = zk.astype(jnp.bfloat16)
         zl = (zk - zh.astype(jnp.float32)).astype(jnp.bfloat16)
-        out_ref[t] = dot(bh, zh) + dot(bh, zl) + dot(bl, zh)
+        high = dot(back, zh)
+        out_ref[t] = high[:ROWS] + high[ROWS:] + dot(back[:ROWS], zl)
 
 
 def add_kernel(a_ref, b_ref, out_ref):
@@ -298,23 +293,19 @@
     piece = shaped((quarter, samp), bf16)
     height = ch * block + 16
     payload = shaped((height, samp), bf16)
-    parts = pl.pallas_call(
-        cut_kernel, out_shape=(piece,) * 4, in_specs=[HBM], out_specs=(VMEM,) * 4,
-        scratch_shapes=[pltpu.SemaphoreType.DMA((4,))], compiler_params=SMALL, name="cut",
-    )(in_hbm(rows))
-    own, core, chip = pl.pallas_call(
-        pack_kernel, out_shape=(payload, payload, shaped((2, height, samp), bf16)),
-        in_specs=[ANY] + [HBM] * 3, out_specs=(VMEM,) * 3,
-        scratch_shapes=[pltpu.VMEM((2, steps, pairs), jnp.int32), pltpu.SemaphoreType.DMA((2 + 4 * ch,))],
+    *parts, own, core, chip = pl.pallas_call(
+        pack_kernel, out_shape=(piece,) * 4 + (payload, payload, shaped((2, height, samp), bf16)),
+        in_specs=[HBM] * 4, out_specs=(VMEM,) * 7,
+        scratch_shapes=[pltpu.VMEM((2, steps, pairs), jnp.int32), pltpu.SemaphoreType.DMA((6 + 4 * ch,))],
         compiler_params=SMALL, name="pack",
-    )(parts[0], in_hbm(cube), in_hbm(pair_local), in_hbm(pair_remote))
+    )(in_hbm(rows), in_hbm(cube), in_hbm(pair_local), in_hbm(pair_remote))
     chip = near(chip, 2)
     blocks = [own, near(core, 1), chip[0], near(chip[1], 1)]
     got = [part if d == 0 else turn(part, d) for d, part in enumerate(parts)]
     give = pl.pallas_call(
-        pick_kernel, out_shape=shaped((2, quarter, samp), bf16), in_specs=[SMEM] + [VMEM] * 4 + [ANY], out_specs=VMEM,
+        pick_kernel, out_shape=shaped((2, quarter, samp), bf16), in_specs=[SMEM] + [VMEM] * 4, out_specs=VMEM,
         compiler_params=SMALL, name="pick",
-    )(in_hbm(owners), *got, own)
+    )(in_hbm(owners), *got)
     mine, theirs = pl.pallas_call(
         core_kernel, out_shape=(piece, piece),
         in_specs=[SMEM] + [VMEM] * 5 + [ANY], out_specs=(VMEM,) * 2,

time: 73.5 us -> 71.7 us (0.976)
  Pallas kernels: 20.8 us -> 18.2 us
  waiting for transfers between devices: 21.3 us -> 22.1 us
    pallas_call x2, Pallas kernels: 12 us -> 10.3 us  [local(): pl.pallas_call(functools.partial(pair_kernel, across), out_shape=(shaped(...]
    pallas_call x2 -> x1, Pallas kernels: 2.64 us -> 1.72 us  [local(): pl.pallas_call(pack_kernel, out_shape=(piece,) * 4 + (payload, payload, s...]
    ppermute x1, waiting for transfers between devices: 0.67 us -> 1.5 us  [local(): lax.ppermute(v, STA, [(k, target(k, dz, dh, n_sta)) for k in range(n_sta)])]
  transfers between devices with their start and end apart: 12 -> 12, of which waited for: 8 -> 8; matrix products, arithmetic and copies ran while one was open for 0% -> 0% of each run, Pallas kernels for 12% -> 11%
where the time goes in v8:
time: 71.7 us; the launch traced here: 71.1 us
  waiting for transfers between devices  22.1 us (31%)
  Pallas kernels  18.2 us (25%)
  starting transfers between devices  16.3 us (23%)
  blocking collectives  14 us (20%)
    all_to_all x1, blocking collectives, local(): slots = lax.all_to_all(slots, ('z', 'xl', 'core'), 0, 0)  14 us
    ppermute x6, waiting for transfers between devices, local(): lax.ppermute(v, CLU, [(i, (i + 4 * d) % n_clu) for i in range(n_clu)])  13.5 us
    ppermute x6, starting transfers between devices, local(): lax.ppermute(v, CLU, [(i, (i + 4 * d) % n_clu) for i in range(n_clu)])  10.5 us
    pallas_call x2, Pallas kernels, local(): pl.pallas_call(functools.partial(pair_kernel, across), out_shape=(shaped(...  10.3 us
    ppermute x5, waiting for transfers between devices, local(): lax.ppermute(v, CLU, [(i, i ^ d) for i in range(n_clu)])  7.18 us
    ppermute x5, starting transfers between devices, local(): lax.ppermute(v, CLU, [(i, i ^ d) for i in range(n_clu)])  3.04 us
    ppermute x1, starting transfers between devices, local(): lax.ppermute(v, STA, [(k, target(k, dz, dh, n_sta)) for k in range(n_sta)])  2.82 us
    pallas_call x1, Pallas kernels, local(): pl.pallas_call(pack_kernel, out_shape=(piece,) * 4 + (payload, payload, s...  1.72 us
  transfers between devices with their start and end apart: 12, of which 8 were waited for; matrix products, arithmetic and copies ran while one was open for 0% of the time, Pallas kernels for 11%

profile of v8, /device:TPU:0, one launch (start us, length us, event | category | flops | bytes accessed | tf_op | source)
XLA Modules:
  0.0 71.1 jit_solution(5303604272819633169)
XLA Ops:
  0.0 1.7 %pack.1 = (bf16[384,256]{1,0:T(8,128)(2,1)S(1)}, bf16[384,256]{1,0:T(8,128)(2,1)S(1)}, bf16[384,256]{1,0:T(8,128)(2,1)S(1)}, bf16[384,256]{1,0:T(8,128)(2,1)S(1)...) custom-call(bf16[1536,256]{1,0:T(8,128)(2,1)} %bitcast.15, ...), custom_call_target="tpu_custom_call" | custom-call | tf_op jit(solution)/shard_map/pack/pallas_call | solution.py:296
  1.7 1.7 %collective-permute-start.1 = (bf16[2,400,256]{2,1,0:T(8,128)(2,1)S(1)}, bf16[2,400,256]{2,1,0:T(8,128)(2,1)S(1)}, u32[]{:S(2)}, u32[]{:S(2)}) collective-permute-start(bf16[2,400,256]{2,1,0:T(8,128)(2,1)S(1)} %get-tuple-element.19), channel_id=1, source_target_pairs={{0,16},{8,24},{16,0},{24,8},{32,48},{40,56},{48,32},{56,40},{64,80... | collective-permute-start | bytes 1228808 | tf_op jit(solution)/shard_map/ppermute | solution.py:289
  3.4 1.6 %collective-permute-start.3 = (bf16[384,256]{1,0:T(8,128)(2,1)S(1)}, bf16[384,256]{1,0:T(8,128)(2,1)S(1)}, u32[]{:S(2)}, u32[]{:S(2)}) collective-permute-start(bf16[384,256]{1,0:T(8,128)(2,1)S(1)} %get-tuple-element.21), channel_id=1, source_target_pairs={{0,32},{8,40},{16,48},{24,56},{32,64},{40,72},{48,80},{56,88},{64,... | collective-permute-start | bytes 589832 | tf_op jit(solution)/shard_map/ppermute | solution.py:290
  5.0 2.9 %collective-permute-start.4 = (bf16[384,256]{1,0:T(8,128)(2,1)S(1)}, bf16[384,256]{1,0:T(8,128)(2,1)S(1)}, u32[]{:S(2)}, u32[]{:S(2)}) collective-permute-start(bf16[384,256]{1,0:T(8,128)(2,1)S(1)} %get-tuple-element.22), channel_id=1, source_target_pairs={{0,64},{8,72},{16,80},{24,88},{32,96},{40,104},{48,112},{56,120},{... | collective-permute-start | bytes 589832 | tf_op jit(solution)/shard_map/ppermute | solution.py:290
  7.9 1.3 %collective-permute-start.5 = (bf16[384,256]{1,0:T(8,128)(2,1)S(1)}, bf16[384,256]{1,0:T(8,128)(2,1)S(1)}, u32[]{:S(2)}, u32[]{:S(2)}) collective-permute-start(bf16[384,256]{1,0:T(8,128)(2,1)S(1)} %get-tuple-element.23), channel_id=1, source_target_pairs={{0,96},{8,104},{16,112},{24,120},{32,0},{40,8},{48,16},{56,24},{64... | collective-permute-start | bytes 589832 | tf_op jit(solution)/shard_map/ppermute | solution.py:290
  9.2 2.1 %collective-permute-done.3.g1 = bf16[384,256]{1,0:T(8,128)(2,1)S(1)} collective-permute-done((bf16[384,256]{1,0:T(8,128)(2,1)S(1)}, bf16[384,256]{1,0:T(8,128)(2,1)S(1)}, u32[]{:S(2)}, u32[]{:S(2)}) %collective-permute-start.3) | collective-permute-done | bytes 196640 | tf_op jit(solution)/shard_map/ppermute | solution.py:290
  11.3 5.1 %collective-permute-done.4.g2 = bf16[384,256]{1,0:T(8,128)(2,1)S(1)} collective-permute-done((bf16[384,256]{1,0:T(8,128)(2,1)S(1)}, bf16[384,256]{1,0:T(8,128)(2,1)S(1)}, u32[]{:S(2)}, u32[]{:S(2)}) %collective-permute-start.4) | collective-permute-done | bytes 196640 | tf_op jit(solution)/shard_map/ppermute | solution.py:290
  18.0 1.0 %collective-permute-done.6.got_ref = bf16[2,384,256]{2,1,0:T(8,128)(2,1)S(1)} collective-permute-done((bf16[2,384,256]{2,1,0:T(8,128)(2,1)S(1)}, bf16[2,384,256]{2,1,0:T(8,128)(2,1)S(1)}, u32[]{:S(2)}, u32[]{:S(2)}) %collective-permute-start.6) | collective-permute-done | bytes 393248 | tf_op jit(solution)/shard_map/ppermute | solution.py:289
  19.0 0.8 %over_core.1 = (bf16[384,256]{1,0:T(8,128)(2,1)S(1)}, bf16[384,256]{1,0:T(8,128)(2,1)S(1)}) custom-call(s32[4]{0:T(128)} %token_ref.1, bf16[384,256]{1,0:T(8,128)(2,1)S(1)} %get-tuple-element.20.g0, bf16[384,256]{1,0:T(8,128)(2,1)S(1)} %collective-permute-done.3.g1, bf16[384,256]{1,0:T(8,128)(2,1)S(1)} %collective-permute-done.4.g2, ...), custom_call_target="tpu_custom_call" | custom-call | tf_op jit(solution)/shard_map/over_core/pallas_call | solution.py:309
  20.6 6.2 %collective-permute-done.7.got_ref = bf16[384,256]{1,0:T(8,128)(2,1)S(1)} collective-permute-done((bf16[384,256]{1,0:T(8,128)(2,1)S(1)}, bf16[384,256]{1,0:T(8,128)(2,1)S(1)}, u32[]{:S(2)}, u32[]{:S(2)}) %collective-permute-start.7) | collective-permute-done | bytes 196640 | tf_op jit(solution)/shard_map/ppermute | solution.py:289
  27.4 2.6 %collective-permute-start.10 = (bf16[384,256]{1,0:T(8,128)(2,1)S(1)}, bf16[384,256]{1,0:T(8,128)(2,1)S(1)}, u32[]{:S(2)}, u32[]{:S(2)}) collective-permute-start(bf16[384,256]{1,0:T(8,128)(2,1)S(1)} %over_x.1.p0), channel_id=1, source_target_pairs={{0,64},{8,72},{16,80},{24,88},{32,96},{40,104},{48,112},{56,120},{... | collective-permute-start | bytes 589832 | tf_op jit(solution)/shard_map/ppermute | solution.py:290
  30.1 1.3 %collective-permute-start.9 = (bf16[384,256]{1,0:T(8,128)(2,1)S(1)}, bf16[384,256]{1,0:T(8,128)(2,1)S(1)}, u32[]{:S(2)}, u32[]{:S(2)}) collective-permute-start(bf16[384,256]{1,0:T(8,128)(2,1)S(1)} %over_x.1.p0), channel_id=1, source_target_pairs={{0,96},{8,104},{16,112},{24,120},{32,0},{40,8},{48,16},{56,24},{64... | collective-permute-start | bytes 589832 | tf_op jit(solution)/shard_map/ppermute | solution.py:290
  31.3 0.8 %collective-permute-start.8 = (bf16[384,256]{1,0:T(8,128)(2,1)S(1)}, bf16[384,256]{1,0:T(8,128)(2,1)S(1)}, u32[]{:S(2)}, u32[]{:S(2)}) collective-permute-start(bf16[384,256]{1,0:T(8,128)(2,1)S(1)} %over_x.1.p0), channel_id=1, source_target_pairs={{0,32},{8,40},{16,48},{24,56},{32,64},{40,72},{48,80},{56,88},{64,... | collective-permute-start | bytes 589832 | tf_op jit(solution)/shard_map/ppermute | solution.py:290
  32.2 1.1 %left.1 = f32[6144,128]{1,0:T(8,128)S(1)} custom-call(bf16[256,768]{1,0:T(8,128)(2,1)S(1)} %copy-done.2, bf16[400,256]{1,0:T(8,128)(2,1)S(1)} %get-tuple-element.17.b0, bf16[400,256]{1,0:T(8,128)(2,1)S(1)} %collective-permute-done.b1, bf16[400,256]{1,0:T(8,128)(2,1)S(1)} %get-tuple-element.29.b2, bf16[400,256]{1,0:T(8,128)(2,1)S(1)} %collective-permute-done.2.b3), custom_call_target="tpu_custom_call" | custom-call | flops 603979776 | bytes 4000000 | tf_op jit(solution)/shard_map/left/pallas_call | solution.py:327
  33.3 3.5 %collective-permute-done.10.p3 = bf16[384,256]{1,0:T(8,128)(2,1)S(1)} collective-permute-done((bf16[384,256]{1,0:T(8,128)(2,1)S(1)}, bf16[384,256]{1,0:T(8,128)(2,1)S(1)}, u32[]{:S(2)}, u32[]{:S(2)}) %collective-permute-start.10) | collective-permute-done | bytes 196640 | tf_op jit(solution)/shard_map/ppermute | solution.py:290
  36.9 1.9 %collective-permute-done.9.p2 = bf16[384,256]{1,0:T(8,128)(2,1)S(1)} collective-permute-done((bf16[384,256]{1,0:T(8,128)(2,1)S(1)}, bf16[384,256]{1,0:T(8,128)(2,1)S(1)}, u32[]{:S(2)}, u32[]{:S(2)}) %collective-permute-start.9) | collective-permute-done | bytes 196640 | tf_op jit(solution)/shard_map/ppermute | solution.py:290
  38.8 0.8 %collective-permute-done.8.p1 = bf16[384,256]{1,0:T(8,128)(2,1)S(1)} collective-permute-done((bf16[384,256]{1,0:T(8,128)(2,1)S(1)}, bf16[384,256]{1,0:T(8,128)(2,1)S(1)}, u32[]{:S(2)}, u32[]{:S(2)}) %collective-permute-start.8) | collective-permute-done | bytes 196640 | tf_op jit(solution)/shard_map/ppermute | solution.py:290
  39.6 1.3 %right.1 = f32[6144,128]{1,0:T(8,128)S(1)} custom-call(bf16[256,768]{1,0:T(8,128)(2,1)S(1)} %copy-done.1, bf16[384,256]{1,0:T(8,128)(2,1)S(1)} %over_x.1.p0, bf16[384,256]{1,0:T(8,128)(2,1)S(1)} %collective-permute-done.8.p1, bf16[384,256]{1,0:T(8,128)(2,1)S(1)} %collective-permute-done.9.p2, bf16[384,256]{1,0:T(8,128)(2,1)S(1)} %collective-permute-done.10.p3), custom_call_target="tpu_custom_call" | custom-call | flops 603979776 | bytes 4000000 | tf_op jit(solution)/shard_map/right/pallas_call | solution.py:331
  40.9 5.2 %pairs.2 = (f32[4,72,256]{2,1,0:T(8,128)S(1)}, s32[4]{0:T(128)S(1)}) custom-call(s32[4]{0:T(128)S(1)} %copy-done.3, s32[2048]{0:T(1024)S(1)} %add.14.local_ref, s32[2048]{0:T(1024)S(1)} %bitcast.13, f32[6144,128]{1,0:T(8,128)S(1)} %left.1, f32[6144,128]{1,0:T(8,128)S(1)} %right.1, bf16[144,384]{1,0:T(8,128)(2,1)S(1)} %copy-done), custom_call_target="tpu_custom_call" | custom-call | flops 603979776 | bytes 4000000 | tf_op jit(solution)/shard_map/pairs/pallas_call | solution.py:339
  46.1 2.8 %collective-permute-start.11 = (f32[4,72,256]{2,1,0:T(8,128)S(1)}, f32[4,72,256]{2,1,0:T(8,128)S(1)}, u32[]{:S(2)}, u32[]{:S(2)}) collective-permute-start(f32[4,72,256]{2,1,0:T(8,128)S(1)} %get-tuple-element.26), channel_id=1, source_target_pairs={{0,1},{1,0},{2,3},{3,2},{4,5},{5,4},{6,7},{7,6},{8,9},{9,8},{10,11... | collective-permute-start | bytes 884744 | tf_op jit(solution)/shard_map/ppermute | solution.py:347
  48.9 5.1 %pairs.3 = (f32[4,72,256]{2,1,0:T(8,128)S(1)}, s32[4]{0:T(128)}) custom-call(s32[4]{0:T(128)S(1)} %get-tuple-element.27.token_ref, s32[2048]{0:T(1024)S(1)} %add.14.local_ref, s32[2048]{0:T(1024)S(1)} %bitcast.14, f32[6144,128]{1,0:T(8,128)S(1)} %left.1, f32[6144,128]{1,0:T(8,128)S(1)} %right.1, bf16[144,384]{1,0:T(8,128)(2,1)S(1)} %copy-done), custom_call_target="tpu_custom_call" | custom-call | flops 603979776 | bytes 4000000 | tf_op jit(solution)/shard_map/pairs/pallas_call | solution.py:339
  54.0 1.5 %collective-permute-done.11.a_ref = f32[4,72,256]{2,1,0:T(8,128)S(1)} collective-permute-done((f32[4,72,256]{2,1,0:T(8,128)S(1)}, f32[4,72,256]{2,1,0:T(8,128)S(1)}, u32[]{:S(2)}, u32[]{:S(2)}) %collective-permute-start.11) | collective-permute-done | bytes 294944 | tf_op jit(solution)/shard_map/ppermute | solution.py:347
  55.6 14.0 %all_to_all.5.got_ref = f32[16,40,128]{2,1,0:T(8,128)S(1)} all-to-all(f32[16,40,128]{2,1,0:T(8,128)S(1)} %add.16), channel_id=1, replica_groups=mesh['y'=4,'xl'=2,'core'=2,'z'=4,'xh'=2] {'z','xl','core'}, dimensions={0} | all-to-all | bytes 655360 | tf_op jit(solution)/shard_map/all_to_all | solution.py:352
  69.6 1.5 %finish.1 = f32[1,4,64,65]{3,2,1,0:T(8,128)} custom-call(s32[1,4]{1,0:T(1,128)} %near_ref.1, f32[16,40,128]{2,1,0:T(8,128)S(1)} %all_to_all.5.got_ref), custom_call_target="tpu_custom_call" | custom-call | tf_op jit(solution)/shard_map/finish/pallas_call | solution.py:353
  (34 shorter events, 3.2 us)
Async XLA Ops:
  0.0 32.1 %copy-start.2 = (bf16[256,768]{1,0:T(8,128)(2,1)S(1)}, bf16[256,768]{1,0:T(8,128)(2,1)}, u32[]{:S(2)}) copy-start(bf16[256,768]{1,0:T(8,128)(2,1)} %constant.10.clone.table_ref) | copy-start | bytes 1179652
  1.7 16.0 %collective-permute-start.1 = (bf16[2,400,256]{2,1,0:T(8,128)(2,1)S(1)}, bf16[2,400,256]{2,1,0:T(8,128)(2,1)S(1)}, u32[]{:S(2)}, u32[]{:S(2)}) collective-permute-start(bf16[2,400,256]{2,1,0:T(8,128)(2,1)S(1)} %get-tuple-element.19), channel_id=1, source_target_pairs={{0,16},{8,24},{16,0},{24,8},{32,48},{40,56},{48,32},{56,40},{64,80... | collective-permute-start | bytes 1228808 | tf_op jit(solution)/shard_map/ppermute | solution.py:289
  3.4 7.9 %collective-permute-start.3 = (bf16[384,256]{1,0:T(8,128)(2,1)S(1)}, bf16[384,256]{1,0:T(8,128)(2,1)S(1)}, u32[]{:S(2)}, u32[]{:S(2)}) collective-permute-start(bf16[384,256]{1,0:T(8,128)(2,1)S(1)} %get-tuple-element.21), channel_id=1, source_target_pairs={{0,32},{8,40},{16,48},{24,56},{32,64},{40,72},{48,80},{56,88},{64,... | collective-permute-start | bytes 589832 | tf_op jit(solution)/shard_map/ppermute | solution.py:290
  5.0 11.4 %collective-permute-start.4 = (bf16[384,256]{1,0:T(8,128)(2,1)S(1)}, bf16[384,256]{1,0:T(8,128)(2,1)S(1)}, u32[]{:S(2)}, u32[]{:S(2)}) collective-permute-start(bf16[384,256]{1,0:T(8,128)(2,1)S(1)} %get-tuple-element.22), channel_id=1, source_target_pairs={{0,64},{8,72},{16,80},{24,88},{32,96},{40,104},{48,112},{56,120},{... | collective-permute-start | bytes 589832 | tf_op jit(solution)/shard_map/ppermute | solution.py:290
  7.9 8.6 %collective-permute-start.5 = (bf16[384,256]{1,0:T(8,128)(2,1)S(1)}, bf16[384,256]{1,0:T(8,128)(2,1)S(1)}, u32[]{:S(2)}, u32[]{:S(2)}) collective-permute-start(bf16[384,256]{1,0:T(8,128)(2,1)S(1)} %get-tuple-element.23), channel_id=1, source_target_pairs={{0,96},{8,104},{16,112},{24,120},{32,0},{40,8},{48,16},{56,24},{64... | collective-permute-start | bytes 589832 | tf_op jit(solution)/shard_map/ppermute | solution.py:290
  17.2 1.8 %collective-permute-start.6 = (bf16[2,384,256]{2,1,0:T(8,128)(2,1)S(1)}, bf16[2,384,256]{2,1,0:T(8,128)(2,1)S(1)}, u32[]{:S(2)}, u32[]{:S(2)}) collective-permute-start(bf16[2,384,256]{2,1,0:T(8,128)(2,1)S(1)} %pick.1), channel_id=1, source_target_pairs={{0,8},{8,0},{16,24},{24,16},{32,40},{40,32},{48,56},{56,48},{64,72... | collective-permute-start | bytes 1179656 | tf_op jit(solution)/shard_map/ppermute | solution.py:289
  17.3 3.2 %collective-permute-start = (bf16[400,256]{1,0:T(8,128)(2,1)S(1)}, bf16[400,256]{1,0:T(8,128)(2,1)S(1)}, u32[]{:S(2)}, u32[]{:S(2)}) collective-permute-start(bf16[400,256]{1,0:T(8,128)(2,1)S(1)} %get-tuple-element.18), channel_id=1, source_target_pairs={{0,8},{8,0},{16,24},{24,16},{32,40},{40,32},{48,56},{56,48},{64,72... | collective-permute-start | bytes 614408 | tf_op jit(solution)/shard_map/ppermute | solution.py:289
  17.8 21.8 %copy-start.1 = (bf16[256,768]{1,0:T(8,128)(2,1)S(1)}, bf16[256,768]{1,0:T(8,128)(2,1)}, u32[]{:S(2)}) copy-start(bf16[256,768]{1,0:T(8,128)(2,1)} %constant.11.clone.table_ref) | copy-start | bytes 1179652
  17.8 2.7 %collective-permute-start.2 = (bf16[400,256]{1,0:T(8,128)(2,1)S(1)}, bf16[400,256]{1,0:T(8,128)(2,1)S(1)}, u32[]{:S(2)}, u32[]{:S(2)}) collective-permute-start(bf16[400,256]{1,0:T(8,128)(2,1)S(1)} %get-tuple-element.30), channel_id=1, source_target_pairs={{0,8},{8,0},{16,24},{24,16},{32,40},{40,32},{48,56},{56,48},{64,72... | collective-permute-start | bytes 614408 | tf_op jit(solution)/shard_map/ppermute | solution.py:289
  19.7 7.0 %collective-permute-start.7 = (bf16[384,256]{1,0:T(8,128)(2,1)S(1)}, bf16[384,256]{1,0:T(8,128)(2,1)S(1)}, u32[]{:S(2)}, u32[]{:S(2)}) collective-permute-start(bf16[384,256]{1,0:T(8,128)(2,1)S(1)} %get-tuple-element.25), channel_id=1, source_target_pairs={{0,16},{8,24},{16,0},{24,8},{32,48},{40,56},{48,32},{56,40},{64,80... | collective-permute-start | bytes 589832 | tf_op jit(solution)/shard_map/ppermute | solution.py:289
  27.4 9.4 %collective-permute-start.10 = (bf16[384,256]{1,0:T(8,128)(2,1)S(1)}, bf16[384,256]{1,0:T(8,128)(2,1)S(1)}, u32[]{:S(2)}, u32[]{:S(2)}) collective-permute-start(bf16[384,256]{1,0:T(8,128)(2,1)S(1)} %over_x.1.p0), channel_id=1, source_target_pairs={{0,64},{8,72},{16,80},{24,88},{32,96},{40,104},{48,112},{56,120},{... | collective-permute-start | bytes 589832 | tf_op jit(solution)/shard_map/ppermute | solution.py:290
  30.1 8.7 %collective-permute-start.9 = (bf16[384,256]{1,0:T(8,128)(2,1)S(1)}, bf16[384,256]{1,0:T(8,128)(2,1)S(1)}, u32[]{:S(2)}, u32[]{:S(2)}) collective-permute-start(bf16[384,256]{1,0:T(8,128)(2,1)S(1)} %over_x.1.p0), channel_id=1, source_target_pairs={{0,96},{8,104},{16,112},{24,120},{32,0},{40,8},{48,16},{56,24},{64... | collective-permute-start | bytes 589832 | tf_op jit(solution)/shard_map/ppermute | solution.py:290
  31.3 8.3 %collective-permute-start.8 = (bf16[384,256]{1,0:T(8,128)(2,1)S(1)}, bf16[384,256]{1,0:T(8,128)(2,1)S(1)}, u32[]{:S(2)}, u32[]{:S(2)}) collective-permute-start(bf16[384,256]{1,0:T(8,128)(2,1)S(1)} %over_x.1.p0), channel_id=1, source_target_pairs={{0,32},{8,40},{16,48},{24,56},{32,64},{40,72},{48,80},{56,88},{64,... | collective-permute-start | bytes 589832 | tf_op jit(solution)/shard_map/ppermute | solution.py:290
  33.3 7.6 %copy-start = (bf16[144,384]{1,0:T(8,128)(2,1)S(1)}, bf16[144,384]{1,0:T(8,128)(2,1)}, u32[]{:S(2)}) copy-start(bf16[144,384]{1,0:T(8,128)(2,1)} %constant.12.clone.back_ref) | copy-start | bytes 331780
  33.3 7.6 %copy-start.3 = (s32[4]{0:T(128)S(1)}, s32[4]{0:T(128)}, u32[]{:S(2)}) copy-start(s32[4]{0:T(128)} %token_ref.1) | copy-start | bytes 52
  46.1 9.4 %collective-permute-start.11 = (f32[4,72,256]{2,1,0:T(8,128)S(1)}, f32[4,72,256]{2,1,0:T(8,128)S(1)}, u32[]{:S(2)}, u32[]{:S(2)}) collective-permute-start(f32[4,72,256]{2,1,0:T(8,128)S(1)} %get-tuple-element.26), channel_id=1, source_target_pairs={{0,1},{1,0},{2,3},{3,2},{4,5},{5,4},{6,7},{7,6},{8,9},{9,8},{10,11... | collective-permute-start | bytes 884744 | tf_op jit(solution)/shard_map/ppermute | solution.py:347

commit v9 on v8

--- a/solution.py
+++ b/solution.py
@@ -111,21 +111,19 @@
                 give_ref[d // 2] = ref[...]
 
 
-def core_kernel(owners_ref, g0, g1, g2, g3, got_ref, _, mine_ref, theirs_ref):
+def core_kernel(owners_ref, g0, g1, g2, g3, got_ref, _, mine_0, mine_1, theirs_0, theirs_1):
     row, step, _, core = place()
-    for d, to in ((0, mine_ref), (2, theirs_ref)):
+    size = mine_0.shape[0]
+    for d, outs in ((0, (mine_0, mine_1)), (2, (theirs_0, theirs_1))):
         owner = owners_ref[step ^ d]
         here = (owner & 1) == core
         behind = jnp.where(here, (row + 4 - (owner >> 2)) & 3, 4)
-        for n, ref in enumerate((g0, g1, g2, g3)):
+        for n, ref in enumerate((g0, g1, g2, g3, got_ref.at[d // 2])):
 
             @pl.when(behind == n)
             def _():
-                to[...] = ref[...]
-
-        @pl.when(behind == 4)
-        def _():
-            to[...] = got_ref[d // 2]
+                for k, to in enumerate(outs):
+                    to[...] = ref[pl.ds(k * size, size), :]
 
 
 def chip_kernel(owners_ref, mine_ref, got_ref, out_ref):
@@ -160,12 +158,14 @@
                 out_ref[to, :] = part[c * events:(c + 1) * events]
 
 
-def right_kernel(table_ref, p0, p1, p2, p3, out_ref):
+def right_kernel(table_ref, *refs):
+    pieces, out_ref = refs[:-1], refs[-1]
     events = out_ref.shape[0] // 24
-    clear_rest(out_ref, 4 * p0.shape[0] // events)
+    size = pieces[0].shape[0]
+    clear_rest(out_ref, len(pieces) * size // events)
     row = place()[0]
-    for behind, p_ref in ((0, p0), (1, p1), (3, p2), (2, p3)):
-        base = ((row + 4 - behind) & 3) * p_ref.shape[0]
+    for n, p_ref in enumerate(pieces):
+        base = (((row + 4 - (0, 1, 3, 2)[n % 4]) & 3) * 2 + n // 4) * size
         x = p_ref[...]
         parts = spectrum(x, table_ref[...], EJ, EI)
         for g in range(x.shape[0] // 32):
@@ -306,16 +306,18 @@
         pick_kernel, out_shape=shaped((2, quarter, samp), bf16), in_specs=[SMEM] + [VMEM] * 4, out_specs=VMEM,
         compiler_params=SMALL, name="pick",
     )(in_hbm(owners), *got)
-    mine, theirs = pl.pallas_call(
-        core_kernel, out_shape=(piece, piece),
-        in_specs=[SMEM] + [VMEM] * 5 + [ANY], out_specs=(VMEM,) * 2,
+    part = shaped((quarter // 2, samp), bf16)
+    *mine, theirs_0, theirs_1 = pl.pallas_call(
+        core_kernel, out_shape=(part,) * 4, in_specs=[SMEM] + [VMEM] * 5 + [ANY], out_specs=(VMEM,) * 4,
         compiler_params=SMALL, name="over_core",
     )(in_hbm(owners), *got, near(give, 1), chip)
-    mine = pl.pallas_call(
-        chip_kernel, out_shape=piece, in_specs=[SMEM] + [VMEM] * 2, out_specs=VMEM,
-        compiler_params=SMALL, name="over_x",
-    )(in_hbm(owners), mine, near(theirs, 2))
-    pieces = [mine] + [turn(mine, d) for d in (1, -1, 2)]
+    pieces = []
+    for kept, sent in zip(mine, [near(theirs_0, 2), near(theirs_1, 2)]):
+        whole = pl.pallas_call(
+            chip_kernel, out_shape=part, in_specs=[SMEM] + [VMEM] * 2, out_specs=VMEM,
+            compiler_params=SMALL, name="over_x",
+        )(in_hbm(owners), kept, sent)
+        pieces += [whole] + [turn(whole, d) for d in (1, -1, 2)]
 
     listed = jnp.stack([b[ch * block:ch * block + 2 * pairs // samp] for b in blocks]).astype(jnp.int32)
     listed = listed.reshape(4, 2, pairs) * 24
@@ -329,7 +331,7 @@
         compiler_params=PARAMS, name="left", cost_estimate=cost,
     )(left_table, *blocks)
     right = pl.pallas_call(
-        right_kernel, out_shape=spectra, in_specs=[VMEM] * 5, out_specs=VMEM,
+        right_kernel, out_shape=spectra, in_specs=[VMEM] * (1 + len(pieces)), out_specs=VMEM,
         compiler_params=PARAMS, name="right", cost_estimate=cost,
     )(right_table, *pieces)
 
@@ -353,7 +355,7 @@
     out = pl.pallas_call(
         final_kernel, out_shape=shaped((1, steps, share, LAGS), f32),
         in_specs=[SMEM, VMEM], out_specs=VMEM, compiler_params=SMALL, name="finish",
-    )(in_hbm(neighbours), slots)
+    )(neighbours, slots)
     return out.transpose(0, 1, 3, 2)
 
 

time: 71.7 us -> 71.3 us (level)
  waiting for transfers between devices: 22.1 us -> 16.3 us
  starting transfers between devices: 16.3 us -> 21.3 us
    ppermute x6 -> x9, starting transfers between devices: 10.5 us -> 14 us  [local(): lax.ppermute(v, CLU, [(i, (i + 4 * d) % n_clu) for i in range(n_clu)])]
    ppermute x5 -> x6, waiting for transfers between devices: 7.18 us -> 4.36 us  [local(): lax.ppermute(v, CLU, [(i, i ^ d) for i in range(n_clu)])]
    ppermute x6 -> x9, waiting for transfers between devices: 13.5 us -> 11.5 us  [local(): lax.ppermute(v, CLU, [(i, (i + 4 * d) % n_clu) for i in range(n_clu)])]
    ppermute x5 -> x6, starting transfers between devices: 3.04 us -> 4.58 us  [local(): lax.ppermute(v, CLU, [(i, i ^ d) for i in range(n_clu)])]
    ppermute x1, waiting for transfers between devices: 1.5 us -> 0.41 us  [local(): lax.ppermute(v, STA, [(k, target(k, dz, dh, n_sta)) for k in range(n_sta)])]
    pallas_call x3 -> x4, Pallas kernels: 2.71 us -> 3.41 us  [the longest x2 1.38 us: local(): pl.pallas_call(chip_kernel, out_shape=part, in_specs=[SMEM] + [VMEM] * 2,...]
  transfers between devices with their start and end apart: 12 -> 16, of which waited for: 8 -> 8; matrix products, arithmetic and copies ran while one was open for 0% -> 0% of each run, Pallas kernels for 11% -> 13%
where the time goes in v9:
time: 71.3 us; the launch traced here: 70.9 us
  starting transfers between devices  21.3 us (30%)
  Pallas kernels  18.8 us (26%)
  waiting for transfers between devices  16.3 us (23%)
  blocking collectives  14 us (20%)
    all_to_all x1, blocking collectives, local(): slots = lax.all_to_all(slots, ('z', 'xl', 'core'), 0, 0)  14 us
    ppermute x9, starting transfers between devices, local(): lax.ppermute(v, CLU, [(i, (i + 4 * d) % n_clu) for i in range(n_clu)])  14 us
    ppermute x9, waiting for transfers between devices, local(): lax.ppermute(v, CLU, [(i, (i + 4 * d) % n_clu) for i in range(n_clu)])  11.5 us
    pallas_call x2, Pallas kernels, local(): pl.pallas_call(functools.partial(pair_kernel, across), out_shape=(shaped(...  10.3 us
    ppermute x6, starting transfers between devices, local(): lax.ppermute(v, CLU, [(i, i ^ d) for i in range(n_clu)])  4.58 us
    ppermute x6, waiting for transfers between devices, local(): lax.ppermute(v, CLU, [(i, i ^ d) for i in range(n_clu)])  4.36 us
    ppermute x1, starting transfers between devices, local(): lax.ppermute(v, STA, [(k, target(k, dz, dh, n_sta)) for k in range(n_sta)])  2.79 us
    pallas_call x1, Pallas kernels, local(): pl.pallas_call(pack_kernel, out_shape=(piece,) * 4 + (payload, payload, s...  1.7 us
  transfers between devices with their start and end apart: 16, of which 8 were waited for; matrix products, arithmetic and copies ran while one was open for 0% of the time, Pallas kernels for 13%

profile of v9, /device:TPU:0, one launch (start us, length us, event | category | flops | bytes accessed | tf_op | source)
XLA Modules:
  0.0 70.9 jit_solution(17903234128946853995)
XLA Ops:
  0.0 1.7 %pack.1 = (bf16[384,256]{1,0:T(8,128)(2,1)S(1)}, bf16[384,256]{1,0:T(8,128)(2,1)S(1)}, bf16[384,256]{1,0:T(8,128)(2,1)S(1)}, bf16[384,256]{1,0:T(8,128)(2,1)S(1)...) custom-call(bf16[1536,256]{1,0:T(8,128)(2,1)} %bitcast.15, ...), custom_call_target="tpu_custom_call" | custom-call | tf_op jit(solution)/shard_map/pack/pallas_call | solution.py:296
  1.7 1.6 %collective-permute-start.1 = (bf16[2,400,256]{2,1,0:T(8,128)(2,1)S(1)}, bf16[2,400,256]{2,1,0:T(8,128)(2,1)S(1)}, u32[]{:S(2)}, u32[]{:S(2)}) collective-permute-start(bf16[2,400,256]{2,1,0:T(8,128)(2,1)S(1)} %get-tuple-element.21), channel_id=1, source_target_pairs={{0,16},{8,24},{16,0},{24,8},{32,48},{40,56},{48,32},{56,40},{64,80... | collective-permute-start | bytes 1228808 | tf_op jit(solution)/shard_map/ppermute | solution.py:289
  3.4 1.6 %collective-permute-start.3 = (bf16[384,256]{1,0:T(8,128)(2,1)S(1)}, bf16[384,256]{1,0:T(8,128)(2,1)S(1)}, u32[]{:S(2)}, u32[]{:S(2)}) collective-permute-start(bf16[384,256]{1,0:T(8,128)(2,1)S(1)} %get-tuple-element.23), channel_id=1, source_target_pairs={{0,32},{8,40},{16,48},{24,56},{32,64},{40,72},{48,80},{56,88},{64,... | collective-permute-start | bytes 589832 | tf_op jit(solution)/shard_map/ppermute | solution.py:290
  4.9 2.9 %collective-permute-start.4 = (bf16[384,256]{1,0:T(8,128)(2,1)S(1)}, bf16[384,256]{1,0:T(8,128)(2,1)S(1)}, u32[]{:S(2)}, u32[]{:S(2)}) collective-permute-start(bf16[384,256]{1,0:T(8,128)(2,1)S(1)} %get-tuple-element.24), channel_id=1, source_target_pairs={{0,64},{8,72},{16,80},{24,88},{32,96},{40,104},{48,112},{56,120},{... | collective-permute-start | bytes 589832 | tf_op jit(solution)/shard_map/ppermute | solution.py:290
  7.8 1.4 %collective-permute-start.5 = (bf16[384,256]{1,0:T(8,128)(2,1)S(1)}, bf16[384,256]{1,0:T(8,128)(2,1)S(1)}, u32[]{:S(2)}, u32[]{:S(2)}) collective-permute-start(bf16[384,256]{1,0:T(8,128)(2,1)S(1)} %get-tuple-element.25), channel_id=1, source_target_pairs={{0,96},{8,104},{16,112},{24,120},{32,0},{40,8},{48,16},{56,24},{64... | collective-permute-start | bytes 589832 | tf_op jit(solution)/shard_map/ppermute | solution.py:290
  9.2 2.1 %collective-permute-done.3.g1 = bf16[384,256]{1,0:T(8,128)(2,1)S(1)} collective-permute-done((bf16[384,256]{1,0:T(8,128)(2,1)S(1)}, bf16[384,256]{1,0:T(8,128)(2,1)S(1)}, u32[]{:S(2)}, u32[]{:S(2)}) %collective-permute-start.3) | collective-permute-done | bytes 196640 | tf_op jit(solution)/shard_map/ppermute | solution.py:290
  11.3 5.1 %collective-permute-done.4.g2 = bf16[384,256]{1,0:T(8,128)(2,1)S(1)} collective-permute-done((bf16[384,256]{1,0:T(8,128)(2,1)S(1)}, bf16[384,256]{1,0:T(8,128)(2,1)S(1)}, u32[]{:S(2)}, u32[]{:S(2)}) %collective-permute-start.4) | collective-permute-done | bytes 196640 | tf_op jit(solution)/shard_map/ppermute | solution.py:290
  18.0 1.0 %collective-permute-done.6.got_ref = bf16[2,384,256]{2,1,0:T(8,128)(2,1)S(1)} collective-permute-done((bf16[2,384,256]{2,1,0:T(8,128)(2,1)S(1)}, bf16[2,384,256]{2,1,0:T(8,128)(2,1)S(1)}, u32[]{:S(2)}, u32[]{:S(2)}) %collective-permute-start.6) | collective-permute-done | bytes 393248 | tf_op jit(solution)/shard_map/ppermute | solution.py:289
  20.5 1.6 %collective-permute-start.11 = (bf16[192,256]{1,0:T(8,128)(2,1)S(1)}, bf16[192,256]{1,0:T(8,128)(2,1)S(1)}, u32[]{:S(2)}, u32[]{:S(2)}) collective-permute-start(bf16[192,256]{1,0:T(8,128)(2,1)S(1)} %get-tuple-element.29), channel_id=1, source_target_pairs={{0,16},{8,24},{16,0},{24,8},{32,48},{40,56},{48,32},{56,40},{64,80... | collective-permute-start | bytes 294920 | tf_op jit(solution)/shard_map/ppermute | solution.py:289
  22.1 3.4 %collective-permute-done.7.got_ref = bf16[192,256]{1,0:T(8,128)(2,1)S(1)} collective-permute-done((bf16[192,256]{1,0:T(8,128)(2,1)S(1)}, bf16[192,256]{1,0:T(8,128)(2,1)S(1)}, u32[]{:S(2)}, u32[]{:S(2)}) %collective-permute-start.7) | collective-permute-done | bytes 98336 | tf_op jit(solution)/shard_map/ppermute | solution.py:289
  26.1 2.6 %collective-permute-start.10 = (bf16[192,256]{1,0:T(8,128)(2,1)S(1)}, bf16[192,256]{1,0:T(8,128)(2,1)S(1)}, u32[]{:S(2)}, u32[]{:S(2)}) collective-permute-start(bf16[192,256]{1,0:T(8,128)(2,1)S(1)} %over_x.2.refs_0_), channel_id=1, source_target_pairs={{0,64},{8,72},{16,80},{24,88},{32,96},{40,104},{48,112},{56,120},{... | collective-permute-start | bytes 294920 | tf_op jit(solution)/shard_map/ppermute | solution.py:290
  28.8 1.3 %collective-permute-start.9 = (bf16[192,256]{1,0:T(8,128)(2,1)S(1)}, bf16[192,256]{1,0:T(8,128)(2,1)S(1)}, u32[]{:S(2)}, u32[]{:S(2)}) collective-permute-start(bf16[192,256]{1,0:T(8,128)(2,1)S(1)} %over_x.2.refs_0_), channel_id=1, source_target_pairs={{0,96},{8,104},{16,112},{24,120},{32,0},{40,8},{48,16},{56,24},{64... | collective-permute-start | bytes 294920 | tf_op jit(solution)/shard_map/ppermute | solution.py:290
  30.1 0.8 %collective-permute-start.8 = (bf16[192,256]{1,0:T(8,128)(2,1)S(1)}, bf16[192,256]{1,0:T(8,128)(2,1)S(1)}, u32[]{:S(2)}, u32[]{:S(2)}) collective-permute-start(bf16[192,256]{1,0:T(8,128)(2,1)S(1)} %over_x.2.refs_0_), channel_id=1, source_target_pairs={{0,32},{8,40},{16,48},{24,56},{32,64},{40,72},{48,80},{56,88},{64,... | collective-permute-start | bytes 294920 | tf_op jit(solution)/shard_map/ppermute | solution.py:290
  31.6 1.0 %collective-permute-start.14 = (bf16[192,256]{1,0:T(8,128)(2,1)S(1)}, bf16[192,256]{1,0:T(8,128)(2,1)S(1)}, u32[]{:S(2)}, u32[]{:S(2)}) collective-permute-start(bf16[192,256]{1,0:T(8,128)(2,1)S(1)} %over_x.3.refs_4_), channel_id=1, source_target_pairs={{0,64},{8,72},{16,80},{24,88},{32,96},{40,104},{48,112},{56,120},{... | collective-permute-start | bytes 294920 | tf_op jit(solution)/shard_map/ppermute | solution.py:290
  32.6 2.1 %collective-permute-start.13 = (bf16[192,256]{1,0:T(8,128)(2,1)S(1)}, bf16[192,256]{1,0:T(8,128)(2,1)S(1)}, u32[]{:S(2)}, u32[]{:S(2)}) collective-permute-start(bf16[192,256]{1,0:T(8,128)(2,1)S(1)} %over_x.3.refs_4_), channel_id=1, source_target_pairs={{0,96},{8,104},{16,112},{24,120},{32,0},{40,8},{48,16},{56,24},{64... | collective-permute-start | bytes 294920 | tf_op jit(solution)/shard_map/ppermute | solution.py:290
  35.0 1.2 %left.1 = f32[6144,128]{1,0:T(8,128)S(1)} custom-call(bf16[256,768]{1,0:T(8,128)(2,1)S(1)} %copy-done.2, bf16[400,256]{1,0:T(8,128)(2,1)S(1)} %get-tuple-element.19.b0, bf16[400,256]{1,0:T(8,128)(2,1)S(1)} %collective-permute-done.b1, bf16[400,256]{1,0:T(8,128)(2,1)S(1)} %get-tuple-element.33.b2, bf16[400,256]{1,0:T(8,128)(2,1)S(1)} %collective-permute-done.2.b3), custom_call_target="tpu_custom_call" | custom-call | flops 603979776 | bytes 4000000 | tf_op jit(solution)/shard_map/left/pallas_call | solution.py:329
  36.2 1.8 %collective-permute-done.8.refs_1_ = bf16[192,256]{1,0:T(8,128)(2,1)S(1)} collective-permute-done((bf16[192,256]{1,0:T(8,128)(2,1)S(1)}, bf16[192,256]{1,0:T(8,128)(2,1)S(1)}, u32[]{:S(2)}, u32[]{:S(2)}) %collective-permute-start.8) | collective-permute-done | bytes 98336 | tf_op jit(solution)/shard_map/ppermute | solution.py:290
  38.6 1.9 %collective-permute-done.12.refs_5_ = bf16[192,256]{1,0:T(8,128)(2,1)S(1)} collective-permute-done((bf16[192,256]{1,0:T(8,128)(2,1)S(1)}, bf16[192,256]{1,0:T(8,128)(2,1)S(1)}, u32[]{:S(2)}, u32[]{:S(2)}) %collective-permute-start.12) | collective-permute-done | bytes 98336 | tf_op jit(solution)/shard_map/ppermute | solution.py:290
  40.5 1.3 %right.1 = f32[6144,128]{1,0:T(8,128)S(1)} custom-call(bf16[256,768]{1,0:T(8,128)(2,1)S(1)} %copy-done.1, bf16[192,256]{1,0:T(8,128)(2,1)S(1)} %over_x.2.refs_0_, bf16[192,256]{1,0:T(8,128)(2,1)S(1)} %collective-permute-done.8.refs_1_, bf16[192,256]{1,0:T(8,128)(2,1)S(1)} %collective-permute-done.9.refs_2_, ...), custom_call_target="tpu_custom_call" | custom-call | flops 603979776 | bytes 4000000 | tf_op jit(solution)/shard_map/right/pallas_call | solution.py:333
  41.8 5.2 %pairs.2 = (f32[4,72,256]{2,1,0:T(8,128)S(1)}, s32[4]{0:T(128)S(1)}) custom-call(s32[4]{0:T(128)S(1)} %copy-done.3, s32[2048]{0:T(1024)S(1)} %add.14.local_ref, s32[2048]{0:T(1024)S(1)} %bitcast.13, f32[6144,128]{1,0:T(8,128)S(1)} %left.1, f32[6144,128]{1,0:T(8,128)S(1)} %right.1, bf16[144,384]{1,0:T(8,128)(2,1)S(1)} %copy-done), custom_call_target="tpu_custom_call" | custom-call | flops 603979776 | bytes 4000000 | tf_op jit(solution)/shard_map/pairs/pallas_call | solution.py:341
  47.0 2.8 %collective-permute-start.15 = (f32[4,72,256]{2,1,0:T(8,128)S(1)}, f32[4,72,256]{2,1,0:T(8,128)S(1)}, u32[]{:S(2)}, u32[]{:S(2)}) collective-permute-start(f32[4,72,256]{2,1,0:T(8,128)S(1)} %get-tuple-element.30), channel_id=1, source_target_pairs={{0,1},{1,0},{2,3},{3,2},{4,5},{5,4},{6,7},{7,6},{8,9},{9,8},{10,11... | collective-permute-start | bytes 884744 | tf_op jit(solution)/shard_map/ppermute | solution.py:349
  49.8 5.1 %pairs.3 = (f32[4,72,256]{2,1,0:T(8,128)S(1)}, s32[4]{0:T(128)}) custom-call(s32[4]{0:T(128)S(1)} %get-tuple-element.31.token_ref, s32[2048]{0:T(1024)S(1)} %add.14.local_ref, s32[2048]{0:T(1024)S(1)} %bitcast.14, f32[6144,128]{1,0:T(8,128)S(1)} %left.1, f32[6144,128]{1,0:T(8,128)S(1)} %right.1, bf16[144,384]{1,0:T(8,128)(2,1)S(1)} %copy-done), custom_call_target="tpu_custom_call" | custom-call | flops 603979776 | bytes 4000000 | tf_op jit(solution)/shard_map/pairs/pallas_call | solution.py:341
  55.5 14.0 %all_to_all.5.got_ref = f32[16,40,128]{2,1,0:T(8,128)S(1)} all-to-all(f32[16,40,128]{2,1,0:T(8,128)S(1)} %add.16), channel_id=1, replica_groups=mesh['y'=4,'xl'=2,'core'=2,'z'=4,'xh'=2] {'z','xl','core'}, dimensions={0} | all-to-all | bytes 655360 | tf_op jit(solution)/shard_map/all_to_all | solution.py:354
  69.5 1.4 %finish.1 = f32[1,4,64,65]{3,2,1,0:T(8,128)} custom-call(s32[1,4]{1,0:T(1,128)S(1)} %copy-done.4, f32[16,40,128]{2,1,0:T(8,128)S(1)} %all_to_all.5.got_ref), custom_call_target="tpu_custom_call" | custom-call | tf_op jit(solution)/shard_map/finish/pallas_call | solution.py:355
  (45 shorter events, 6.0 us)
Async XLA Ops:
  0.0 35.0 %copy-start.2 = (bf16[256,768]{1,0:T(8,128)(2,1)S(1)}, bf16[256,768]{1,0:T(8,128)(2,1)}, u32[]{:S(2)}) copy-start(bf16[256,768]{1,0:T(8,128)(2,1)} %constant.10.clone.table_ref) | copy-start | bytes 1179652
  1.7 16.0 %collective-permute-start.1 = (bf16[2,400,256]{2,1,0:T(8,128)(2,1)S(1)}, bf16[2,400,256]{2,1,0:T(8,128)(2,1)S(1)}, u32[]{:S(2)}, u32[]{:S(2)}) collective-permute-start(bf16[2,400,256]{2,1,0:T(8,128)(2,1)S(1)} %get-tuple-element.21), channel_id=1, source_target_pairs={{0,16},{8,24},{16,0},{24,8},{32,48},{40,56},{48,32},{56,40},{64,80... | collective-permute-start | bytes 1228808 | tf_op jit(solution)/shard_map/ppermute | solution.py:289
  3.4 7.9 %collective-permute-start.3 = (bf16[384,256]{1,0:T(8,128)(2,1)S(1)}, bf16[384,256]{1,0:T(8,128)(2,1)S(1)}, u32[]{:S(2)}, u32[]{:S(2)}) collective-permute-start(bf16[384,256]{1,0:T(8,128)(2,1)S(1)} %get-tuple-element.23), channel_id=1, source_target_pairs={{0,32},{8,40},{16,48},{24,56},{32,64},{40,72},{48,80},{56,88},{64,... | collective-permute-start | bytes 589832 | tf_op jit(solution)/shard_map/ppermute | solution.py:290
  4.9 11.4 %collective-permute-start.4 = (bf16[384,256]{1,0:T(8,128)(2,1)S(1)}, bf16[384,256]{1,0:T(8,128)(2,1)S(1)}, u32[]{:S(2)}, u32[]{:S(2)}) collective-permute-start(bf16[384,256]{1,0:T(8,128)(2,1)S(1)} %get-tuple-element.24), channel_id=1, source_target_pairs={{0,64},{8,72},{16,80},{24,88},{32,96},{40,104},{48,112},{56,120},{... | collective-permute-start | bytes 589832 | tf_op jit(solution)/shard_map/ppermute | solution.py:290
  7.8 8.6 %collective-permute-start.5 = (bf16[384,256]{1,0:T(8,128)(2,1)S(1)}, bf16[384,256]{1,0:T(8,128)(2,1)S(1)}, u32[]{:S(2)}, u32[]{:S(2)}) collective-permute-start(bf16[384,256]{1,0:T(8,128)(2,1)S(1)} %get-tuple-element.25), channel_id=1, source_target_pairs={{0,96},{8,104},{16,112},{24,120},{32,0},{40,8},{48,16},{56,24},{64... | collective-permute-start | bytes 589832 | tf_op jit(solution)/shard_map/ppermute | solution.py:290
  17.1 1.8 %collective-permute-start.6 = (bf16[2,384,256]{2,1,0:T(8,128)(2,1)S(1)}, bf16[2,384,256]{2,1,0:T(8,128)(2,1)S(1)}, u32[]{:S(2)}, u32[]{:S(2)}) collective-permute-start(bf16[2,384,256]{2,1,0:T(8,128)(2,1)S(1)} %pick.1), channel_id=1, source_target_pairs={{0,8},{8,0},{16,24},{24,16},{32,40},{40,32},{48,56},{56,48},{64,72... | collective-permute-start | bytes 1179656 | tf_op jit(solution)/shard_map/ppermute | solution.py:289
  17.2 3.2 %collective-permute-start = (bf16[400,256]{1,0:T(8,128)(2,1)S(1)}, bf16[400,256]{1,0:T(8,128)(2,1)S(1)}, u32[]{:S(2)}, u32[]{:S(2)}) collective-permute-start(bf16[400,256]{1,0:T(8,128)(2,1)S(1)} %get-tuple-element.20), channel_id=1, source_target_pairs={{0,8},{8,0},{16,24},{24,16},{32,40},{40,32},{48,56},{56,48},{64,72... | collective-permute-start | bytes 614408 | tf_op jit(solution)/shard_map/ppermute | solution.py:289
  17.8 22.8 %copy-start.1 = (bf16[256,768]{1,0:T(8,128)(2,1)S(1)}, bf16[256,768]{1,0:T(8,128)(2,1)}, u32[]{:S(2)}) copy-start(bf16[256,768]{1,0:T(8,128)(2,1)} %constant.11.clone.table_ref) | copy-start | bytes 1179652
  17.8 4.3 %collective-permute-start.2 = (bf16[400,256]{1,0:T(8,128)(2,1)S(1)}, bf16[400,256]{1,0:T(8,128)(2,1)S(1)}, u32[]{:S(2)}, u32[]{:S(2)}) collective-permute-start(bf16[400,256]{1,0:T(8,128)(2,1)S(1)} %get-tuple-element.34), channel_id=1, source_target_pairs={{0,8},{8,0},{16,24},{24,16},{32,40},{40,32},{48,56},{56,48},{64,72... | collective-permute-start | bytes 614408 | tf_op jit(solution)/shard_map/ppermute | solution.py:289
  19.7 5.7 %collective-permute-start.7 = (bf16[192,256]{1,0:T(8,128)(2,1)S(1)}, bf16[192,256]{1,0:T(8,128)(2,1)S(1)}, u32[]{:S(2)}, u32[]{:S(2)}) collective-permute-start(bf16[192,256]{1,0:T(8,128)(2,1)S(1)} %get-tuple-element.27), channel_id=1, source_target_pairs={{0,16},{8,24},{16,0},{24,8},{32,48},{40,56},{48,32},{56,40},{64,80... | collective-permute-start | bytes 294920 | tf_op jit(solution)/shard_map/ppermute | solution.py:289
  20.5 10.4 %collective-permute-start.11 = (bf16[192,256]{1,0:T(8,128)(2,1)S(1)}, bf16[192,256]{1,0:T(8,128)(2,1)S(1)}, u32[]{:S(2)}, u32[]{:S(2)}) collective-permute-start(bf16[192,256]{1,0:T(8,128)(2,1)S(1)} %get-tuple-element.29), channel_id=1, source_target_pairs={{0,16},{8,24},{16,0},{24,8},{32,48},{40,56},{48,32},{56,40},{64,80... | collective-permute-start | bytes 294920 | tf_op jit(solution)/shard_map/ppermute | solution.py:289
  26.1 8.6 %collective-permute-start.10 = (bf16[192,256]{1,0:T(8,128)(2,1)S(1)}, bf16[192,256]{1,0:T(8,128)(2,1)S(1)}, u32[]{:S(2)}, u32[]{:S(2)}) collective-permute-start(bf16[192,256]{1,0:T(8,128)(2,1)S(1)} %over_x.2.refs_0_), channel_id=1, source_target_pairs={{0,64},{8,72},{16,80},{24,88},{32,96},{40,104},{48,112},{56,120},{... | collective-permute-start | bytes 294920 | tf_op jit(solution)/shard_map/ppermute | solution.py:290
  28.8 7.4 %collective-permute-start.9 = (bf16[192,256]{1,0:T(8,128)(2,1)S(1)}, bf16[192,256]{1,0:T(8,128)(2,1)S(1)}, u32[]{:S(2)}, u32[]{:S(2)}) collective-permute-start(bf16[192,256]{1,0:T(8,128)(2,1)S(1)} %over_x.2.refs_0_), channel_id=1, source_target_pairs={{0,96},{8,104},{16,112},{24,120},{32,0},{40,8},{48,16},{56,24},{64... | collective-permute-start | bytes 294920 | tf_op jit(solution)/shard_map/ppermute | solution.py:290
  30.1 7.9 %collective-permute-start.8 = (bf16[192,256]{1,0:T(8,128)(2,1)S(1)}, bf16[192,256]{1,0:T(8,128)(2,1)S(1)}, u32[]{:S(2)}, u32[]{:S(2)}) collective-permute-start(bf16[192,256]{1,0:T(8,128)(2,1)S(1)} %over_x.2.refs_0_), channel_id=1, source_target_pairs={{0,32},{8,40},{16,48},{24,56},{32,64},{40,72},{48,80},{56,88},{64,... | collective-permute-start | bytes 294920 | tf_op jit(solution)/shard_map/ppermute | solution.py:290
  31.6 6.4 %collective-permute-start.14 = (bf16[192,256]{1,0:T(8,128)(2,1)S(1)}, bf16[192,256]{1,0:T(8,128)(2,1)S(1)}, u32[]{:S(2)}, u32[]{:S(2)}) collective-permute-start(bf16[192,256]{1,0:T(8,128)(2,1)S(1)} %over_x.3.refs_4_), channel_id=1, source_target_pairs={{0,64},{8,72},{16,80},{24,88},{32,96},{40,104},{48,112},{56,120},{... | collective-permute-start | bytes 294920 | tf_op jit(solution)/shard_map/ppermute | solution.py:290
  32.6 6.0 %collective-permute-start.13 = (bf16[192,256]{1,0:T(8,128)(2,1)S(1)}, bf16[192,256]{1,0:T(8,128)(2,1)S(1)}, u32[]{:S(2)}, u32[]{:S(2)}) collective-permute-start(bf16[192,256]{1,0:T(8,128)(2,1)S(1)} %over_x.3.refs_4_), channel_id=1, source_target_pairs={{0,96},{8,104},{16,112},{24,120},{32,0},{40,8},{48,16},{56,24},{64... | collective-permute-start | bytes 294920 | tf_op jit(solution)/shard_map/ppermute | solution.py:290
  34.7 5.8 %collective-permute-start.12 = (bf16[192,256]{1,0:T(8,128)(2,1)S(1)}, bf16[192,256]{1,0:T(8,128)(2,1)S(1)}, u32[]{:S(2)}, u32[]{:S(2)}) collective-permute-start(bf16[192,256]{1,0:T(8,128)(2,1)S(1)} %over_x.3.refs_4_), channel_id=1, source_target_pairs={{0,32},{8,40},{16,48},{24,56},{32,64},{40,72},{48,80},{56,88},{64,... | collective-permute-start | bytes 294920 | tf_op jit(solution)/shard_map/ppermute | solution.py:290
  36.2 5.6 %copy-start = (bf16[144,384]{1,0:T(8,128)(2,1)S(1)}, bf16[144,384]{1,0:T(8,128)(2,1)}, u32[]{:S(2)}) copy-start(bf16[144,384]{1,0:T(8,128)(2,1)} %constant.12.clone.back_ref) | copy-start | bytes 331780
  36.2 5.6 %copy-start.3 = (s32[4]{0:T(128)S(1)}, s32[4]{0:T(128)}, u32[]{:S(2)}) copy-start(s32[4]{0:T(128)} %token_ref.1) | copy-start | bytes 52
  47.0 8.3 %collective-permute-start.15 = (f32[4,72,256]{2,1,0:T(8,128)S(1)}, f32[4,72,256]{2,1,0:T(8,128)S(1)}, u32[]{:S(2)}, u32[]{:S(2)}) collective-permute-start(f32[4,72,256]{2,1,0:T(8,128)S(1)} %get-tuple-element.30), channel_id=1, source_target_pairs={{0,1},{1,0},{2,3},{3,2},{4,5},{5,4},{6,7},{7,6},{8,9},{9,8},{10,11... | collective-permute-start | bytes 884744 | tf_op jit(solution)/shard_map/ppermute | solution.py:349
  49.8 19.6 %copy-start.4 = (s32[1,4]{1,0:T(1,128)S(1)}, s32[1,4]{1,0:T(1,128)}, u32[]{:S(2)}) copy-start(s32[1,4]{1,0:T(1,128)} %near_ref.1) | copy-start | bytes 52

commit v10 on v9

--- a/solution.py
+++ b/solution.py
@@ -1,4 +1,3 @@
-import functools
 import math
 
 import jax
@@ -146,7 +145,7 @@
             out_ref[pl.ds(k * 8 + c, events, stride=24), :] = jnp.zeros((events, 128), jnp.float32)
 
 
-def left_kernel(table_ref, b0, b1, b2, b3, out_ref):
+def left_kernel(table_ref, b0, b1, b2, b3, _, out_ref):
     events = out_ref.shape[0] // 24 // 4
     channels = b0.shape[0] // events
     clear_rest(out_ref, channels)
@@ -158,8 +157,7 @@
                 out_ref[to, :] = part[c * events:(c + 1) * events]
 
 
-def right_kernel(table_ref, *refs):
-    pieces, out_ref = refs[:-1], refs[-1]
+def right_spectra(table_ref, pieces, out_ref):
     events = out_ref.shape[0] // 24
     size = pieces[0].shape[0]
     clear_rest(out_ref, len(pieces) * size // events)
@@ -195,13 +193,22 @@
     return ((k // 2 + dz) % (count // 2)) * 2 + (k % 2 + dh) % 2
 
 
-def pair_kernel(across, token_ref, local_ref, remote_ref, left, right, back_ref, out_ref, next_ref, z):
+def first_kernel(lists_ref, left, back_ref, table_ref, *refs):
+    pieces, (out_ref, right, z) = refs[:-3], refs[-3:]
+    right_spectra(table_ref, pieces, right)
+    pair_products(1, lists_ref, left, right, back_ref, out_ref, z)
+
+
+def second_kernel(lists_ref, left, back_ref, right, _, out_ref, z):
+    pair_products(0, lists_ref, left, right, back_ref, out_ref, z)
+
+
+def pair_products(across, lists_ref, left, right, back_ref, out_ref, z):
     width = out_ref.shape[2]
     half = out_ref.shape[0]
-    next_ref[0] = token_ref[0]
     sta = lax.axis_index(STA)
     share = width // 4
-    pairs = local_ref.shape[0] // 4
+    pairs = lists_ref.shape[0] // 8
     back = back_ref[...]
     contract = (((1,), (1,)), ((), ()))
     dot = lambda a, b: lax.dot_general(a, b, contract, preferred_element_type=jnp.float32)
@@ -217,8 +224,8 @@
                 at = q * pairs + first + (g & 7) * 8
                 products = [[], [], []]
                 for p in range(8):
-                    i = pl.multiple_of(local_ref[at + p], 8)
-                    j = pl.multiple_of(remote_ref[at + p], 8)
+                    i = pl.multiple_of(lists_ref[at + p], 8)
+                    j = pl.multiple_of(lists_ref[at + 4 * pairs + p], 8)
                     xa, xb, xc = left[pl.ds(i, 8)], left[pl.ds(i + 8, 8)], left[pl.ds(i + 16, 8)]
                     ya, yb, yc = right[pl.ds(j, 8)], right[pl.ds(j + 8, 8)], right[pl.ds(j + 16, 8)]
                     for col, v in enumerate((xa * ya + xb * yb, xb * ya - xa * yb, xc * yc)):
@@ -322,35 +329,29 @@
     listed = jnp.stack([b[ch * block:ch * block + 2 * pairs // samp] for b in blocks]).astype(jnp.int32)
     listed = listed.reshape(4, 2, pairs) * 24
     first = listed[:, 0] + jnp.arange(4, dtype=jnp.int32)[:, None] * (block * 24)
-    first, second = first.reshape(4 * pairs), listed[:, 1].reshape(4 * pairs)
+    lists = jnp.concatenate([first.reshape(4 * pairs), listed[:, 1].reshape(4 * pairs)])
 
     spectra = shaped((ev * 24, 128), f32)
     cost = pl.CostEstimate(flops=2 * ch * ev * samp * 768, bytes_accessed=4000000, transcendentals=0)
     left = pl.pallas_call(
-        left_kernel, out_shape=spectra, in_specs=[VMEM] * 5, out_specs=VMEM,
+        left_kernel, out_shape=spectra, in_specs=[VMEM] * 5 + [ANY], out_specs=VMEM,
         compiler_params=PARAMS, name="left", cost_estimate=cost,
-    )(left_table, *blocks)
-    right = pl.pallas_call(
-        right_kernel, out_shape=spectra, in_specs=[VMEM] * (1 + len(pieces)), out_specs=VMEM,
-        compiler_params=PARAMS, name="right", cost_estimate=cost,
-    )(right_table, *pieces)
-
-    halves = []
-    token = owners
-    for across in (1, 0):
-        raw, token = pl.pallas_call(
-            functools.partial(pair_kernel, across),
-            out_shape=(shaped((n_sta // 2, ROWS, 4 * share), f32), shaped((steps,), jnp.int32)),
-            in_specs=[SMEM] * 3 + [VMEM] * 3, out_specs=(VMEM, SMEM),
-            scratch_shapes=[pltpu.VMEM((4 * share, 384), f32)],
-            compiler_params=PARAMS, name="pairs", cost_estimate=cost,
-        )(token, first, second, left, right, back_table)
-        halves.append(raw)
+    )(left_table, *blocks, pieces[1])
+    raw = shaped((n_sta // 2, ROWS, 4 * share), f32)
+    products = pltpu.VMEM((4 * share, 384), f32)
+    far, right = pl.pallas_call(
+        first_kernel, out_shape=(raw, spectra), in_specs=[SMEM] + [VMEM] * (3 + len(pieces)), out_specs=(VMEM,) * 2,
+        scratch_shapes=[products], compiler_params=PARAMS, name="first", cost_estimate=cost,
+    )(lists, left, back_table, right_table, *pieces)
+    here = pl.pallas_call(
+        second_kernel, out_shape=raw, in_specs=[SMEM] + [VMEM] * 3 + [ANY], out_specs=VMEM,
+        scratch_shapes=[products], compiler_params=PARAMS, name="second", cost_estimate=cost,
+    )(lists, left, back_table, right, far)
     hop = lambda v, dz, dh: lax.ppermute(v, STA, [(k, target(k, dz, dh, n_sta)) for k in range(n_sta)])
     slots = pl.pallas_call(
         add_kernel, out_shape=shaped((2 * n_sta, TALL, 2 * share), f32), in_specs=[VMEM] * 2, out_specs=VMEM,
         compiler_params=SMALL, name="add",
-    )(hop(halves[0], 0, 1), halves[1])
+    )(hop(far, 0, 1), here)
     slots = lax.all_to_all(slots, ("z", "xl", "core"), 0, 0)
     out = pl.pallas_call(
         final_kernel, out_shape=shaped((1, steps, share, LAGS), f32),

time: 71.3 us -> 73.2 us (1.027)
  Pallas kernels: 18.8 us -> 20.6 us
  waiting for transfers between devices: 16.3 us -> 14.9 us
  local copies, waits for them, and re-layouts: 0.21 us -> 1.55 us
    ppermute x6, waiting for transfers between devices: 4.36 us -> 3.46 us  [local(): lax.ppermute(v, CLU, [(i, i ^ d) for i in range(n_clu)])]
    pallas_call x4 -> x3, Pallas kernels: 12.7 us -> 13.2 us  [the longest x1 6.14 us: local(): pl.pallas_call(first_kernel, out_shape=(raw, spectra), in_specs=[SMEM] +...]
  transfers between devices with their start and end apart: 16 -> 16, of which waited for: 8 -> 7; matrix products, arithmetic and copies ran while one was open for 0% -> 2% of each run, Pallas kernels for 13% -> 15%
where the time goes in v10:
time: 73.2 us; the launch traced here: 72.6 us
  starting transfers between devices  21.4 us (29%)
  Pallas kernels  20.6 us (28%)
  waiting for transfers between devices  14.9 us (20%)
  blocking collectives  14 us (19%)
  local copies, waits for them, and re-layouts  1.55 us (2%)
    ppermute x9, starting transfers between devices, local(): lax.ppermute(v, CLU, [(i, (i + 4 * d) % n_clu) for i in range(n_clu)])  14.3 us
    all_to_all x1, blocking collectives, local(): slots = lax.all_to_all(slots, ('z', 'xl', 'core'), 0, 0)  14 us
    ppermute x9, waiting for transfers between devices, local(): lax.ppermute(v, CLU, [(i, (i + 4 * d) % n_clu) for i in range(n_clu)])  10.9 us
    pallas_call x1, Pallas kernels, local(): pl.pallas_call(first_kernel, out_shape=(raw, spectra), in_specs=[SMEM] +...  6.14 us
    pallas_call x1, Pallas kernels, local(): pl.pallas_call(second_kernel, out_shape=raw, in_specs=[SMEM] + [VMEM] * 3...  4.9 us
    ppermute x6, starting transfers between devices, local(): lax.ppermute(v, CLU, [(i, i ^ d) for i in range(n_clu)])  4.29 us
    ppermute x6, waiting for transfers between devices, local(): lax.ppermute(v, CLU, [(i, i ^ d) for i in range(n_clu)])  3.46 us
    ppermute x1, starting transfers between devices, local(): lax.ppermute(v, STA, [(k, target(k, dz, dh, n_sta)) for k in range(n_sta)])  2.78 us
  transfers between devices with their start and end apart: 16, of which 7 were waited for; matrix products, arithmetic and copies ran while one was open for 2% of the time, Pallas kernels for 15%

profile of v10, /device:TPU:0, one launch (start us, length us, event | category | flops | bytes accessed | tf_op | source)
XLA Modules:
  0.0 72.6 jit_solution(8204900628582257274)
XLA Ops:
  0.0 2.4 %pack.1 = (bf16[384,256]{1,0:T(8,128)(2,1)S(1)}, bf16[384,256]{1,0:T(8,128)(2,1)S(1)}, bf16[384,256]{1,0:T(8,128)(2,1)S(1)}, bf16[384,256]{1,0:T(8,128)(2,1)S(1)...) custom-call(bf16[1536,256]{1,0:T(8,128)(2,1)} %bitcast.13, ...), custom_call_target="tpu_custom_call" | custom-call | tf_op jit(solution)/shard_map/pack/pallas_call | solution.py:303
  2.4 1.7 %collective-permute-start.1 = (bf16[2,400,256]{2,1,0:T(8,128)(2,1)S(1)}, bf16[2,400,256]{2,1,0:T(8,128)(2,1)S(1)}, u32[]{:S(2)}, u32[]{:S(2)}) collective-permute-start(bf16[2,400,256]{2,1,0:T(8,128)(2,1)S(1)} %get-tuple-element.20), channel_id=1, source_target_pairs={{0,16},{8,24},{16,0},{24,8},{32,48},{40,56},{48,32},{56,40},{64,80... | collective-permute-start | bytes 1228808 | tf_op jit(solution)/shard_map/ppermute | solution.py:296
  4.0 1.6 %collective-permute-start.3 = (bf16[384,256]{1,0:T(8,128)(2,1)S(1)}, bf16[384,256]{1,0:T(8,128)(2,1)S(1)}, u32[]{:S(2)}, u32[]{:S(2)}) collective-permute-start(bf16[384,256]{1,0:T(8,128)(2,1)S(1)} %get-tuple-element.22), channel_id=1, source_target_pairs={{0,32},{8,40},{16,48},{24,56},{32,64},{40,72},{48,80},{56,88},{64,... | collective-permute-start | bytes 589832 | tf_op jit(solution)/shard_map/ppermute | solution.py:297
  5.6 2.9 %collective-permute-start.4 = (bf16[384,256]{1,0:T(8,128)(2,1)S(1)}, bf16[384,256]{1,0:T(8,128)(2,1)S(1)}, u32[]{:S(2)}, u32[]{:S(2)}) collective-permute-start(bf16[384,256]{1,0:T(8,128)(2,1)S(1)} %get-tuple-element.23), channel_id=1, source_target_pairs={{0,64},{8,72},{16,80},{24,88},{32,96},{40,104},{48,112},{56,120},{... | collective-permute-start | bytes 589832 | tf_op jit(solution)/shard_map/ppermute | solution.py:297
  8.5 1.3 %collective-permute-start.5 = (bf16[384,256]{1,0:T(8,128)(2,1)S(1)}, bf16[384,256]{1,0:T(8,128)(2,1)S(1)}, u32[]{:S(2)}, u32[]{:S(2)}) collective-permute-start(bf16[384,256]{1,0:T(8,128)(2,1)S(1)} %get-tuple-element.24), channel_id=1, source_target_pairs={{0,96},{8,104},{16,112},{24,120},{32,0},{40,8},{48,16},{56,24},{64... | collective-permute-start | bytes 589832 | tf_op jit(solution)/shard_map/ppermute | solution.py:297
  9.9 2.1 %collective-permute-done.3.g1 = bf16[384,256]{1,0:T(8,128)(2,1)S(1)} collective-permute-done((bf16[384,256]{1,0:T(8,128)(2,1)S(1)}, bf16[384,256]{1,0:T(8,128)(2,1)S(1)}, u32[]{:S(2)}, u32[]{:S(2)}) %collective-permute-start.3) | collective-permute-done | bytes 196640 | tf_op jit(solution)/shard_map/ppermute | solution.py:297
  11.9 5.1 %collective-permute-done.4.g2 = bf16[384,256]{1,0:T(8,128)(2,1)S(1)} collective-permute-done((bf16[384,256]{1,0:T(8,128)(2,1)S(1)}, bf16[384,256]{1,0:T(8,128)(2,1)S(1)}, u32[]{:S(2)}, u32[]{:S(2)}) %collective-permute-start.4) | collective-permute-done | bytes 196640 | tf_op jit(solution)/shard_map/ppermute | solution.py:297
  17.1 0.7 %pick.1 = bf16[2,384,256]{2,1,0:T(8,128)(2,1)S(1)} custom-call(s32[4]{0:T(128)} %owners_ref.7, bf16[384,256]{1,0:T(8,128)(2,1)S(1)} %get-tuple-element.21.g0, bf16[384,256]{1,0:T(8,128)(2,1)S(1)} %collective-permute-done.3.g1, bf16[384,256]{1,0:T(8,128)(2,1)S(1)} %collective-permute-done.4.g2, bf16[384,256]{1,0:T(8,128)(2,1)S(1)} %collective-permute-done.5.g3), custom_call_target="tpu_custom_call" | custom-call | tf_op jit(solution)/shard_map/pick/pallas_call | solution.py:312
  19.6 1.4 %over_core.1 = (bf16[192,256]{1,0:T(8,128)(2,1)S(1)}, bf16[192,256]{1,0:T(8,128)(2,1)S(1)}, bf16[192,256]{1,0:T(8,128)(2,1)}, bf16[192,256]{1,0:T(8,128)(2,1)}) custom-call(s32[4]{0:T(128)} %owners_ref.7, bf16[384,256]{1,0:T(8,128)(2,1)S(1)} %get-tuple-element.21.g0, bf16[384,256]{1,0:T(8,128)(2,1)S(1)} %collective-permute-done.3.g1, ...), custom_call_target="tpu_custom_call" | custom-call | tf_op jit(solution)/shard_map/over_core/pallas_call | solution.py:317
  21.6 1.5 %collective-permute-start.11 = (bf16[192,256]{1,0:T(8,128)(2,1)}, bf16[192,256]{1,0:T(8,128)(2,1)S(1)}, u32[]{:S(2)}, u32[]{:S(2)}) collective-permute-start(bf16[192,256]{1,0:T(8,128)(2,1)} %get-tuple-element.28), channel_id=1, source_target_pairs={{0,16},{8,24},{16,0},{24,8},{32,48},{40,56},{48,32},{56,40},{64,80... | collective-permute-start | bytes 294920 | tf_op jit(solution)/shard_map/ppermute | solution.py:296
  23.8 3.1 %collective-permute-done.7.got_ref = bf16[192,256]{1,0:T(8,128)(2,1)S(1)} collective-permute-done((bf16[192,256]{1,0:T(8,128)(2,1)}, bf16[192,256]{1,0:T(8,128)(2,1)S(1)}, u32[]{:S(2)}, u32[]{:S(2)}) %collective-permute-start.7) | collective-permute-done | bytes 98336 | tf_op jit(solution)/shard_map/ppermute | solution.py:296
  27.6 1.2 %collective-permute-start.8 = (bf16[192,256]{1,0:T(8,128)(2,1)S(1)}, bf16[192,256]{1,0:T(8,128)(2,1)S(1)}, u32[]{:S(2)}, u32[]{:S(2)}) collective-permute-start(bf16[192,256]{1,0:T(8,128)(2,1)S(1)} %over_x.2.refs_0_), channel_id=1, source_target_pairs={{0,32},{8,40},{16,48},{24,56},{32,64},{40,72},{48,80},{56,88},{64,... | collective-permute-start | bytes 294920 | tf_op jit(solution)/shard_map/ppermute | solution.py:297
  28.9 2.5 %collective-permute-start.10 = (bf16[192,256]{1,0:T(8,128)(2,1)S(1)}, bf16[192,256]{1,0:T(8,128)(2,1)S(1)}, u32[]{:S(2)}, u32[]{:S(2)}) collective-permute-start(bf16[192,256]{1,0:T(8,128)(2,1)S(1)} %over_x.2.refs_0_), channel_id=1, source_target_pairs={{0,64},{8,72},{16,80},{24,88},{32,96},{40,104},{48,112},{56,120},{... | collective-permute-start | bytes 294920 | tf_op jit(solution)/shard_map/ppermute | solution.py:297
  31.3 1.7 %collective-permute-start.9 = (bf16[192,256]{1,0:T(8,128)(2,1)S(1)}, bf16[192,256]{1,0:T(8,128)(2,1)S(1)}, u32[]{:S(2)}, u32[]{:S(2)}) collective-permute-start(bf16[192,256]{1,0:T(8,128)(2,1)S(1)} %over_x.2.refs_0_), channel_id=1, source_target_pairs={{0,96},{8,104},{16,112},{24,120},{32,0},{40,8},{48,16},{56,24},{64... | collective-permute-start | bytes 294920 | tf_op jit(solution)/shard_map/ppermute | solution.py:297
  33.7 1.0 %collective-permute-start.14 = (bf16[192,256]{1,0:T(8,128)(2,1)S(1)}, bf16[192,256]{1,0:T(8,128)(2,1)S(1)}, u32[]{:S(2)}, u32[]{:S(2)}) collective-permute-start(bf16[192,256]{1,0:T(8,128)(2,1)S(1)} %over_x.3.refs_4_), channel_id=1, source_target_pairs={{0,64},{8,72},{16,80},{24,88},{32,96},{40,104},{48,112},{56,120},{... | collective-permute-start | bytes 294920 | tf_op jit(solution)/shard_map/ppermute | solution.py:297
  34.8 2.1 %collective-permute-start.13 = (bf16[192,256]{1,0:T(8,128)(2,1)S(1)}, bf16[192,256]{1,0:T(8,128)(2,1)S(1)}, u32[]{:S(2)}, u32[]{:S(2)}) collective-permute-start(bf16[192,256]{1,0:T(8,128)(2,1)S(1)} %over_x.3.refs_4_), channel_id=1, source_target_pairs={{0,96},{8,104},{16,112},{24,120},{32,0},{40,8},{48,16},{56,24},{64... | collective-permute-start | bytes 294920 | tf_op jit(solution)/shard_map/ppermute | solution.py:297
  36.8 2.1 %left.1 = f32[6144,128]{1,0:T(8,128)S(1)} custom-call(bf16[256,768]{1,0:T(8,128)(2,1)S(1)} %copy-done.2, bf16[400,256]{1,0:T(8,128)(2,1)S(1)} %get-tuple-element.18.b0, bf16[400,256]{1,0:T(8,128)(2,1)S(1)} %collective-permute-done.b1, bf16[400,256]{1,0:T(8,128)(2,1)S(1)} %get-tuple-element.31.b2, bf16[400,256]{1,0:T(8,128)(2,1)} %collective-permute-done.2.b3, ...), custom_call_target="tpu_custom_call" | custom-call | flops 603979776 | bytes 4000000 | tf_op jit(solution)/shard_map/left/pallas_call | solution.py:336
  39.0 0.9 %collective-permute-done.14.refs_7_ = bf16[192,256]{1,0:T(8,128)(2,1)S(1)} collective-permute-done((bf16[192,256]{1,0:T(8,128)(2,1)S(1)}, bf16[192,256]{1,0:T(8,128)(2,1)S(1)}, u32[]{:S(2)}, u32[]{:S(2)}) %collective-permute-start.14) | collective-permute-done | bytes 98336 | tf_op jit(solution)/shard_map/ppermute | solution.py:297
  39.9 2.7 %collective-permute-done.12.refs_5_ = bf16[192,256]{1,0:T(8,128)(2,1)S(1)} collective-permute-done((bf16[192,256]{1,0:T(8,128)(2,1)S(1)}, bf16[192,256]{1,0:T(8,128)(2,1)S(1)}, u32[]{:S(2)}, u32[]{:S(2)}) %collective-permute-start.12) | collective-permute-done | bytes 98336 | tf_op jit(solution)/shard_map/ppermute | solution.py:297
  42.7 6.1 %first.1 = (f32[4,72,256]{2,1,0:T(8,128)S(1)}, f32[6144,128]{1,0:T(8,128)S(1)}) custom-call(s32[4096]{0:T(1024)S(1)} %pad_add_fusion.lists_ref, f32[6144,128]{1,0:T(8,128)S(1)} %left.1, bf16[144,384]{1,0:T(8,128)(2,1)S(1)} %copy-done, bf16[256,768]{1,0:T(8,128)(2,1)S(1)} %copy-done.1, bf16[192,256]{1,0:T(8,128)(2,1)S(1)} %over_x.2.refs_0_, ...), custom_call_target="tpu_custom_call" | custom-call | flops 603979776 | bytes 4000000 | tf_op jit(solution)/shard_map/first/pallas_call | solution.py:342
  48.8 2.8 %collective-permute-start.15 = (f32[4,72,256]{2,1,0:T(8,128)S(1)}, f32[4,72,256]{2,1,0:T(8,128)S(1)}, u32[]{:S(2)}, u32[]{:S(2)}) collective-permute-start(f32[4,72,256]{2,1,0:T(8,128)S(1)} %get-tuple-element.29._), channel_id=1, source_target_pairs={{0,1},{1,0},{2,3},{3,2},{4,5},{5,4},{6,7},{7,6},{8,9},{9,8},{10,11... | collective-permute-start | bytes 884744 | tf_op jit(solution)/shard_map/ppermute | solution.py:350
  51.6 4.9 %second.1.b_ref = f32[4,72,256]{2,1,0:T(8,128)S(1)} custom-call(s32[4096]{0:T(1024)S(1)} %pad_add_fusion.lists_ref, f32[6144,128]{1,0:T(8,128)S(1)} %left.1, bf16[144,384]{1,0:T(8,128)(2,1)S(1)} %copy-done, f32[6144,128]{1,0:T(8,128)S(1)} %get-tuple-element.30.right, f32[4,72,256]{2,1,0:T(8,128)S(1)} %get-tuple-element.29._), custom_call_target="tpu_custom_call" | custom-call | flops 603979776 | bytes 4000000 | tf_op jit(solution)/shard_map/second/pallas_call | solution.py:346
  57.3 14.0 %all_to_all.5.got_ref = f32[16,40,128]{2,1,0:T(8,128)S(1)} all-to-all(f32[16,40,128]{2,1,0:T(8,128)S(1)} %add.18), channel_id=1, replica_groups=mesh['y'=4,'xl'=2,'core'=2,'z'=4,'xh'=2] {'z','xl','core'}, dimensions={0} | all-to-all | bytes 655360 | tf_op jit(solution)/shard_map/all_to_all | solution.py:355
  71.2 1.4 %finish.1 = f32[1,4,64,65]{3,2,1,0:T(8,128)} custom-call(s32[1,4]{1,0:T(1,128)S(1)} %copy-done.3, f32[16,40,128]{2,1,0:T(8,128)S(1)} %all_to_all.5.got_ref), custom_call_target="tpu_custom_call" | custom-call | tf_op jit(solution)/shard_map/finish/pallas_call | solution.py:356
  (43 shorter events, 5.2 us)
Async XLA Ops:
  0.0 36.8 %copy-start.2 = (bf16[256,768]{1,0:T(8,128)(2,1)S(1)}, bf16[256,768]{1,0:T(8,128)(2,1)}, u32[]{:S(2)}) copy-start(bf16[256,768]{1,0:T(8,128)(2,1)} %constant.10.clone.table_ref) | copy-start | bytes 1179652
  2.4 15.5 %collective-permute-start.1 = (bf16[2,400,256]{2,1,0:T(8,128)(2,1)S(1)}, bf16[2,400,256]{2,1,0:T(8,128)(2,1)S(1)}, u32[]{:S(2)}, u32[]{:S(2)}) collective-permute-start(bf16[2,400,256]{2,1,0:T(8,128)(2,1)S(1)} %get-tuple-element.20), channel_id=1, source_target_pairs={{0,16},{8,24},{16,0},{24,8},{32,48},{40,56},{48,32},{56,40},{64,80... | collective-permute-start | bytes 1228808 | tf_op jit(solution)/shard_map/ppermute | solution.py:296
  4.0 7.9 %collective-permute-start.3 = (bf16[384,256]{1,0:T(8,128)(2,1)S(1)}, bf16[384,256]{1,0:T(8,128)(2,1)S(1)}, u32[]{:S(2)}, u32[]{:S(2)}) collective-permute-start(bf16[384,256]{1,0:T(8,128)(2,1)S(1)} %get-tuple-element.22), channel_id=1, source_target_pairs={{0,32},{8,40},{16,48},{24,56},{32,64},{40,72},{48,80},{56,88},{64,... | collective-permute-start | bytes 589832 | tf_op jit(solution)/shard_map/ppermute | solution.py:297
  5.6 11.4 %collective-permute-start.4 = (bf16[384,256]{1,0:T(8,128)(2,1)S(1)}, bf16[384,256]{1,0:T(8,128)(2,1)S(1)}, u32[]{:S(2)}, u32[]{:S(2)}) collective-permute-start(bf16[384,256]{1,0:T(8,128)(2,1)S(1)} %get-tuple-element.23), channel_id=1, source_target_pairs={{0,64},{8,72},{16,80},{24,88},{32,96},{40,104},{48,112},{56,120},{... | collective-permute-start | bytes 589832 | tf_op jit(solution)/shard_map/ppermute | solution.py:297
  8.5 8.6 %collective-permute-start.5 = (bf16[384,256]{1,0:T(8,128)(2,1)S(1)}, bf16[384,256]{1,0:T(8,128)(2,1)S(1)}, u32[]{:S(2)}, u32[]{:S(2)}) collective-permute-start(bf16[384,256]{1,0:T(8,128)(2,1)S(1)} %get-tuple-element.24), channel_id=1, source_target_pairs={{0,96},{8,104},{16,112},{24,120},{32,0},{40,8},{48,16},{56,24},{64... | collective-permute-start | bytes 589832 | tf_op jit(solution)/shard_map/ppermute | solution.py:297
  9.9 9.3 %collective-permute-start = (bf16[400,256]{1,0:T(8,128)(2,1)}, bf16[400,256]{1,0:T(8,128)(2,1)S(1)}, u32[]{:S(2)}, u32[]{:S(2)}) collective-permute-start(bf16[400,256]{1,0:T(8,128)(2,1)} %get-tuple-element.19), channel_id=1, source_target_pairs={{0,8},{8,0},{16,24},{24,16},{32,40},{40,32},{48,56},{56,48},{64,72... | collective-permute-start | bytes 614408 | tf_op jit(solution)/shard_map/ppermute | solution.py:296
  17.8 1.8 %collective-permute-start.6 = (bf16[2,384,256]{2,1,0:T(8,128)(2,1)S(1)}, bf16[2,384,256]{2,1,0:T(8,128)(2,1)S(1)}, u32[]{:S(2)}, u32[]{:S(2)}) collective-permute-start(bf16[2,384,256]{2,1,0:T(8,128)(2,1)S(1)} %pick.1), channel_id=1, source_target_pairs={{0,8},{8,0},{16,24},{24,16},{32,40},{40,32},{48,56},{56,48},{64,72... | collective-permute-start | bytes 1179656 | tf_op jit(solution)/shard_map/ppermute | solution.py:296
  18.6 4.5 %collective-permute-start.2 = (bf16[400,256]{1,0:T(8,128)(2,1)}, bf16[400,256]{1,0:T(8,128)(2,1)}, u32[]{:S(2)}, u32[]{:S(2)}) collective-permute-start(bf16[400,256]{1,0:T(8,128)(2,1)} %get-tuple-element.32), channel_id=1, source_target_pairs={{0,8},{8,0},{16,24},{24,16},{32,40},{40,32},{48,56},{56,48},{64,72... | collective-permute-start | bytes 614408 | tf_op jit(solution)/shard_map/ppermute | solution.py:296
  19.3 23.4 %copy-start = (bf16[144,384]{1,0:T(8,128)(2,1)S(1)}, bf16[144,384]{1,0:T(8,128)(2,1)}, u32[]{:S(2)}) copy-start(bf16[144,384]{1,0:T(8,128)(2,1)} %constant.12.clone.back_ref) | copy-start | bytes 331780
  19.3 23.4 %copy-start.1 = (bf16[256,768]{1,0:T(8,128)(2,1)S(1)}, bf16[256,768]{1,0:T(8,128)(2,1)}, u32[]{:S(2)}) copy-start(bf16[256,768]{1,0:T(8,128)(2,1)} %constant.11.clone.table_ref) | copy-start | bytes 1179652
  21.0 5.9 %collective-permute-start.7 = (bf16[192,256]{1,0:T(8,128)(2,1)}, bf16[192,256]{1,0:T(8,128)(2,1)S(1)}, u32[]{:S(2)}, u32[]{:S(2)}) collective-permute-start(bf16[192,256]{1,0:T(8,128)(2,1)} %get-tuple-element.26), channel_id=1, source_target_pairs={{0,16},{8,24},{16,0},{24,8},{32,48},{40,56},{48,32},{56,40},{64,80... | collective-permute-start | bytes 294920 | tf_op jit(solution)/shard_map/ppermute | solution.py:296
  21.6 11.4 %collective-permute-start.11 = (bf16[192,256]{1,0:T(8,128)(2,1)}, bf16[192,256]{1,0:T(8,128)(2,1)S(1)}, u32[]{:S(2)}, u32[]{:S(2)}) collective-permute-start(bf16[192,256]{1,0:T(8,128)(2,1)} %get-tuple-element.28), channel_id=1, source_target_pairs={{0,16},{8,24},{16,0},{24,8},{32,48},{40,56},{48,32},{56,40},{64,80... | collective-permute-start | bytes 294920 | tf_op jit(solution)/shard_map/ppermute | solution.py:296
  27.6 9.2 %collective-permute-start.8 = (bf16[192,256]{1,0:T(8,128)(2,1)S(1)}, bf16[192,256]{1,0:T(8,128)(2,1)S(1)}, u32[]{:S(2)}, u32[]{:S(2)}) collective-permute-start(bf16[192,256]{1,0:T(8,128)(2,1)S(1)} %over_x.2.refs_0_), channel_id=1, source_target_pairs={{0,32},{8,40},{16,48},{24,56},{32,64},{40,72},{48,80},{56,88},{64,... | collective-permute-start | bytes 294920 | tf_op jit(solution)/shard_map/ppermute | solution.py:297
  28.9 10.1 %collective-permute-start.10 = (bf16[192,256]{1,0:T(8,128)(2,1)S(1)}, bf16[192,256]{1,0:T(8,128)(2,1)S(1)}, u32[]{:S(2)}, u32[]{:S(2)}) collective-permute-start(bf16[192,256]{1,0:T(8,128)(2,1)S(1)} %over_x.2.refs_0_), channel_id=1, source_target_pairs={{0,64},{8,72},{16,80},{24,88},{32,96},{40,104},{48,112},{56,120},{... | collective-permute-start | bytes 294920 | tf_op jit(solution)/shard_map/ppermute | solution.py:297
  31.3 7.6 %collective-permute-start.9 = (bf16[192,256]{1,0:T(8,128)(2,1)S(1)}, bf16[192,256]{1,0:T(8,128)(2,1)S(1)}, u32[]{:S(2)}, u32[]{:S(2)}) collective-permute-start(bf16[192,256]{1,0:T(8,128)(2,1)S(1)} %over_x.2.refs_0_), channel_id=1, source_target_pairs={{0,96},{8,104},{16,112},{24,120},{32,0},{40,8},{48,16},{56,24},{64... | collective-permute-start | bytes 294920 | tf_op jit(solution)/shard_map/ppermute | solution.py:297
  33.7 6.2 %collective-permute-start.14 = (bf16[192,256]{1,0:T(8,128)(2,1)S(1)}, bf16[192,256]{1,0:T(8,128)(2,1)S(1)}, u32[]{:S(2)}, u32[]{:S(2)}) collective-permute-start(bf16[192,256]{1,0:T(8,128)(2,1)S(1)} %over_x.3.refs_4_), channel_id=1, source_target_pairs={{0,64},{8,72},{16,80},{24,88},{32,96},{40,104},{48,112},{56,120},{... | collective-permute-start | bytes 294920 | tf_op jit(solution)/shard_map/ppermute | solution.py:297
  34.8 5.2 %collective-permute-start.13 = (bf16[192,256]{1,0:T(8,128)(2,1)S(1)}, bf16[192,256]{1,0:T(8,128)(2,1)S(1)}, u32[]{:S(2)}, u32[]{:S(2)}) collective-permute-start(bf16[192,256]{1,0:T(8,128)(2,1)S(1)} %over_x.3.refs_4_), channel_id=1, source_target_pairs={{0,96},{8,104},{16,112},{24,120},{32,0},{40,8},{48,16},{56,24},{64... | collective-permute-start | bytes 294920 | tf_op jit(solution)/shard_map/ppermute | solution.py:297
  36.8 5.8 %collective-permute-start.12 = (bf16[192,256]{1,0:T(8,128)(2,1)S(1)}, bf16[192,256]{1,0:T(8,128)(2,1)S(1)}, u32[]{:S(2)}, u32[]{:S(2)}) collective-permute-start(bf16[192,256]{1,0:T(8,128)(2,1)S(1)} %over_x.3.refs_4_), channel_id=1, source_target_pairs={{0,32},{8,40},{16,48},{24,56},{32,64},{40,72},{48,80},{56,88},{64,... | collective-permute-start | bytes 294920 | tf_op jit(solution)/shard_map/ppermute | solution.py:297
  48.8 8.3 %collective-permute-start.15 = (f32[4,72,256]{2,1,0:T(8,128)S(1)}, f32[4,72,256]{2,1,0:T(8,128)S(1)}, u32[]{:S(2)}, u32[]{:S(2)}) collective-permute-start(f32[4,72,256]{2,1,0:T(8,128)S(1)} %get-tuple-element.29._), channel_id=1, source_target_pairs={{0,1},{1,0},{2,3},{3,2},{4,5},{5,4},{6,7},{7,6},{8,9},{9,8},{10,11... | collective-permute-start | bytes 884744 | tf_op jit(solution)/shard_map/ppermute | solution.py:350
  51.6 19.7 %copy-start.3 = (s32[1,4]{1,0:T(1,128)S(1)}, s32[1,4]{1,0:T(1,128)}, u32[]{:S(2)}) copy-start(s32[1,4]{1,0:T(1,128)} %near_ref.1) | copy-start | bytes 52

commit v11 on v9

--- a/solution.py
+++ b/solution.py
@@ -195,10 +195,10 @@
     return ((k // 2 + dz) % (count // 2)) * 2 + (k % 2 + dh) % 2
 
 
-def pair_kernel(across, token_ref, local_ref, remote_ref, left, right, back_ref, out_ref, next_ref, z):
+def pair_kernel(across, local_ref, remote_ref, left, right, back_ref, *refs):
+    out_ref, z = refs[-2:]
     width = out_ref.shape[2]
     half = out_ref.shape[0]
-    next_ref[0] = token_ref[0]
     sta = lax.axis_index(STA)
     share = width // 4
     pairs = local_ref.shape[0] // 4
@@ -336,16 +336,13 @@
     )(right_table, *pieces)
 
     halves = []
-    token = owners
     for across in (1, 0):
-        raw, token = pl.pallas_call(
-            functools.partial(pair_kernel, across),
-            out_shape=(shaped((n_sta // 2, ROWS, 4 * share), f32), shaped((steps,), jnp.int32)),
-            in_specs=[SMEM] * 3 + [VMEM] * 3, out_specs=(VMEM, SMEM),
+        halves.append(pl.pallas_call(
+            functools.partial(pair_kernel, across), out_shape=shaped((n_sta // 2, ROWS, 4 * share), f32),
+            in_specs=[SMEM] * 2 + [VMEM] * 3 + [ANY] * len(halves), out_specs=VMEM,
             scratch_shapes=[pltpu.VMEM((4 * share, 384), f32)],
             compiler_params=PARAMS, name="pairs", cost_estimate=cost,
-        )(token, first, second, left, right, back_table)
-        halves.append(raw)
+        )(first, second, left, right, back_table, *halves))
     hop = lambda v, dz, dh: lax.ppermute(v, STA, [(k, target(k, dz, dh, n_sta)) for k in range(n_sta)])
     slots = pl.pallas_call(
         add_kernel, out_shape=shaped((2 * n_sta, TALL, 2 * share), f32), in_specs=[VMEM] * 2, out_specs=VMEM,

time: 71.3 us -> 71 us (level)
  no operation moved by 1% of the time
where the time goes in v11:
time: 71 us; the launch traced here: 70.5 us
  starting transfers between devices  21.4 us (30%)
  Pallas kernels  18.2 us (26%)
  waiting for transfers between devices  16.5 us (23%)
  blocking collectives  14 us (20%)
    ppermute x9, starting transfers between devices, local(): lax.ppermute(v, CLU, [(i, (i + 4 * d) % n_clu) for i in range(n_clu)])  14 us
    all_to_all x1, blocking collectives, local(): slots = lax.all_to_all(slots, ('z', 'xl', 'core'), 0, 0)  14 us
    ppermute x9, waiting for transfers between devices, local(): lax.ppermute(v, CLU, [(i, (i + 4 * d) % n_clu) for i in range(n_clu)])  11.5 us
    pallas_call x2, Pallas kernels, local(): pl.pallas_call(functools.partial(pair_kernel, across), out_shape=shaped((...  9.7 us
    ppermute x6, starting transfers between devices, local(): lax.ppermute(v, CLU, [(i, i ^ d) for i in range(n_clu)])  4.58 us
    ppermute x6, waiting for transfers between devices, local(): lax.ppermute(v, CLU, [(i, i ^ d) for i in range(n_clu)])  4.36 us
    ppermute x1, starting transfers between devices, local(): lax.ppermute(v, STA, [(k, target(k, dz, dh, n_sta)) for k in range(n_sta)])  2.81 us
    pallas_call x1, Pallas kernels, local(): pl.pallas_call(pack_kernel, out_shape=(piece,) * 4 + (payload, payload, s...  1.7 us
  transfers between devices with their start and end apart: 16, of which 8 were waited for; matrix products, arithmetic and copies ran while one was open for 0% of the time, Pallas kernels for 13%

profile of v11, /device:TPU:0, one launch (start us, length us, event | category | flops | bytes accessed | tf_op | source)
XLA Modules:
  0.0 70.5 jit_solution(7022458445617691258)
XLA Ops:
  0.0 1.7 %pack.1 = (bf16[384,256]{1,0:T(8,128)(2,1)S(1)}, bf16[384,256]{1,0:T(8,128)(2,1)S(1)}, bf16[384,256]{1,0:T(8,128)(2,1)S(1)}, bf16[384,256]{1,0:T(8,128)(2,1)S(1)...) custom-call(bf16[1536,256]{1,0:T(8,128)(2,1)} %bitcast.15, ...), custom_call_target="tpu_custom_call" | custom-call | tf_op jit(solution)/shard_map/pack/pallas_call | solution.py:296
  1.7 1.6 %collective-permute-start.1 = (bf16[2,400,256]{2,1,0:T(8,128)(2,1)S(1)}, bf16[2,400,256]{2,1,0:T(8,128)(2,1)S(1)}, u32[]{:S(2)}, u32[]{:S(2)}) collective-permute-start(bf16[2,400,256]{2,1,0:T(8,128)(2,1)S(1)} %get-tuple-element.18), channel_id=1, source_target_pairs={{0,16},{8,24},{16,0},{24,8},{32,48},{40,56},{48,32},{56,40},{64,80... | collective-permute-start | bytes 1228808 | tf_op jit(solution)/shard_map/ppermute | solution.py:289
  3.4 1.6 %collective-permute-start.3 = (bf16[384,256]{1,0:T(8,128)(2,1)S(1)}, bf16[384,256]{1,0:T(8,128)(2,1)S(1)}, u32[]{:S(2)}, u32[]{:S(2)}) collective-permute-start(bf16[384,256]{1,0:T(8,128)(2,1)S(1)} %get-tuple-element.20), channel_id=1, source_target_pairs={{0,32},{8,40},{16,48},{24,56},{32,64},{40,72},{48,80},{56,88},{64,... | collective-permute-start | bytes 589832 | tf_op jit(solution)/shard_map/ppermute | solution.py:290
  4.9 2.9 %collective-permute-start.4 = (bf16[384,256]{1,0:T(8,128)(2,1)S(1)}, bf16[384,256]{1,0:T(8,128)(2,1)S(1)}, u32[]{:S(2)}, u32[]{:S(2)}) collective-permute-start(bf16[384,256]{1,0:T(8,128)(2,1)S(1)} %get-tuple-element.21), channel_id=1, source_target_pairs={{0,64},{8,72},{16,80},{24,88},{32,96},{40,104},{48,112},{56,120},{... | collective-permute-start | bytes 589832 | tf_op jit(solution)/shard_map/ppermute | solution.py:290
  7.8 1.4 %collective-permute-start.5 = (bf16[384,256]{1,0:T(8,128)(2,1)S(1)}, bf16[384,256]{1,0:T(8,128)(2,1)S(1)}, u32[]{:S(2)}, u32[]{:S(2)}) collective-permute-start(bf16[384,256]{1,0:T(8,128)(2,1)S(1)} %get-tuple-element.22), channel_id=1, source_target_pairs={{0,96},{8,104},{16,112},{24,120},{32,0},{40,8},{48,16},{56,24},{64... | collective-permute-start | bytes 589832 | tf_op jit(solution)/shard_map/ppermute | solution.py:290
  9.2 2.1 %collective-permute-done.3.g1 = bf16[384,256]{1,0:T(8,128)(2,1)S(1)} collective-permute-done((bf16[384,256]{1,0:T(8,128)(2,1)S(1)}, bf16[384,256]{1,0:T(8,128)(2,1)S(1)}, u32[]{:S(2)}, u32[]{:S(2)}) %collective-permute-start.3) | collective-permute-done | bytes 196640 | tf_op jit(solution)/shard_map/ppermute | solution.py:290
  11.3 5.1 %collective-permute-done.4.g2 = bf16[384,256]{1,0:T(8,128)(2,1)S(1)} collective-permute-done((bf16[384,256]{1,0:T(8,128)(2,1)S(1)}, bf16[384,256]{1,0:T(8,128)(2,1)S(1)}, u32[]{:S(2)}, u32[]{:S(2)}) %collective-permute-start.4) | collective-permute-done | bytes 196640 | tf_op jit(solution)/shard_map/ppermute | solution.py:290
  18.0 1.0 %collective-permute-done.6.got_ref = bf16[2,384,256]{2,1,0:T(8,128)(2,1)S(1)} collective-permute-done((bf16[2,384,256]{2,1,0:T(8,128)(2,1)S(1)}, bf16[2,384,256]{2,1,0:T(8,128)(2,1)S(1)}, u32[]{:S(2)}, u32[]{:S(2)}) %collective-permute-start.6) | collective-permute-done | bytes 393248 | tf_op jit(solution)/shard_map/ppermute | solution.py:289
  20.5 1.6 %collective-permute-start.11 = (bf16[192,256]{1,0:T(8,128)(2,1)S(1)}, bf16[192,256]{1,0:T(8,128)(2,1)S(1)}, u32[]{:S(2)}, u32[]{:S(2)}) collective-permute-start(bf16[192,256]{1,0:T(8,128)(2,1)S(1)} %get-tuple-element.26), channel_id=1, source_target_pairs={{0,16},{8,24},{16,0},{24,8},{32,48},{40,56},{48,32},{56,40},{64,80... | collective-permute-start | bytes 294920 | tf_op jit(solution)/shard_map/ppermute | solution.py:289
  22.1 3.4 %collective-permute-done.7.got_ref = bf16[192,256]{1,0:T(8,128)(2,1)S(1)} collective-permute-done((bf16[192,256]{1,0:T(8,128)(2,1)S(1)}, bf16[192,256]{1,0:T(8,128)(2,1)S(1)}, u32[]{:S(2)}, u32[]{:S(2)}) %collective-permute-start.7) | collective-permute-done | bytes 98336 | tf_op jit(solution)/shard_map/ppermute | solution.py:289
  26.1 2.6 %collective-permute-start.10 = (bf16[192,256]{1,0:T(8,128)(2,1)S(1)}, bf16[192,256]{1,0:T(8,128)(2,1)S(1)}, u32[]{:S(2)}, u32[]{:S(2)}) collective-permute-start(bf16[192,256]{1,0:T(8,128)(2,1)S(1)} %over_x.2.refs_0_), channel_id=1, source_target_pairs={{0,64},{8,72},{16,80},{24,88},{32,96},{40,104},{48,112},{56,120},{... | collective-permute-start | bytes 294920 | tf_op jit(solution)/shard_map/ppermute | solution.py:290
  28.8 1.3 %collective-permute-start.9 = (bf16[192,256]{1,0:T(8,128)(2,1)S(1)}, bf16[192,256]{1,0:T(8,128)(2,1)S(1)}, u32[]{:S(2)}, u32[]{:S(2)}) collective-permute-start(bf16[192,256]{1,0:T(8,128)(2,1)S(1)} %over_x.2.refs_0_), channel_id=1, source_target_pairs={{0,96},{8,104},{16,112},{24,120},{32,0},{40,8},{48,16},{56,24},{64... | collective-permute-start | bytes 294920 | tf_op jit(solution)/shard_map/ppermute | solution.py:290
  30.1 0.8 %collective-permute-start.8 = (bf16[192,256]{1,0:T(8,128)(2,1)S(1)}, bf16[192,256]{1,0:T(8,128)(2,1)S(1)}, u32[]{:S(2)}, u32[]{:S(2)}) collective-permute-start(bf16[192,256]{1,0:T(8,128)(2,1)S(1)} %over_x.2.refs_0_), channel_id=1, source_target_pairs={{0,32},{8,40},{16,48},{24,56},{32,64},{40,72},{48,80},{56,88},{64,... | collective-permute-start | bytes 294920 | tf_op jit(solution)/shard_map/ppermute | solution.py:290
  31.6 1.0 %collective-permute-start.14 = (bf16[192,256]{1,0:T(8,128)(2,1)S(1)}, bf16[192,256]{1,0:T(8,128)(2,1)S(1)}, u32[]{:S(2)}, u32[]{:S(2)}) collective-permute-start(bf16[192,256]{1,0:T(8,128)(2,1)S(1)} %over_x.3.refs_4_), channel_id=1, source_target_pairs={{0,64},{8,72},{16,80},{24,88},{32,96},{40,104},{48,112},{56,120},{... | collective-permute-start | bytes 294920 | tf_op jit(solution)/shard_map/ppermute | solution.py:290
  32.6 2.1 %collective-permute-start.13 = (bf16[192,256]{1,0:T(8,128)(2,1)S(1)}, bf16[192,256]{1,0:T(8,128)(2,1)S(1)}, u32[]{:S(2)}, u32[]{:S(2)}) collective-permute-start(bf16[192,256]{1,0:T(8,128)(2,1)S(1)} %over_x.3.refs_4_), channel_id=1, source_target_pairs={{0,96},{8,104},{16,112},{24,120},{32,0},{40,8},{48,16},{56,24},{64... | collective-permute-start | bytes 294920 | tf_op jit(solution)/shard_map/ppermute | solution.py:290
  35.0 1.1 %left.1 = f32[6144,128]{1,0:T(8,128)S(1)} custom-call(bf16[256,768]{1,0:T(8,128)(2,1)S(1)} %copy-done.2, bf16[400,256]{1,0:T(8,128)(2,1)S(1)} %get-tuple-element.16.b0, bf16[400,256]{1,0:T(8,128)(2,1)S(1)} %collective-permute-done.b1, bf16[400,256]{1,0:T(8,128)(2,1)S(1)} %get-tuple-element.27.b2, bf16[400,256]{1,0:T(8,128)(2,1)S(1)} %collective-permute-done.2.b3), custom_call_target="tpu_custom_call" | custom-call | flops 603979776 | bytes 4000000 | tf_op jit(solution)/shard_map/left/pallas_call | solution.py:329
  36.2 1.8 %collective-permute-done.8.refs_1_ = bf16[192,256]{1,0:T(8,128)(2,1)S(1)} collective-permute-done((bf16[192,256]{1,0:T(8,128)(2,1)S(1)}, bf16[192,256]{1,0:T(8,128)(2,1)S(1)}, u32[]{:S(2)}, u32[]{:S(2)}) %collective-permute-start.8) | collective-permute-done | bytes 98336 | tf_op jit(solution)/shard_map/ppermute | solution.py:290
  38.6 1.9 %collective-permute-done.12.refs_5_ = bf16[192,256]{1,0:T(8,128)(2,1)S(1)} collective-permute-done((bf16[192,256]{1,0:T(8,128)(2,1)S(1)}, bf16[192,256]{1,0:T(8,128)(2,1)S(1)}, u32[]{:S(2)}, u32[]{:S(2)}) %collective-permute-start.12) | collective-permute-done | bytes 98336 | tf_op jit(solution)/shard_map/ppermute | solution.py:290
  40.5 1.3 %right.1 = f32[6144,128]{1,0:T(8,128)S(1)} custom-call(bf16[256,768]{1,0:T(8,128)(2,1)S(1)} %copy-done.1, bf16[192,256]{1,0:T(8,128)(2,1)S(1)} %over_x.2.refs_0_, bf16[192,256]{1,0:T(8,128)(2,1)S(1)} %collective-permute-done.8.refs_1_, bf16[192,256]{1,0:T(8,128)(2,1)S(1)} %collective-permute-done.9.refs_2_, ...), custom_call_target="tpu_custom_call" | custom-call | flops 603979776 | bytes 4000000 | tf_op jit(solution)/shard_map/right/pallas_call | solution.py:333
  41.8 4.9 %pairs.2.refs_0_ = f32[4,72,256]{2,1,0:T(8,128)S(1)} custom-call(s32[2048]{0:T(1024)S(1)} %add.14.local_ref, s32[2048]{0:T(1024)S(1)} %bitcast.13, f32[6144,128]{1,0:T(8,128)S(1)} %left.1, f32[6144,128]{1,0:T(8,128)S(1)} %right.1, bf16[144,384]{1,0:T(8,128)(2,1)S(1)} %copy-done), custom_call_target="tpu_custom_call" | custom-call | flops 603979776 | bytes 4000000 | tf_op jit(solution)/shard_map/pairs/pallas_call | solution.py:340
  46.7 2.8 %collective-permute-start.15 = (f32[4,72,256]{2,1,0:T(8,128)S(1)}, f32[4,72,256]{2,1,0:T(8,128)S(1)}, u32[]{:S(2)}, u32[]{:S(2)}) collective-permute-start(f32[4,72,256]{2,1,0:T(8,128)S(1)} %pairs.2.refs_0_), channel_id=1, source_target_pairs={{0,1},{1,0},{2,3},{3,2},{4,5},{5,4},{6,7},{7,6},{8,9},{9,8},{10,11... | collective-permute-start | bytes 884744 | tf_op jit(solution)/shard_map/ppermute | solution.py:346
  49.5 4.8 %pairs.3.b_ref = f32[4,72,256]{2,1,0:T(8,128)S(1)} custom-call(s32[2048]{0:T(1024)S(1)} %add.14.local_ref, s32[2048]{0:T(1024)S(1)} %bitcast.14, f32[6144,128]{1,0:T(8,128)S(1)} %left.1, f32[6144,128]{1,0:T(8,128)S(1)} %right.1, bf16[144,384]{1,0:T(8,128)(2,1)S(1)} %copy-done, f32[4,72,256]{2,1,0:T(8,128)S(1)} %pairs.2.refs_0_), custom_call_target="tpu_custom_call" | custom-call | flops 603979776 | bytes 4000000 | tf_op jit(solution)/shard_map/pairs/pallas_call | solution.py:340
  55.2 14.0 %all_to_all.5.got_ref = f32[16,40,128]{2,1,0:T(8,128)S(1)} all-to-all(f32[16,40,128]{2,1,0:T(8,128)S(1)} %add.16), channel_id=1, replica_groups=mesh['y'=4,'xl'=2,'core'=2,'z'=4,'xh'=2] {'z','xl','core'}, dimensions={0} | all-to-all | bytes 655360 | tf_op jit(solution)/shard_map/all_to_all | solution.py:351
  69.1 1.4 %finish.1 = f32[1,4,64,65]{3,2,1,0:T(8,128)} custom-call(s32[1,4]{1,0:T(1,128)S(1)} %copy-done.3, f32[16,40,128]{2,1,0:T(8,128)S(1)} %all_to_all.5.got_ref), custom_call_target="tpu_custom_call" | custom-call | tf_op jit(solution)/shard_map/finish/pallas_call | solution.py:352
  (43 shorter events, 6.2 us)
Async XLA Ops:
  0.0 35.0 %copy-start.2 = (bf16[256,768]{1,0:T(8,128)(2,1)S(1)}, bf16[256,768]{1,0:T(8,128)(2,1)}, u32[]{:S(2)}) copy-start(bf16[256,768]{1,0:T(8,128)(2,1)} %constant.10.clone.table_ref) | copy-start | bytes 1179652
  1.7 16.0 %collective-permute-start.1 = (bf16[2,400,256]{2,1,0:T(8,128)(2,1)S(1)}, bf16[2,400,256]{2,1,0:T(8,128)(2,1)S(1)}, u32[]{:S(2)}, u32[]{:S(2)}) collective-permute-start(bf16[2,400,256]{2,1,0:T(8,128)(2,1)S(1)} %get-tuple-element.18), channel_id=1, source_target_pairs={{0,16},{8,24},{16,0},{24,8},{32,48},{40,56},{48,32},{56,40},{64,80... | collective-permute-start | bytes 1228808 | tf_op jit(solution)/shard_map/ppermute | solution.py:289
  3.4 7.9 %collective-permute-start.3 = (bf16[384,256]{1,0:T(8,128)(2,1)S(1)}, bf16[384,256]{1,0:T(8,128)(2,1)S(1)}, u32[]{:S(2)}, u32[]{:S(2)}) collective-permute-start(bf16[384,256]{1,0:T(8,128)(2,1)S(1)} %get-tuple-element.20), channel_id=1, source_target_pairs={{0,32},{8,40},{16,48},{24,56},{32,64},{40,72},{48,80},{56,88},{64,... | collective-permute-start | bytes 589832 | tf_op jit(solution)/shard_map/ppermute | solution.py:290
  4.9 11.4 %collective-permute-start.4 = (bf16[384,256]{1,0:T(8,128)(2,1)S(1)}, bf16[384,256]{1,0:T(8,128)(2,1)S(1)}, u32[]{:S(2)}, u32[]{:S(2)}) collective-permute-start(bf16[384,256]{1,0:T(8,128)(2,1)S(1)} %get-tuple-element.21), channel_id=1, source_target_pairs={{0,64},{8,72},{16,80},{24,88},{32,96},{40,104},{48,112},{56,120},{... | collective-permute-start | bytes 589832 | tf_op jit(solution)/shard_map/ppermute | solution.py:290
  7.8 8.6 %collective-permute-start.5 = (bf16[384,256]{1,0:T(8,128)(2,1)S(1)}, bf16[384,256]{1,0:T(8,128)(2,1)S(1)}, u32[]{:S(2)}, u32[]{:S(2)}) collective-permute-start(bf16[384,256]{1,0:T(8,128)(2,1)S(1)} %get-tuple-element.22), channel_id=1, source_target_pairs={{0,96},{8,104},{16,112},{24,120},{32,0},{40,8},{48,16},{56,24},{64... | collective-permute-start | bytes 589832 | tf_op jit(solution)/shard_map/ppermute | solution.py:290
  17.1 1.8 %collective-permute-start.6 = (bf16[2,384,256]{2,1,0:T(8,128)(2,1)S(1)}, bf16[2,384,256]{2,1,0:T(8,128)(2,1)S(1)}, u32[]{:S(2)}, u32[]{:S(2)}) collective-permute-start(bf16[2,384,256]{2,1,0:T(8,128)(2,1)S(1)} %pick.1), channel_id=1, source_target_pairs={{0,8},{8,0},{16,24},{24,16},{32,40},{40,32},{48,56},{56,48},{64,72... | collective-permute-start | bytes 1179656 | tf_op jit(solution)/shard_map/ppermute | solution.py:289
  17.2 3.2 %collective-permute-start = (bf16[400,256]{1,0:T(8,128)(2,1)S(1)}, bf16[400,256]{1,0:T(8,128)(2,1)S(1)}, u32[]{:S(2)}, u32[]{:S(2)}) collective-permute-start(bf16[400,256]{1,0:T(8,128)(2,1)S(1)} %get-tuple-element.17), channel_id=1, source_target_pairs={{0,8},{8,0},{16,24},{24,16},{32,40},{40,32},{48,56},{56,48},{64,72... | collective-permute-start | bytes 614408 | tf_op jit(solution)/shard_map/ppermute | solution.py:289
  17.8 22.8 %copy-start.1 = (bf16[256,768]{1,0:T(8,128)(2,1)S(1)}, bf16[256,768]{1,0:T(8,128)(2,1)}, u32[]{:S(2)}) copy-start(bf16[256,768]{1,0:T(8,128)(2,1)} %constant.11.clone.table_ref) | copy-start | bytes 1179652
  17.8 4.3 %collective-permute-start.2 = (bf16[400,256]{1,0:T(8,128)(2,1)S(1)}, bf16[400,256]{1,0:T(8,128)(2,1)S(1)}, u32[]{:S(2)}, u32[]{:S(2)}) collective-permute-start(bf16[400,256]{1,0:T(8,128)(2,1)S(1)} %get-tuple-element.28), channel_id=1, source_target_pairs={{0,8},{8,0},{16,24},{24,16},{32,40},{40,32},{48,56},{56,48},{64,72... | collective-permute-start | bytes 614408 | tf_op jit(solution)/shard_map/ppermute | solution.py:289
  19.7 5.7 %collective-permute-start.7 = (bf16[192,256]{1,0:T(8,128)(2,1)S(1)}, bf16[192,256]{1,0:T(8,128)(2,1)S(1)}, u32[]{:S(2)}, u32[]{:S(2)}) collective-permute-start(bf16[192,256]{1,0:T(8,128)(2,1)S(1)} %get-tuple-element.24), channel_id=1, source_target_pairs={{0,16},{8,24},{16,0},{24,8},{32,48},{40,56},{48,32},{56,40},{64,80... | collective-permute-start | bytes 294920 | tf_op jit(solution)/shard_map/ppermute | solution.py:289
  20.5 10.4 %collective-permute-start.11 = (bf16[192,256]{1,0:T(8,128)(2,1)S(1)}, bf16[192,256]{1,0:T(8,128)(2,1)S(1)}, u32[]{:S(2)}, u32[]{:S(2)}) collective-permute-start(bf16[192,256]{1,0:T(8,128)(2,1)S(1)} %get-tuple-element.26), channel_id=1, source_target_pairs={{0,16},{8,24},{16,0},{24,8},{32,48},{40,56},{48,32},{56,40},{64,80... | collective-permute-start | bytes 294920 | tf_op jit(solution)/shard_map/ppermute | solution.py:289
  26.1 8.6 %collective-permute-start.10 = (bf16[192,256]{1,0:T(8,128)(2,1)S(1)}, bf16[192,256]{1,0:T(8,128)(2,1)S(1)}, u32[]{:S(2)}, u32[]{:S(2)}) collective-permute-start(bf16[192,256]{1,0:T(8,128)(2,1)S(1)} %over_x.2.refs_0_), channel_id=1, source_target_pairs={{0,64},{8,72},{16,80},{24,88},{32,96},{40,104},{48,112},{56,120},{... | collective-permute-start | bytes 294920 | tf_op jit(solution)/shard_map/ppermute | solution.py:290
  28.8 7.4 %collective-permute-start.9 = (bf16[192,256]{1,0:T(8,128)(2,1)S(1)}, bf16[192,256]{1,0:T(8,128)(2,1)S(1)}, u32[]{:S(2)}, u32[]{:S(2)}) collective-permute-start(bf16[192,256]{1,0:T(8,128)(2,1)S(1)} %over_x.2.refs_0_), channel_id=1, source_target_pairs={{0,96},{8,104},{16,112},{24,120},{32,0},{40,8},{48,16},{56,24},{64... | collective-permute-start | bytes 294920 | tf_op jit(solution)/shard_map/ppermute | solution.py:290
  30.1 7.9 %collective-permute-start.8 = (bf16[192,256]{1,0:T(8,128)(2,1)S(1)}, bf16[192,256]{1,0:T(8,128)(2,1)S(1)}, u32[]{:S(2)}, u32[]{:S(2)}) collective-permute-start(bf16[192,256]{1,0:T(8,128)(2,1)S(1)} %over_x.2.refs_0_), channel_id=1, source_target_pairs={{0,32},{8,40},{16,48},{24,56},{32,64},{40,72},{48,80},{56,88},{64,... | collective-permute-start | bytes 294920 | tf_op jit(solution)/shard_map/ppermute | solution.py:290
  31.6 6.4 %collective-permute-start.14 = (bf16[192,256]{1,0:T(8,128)(2,1)S(1)}, bf16[192,256]{1,0:T(8,128)(2,1)S(1)}, u32[]{:S(2)}, u32[]{:S(2)}) collective-permute-start(bf16[192,256]{1,0:T(8,128)(2,1)S(1)} %over_x.3.refs_4_), channel_id=1, source_target_pairs={{0,64},{8,72},{16,80},{24,88},{32,96},{40,104},{48,112},{56,120},{... | collective-permute-start | bytes 294920 | tf_op jit(solution)/shard_map/ppermute | solution.py:290
  32.6 6.0 %collective-permute-start.13 = (bf16[192,256]{1,0:T(8,128)(2,1)S(1)}, bf16[192,256]{1,0:T(8,128)(2,1)S(1)}, u32[]{:S(2)}, u32[]{:S(2)}) collective-permute-start(bf16[192,256]{1,0:T(8,128)(2,1)S(1)} %over_x.3.refs_4_), channel_id=1, source_target_pairs={{0,96},{8,104},{16,112},{24,120},{32,0},{40,8},{48,16},{56,24},{64... | collective-permute-start | bytes 294920 | tf_op jit(solution)/shard_map/ppermute | solution.py:290
  34.7 5.8 %collective-permute-start.12 = (bf16[192,256]{1,0:T(8,128)(2,1)S(1)}, bf16[192,256]{1,0:T(8,128)(2,1)S(1)}, u32[]{:S(2)}, u32[]{:S(2)}) collective-permute-start(bf16[192,256]{1,0:T(8,128)(2,1)S(1)} %over_x.3.refs_4_), channel_id=1, source_target_pairs={{0,32},{8,40},{16,48},{24,56},{32,64},{40,72},{48,80},{56,88},{64,... | collective-permute-start | bytes 294920 | tf_op jit(solution)/shard_map/ppermute | solution.py:290
  36.2 5.6 %copy-start = (bf16[144,384]{1,0:T(8,128)(2,1)S(1)}, bf16[144,384]{1,0:T(8,128)(2,1)}, u32[]{:S(2)}) copy-start(bf16[144,384]{1,0:T(8,128)(2,1)} %constant.12.clone.back_ref) | copy-start | bytes 331780
  46.7 22.4 %copy-start.3 = (s32[1,4]{1,0:T(1,128)S(1)}, s32[1,4]{1,0:T(1,128)}, u32[]{:S(2)}) copy-start(s32[1,4]{1,0:T(1,128)} %near_ref.1) | copy-start | bytes 52
  46.7 8.3 %collective-permute-start.15 = (f32[4,72,256]{2,1,0:T(8,128)S(1)}, f32[4,72,256]{2,1,0:T(8,128)S(1)}, u32[]{:S(2)}, u32[]{:S(2)}) collective-permute-start(f32[4,72,256]{2,1,0:T(8,128)S(1)} %pairs.2.refs_0_), channel_id=1, source_target_pairs={{0,1},{1,0},{2,3},{3,2},{4,5},{5,4},{6,7},{7,6},{8,9},{9,8},{10,11... | collective-permute-start | bytes 884744 | tf_op jit(solution)/shard_map/ppermute | solution.py:346

commit v12 on v11

--- a/solution.py
+++ b/solution.py
@@ -310,13 +310,13 @@
     *mine, theirs_0, theirs_1 = pl.pallas_call(
         core_kernel, out_shape=(part,) * 4, in_specs=[SMEM] + [VMEM] * 5 + [ANY], out_specs=(VMEM,) * 4,
         compiler_params=SMALL, name="over_core",
-    )(in_hbm(owners), *got, near(give, 1), chip)
+    )(owners, *got, near(give, 1), chip)
     pieces = []
     for kept, sent in zip(mine, [near(theirs_0, 2), near(theirs_1, 2)]):
         whole = pl.pallas_call(
             chip_kernel, out_shape=part, in_specs=[SMEM] + [VMEM] * 2, out_specs=VMEM,
             compiler_params=SMALL, name="over_x",
-        )(in_hbm(owners), kept, sent)
+        )(owners, kept, sent)
         pieces += [whole] + [turn(whole, d) for d in (1, -1, 2)]
 
     listed = jnp.stack([b[ch * block:ch * block + 2 * pairs // samp] for b in blocks]).astype(jnp.int32)

time: 71 us -> 70.6 us (level)
  transfers between devices with their start and end apart: 16 -> 16, of which waited for: 8 -> 8; matrix products, arithmetic and copies ran while one was open for 0% -> 0% of each run, Pallas kernels for 13% -> 12%
where the time goes in v12:
time: 70.6 us; the launch traced here: 70.2 us
  starting transfers between devices  21.4 us (30%)
  Pallas kernels  17.9 us (25%)
  waiting for transfers between devices  16.5 us (23%)
  blocking collectives  14 us (20%)
    ppermute x9, starting transfers between devices, local(): lax.ppermute(v, CLU, [(i, (i + 4 * d) % n_clu) for i in range(n_clu)])  14 us
    all_to_all x1, blocking collectives, local(): slots = lax.all_to_all(slots, ('z', 'xl', 'core'), 0, 0)  14 us
    ppermute x9, waiting for transfers between devices, local(): lax.ppermute(v, CLU, [(i, (i + 4 * d) % n_clu) for i in range(n_clu)])  11.5 us
    pallas_call x2, Pallas kernels, local(): pl.pallas_call(functools.partial(pair_kernel, across), out_shape=shaped((...  9.69 us
    ppermute x6, starting transfers between devices, local(): lax.ppermute(v, CLU, [(i, i ^ d) for i in range(n_clu)])  4.59 us
    ppermute x6, waiting for transfers between devices, local(): lax.ppermute(v, CLU, [(i, i ^ d) for i in range(n_clu)])  4.36 us
    ppermute x1, starting transfers between devices, local(): lax.ppermute(v, STA, [(k, target(k, dz, dh, n_sta)) for k in range(n_sta)])  2.81 us
    pallas_call x1, Pallas kernels, local(): pl.pallas_call(pack_kernel, out_shape=(piece,) * 4 + (payload, payload, s...  1.7 us
  transfers between devices with their start and end apart: 16, of which 8 were waited for; matrix products, arithmetic and copies ran while one was open for 0% of the time, Pallas kernels for 12%

profile of v12, /device:TPU:0, one launch (start us, length us, event | category | flops | bytes accessed | tf_op | source)
XLA Modules:
  0.0 70.2 jit_solution(10047990714388340095)
XLA Ops:
  0.0 1.7 %pack.1 = (bf16[384,256]{1,0:T(8,128)(2,1)S(1)}, bf16[384,256]{1,0:T(8,128)(2,1)S(1)}, bf16[384,256]{1,0:T(8,128)(2,1)S(1)}, bf16[384,256]{1,0:T(8,128)(2,1)S(1)...) custom-call(bf16[1536,256]{1,0:T(8,128)(2,1)} %bitcast.15, ...), custom_call_target="tpu_custom_call" | custom-call | tf_op jit(solution)/shard_map/pack/pallas_call | solution.py:296
  1.7 1.7 %collective-permute-start.1 = (bf16[2,400,256]{2,1,0:T(8,128)(2,1)S(1)}, bf16[2,400,256]{2,1,0:T(8,128)(2,1)S(1)}, u32[]{:S(2)}, u32[]{:S(2)}) collective-permute-start(bf16[2,400,256]{2,1,0:T(8,128)(2,1)S(1)} %get-tuple-element.18), channel_id=1, source_target_pairs={{0,16},{8,24},{16,0},{24,8},{32,48},{40,56},{48,32},{56,40},{64,80... | collective-permute-start | bytes 1228808 | tf_op jit(solution)/shard_map/ppermute | solution.py:289
  3.4 1.6 %collective-permute-start.3 = (bf16[384,256]{1,0:T(8,128)(2,1)S(1)}, bf16[384,256]{1,0:T(8,128)(2,1)S(1)}, u32[]{:S(2)}, u32[]{:S(2)}) collective-permute-start(bf16[384,256]{1,0:T(8,128)(2,1)S(1)} %get-tuple-element.20), channel_id=1, source_target_pairs={{0,32},{8,40},{16,48},{24,56},{32,64},{40,72},{48,80},{56,88},{64,... | collective-permute-start | bytes 589832 | tf_op jit(solution)/shard_map/ppermute | solution.py:290
  4.9 2.9 %collective-permute-start.4 = (bf16[384,256]{1,0:T(8,128)(2,1)S(1)}, bf16[384,256]{1,0:T(8,128)(2,1)S(1)}, u32[]{:S(2)}, u32[]{:S(2)}) collective-permute-start(bf16[384,256]{1,0:T(8,128)(2,1)S(1)} %get-tuple-element.21), channel_id=1, source_target_pairs={{0,64},{8,72},{16,80},{24,88},{32,96},{40,104},{48,112},{56,120},{... | collective-permute-start | bytes 589832 | tf_op jit(solution)/shard_map/ppermute | solution.py:290
  7.8 1.4 %collective-permute-start.5 = (bf16[384,256]{1,0:T(8,128)(2,1)S(1)}, bf16[384,256]{1,0:T(8,128)(2,1)S(1)}, u32[]{:S(2)}, u32[]{:S(2)}) collective-permute-start(bf16[384,256]{1,0:T(8,128)(2,1)S(1)} %get-tuple-element.22), channel_id=1, source_target_pairs={{0,96},{8,104},{16,112},{24,120},{32,0},{40,8},{48,16},{56,24},{64... | collective-permute-start | bytes 589832 | tf_op jit(solution)/shard_map/ppermute | solution.py:290
  9.2 2.1 %collective-permute-done.3.g1 = bf16[384,256]{1,0:T(8,128)(2,1)S(1)} collective-permute-done((bf16[384,256]{1,0:T(8,128)(2,1)S(1)}, bf16[384,256]{1,0:T(8,128)(2,1)S(1)}, u32[]{:S(2)}, u32[]{:S(2)}) %collective-permute-start.3) | collective-permute-done | bytes 196640 | tf_op jit(solution)/shard_map/ppermute | solution.py:290
  11.3 5.1 %collective-permute-done.4.g2 = bf16[384,256]{1,0:T(8,128)(2,1)S(1)} collective-permute-done((bf16[384,256]{1,0:T(8,128)(2,1)S(1)}, bf16[384,256]{1,0:T(8,128)(2,1)S(1)}, u32[]{:S(2)}, u32[]{:S(2)}) %collective-permute-start.4) | collective-permute-done | bytes 196640 | tf_op jit(solution)/shard_map/ppermute | solution.py:290
  18.0 1.0 %collective-permute-done.6.got_ref = bf16[2,384,256]{2,1,0:T(8,128)(2,1)S(1)} collective-permute-done((bf16[2,384,256]{2,1,0:T(8,128)(2,1)S(1)}, bf16[2,384,256]{2,1,0:T(8,128)(2,1)S(1)}, u32[]{:S(2)}, u32[]{:S(2)}) %collective-permute-start.6) | collective-permute-done | bytes 393248 | tf_op jit(solution)/shard_map/ppermute | solution.py:289
  20.4 1.6 %collective-permute-start.11 = (bf16[192,256]{1,0:T(8,128)(2,1)S(1)}, bf16[192,256]{1,0:T(8,128)(2,1)S(1)}, u32[]{:S(2)}, u32[]{:S(2)}) collective-permute-start(bf16[192,256]{1,0:T(8,128)(2,1)S(1)} %get-tuple-element.26), channel_id=1, source_target_pairs={{0,16},{8,24},{16,0},{24,8},{32,48},{40,56},{48,32},{56,40},{64,80... | collective-permute-start | bytes 294920 | tf_op jit(solution)/shard_map/ppermute | solution.py:289
  21.9 3.4 %collective-permute-done.7.got_ref = bf16[192,256]{1,0:T(8,128)(2,1)S(1)} collective-permute-done((bf16[192,256]{1,0:T(8,128)(2,1)S(1)}, bf16[192,256]{1,0:T(8,128)(2,1)S(1)}, u32[]{:S(2)}, u32[]{:S(2)}) %collective-permute-start.7) | collective-permute-done | bytes 98336 | tf_op jit(solution)/shard_map/ppermute | solution.py:289
  25.9 2.6 %collective-permute-start.10 = (bf16[192,256]{1,0:T(8,128)(2,1)S(1)}, bf16[192,256]{1,0:T(8,128)(2,1)S(1)}, u32[]{:S(2)}, u32[]{:S(2)}) collective-permute-start(bf16[192,256]{1,0:T(8,128)(2,1)S(1)} %over_x.2.refs_0_), channel_id=1, source_target_pairs={{0,64},{8,72},{16,80},{24,88},{32,96},{40,104},{48,112},{56,120},{... | collective-permute-start | bytes 294920 | tf_op jit(solution)/shard_map/ppermute | solution.py:290
  28.6 1.3 %collective-permute-start.9 = (bf16[192,256]{1,0:T(8,128)(2,1)S(1)}, bf16[192,256]{1,0:T(8,128)(2,1)S(1)}, u32[]{:S(2)}, u32[]{:S(2)}) collective-permute-start(bf16[192,256]{1,0:T(8,128)(2,1)S(1)} %over_x.2.refs_0_), channel_id=1, source_target_pairs={{0,96},{8,104},{16,112},{24,120},{32,0},{40,8},{48,16},{56,24},{64... | collective-permute-start | bytes 294920 | tf_op jit(solution)/shard_map/ppermute | solution.py:290
  29.9 0.8 %collective-permute-start.8 = (bf16[192,256]{1,0:T(8,128)(2,1)S(1)}, bf16[192,256]{1,0:T(8,128)(2,1)S(1)}, u32[]{:S(2)}, u32[]{:S(2)}) collective-permute-start(bf16[192,256]{1,0:T(8,128)(2,1)S(1)} %over_x.2.refs_0_), channel_id=1, source_target_pairs={{0,32},{8,40},{16,48},{24,56},{32,64},{40,72},{48,80},{56,88},{64,... | collective-permute-start | bytes 294920 | tf_op jit(solution)/shard_map/ppermute | solution.py:290
  31.2 1.0 %collective-permute-start.14 = (bf16[192,256]{1,0:T(8,128)(2,1)S(1)}, bf16[192,256]{1,0:T(8,128)(2,1)S(1)}, u32[]{:S(2)}, u32[]{:S(2)}) collective-permute-start(bf16[192,256]{1,0:T(8,128)(2,1)S(1)} %over_x.3.refs_4_), channel_id=1, source_target_pairs={{0,64},{8,72},{16,80},{24,88},{32,96},{40,104},{48,112},{56,120},{... | collective-permute-start | bytes 294920 | tf_op jit(solution)/shard_map/ppermute | solution.py:290
  32.3 2.1 %collective-permute-start.13 = (bf16[192,256]{1,0:T(8,128)(2,1)S(1)}, bf16[192,256]{1,0:T(8,128)(2,1)S(1)}, u32[]{:S(2)}, u32[]{:S(2)}) collective-permute-start(bf16[192,256]{1,0:T(8,128)(2,1)S(1)} %over_x.3.refs_4_), channel_id=1, source_target_pairs={{0,96},{8,104},{16,112},{24,120},{32,0},{40,8},{48,16},{56,24},{64... | collective-permute-start | bytes 294920 | tf_op jit(solution)/shard_map/ppermute | solution.py:290
  34.7 1.1 %left.1 = f32[6144,128]{1,0:T(8,128)S(1)} custom-call(bf16[256,768]{1,0:T(8,128)(2,1)S(1)} %copy-done.2, bf16[400,256]{1,0:T(8,128)(2,1)S(1)} %get-tuple-element.16.b0, bf16[400,256]{1,0:T(8,128)(2,1)S(1)} %collective-permute-done.b1, bf16[400,256]{1,0:T(8,128)(2,1)S(1)} %get-tuple-element.27.b2, bf16[400,256]{1,0:T(8,128)(2,1)S(1)} %collective-permute-done.2.b3), custom_call_target="tpu_custom_call" | custom-call | flops 603979776 | bytes 4000000 | tf_op jit(solution)/shard_map/left/pallas_call | solution.py:329
  35.9 1.9 %collective-permute-done.8.refs_1_ = bf16[192,256]{1,0:T(8,128)(2,1)S(1)} collective-permute-done((bf16[192,256]{1,0:T(8,128)(2,1)S(1)}, bf16[192,256]{1,0:T(8,128)(2,1)S(1)}, u32[]{:S(2)}, u32[]{:S(2)}) %collective-permute-start.8) | collective-permute-done | bytes 98336 | tf_op jit(solution)/shard_map/ppermute | solution.py:290
  38.3 1.9 %collective-permute-done.12.refs_5_ = bf16[192,256]{1,0:T(8,128)(2,1)S(1)} collective-permute-done((bf16[192,256]{1,0:T(8,128)(2,1)S(1)}, bf16[192,256]{1,0:T(8,128)(2,1)S(1)}, u32[]{:S(2)}, u32[]{:S(2)}) %collective-permute-start.12) | collective-permute-done | bytes 98336 | tf_op jit(solution)/shard_map/ppermute | solution.py:290
  40.2 1.3 %right.1 = f32[6144,128]{1,0:T(8,128)S(1)} custom-call(bf16[256,768]{1,0:T(8,128)(2,1)S(1)} %copy-done.1, bf16[192,256]{1,0:T(8,128)(2,1)S(1)} %over_x.2.refs_0_, bf16[192,256]{1,0:T(8,128)(2,1)S(1)} %collective-permute-done.8.refs_1_, bf16[192,256]{1,0:T(8,128)(2,1)S(1)} %collective-permute-done.9.refs_2_, ...), custom_call_target="tpu_custom_call" | custom-call | flops 603979776 | bytes 4000000 | tf_op jit(solution)/shard_map/right/pallas_call | solution.py:333
  41.5 4.9 %pairs.2.refs_0_ = f32[4,72,256]{2,1,0:T(8,128)S(1)} custom-call(s32[2048]{0:T(1024)S(1)} %add.14.local_ref, s32[2048]{0:T(1024)S(1)} %bitcast.13, f32[6144,128]{1,0:T(8,128)S(1)} %left.1, f32[6144,128]{1,0:T(8,128)S(1)} %right.1, bf16[144,384]{1,0:T(8,128)(2,1)S(1)} %copy-done), custom_call_target="tpu_custom_call" | custom-call | flops 603979776 | bytes 4000000 | tf_op jit(solution)/shard_map/pairs/pallas_call | solution.py:340
  46.4 2.8 %collective-permute-start.15 = (f32[4,72,256]{2,1,0:T(8,128)S(1)}, f32[4,72,256]{2,1,0:T(8,128)S(1)}, u32[]{:S(2)}, u32[]{:S(2)}) collective-permute-start(f32[4,72,256]{2,1,0:T(8,128)S(1)} %pairs.2.refs_0_), channel_id=1, source_target_pairs={{0,1},{1,0},{2,3},{3,2},{4,5},{5,4},{6,7},{7,6},{8,9},{9,8},{10,11... | collective-permute-start | bytes 884744 | tf_op jit(solution)/shard_map/ppermute | solution.py:346
  49.2 4.8 %pairs.3.b_ref = f32[4,72,256]{2,1,0:T(8,128)S(1)} custom-call(s32[2048]{0:T(1024)S(1)} %add.14.local_ref, s32[2048]{0:T(1024)S(1)} %bitcast.14, f32[6144,128]{1,0:T(8,128)S(1)} %left.1, f32[6144,128]{1,0:T(8,128)S(1)} %right.1, bf16[144,384]{1,0:T(8,128)(2,1)S(1)} %copy-done, f32[4,72,256]{2,1,0:T(8,128)S(1)} %pairs.2.refs_0_), custom_call_target="tpu_custom_call" | custom-call | flops 603979776 | bytes 4000000 | tf_op jit(solution)/shard_map/pairs/pallas_call | solution.py:340
  54.8 14.0 %all_to_all.5.got_ref = f32[16,40,128]{2,1,0:T(8,128)S(1)} all-to-all(f32[16,40,128]{2,1,0:T(8,128)S(1)} %add.16), channel_id=1, replica_groups=mesh['y'=4,'xl'=2,'core'=2,'z'=4,'xh'=2] {'z','xl','core'}, dimensions={0} | all-to-all | bytes 655360 | tf_op jit(solution)/shard_map/all_to_all | solution.py:351
  68.8 1.4 %finish.1 = f32[1,4,64,65]{3,2,1,0:T(8,128)} custom-call(s32[1,4]{1,0:T(1,128)S(1)} %copy-done.4, f32[16,40,128]{2,1,0:T(8,128)S(1)} %all_to_all.5.got_ref), custom_call_target="tpu_custom_call" | custom-call | tf_op jit(solution)/shard_map/finish/pallas_call | solution.py:352
  (45 shorter events, 5.8 us)
Async XLA Ops:
  0.0 34.7 %copy-start.2 = (bf16[256,768]{1,0:T(8,128)(2,1)S(1)}, bf16[256,768]{1,0:T(8,128)(2,1)}, u32[]{:S(2)}) copy-start(bf16[256,768]{1,0:T(8,128)(2,1)} %constant.10.clone.table_ref) | copy-start | bytes 1179652
  0.0 19.0 %copy-start.3 = (s32[4]{0:T(128)S(1)}, s32[4]{0:T(128)}, u32[]{:S(2)}) copy-start(s32[4]{0:T(128)} %owners_ref.7) | copy-start | bytes 52
  1.7 16.0 %collective-permute-start.1 = (bf16[2,400,256]{2,1,0:T(8,128)(2,1)S(1)}, bf16[2,400,256]{2,1,0:T(8,128)(2,1)S(1)}, u32[]{:S(2)}, u32[]{:S(2)}) collective-permute-start(bf16[2,400,256]{2,1,0:T(8,128)(2,1)S(1)} %get-tuple-element.18), channel_id=1, source_target_pairs={{0,16},{8,24},{16,0},{24,8},{32,48},{40,56},{48,32},{56,40},{64,80... | collective-permute-start | bytes 1228808 | tf_op jit(solution)/shard_map/ppermute | solution.py:289
  3.4 7.9 %collective-permute-start.3 = (bf16[384,256]{1,0:T(8,128)(2,1)S(1)}, bf16[384,256]{1,0:T(8,128)(2,1)S(1)}, u32[]{:S(2)}, u32[]{:S(2)}) collective-permute-start(bf16[384,256]{1,0:T(8,128)(2,1)S(1)} %get-tuple-element.20), channel_id=1, source_target_pairs={{0,32},{8,40},{16,48},{24,56},{32,64},{40,72},{48,80},{56,88},{64,... | collective-permute-start | bytes 589832 | tf_op jit(solution)/shard_map/ppermute | solution.py:290
  4.9 11.4 %collective-permute-start.4 = (bf16[384,256]{1,0:T(8,128)(2,1)S(1)}, bf16[384,256]{1,0:T(8,128)(2,1)S(1)}, u32[]{:S(2)}, u32[]{:S(2)}) collective-permute-start(bf16[384,256]{1,0:T(8,128)(2,1)S(1)} %get-tuple-element.21), channel_id=1, source_target_pairs={{0,64},{8,72},{16,80},{24,88},{32,96},{40,104},{48,112},{56,120},{... | collective-permute-start | bytes 589832 | tf_op jit(solution)/shard_map/ppermute | solution.py:290
  7.8 8.6 %collective-permute-start.5 = (bf16[384,256]{1,0:T(8,128)(2,1)S(1)}, bf16[384,256]{1,0:T(8,128)(2,1)S(1)}, u32[]{:S(2)}, u32[]{:S(2)}) collective-permute-start(bf16[384,256]{1,0:T(8,128)(2,1)S(1)} %get-tuple-element.22), channel_id=1, source_target_pairs={{0,96},{8,104},{16,112},{24,120},{32,0},{40,8},{48,16},{56,24},{64... | collective-permute-start | bytes 589832 | tf_op jit(solution)/shard_map/ppermute | solution.py:290
  17.2 1.8 %collective-permute-start.6 = (bf16[2,384,256]{2,1,0:T(8,128)(2,1)S(1)}, bf16[2,384,256]{2,1,0:T(8,128)(2,1)S(1)}, u32[]{:S(2)}, u32[]{:S(2)}) collective-permute-start(bf16[2,384,256]{2,1,0:T(8,128)(2,1)S(1)} %pick.1), channel_id=1, source_target_pairs={{0,8},{8,0},{16,24},{24,16},{32,40},{40,32},{48,56},{56,48},{64,72... | collective-permute-start | bytes 1179656 | tf_op jit(solution)/shard_map/ppermute | solution.py:289
  17.2 3.1 %collective-permute-start = (bf16[400,256]{1,0:T(8,128)(2,1)S(1)}, bf16[400,256]{1,0:T(8,128)(2,1)S(1)}, u32[]{:S(2)}, u32[]{:S(2)}) collective-permute-start(bf16[400,256]{1,0:T(8,128)(2,1)S(1)} %get-tuple-element.17), channel_id=1, source_target_pairs={{0,8},{8,0},{16,24},{24,16},{32,40},{40,32},{48,56},{56,48},{64,72... | collective-permute-start | bytes 614408 | tf_op jit(solution)/shard_map/ppermute | solution.py:289
  17.8 22.4 %copy-start.1 = (bf16[256,768]{1,0:T(8,128)(2,1)S(1)}, bf16[256,768]{1,0:T(8,128)(2,1)}, u32[]{:S(2)}) copy-start(bf16[256,768]{1,0:T(8,128)(2,1)} %constant.11.clone.table_ref) | copy-start | bytes 1179652
  17.8 4.1 %collective-permute-start.2 = (bf16[400,256]{1,0:T(8,128)(2,1)S(1)}, bf16[400,256]{1,0:T(8,128)(2,1)S(1)}, u32[]{:S(2)}, u32[]{:S(2)}) collective-permute-start(bf16[400,256]{1,0:T(8,128)(2,1)S(1)} %get-tuple-element.28), channel_id=1, source_target_pairs={{0,8},{8,0},{16,24},{24,16},{32,40},{40,32},{48,56},{56,48},{64,72... | collective-permute-start | bytes 614408 | tf_op jit(solution)/shard_map/ppermute | solution.py:289
  19.6 5.7 %collective-permute-start.7 = (bf16[192,256]{1,0:T(8,128)(2,1)S(1)}, bf16[192,256]{1,0:T(8,128)(2,1)S(1)}, u32[]{:S(2)}, u32[]{:S(2)}) collective-permute-start(bf16[192,256]{1,0:T(8,128)(2,1)S(1)} %get-tuple-element.24), channel_id=1, source_target_pairs={{0,16},{8,24},{16,0},{24,8},{32,48},{40,56},{48,32},{56,40},{64,80... | collective-permute-start | bytes 294920 | tf_op jit(solution)/shard_map/ppermute | solution.py:289
  20.4 10.3 %collective-permute-start.11 = (bf16[192,256]{1,0:T(8,128)(2,1)S(1)}, bf16[192,256]{1,0:T(8,128)(2,1)S(1)}, u32[]{:S(2)}, u32[]{:S(2)}) collective-permute-start(bf16[192,256]{1,0:T(8,128)(2,1)S(1)} %get-tuple-element.26), channel_id=1, source_target_pairs={{0,16},{8,24},{16,0},{24,8},{32,48},{40,56},{48,32},{56,40},{64,80... | collective-permute-start | bytes 294920 | tf_op jit(solution)/shard_map/ppermute | solution.py:289
  25.9 8.5 %collective-permute-start.10 = (bf16[192,256]{1,0:T(8,128)(2,1)S(1)}, bf16[192,256]{1,0:T(8,128)(2,1)S(1)}, u32[]{:S(2)}, u32[]{:S(2)}) collective-permute-start(bf16[192,256]{1,0:T(8,128)(2,1)S(1)} %over_x.2.refs_0_), channel_id=1, source_target_pairs={{0,64},{8,72},{16,80},{24,88},{32,96},{40,104},{48,112},{56,120},{... | collective-permute-start | bytes 294920 | tf_op jit(solution)/shard_map/ppermute | solution.py:290
  28.6 7.3 %collective-permute-start.9 = (bf16[192,256]{1,0:T(8,128)(2,1)S(1)}, bf16[192,256]{1,0:T(8,128)(2,1)S(1)}, u32[]{:S(2)}, u32[]{:S(2)}) collective-permute-start(bf16[192,256]{1,0:T(8,128)(2,1)S(1)} %over_x.2.refs_0_), channel_id=1, source_target_pairs={{0,96},{8,104},{16,112},{24,120},{32,0},{40,8},{48,16},{56,24},{64... | collective-permute-start | bytes 294920 | tf_op jit(solution)/shard_map/ppermute | solution.py:290
  29.9 7.8 %collective-permute-start.8 = (bf16[192,256]{1,0:T(8,128)(2,1)S(1)}, bf16[192,256]{1,0:T(8,128)(2,1)S(1)}, u32[]{:S(2)}, u32[]{:S(2)}) collective-permute-start(bf16[192,256]{1,0:T(8,128)(2,1)S(1)} %over_x.2.refs_0_), channel_id=1, source_target_pairs={{0,32},{8,40},{16,48},{24,56},{32,64},{40,72},{48,80},{56,88},{64,... | collective-permute-start | bytes 294920 | tf_op jit(solution)/shard_map/ppermute | solution.py:290
  31.2 6.5 %collective-permute-start.14 = (bf16[192,256]{1,0:T(8,128)(2,1)S(1)}, bf16[192,256]{1,0:T(8,128)(2,1)S(1)}, u32[]{:S(2)}, u32[]{:S(2)}) collective-permute-start(bf16[192,256]{1,0:T(8,128)(2,1)S(1)} %over_x.3.refs_4_), channel_id=1, source_target_pairs={{0,64},{8,72},{16,80},{24,88},{32,96},{40,104},{48,112},{56,120},{... | collective-permute-start | bytes 294920 | tf_op jit(solution)/shard_map/ppermute | solution.py:290
  32.3 6.0 %collective-permute-start.13 = (bf16[192,256]{1,0:T(8,128)(2,1)S(1)}, bf16[192,256]{1,0:T(8,128)(2,1)S(1)}, u32[]{:S(2)}, u32[]{:S(2)}) collective-permute-start(bf16[192,256]{1,0:T(8,128)(2,1)S(1)} %over_x.3.refs_4_), channel_id=1, source_target_pairs={{0,96},{8,104},{16,112},{24,120},{32,0},{40,8},{48,16},{56,24},{64... | collective-permute-start | bytes 294920 | tf_op jit(solution)/shard_map/ppermute | solution.py:290
  34.3 5.8 %collective-permute-start.12 = (bf16[192,256]{1,0:T(8,128)(2,1)S(1)}, bf16[192,256]{1,0:T(8,128)(2,1)S(1)}, u32[]{:S(2)}, u32[]{:S(2)}) collective-permute-start(bf16[192,256]{1,0:T(8,128)(2,1)S(1)} %over_x.3.refs_4_), channel_id=1, source_target_pairs={{0,32},{8,40},{16,48},{24,56},{32,64},{40,72},{48,80},{56,88},{64,... | collective-permute-start | bytes 294920 | tf_op jit(solution)/shard_map/ppermute | solution.py:290
  35.8 5.6 %copy-start = (bf16[144,384]{1,0:T(8,128)(2,1)S(1)}, bf16[144,384]{1,0:T(8,128)(2,1)}, u32[]{:S(2)}) copy-start(bf16[144,384]{1,0:T(8,128)(2,1)} %constant.12.clone.back_ref) | copy-start | bytes 331780
  46.3 22.4 %copy-start.4 = (s32[1,4]{1,0:T(1,128)S(1)}, s32[1,4]{1,0:T(1,128)}, u32[]{:S(2)}) copy-start(s32[1,4]{1,0:T(1,128)} %near_ref.1) | copy-start | bytes 52
  46.4 8.3 %collective-permute-start.15 = (f32[4,72,256]{2,1,0:T(8,128)S(1)}, f32[4,72,256]{2,1,0:T(8,128)S(1)}, u32[]{:S(2)}, u32[]{:S(2)}) collective-permute-start(f32[4,72,256]{2,1,0:T(8,128)S(1)} %pairs.2.refs_0_), channel_id=1, source_target_pairs={{0,1},{1,0},{2,3},{3,2},{4,5},{5,4},{6,7},{7,6},{8,9},{9,8},{10,11... | collective-permute-start | bytes 884744 | tf_op jit(solution)/shard_map/ppermute | solution.py:346
